TPU v7x, 32 devices: a whole 2x2x4 slice. The times are simulated.
32 devices in a mesh: seq: 8 (over z, y), batch: 4 (over x, core).
Axes of the slice: x: 2, y: 2, z: 4, core: 2. Of those that a mesh axis runs over, the one named last changes fastest.
Arguments:
- tokens: bfloat16 [8, 2048, 512], P('batch', 'seq'), may hold values from -6 to 6
- norm_gain: bfloat16 [2, 512], P(None, 'seq'), may hold values from 0.099609375 to 1.8984375
- w_forget: bfloat16 [2, 512, 1024], P(None, 'seq', 'batch'), may hold values from -0.25 to 0.25
- w_input: bfloat16 [2, 512, 1024], P(None, 'seq', 'batch'), may hold values from -0.25 to 0.25
- w_cand: bfloat16 [2, 512, 1024], P(None, 'seq', 'batch'), may hold values from -0.25 to 0.25
- forget_bias: bfloat16 [2, 1024], P(None, 'seq'), may hold values from 1 to 4
- input_bias: bfloat16 [2, 1024], P(None, 'seq'), may hold values from -10 to -4
- w_out: bfloat16 [2, 1024, 512], P(None, 'seq', 'batch'), may hold values from -0.1875 to 0.1875
- mlp_gain: bfloat16 [2, 512], P(None, 'seq'), may hold values from 0.099609375 to 1.8984375
- w_up: bfloat16 [2, 512, 2048], P(None, 'seq', 'batch'), may hold values from -0.25 to 0.25
- w_down: bfloat16 [2, 2048, 512], P(None, 'seq', 'batch'), may hold values from -0.125 to 0.125
- cotangent: bfloat16 [8, 2048, 512], P('batch', 'seq'), may hold values from -6 to 6
Outputs:
- output: bfloat16 [8, 2048, 512], P('batch', 'seq')
- grad_tokens: bfloat16 [8, 2048, 512], P('batch', 'seq')
- grad_norm_gain: float32 [2, 512], P(None, 'seq')
- grad_w_forget: float32 [2, 512, 1024], P(None, 'seq', 'batch')
- grad_w_input: float32 [2, 512, 1024], P(None, 'seq', 'batch')
- grad_w_cand: float32 [2, 512, 1024], P(None, 'seq', 'batch')
- grad_forget_bias: float32 [2, 1024], P(None, 'seq')
- grad_input_bias: float32 [2, 1024], P(None, 'seq')
- grad_w_out: float32 [2, 1024, 512], P(None, 'seq', 'batch')
- grad_mlp_gain: float32 [2, 512], P(None, 'seq')
- grad_w_up: float32 [2, 512, 2048], P(None, 'seq', 'batch')
- grad_w_down: float32 [2, 2048, 512], P(None, 'seq', 'batch')
All inputs are finite; a program needn't handle non-finite values.
Results may differ from a plain program's by a relative error of at most 0.011.
Values may be sent and summed in bfloat16 or wider, within the bound.
No kernel may reach another device: no remote copies, remote signals or barrier semaphores. Data moves between devices by JAX's collectives and lax.ppermute only.
A program may use at most 192 MiB of HBM per device.

v0:
```python
import jax
import jax.numpy as jnp
from jax import lax
from jax.sharding import PartitionSpec as P

LAYERS = 2
MICRO = 2


epsilon = 1e-05
vector_members = (0, 4, 5, 7)


def entering_2(value, axis, join, neutral, backward):
    count, mine = (lax.axis_size(axis), lax.axis_index(axis))
    pieces = jax.tree.map(lambda part: lax.all_gather(part, axis), value)
    if backward:
        pieces = jax.tree.map(lambda part: part[::-1], pieces)
        mine = count - 1 - mine
    so_far = jax.tree.map(
        lambda part, zero: jnp.full_like(part, 0) + jnp.asarray(zero, part.dtype), value, neutral
    )

    def turn(position, so_far):
        longer = join(so_far, jax.tree.map(lambda part: part[position], pieces))
        return jax.tree.map(lambda new, old: jnp.where(position < mine, new, old), longer, so_far)

    return lax.fori_loop(0, count - 1, turn, so_far)


def as_sent(array):

    def short(part):
        return part.astype(jnp.bfloat16) if part.dtype == jnp.float32 else part

    return jax.tree.map(short, array)


def rms_norm(values, gain_vec):
    return (
        values * lax.rsqrt(jnp.mean(values * values, axis=-1, keepdims=True) + epsilon) * gain_vec
    )


def link(earlier, latter):
    return (earlier[0] * latter[0], latter[0] * earlier[1] + latter[1])


def gate_pair(z_forget, z_input, z_cand):
    differ = jax.nn.softplus(-z_forget) - jax.nn.softplus(-z_input)
    return (jax.nn.sigmoid(-differ), jax.nn.sigmoid(differ) * jax.nn.softplus(z_cand))


def gelu_exact(values):
    return jax.nn.gelu(values, approximate=False)


def matmul(form, left, right):
    return jnp.einsum(form, left, right, preferred_element_type=jnp.float32)


def flatten_layer(shards, layer_at):
    return tuple((member[layer_at].reshape(1, -1) for member in shards))


def assemble(gathered, shards, seq_count, batch_count):
    pieces = []
    for member_at in range(len(gathered)):
        whole = gathered[member_at]
        if member_at in vector_members:
            width = shards[member_at].shape[1]
            pieces.append(
                whole.reshape(seq_count, batch_count, width)[:, 0].reshape(seq_count * width)
            )
        else:
            row_count, col_count = shards[member_at].shape[1:]
            pieces.append(
                whole.reshape(seq_count, batch_count, row_count, col_count)
                .transpose(0, 2, 1, 3)
                .reshape(seq_count * row_count, batch_count * col_count)
            )
    return tuple(pieces)


def layer_forward(stream, weights):
    gain_one, forget_w, input_w, cand_w, forget_b, input_b, out_w, gain_two, up_w, down_w = weights
    normed = rms_norm(stream, gain_one.astype(jnp.float32)).astype(jnp.bfloat16)
    z_forget = matmul("std,dh->sth", normed, forget_w) + forget_b.astype(jnp.float32)
    z_input = matmul("std,dh->sth", normed, input_w) + input_b.astype(jnp.float32)
    z_cand = matmul("std,dh->sth", normed, cand_w)
    decay, inflow = gate_pair(z_forget, z_input, z_cand)
    prefix, local_state = lax.associative_scan(link, (decay, inflow), axis=1)
    unity = jnp.ones_like(decay[:, 0])
    before = entering_2(
        (prefix[:, -1], local_state[:, -1]), "seq", link, (unity, jnp.zeros_like(unity)), False
    )
    entering = before[1]
    hidden = local_state + prefix * entering[:, None]
    hidden_b = hidden.astype(jnp.bfloat16)
    middle = stream + matmul("sth,hd->std", hidden_b, out_w)
    normed_two = rms_norm(middle, gain_two.astype(jnp.float32)).astype(jnp.bfloat16)
    pre_act = matmul("std,dh->sth", normed_two, up_w)
    act_b = gelu_exact(pre_act).astype(jnp.bfloat16)
    result = middle + matmul("sth,hd->std", act_b, down_w)
    kept = (
        stream,
        normed,
        z_forget,
        z_input,
        z_cand,
        decay,
        hidden,
        entering,
        hidden_b,
        middle,
        normed_two,
        pre_act,
        act_b,
    )
    return (result, kept)


def layer_backward(grad_out, weights, kept):
    gain_one, forget_w, input_w, cand_w, forget_b, input_b, out_w, gain_two, up_w, down_w = weights
    (
        stream,
        normed,
        z_forget,
        z_input,
        z_cand,
        decay,
        hidden,
        entering,
        hidden_b,
        middle,
        normed_two,
        pre_act,
        act_b,
    ) = kept
    grad_out_b = grad_out.astype(jnp.bfloat16)
    grad_down = matmul("sth,std->hd", act_b, grad_out_b)
    grad_act = matmul("std,hd->sth", grad_out_b, down_w)
    gelu_back = jax.vjp(gelu_exact, pre_act)[1]
    grad_pre = gelu_back(grad_act)[0].astype(jnp.bfloat16)
    grad_up = matmul("std,sth->dh", normed_two, grad_pre)
    grad_normed_two = matmul("sth,dh->std", grad_pre, up_w)
    norm_back_two = jax.vjp(rms_norm, middle, gain_two.astype(jnp.float32))[1]
    grad_mid_part, grad_gain_two = norm_back_two(grad_normed_two)
    grad_mid = grad_out + grad_mid_part
    grad_mid_b = grad_mid.astype(jnp.bfloat16)
    grad_outw = matmul("sth,std->hd", hidden_b, grad_mid_b)
    grad_hidden = matmul("std,hd->sth", grad_mid_b, out_w)
    unity = jnp.ones_like(decay[:, 0])
    onward = jnp.concatenate([decay[:, 1:], unity[:, None]], axis=1)
    tail_prod, local_grad = lax.associative_scan(link, (onward, grad_hidden), reverse=True, axis=1)
    leading = decay[:, 0]
    after = entering_2(
        (leading * tail_prod[:, 0], leading * local_grad[:, 0]),
        "seq",
        link,
        (unity, jnp.zeros_like(unity)),
        True,
    )
    grad_state = local_grad + tail_prod * after[1][:, None]
    previous = jnp.concatenate([entering[:, None], hidden[:, :-1]], axis=1)
    gate_back = jax.vjp(gate_pair, z_forget, z_input, z_cand)[1]
    grad_zf, grad_zi, grad_zc = gate_back((grad_state * previous, grad_state))
    grad_zf = grad_zf.astype(jnp.bfloat16)
    grad_zi = grad_zi.astype(jnp.bfloat16)
    grad_zc = grad_zc.astype(jnp.bfloat16)
    grad_fbias = jnp.sum(grad_zf.astype(jnp.float32), axis=(0, 1))
    grad_ibias = jnp.sum(grad_zi.astype(jnp.float32), axis=(0, 1))
    grad_forget = matmul("std,sth->dh", normed, grad_zf)
    grad_input = matmul("std,sth->dh", normed, grad_zi)
    grad_cand = matmul("std,sth->dh", normed, grad_zc)
    grad_normed = (
        matmul("sth,dh->std", grad_zf, forget_w)
        + matmul("sth,dh->std", grad_zi, input_w)
        + matmul("sth,dh->std", grad_zc, cand_w)
    )
    norm_back_one = jax.vjp(rms_norm, stream, gain_one.astype(jnp.float32))[1]
    grad_in_part, grad_gain_one = norm_back_one(grad_normed)
    grads = (
        grad_gain_one,
        grad_forget,
        grad_input,
        grad_cand,
        grad_fbias,
        grad_ibias,
        grad_outw,
        grad_gain_two,
        grad_up,
        grad_down,
    )
    return (grad_mid + grad_in_part, grads)


def spread_layer(totals, seq_count, batch_count):
    pieces = []
    for member_at in range(len(totals)):
        whole = totals[member_at]
        if member_at in vector_members:
            width = whole.shape[0] // seq_count
            pieces.append(
                jnp.broadcast_to(
                    whole.reshape(seq_count, 1, width), (seq_count, batch_count, width)
                ).reshape(seq_count * batch_count, width)
            )
        else:
            row_count = whole.shape[0] // seq_count
            col_count = whole.shape[1] // batch_count
            pieces.append(
                whole.reshape(seq_count, row_count, batch_count, col_count)
                .transpose(0, 2, 1, 3)
                .reshape(seq_count * batch_count, row_count * col_count)
            )
    return tuple(pieces)


def body(
    tokens,
    norm_gain,
    w_forget,
    w_input,
    w_cand,
    forget_bias,
    input_bias,
    w_out,
    mlp_gain,
    w_up,
    w_down,
    cotangent,
):
    shards = (
        norm_gain,
        w_forget,
        w_input,
        w_cand,
        forget_bias,
        input_bias,
        w_out,
        mlp_gain,
        w_up,
        w_down,
    )
    seq_count = lax.axis_size("seq")
    batch_count = lax.axis_size("batch")
    totals = []
    for layer_at in range(LAYERS):
        zeros_list = []
        for member_at in range(len(shards)):
            if member_at in vector_members:
                zeros_list.append(jnp.zeros((seq_count * shards[member_at].shape[1],), jnp.float32))
            else:
                zeros_list.append(
                    jnp.zeros(
                        (
                            seq_count * shards[member_at].shape[1],
                            batch_count * shards[member_at].shape[2],
                        ),
                        jnp.float32,
                    )
                )
        totals.append(tuple(zeros_list))
    share = tokens.shape[0] // MICRO
    outputs = []
    input_grads = []
    for micro_at in range(MICRO):
        current = [
            assemble(
                lax.all_gather(
                    as_sent(flatten_layer(shards, layer_at)), ("seq", "batch"), axis=0, tiled=True
                ),
                shards,
                seq_count,
                batch_count,
            )
            for layer_at in range(LAYERS)
        ]
        stream = tokens[micro_at * share : (micro_at + 1) * share].astype(jnp.float32)
        saved = []
        for layer_at in range(LAYERS):
            stream, kept = layer_forward(stream, current[layer_at])
            saved.append(kept)
        outputs.append(stream.astype(jnp.bfloat16))
        grad_stream = cotangent[micro_at * share : (micro_at + 1) * share].astype(jnp.float32)
        for layer_at in reversed(range(LAYERS)):
            grad_stream, layer_grads = layer_backward(
                grad_stream, current[layer_at], saved[layer_at]
            )
            totals[layer_at] = tuple(
                (total + fresh for total, fresh in zip(totals[layer_at], layer_grads))
            )
        input_grads.append(grad_stream.astype(jnp.bfloat16))
    reduced = []
    for layer_at in range(LAYERS):
        summed = lax.psum_scatter(
            spread_layer(totals[layer_at], seq_count, batch_count),
            ("seq", "batch"),
            scatter_dimension=0,
            tiled=True,
        )
        reduced.append(
            tuple(
                (
                    summed[member_at].reshape(shards[member_at].shape[1:])
                    for member_at in range(len(shards))
                )
            )
        )
    local_grads = tuple(
        (
            jnp.stack([reduced[layer_at][member_at] for layer_at in range(LAYERS)])
            for member_at in range(len(shards))
        )
    )
    return (jnp.concatenate(outputs, axis=0), jnp.concatenate(input_grads, axis=0)) + local_grads


def solution(mesh):
    return jax.shard_map(
        body,
        mesh=mesh,
        in_specs=(
            P("batch", "seq", None),
            P(None, "seq"),
            P(None, "seq", "batch"),
            P(None, "seq", "batch"),
            P(None, "seq", "batch"),
            P(None, "seq"),
            P(None, "seq"),
            P(None, "seq", "batch"),
            P(None, "seq"),
            P(None, "seq", "batch"),
            P(None, "seq", "batch"),
            P("batch", "seq", None),
        ),
        out_specs=(
            P("batch", "seq", None),
            P("batch", "seq", None),
            P(None, "seq"),
            P(None, "seq", "batch"),
            P(None, "seq", "batch"),
            P(None, "seq", "batch"),
            P(None, "seq"),
            P(None, "seq"),
            P(None, "seq", "batch"),
            P(None, "seq"),
            P(None, "seq", "batch"),
            P(None, "seq", "batch"),
        ),
        check_vma=False,
    )
```

profile of v0, /device:TPU:0, one launch (start us, length us, event | category | flops | bytes accessed | tf_op | source)
XLA Modules:
  0.0 3091.3 jit_solution(1051961580755494533)
XLA Ops:
  21.1 43.0 %all-gather = bf16[32,1,64]{2,1,0:T(2,128)(2,1)S(1)} all-gather(bf16[1,1,64]{2,1,0:T(2,128)(2,1)S(1)} %get-tuple-element.1439), channel_id=1, replica_groups=mesh['seq'=8,'batch'=4] {'seq','batch'}, dimensions={0}, use_global_device_ids=true | all-gather | bytes 4224 | tf_op jit(solution)/shard_map/all_gather | solution.py:271
  64.2 36.4 %all-gather.4 = bf16[32,1,128]{2,1,0:T(2,128)(2,1)S(1)} all-gather(bf16[1,1,128]{2,1,0:T(2,128)(2,1)S(1)} %get-tuple-element.1437), channel_id=1, replica_groups=mesh['seq'=8,'batch'=4] {'seq','batch'}, dimensions={0}, use_global_device_ids=true | all-gather | bytes 8448 | tf_op jit(solution)/shard_map/all_gather | solution.py:271
  100.7 37.8 %all-gather.2 = bf16[32,1,128]{2,1,0:T(2,128)(2,1)S(1)} all-gather(bf16[1,1,128]{2,1,0:T(2,128)(2,1)S(1)} %get-tuple-element.1435), channel_id=1, replica_groups=mesh['seq'=8,'batch'=4] {'seq','batch'}, dimensions={0}, use_global_device_ids=true | all-gather | bytes 8448 | tf_op jit(solution)/shard_map/all_gather | solution.py:271
  138.6 36.4 %all-gather.7 = bf16[32,1,64]{2,1,0:T(2,128)(2,1)S(1)} all-gather(bf16[1,1,64]{2,1,0:T(2,128)(2,1)S(1)} %get-tuple-element.1433), channel_id=1, replica_groups=mesh['seq'=8,'batch'=4] {'seq','batch'}, dimensions={0}, use_global_device_ids=true | all-gather | bytes 4224 | tf_op jit(solution)/shard_map/all_gather | solution.py:271
  176.3 37.8 %all-gather.10 = bf16[32,1,64]{2,1,0:T(2,128)(2,1)S(1)} all-gather(bf16[1,1,64]{2,1,0:T(2,128)(2,1)S(1)} %get-tuple-element.1438), channel_id=1, replica_groups=mesh['seq'=8,'batch'=4] {'seq','batch'}, dimensions={0}, use_global_device_ids=true | all-gather | bytes 4224 | tf_op jit(solution)/shard_map/all_gather | solution.py:271
  214.7 36.4 %all-gather.14 = bf16[32,1,128]{2,1,0:T(2,128)(2,1)S(1)} all-gather(bf16[1,1,128]{2,1,0:T(2,128)(2,1)S(1)} %get-tuple-element.1436), channel_id=1, replica_groups=mesh['seq'=8,'batch'=4] {'seq','batch'}, dimensions={0}, use_global_device_ids=true | all-gather | bytes 8448 | tf_op jit(solution)/shard_map/all_gather | solution.py:271
  251.7 37.8 %all-gather.12 = bf16[32,1,128]{2,1,0:T(2,128)(2,1)S(1)} all-gather(bf16[1,1,128]{2,1,0:T(2,128)(2,1)S(1)} %get-tuple-element.1434), channel_id=1, replica_groups=mesh['seq'=8,'batch'=4] {'seq','batch'}, dimensions={0}, use_global_device_ids=true | all-gather | bytes 8448 | tf_op jit(solution)/shard_map/all_gather | solution.py:271
  290.1 36.7 %all-gather.17 = bf16[32,1,64]{2,1,0:T(2,128)(2,1)S(1)} all-gather(bf16[1,1,64]{2,1,0:T(2,128)(2,1)S(1)} %get-tuple-element.1432), channel_id=1, replica_groups=mesh['seq'=8,'batch'=4] {'seq','batch'}, dimensions={0}, use_global_device_ids=true | all-gather | bytes 4224 | tf_op jit(solution)/shard_map/all_gather | solution.py:271
  578.3 30.6 all_gather.160
  609.6 30.5 all_gather.161
  701.4 30.5 all_gather.142
  732.7 30.4 all_gather.143
  1183.3 30.4 all_gather.162
  1214.5 30.4 all_gather.163
  1343.0 30.4 all_gather.154
  1374.2 30.4 all_gather.155
  1786.4 30.4 all_gather.168
  1816.8 30.4 all_gather.169
  1875.5 30.4 all_gather.164
  1905.9 30.4 all_gather.165
  2220.0 30.4 all_gather.167
  2295.0 30.4 all_gather.170
  2325.4 30.4 all_gather.171
  2541.4 528.8 %all-reduce.291.cloned.1.call-done = (f32[32,16384]{1,0:T(8,128)}, f32[32,16384]{1,0:T(8,128)}, f32[32,16384]{1,0:T(8,128)}, f32[32,16384]{1,0:T(8,128)}, f32[32...) async-done(((f32[32,16384]{1,0:T(8,128)}, ...) | async-done | bytes 33554448
  (2237 shorter events, 1783.6 us)
Async XLA Ops:
  7.2 320.3 %all-gather.37.cloned.1.call-start = ((), (), s32[]{:S(2)}) async-start(), calls=%async_computation.2 | async-start | bytes 2162688 | tf_op jit(solution)/shard_map/all_gather | solution.py:271
  8.8 129.8 %copy-start.395 = (bf16[2,64]{1,0:T(2,128)(2,1)S(1)}, bf16[2,64]{1,0:T(2,128)(2,1)}, u32[]{:S(2)}) copy-start(bf16[2,64]{1,0:T(2,128)(2,1)} %param.37) | copy-start | bytes 772
  8.8 328.7 %all-gather.35.cloned.1.call-start = ((), (), s32[]{:S(2)}) async-start(), calls=%async_computation.1 | async-start | bytes 2162688 | tf_op jit(solution)/shard_map/all_gather | solution.py:271
  10.3 336.9 %all-gather.33.cloned.1.call-start = ((), (), s32[]{:S(2)}) async-start(), calls=%async_computation | async-start | bytes 2162688 | tf_op jit(solution)/shard_map/all_gather | solution.py:271
  11.8 531.6 %all-gather.39.cloned.1.call-start = ((), (), s32[]{:S(2)}) async-start(), calls=%async_computation.3 | async-start | bytes 2162688 | tf_op jit(solution)/shard_map/all_gather | solution.py:271
  13.3 632.7 %all-gather.51.cloned.1.call-start = ((), (), s32[]{:S(2)}) async-start(), calls=%async_computation.9 | async-start | bytes 2162688 | tf_op jit(solution)/shard_map/all_gather | solution.py:271
  14.0 753.6 %all-gather.49.cloned.1.call-start = ((), (), s32[]{:S(2)}) async-start(), calls=%async_computation.8 | async-start | bytes 2162688 | tf_op jit(solution)/shard_map/all_gather | solution.py:271
  14.7 762.9 %all-gather.47.cloned.1.call-start = ((), (), s32[]{:S(2)}) async-start(), calls=%async_computation.7 | async-start | bytes 2162688 | tf_op jit(solution)/shard_map/all_gather | solution.py:271
  15.5 771.5 %all-gather.45.cloned.1.call-start = ((), (), s32[]{:S(2)}) async-start(), calls=%async_computation.6 | async-start | bytes 2162688 | tf_op jit(solution)/shard_map/all_gather | solution.py:271
  16.2 808.8 %all-gather.41.cloned.1.call-start = ((), (), s32[]{:S(2)}) async-start(), calls=%async_computation.4 | async-start | bytes 4325376 | tf_op jit(solution)/shard_map/all_gather | solution.py:271
  17.9 827.0 %all-gather.43.cloned.1.call-start = ((), (), s32[]{:S(2)}) async-start(), calls=%async_computation.5 | async-start | bytes 4325376 | tf_op jit(solution)/shard_map/all_gather | solution.py:271
  18.7 1143.5 %all-gather.53.cloned.1.call-start = ((), (), s32[]{:S(2)}) async-start(), calls=%async_computation.10 | async-start | bytes 4325376 | tf_op jit(solution)/shard_map/all_gather | solution.py:271
  19.4 1232.1 %all-gather.55.cloned.1.call-start = ((), (), s32[]{:S(2)}) async-start(), calls=%async_computation.11 | async-start | bytes 4325376 | tf_op jit(solution)/shard_map/all_gather | solution.py:271
  20.2 2516.2 %all-reduce.289.cloned.1.call-start = ((), (), s32[]{:S(2)}) async-start(), calls=%async_computation.12 | async-start | bytes 262144
  20.5 315.0 %copy-start.382 = (f32[256]{0:T(256)}, f32[256]{0:T(256)S(1)}, u32[]{:S(2)}) copy-start(f32[256]{0:T(256)S(1)} %get-tuple-element.982) | copy-start | bytes 3076
  20.5 337.3 %copy-start.239 = (f32[256]{0:T(256)}, f32[256]{0:T(256)S(1)}, u32[]{:S(2)}) copy-start(f32[256]{0:T(256)S(1)} %fusion.430) | copy-start | bytes 3076
  64.2 391.2 %copy-start.201 = (f32[512]{0:T(512)}, f32[512]{0:T(512)S(1)}, u32[]{:S(2)}) copy-start(f32[512]{0:T(512)S(1)} %reshape.1540) | copy-start | bytes 6148
  100.7 256.6 %copy-start.255 = (f32[8,1,128]{2,1,0:T(1,128)}, f32[8,1,128]{2,1,0:T(1,128)S(1)}, u32[]{:S(2)}) copy-start(f32[8,1,128]{2,1,0:T(1,128)S(1)} %slice_convert_fusion.5) | copy-start | bytes 12292
  138.5 219.3 %copy-start.257 = (f32[8,1,128]{2,1,0:T(1,128)}, f32[8,1,128]{2,1,0:T(1,128)S(1)}, u32[]{:S(2)}) copy-start(f32[8,1,128]{2,1,0:T(1,128)S(1)} %slice_convert_fusion.6) | copy-start | bytes 12292
  552.3 213.9 %copy-start.7 = (bf16[8,128,4,128]{1,0,3,2:T(8,128)(2,1)}, bf16[8,128,4,128]{1,0,3,2:T(8,128)(2,1)S(1)}, u32[]{:S(2)}) copy-start(bf16[8,128,4,128]{1,0,3,2:T(8,128)(2,1)S(1)} %copy.63) | copy-start | bytes 3145732
  646.0 223.1 %copy-start.282 = (f32[256]{0:T(256)}, f32[256]{0:T(256)S(1)}, u32[]{:S(2)}) copy-start(f32[256]{0:T(256)S(1)} %fusion.431) | copy-start | bytes 3076
  767.6 109.2 %copy-start.277 = (f32[256]{0:T(256)}, f32[256]{0:T(256)S(1)}, u32[]{:S(2)}) copy-start(f32[256]{0:T(256)S(1)} %fusion.427) | copy-start | bytes 3076
  1957.6 127.5 %copy-start.71 = (f32[1,256,512]{2,1,0:T(8,128)}, f32[1,256,512]{2,1,0:T(8,128)S(1)}, u32[]{:S(2)}) copy-start(f32[1,256,512]{2,1,0:T(8,128)S(1)} %get-tuple-element.1420) | copy-start | bytes 1572868
  2413.7 656.5 %all-reduce.291.cloned.1.call-start = ((), (), s32[]{:S(2)}) async-start(), calls=%async_computation.13 | async-start | bytes 67108864
  (390 other events, 3540.2 us)
Sparse Core Ops, SparseCore 0:
  11.5 59.1 all-gather.36
  74.1 55.2 all-gather.34
  132.9 55.2 all-gather.32
  190.9 55.3 all-gather.38
  249.0 55.2 all-gather.50
  307.0 55.2 all-gather.48
  365.1 55.2 all-gather.46
  423.2 55.2 all-gather.44
  481.3 60.8 all-gather.40
  545.0 60.6 all-gather.42
  608.6 60.4 all-gather.52
  671.7 60.4 all-gather.54
  2413.9 122.4 all-reduce.288
  2542.7 527.4 all-reduce.290
where the time goes:
time: 3130 us; the launch traced here: 3090 us
  local copies, waits for them, and re-layouts  1150 us (37%)
  blocking collectives  789 us (25%)
  waiting for transfers between devices  541 us (17%)
  other arithmetic  463 us (15%)
  matrix products  127 us (4%)
    unnamed x16, waiting for transfers between devices  541 us
    all_gather x16, blocking collectives, entering_2(): pieces = jax.tree.map(lambda part: lax.all_gather(part, axis), value)  487 us
    slice x216, local copies, waits for them, and re-layouts, layer_backward(): lax.associative_scan(link, (onward, grad_hidden), reverse=True, axis=1)  319 us
    all_gather x8, blocking collectives, body(): lax.all_gather(as_sent(flatten_layer(shards, layer_at)), ('seq', 'batch')...  302 us
    slice x208, local copies, waits for them, and re-layouts, layer_forward(): prefix, local_state = lax.associative_scan(link, (decay, inflow), axis=1)  302 us
    dot_general x72, matrix products, matmul(): return jnp.einsum(form, left, right, preferred_element_type=jnp.float32)  127 us
    all_gather x12, other arithmetic, body(): lax.all_gather(as_sent(flatten_layer(shards, layer_at)), ('seq', 'batch')...  119 us
    pad x112, local copies, waits for them, and re-layouts, layer_forward(): prefix, local_state = lax.associative_scan(link, (decay, inflow), axis=1)  115 us
  transfers between devices with their start and end apart: 14, of which 2 were waited for; matrix products, arithmetic and copies ran while one was open for 28% of the time, Pallas kernels for 0%

commit v1 on v0

v1 whole, which is shorter than its diff:
```python
import functools

import jax
import jax.numpy as jnp
from jax import lax
from jax.experimental import pallas as pl
from jax.experimental.pallas import tpu as pltpu
from jax.sharding import PartitionSpec as P

LAYERS = 2
EPS = 1e-05
NS, NB, LANE = 8, 4, 128
CHUNKS = 8
VMEM = 56 * 1024 * 1024
F32, BF16 = jnp.float32, jnp.bfloat16


def dot(left, right):
    return lax.dot_general(left, right, (((1,), (0,)), ((), ())), preferred_element_type=F32)


def dot_nt(left, right):
    return lax.dot_general(left, right, (((1,), (1,)), ((), ())), preferred_element_type=F32)


def dot_tn(left, right):
    return lax.dot_general(left, right, (((0,), (0,)), ((), ())), preferred_element_type=F32)


def columns_of(ref, start, rows, slabs):
    parts = [
        ref[:, 0, start + j * rows : start + (j + 1) * rows, :].reshape(NS * rows, LANE)
        for j in range(slabs)
    ]
    return jnp.concatenate(parts, axis=1)


def rows_of(ref):
    parts = [ref[:, j].reshape(-1, LANE) for j in range(NB)]
    return jnp.concatenate(parts, axis=1)


def rms_scale(values):
    return lax.rsqrt(jnp.mean(values * values, axis=-1, keepdims=True) + EPS)


def rms_back(values, gain, grad):
    scale = rms_scale(values)
    unit = values * scale
    inner = grad * gain
    back = scale * (inner - unit * jnp.mean(inner * unit, axis=-1, keepdims=True))
    return back, jnp.sum(grad * unit, axis=0, keepdims=True)


def gate_kernel(
    seqs, steps, x_ref, gain_ref, bias_ref, w_ref,
    normed_ref, decay_ref, inflow_ref, cand_ref, ff_ref, fi_ref, fc_ref, cp_ref, ch_ref, fin_ref,
    zf, zi, zc,
):
    rows = w_ref.shape[2] // 6
    width = 2 * LANE

    @pl.when(pl.program_id(0) == 0)
    def _():
        x = x_ref[...].astype(F32)
        normed_ref[...] = (x * rms_scale(x) * gain_ref[...]).astype(BF16)

    normed = normed_ref[...]
    zf[...] = dot(normed, columns_of(w_ref, 0, rows, 2)) + bias_ref[0:1, :]
    zi[...] = dot(normed, columns_of(w_ref, 2 * rows, rows, 2)) + bias_ref[1:2, :]
    zc[...] = dot(normed, columns_of(w_ref, 4 * rows, rows, 2))

    block = 4 * CHUNKS

    def turn(at, carry):
        carry = list(carry)
        for seq in range(seqs):
            span = pl.ds(pl.multiple_of(seq * steps * CHUNKS + at * block, block), block)
            f, i, c = zf[span, :], zi[span, :], zc[span, :]
            low = jnp.minimum(jnp.minimum(f, i), 0.0)
            e0, ef, ei = jnp.exp(low), jnp.exp(low - f), jnp.exp(low - i)
            a, b = e0 + ef, e0 + ei
            inv = 1.0 / (a + b)
            decay, other = b * inv, a * inv
            ec = jnp.exp(-jnp.abs(c))
            cand = jnp.maximum(c, 0.0) + jnp.log1p(ec)
            slope = jnp.where(c >= 0.0, 1.0, ec) / (1.0 + ec)
            inflow = other * cand
            decay_ref[span, :] = decay
            inflow_ref[span, :] = inflow
            cand_ref[span, :] = cand
            ff_ref[span, :] = (ef * inv * decay).astype(BF16)
            fi_ref[span, :] = (ei * inv * other).astype(BF16)
            fc_ref[span, :] = (other * slope).astype(BF16)
            prod, state = carry[2 * seq], carry[2 * seq + 1]
            for k in range(4):
                d = decay[k * CHUNKS : (k + 1) * CHUNKS]
                prod = prod * d
                state = state * d + inflow[k * CHUNKS : (k + 1) * CHUNKS]
            carry[2 * seq], carry[2 * seq + 1] = prod, state
        return tuple(carry)

    one, zero = jnp.ones((CHUNKS, width), F32), jnp.zeros((CHUNKS, width), F32)
    carry = lax.fori_loop(0, steps // 4, turn, (one, zero) * seqs)
    for seq in range(seqs):
        prod, state = carry[2 * seq], carry[2 * seq + 1]
        cp_ref[seq], ch_ref[seq] = prod, state
        whole, last = prod[0:1], state[0:1]
        for c in range(1, CHUNKS):
            whole, last = whole * prod[c : c + 1], last * prod[c : c + 1] + state[c : c + 1]
        fin_ref[seq : seq + 1, :] = whole
        fin_ref[seqs + seq : seqs + seq + 1, :] = last


def mix_kernel(
    seqs, steps, x_ref, gain_ref, decay_ref, inflow_ref, cp_ref, ch_ref, ent_ref, wo_ref, wu_ref, wd_ref,
    hidden_ref, hb_ref, e_ref, mid_ref, n2_ref, act_ref, slope_ref, out_ref,
    acc, pre,
):
    at_step = pl.program_id(0)
    block = 4 * CHUNKS

    @pl.when(at_step == 0)
    def _():
        acc[...] = x_ref[...].astype(F32)

    @pl.when(at_step < NB)
    def _():
        for seq in range(seqs):
            state = ent_ref[seq : seq + 1, :]
            for c in range(CHUNKS):
                e_ref[seq, c : c + 1, :] = state
                state = state * cp_ref[seq, c : c + 1, :] + ch_ref[seq, c : c + 1, :]

        def turn(at, carry):
            carry = list(carry)
            for seq in range(seqs):
                span = pl.ds(pl.multiple_of(seq * steps * CHUNKS + at * block, block), block)
                d, u = decay_ref[span, :], inflow_ref[span, :]
                state, found = carry[seq], []
                for k in range(4):
                    state = state * d[k * CHUNKS : (k + 1) * CHUNKS] + u[k * CHUNKS : (k + 1) * CHUNKS]
                    found.append(state)
                carry[seq] = state
                hidden = jnp.concatenate(found, axis=0)
                hidden_ref[span, :] = hidden
                hb_ref[span, :] = hidden.astype(BF16)
            return tuple(carry)

        lax.fori_loop(0, steps // 4, turn, tuple(e_ref[seq] for seq in range(seqs)))
        acc[...] += dot(hb_ref[...], rows_of(wo_ref))

    @pl.when(at_step == NB - 1)
    def _():
        middle = acc[...]
        mid_ref[...] = middle
        n2_ref[...] = (middle * rms_scale(middle) * gain_ref[...]).astype(BF16)

    @pl.when(at_step >= NB)
    def _():
        pre[...] = dot(n2_ref[...], columns_of(wu_ref, 0, wu_ref.shape[2] // 4, 4))

        def turn(at, _):
            span = pl.ds(pl.multiple_of(at * 16, 16), 16)
            v = pre[span, :]
            phi = 0.5 + 0.5 * lax.erf(v * 0.7071067811865476)
            act_ref[span, :] = (v * phi).astype(BF16)
            slope_ref[span, :] = (phi + v * (0.3989422804014327 * jnp.exp(v * v * -0.5))).astype(BF16)
            return 0

        lax.fori_loop(0, pre.shape[0] // 16, turn, 0)
        acc[...] += dot(act_ref[...], rows_of(wd_ref))

    @pl.when(at_step == 2 * NB - 1)
    def _():
        out_ref[...] = acc[...].astype(out_ref.dtype)


def mlp_back_kernel(
    seqs, steps, g_ref, gain_ref, mid_ref, slope_ref, decay_ref, wo_ref, wu_ref, wd_ref,
    gr_ref, gpre_ref, gmid_ref, go_ref, ggain_ref, gh_ref, cp_ref, ca_ref, fin_ref,
    acc,
):
    at_step = pl.program_id(0)
    block = 4 * CHUNKS
    width = decay_ref.shape[1]

    @pl.when(at_step == 0)
    def _():
        gr_ref[...] = g_ref[...].astype(BF16)
        acc[...] = jnp.zeros_like(acc)

    @pl.when(at_step < NB)
    def _():
        gact = dot_nt(gr_ref[...], rows_of(wd_ref))
        gpre_ref[...] = (gact * slope_ref[...].astype(F32)).astype(BF16)
        acc[...] += dot_nt(gpre_ref[...], columns_of(wu_ref, 0, wu_ref.shape[2] // 4, 4))

    @pl.when(at_step == NB - 1)
    def _():
        back, ggain = rms_back(mid_ref[...], gain_ref[...], acc[...])
        ggain_ref[...] = ggain
        gmid = g_ref[...].astype(F32) + back
        gmid_ref[...] = gmid
        go_ref[...] = gmid.astype(BF16)

    @pl.when(at_step >= NB)
    def _():
        gh_ref[...] = dot_nt(go_ref[...], rows_of(wo_ref))

        def turn(turn_at, carry):
            at = steps // 4 - 1 - turn_at
            carry = list(carry)
            for seq in range(seqs):
                span = pl.ds(pl.multiple_of(seq * steps * CHUNKS + at * block, block), block)
                d, g = decay_ref[span, :], gh_ref[span, :]
                prod, state = carry[2 * seq], carry[2 * seq + 1]
                for k in reversed(range(4)):
                    dk = d[k * CHUNKS : (k + 1) * CHUNKS]
                    prod = prod * dk
                    state = dk * (g[k * CHUNKS : (k + 1) * CHUNKS] + state)
                carry[2 * seq], carry[2 * seq + 1] = prod, state
            return tuple(carry)

        one, zero = jnp.ones((CHUNKS, width), F32), jnp.zeros((CHUNKS, width), F32)
        carry = lax.fori_loop(0, steps // 4, turn, (one, zero) * seqs)
        for seq in range(seqs):
            prod, state = carry[2 * seq], carry[2 * seq + 1]
            cp_ref[seq], ca_ref[seq] = prod, state
            whole, last = prod[CHUNKS - 1 :], state[CHUNKS - 1 :]
            for c in reversed(range(CHUNKS - 1)):
                whole, last = whole * prod[c : c + 1], last * prod[c : c + 1] + state[c : c + 1]
            fin_ref[seq : seq + 1, :] = whole
            fin_ref[seqs + seq : seqs + seq + 1, :] = last


def gate_back_kernel(
    seqs, steps, x_ref, gain_ref, gmid_ref, gh_ref, decay_ref, hidden_ref, e_ref, cand_ref, ff_ref, fi_ref, fc_ref,
    cp_ref, ca_ref, ent_ref, w_ref,
    dzf_ref, dzi_ref, dzc_ref, gbias_ref, gstream_ref, ggain_ref,
    acc, start,
):
    at_step = pl.program_id(0)
    block = 4 * CHUNKS
    width = decay_ref.shape[1]
    rows = w_ref.shape[2] // 6

    @pl.when(at_step == 0)
    def _():
        acc[...] = jnp.zeros_like(acc)

    for seq in range(seqs):
        state = ent_ref[seq : seq + 1, :]
        for c in reversed(range(CHUNKS)):
            start[seq, c : c + 1, :] = state
            state = state * cp_ref[seq, c : c + 1, :] + ca_ref[seq, c : c + 1, :]

    def turn(turn_at, carry):
        at = steps // 4 - 1 - turn_at
        carry = list(carry)
        sum_f, sum_i = carry[seqs], carry[seqs + 1]
        for seq in range(seqs):
            base = seq * steps * CHUNKS + at * block
            span = pl.ds(pl.multiple_of(base, block), block)
            before = hidden_ref[pl.ds(pl.multiple_of(jnp.maximum(base - CHUNKS, 0), CHUNKS), CHUNKS), :]
            before = jnp.where(at == 0, e_ref[seq], before)
            d, g = decay_ref[span, :], gh_ref[span, :]
            previous = jnp.concatenate([before, hidden_ref[span, :][: block - CHUNKS]], axis=0)
            state, found = carry[seq], []
            for k in reversed(range(4)):
                now = g[k * CHUNKS : (k + 1) * CHUNKS] + state
                found.append(now)
                state = d[k * CHUNKS : (k + 1) * CHUNKS] * now
            carry[seq] = state
            gstate = jnp.concatenate(found[::-1], axis=0)
            both = gstate * (cand_ref[span, :] - previous)
            dzf = (-ff_ref[span, :].astype(F32) * both).astype(BF16)
            dzi = (fi_ref[span, :].astype(F32) * both).astype(BF16)
            dzf_ref[span, :] = dzf
            dzi_ref[span, :] = dzi
            dzc_ref[span, :] = (fc_ref[span, :].astype(F32) * gstate).astype(BF16)
            wide_f, wide_i = dzf.astype(F32), dzi.astype(F32)
            for k in range(4):
                sum_f = sum_f + wide_f[k * CHUNKS : (k + 1) * CHUNKS]
                sum_i = sum_i + wide_i[k * CHUNKS : (k + 1) * CHUNKS]
        carry[seqs], carry[seqs + 1] = sum_f, sum_i
        return tuple(carry)

    zero = jnp.zeros((CHUNKS, width), F32)
    carry = lax.fori_loop(0, steps // 4, turn, tuple(start[seq] for seq in range(seqs)) + (zero, zero))
    gbias_ref[0:1, :] = jnp.sum(carry[seqs], axis=0, keepdims=True)
    gbias_ref[1:2, :] = jnp.sum(carry[seqs + 1], axis=0, keepdims=True)
    acc[...] += (
        dot_nt(dzf_ref[...], columns_of(w_ref, 0, rows, 2))
        + dot_nt(dzi_ref[...], columns_of(w_ref, 2 * rows, rows, 2))
        + dot_nt(dzc_ref[...], columns_of(w_ref, 4 * rows, rows, 2))
    )

    @pl.when(at_step == NB - 1)
    def _():
        back, ggain = rms_back(x_ref[...].astype(F32), gain_ref[...], acc[...])
        ggain_ref[...] = ggain
        gstream_ref[...] = (gmid_ref[...] + back).astype(gstream_ref.dtype)


def put_columns(ref, start, rows, slabs, value):
    for j in range(slabs):
        part = value[:, j * LANE : (j + 1) * LANE].astype(BF16)
        ref[:, 0, start + j * rows : start + (j + 1) * rows, :] = part.reshape(NS, rows, LANE)


def put_rows(ref, value):
    for j in range(NB):
        part = value[:, j * LANE : (j + 1) * LANE].astype(BF16)
        ref[:, j] = part.reshape(ref.shape[0], -1, LANE)


def mlp_weight_kernel(act_ref, gr_ref, n2_ref, gpre_ref, hb_ref, go_ref, gu_ref, gd_ref, go_out_ref):
    put_columns(gu_ref, 0, gu_ref.shape[2] // 4, 4, dot_tn(n2_ref[...], gpre_ref[...]))
    put_rows(gd_ref, dot_tn(act_ref[...], gr_ref[...]))
    put_rows(go_out_ref, dot_tn(hb_ref[...], go_ref[...]))


def gate_weight_kernel(normed_ref, dzf_ref, dzi_ref, dzc_ref, g_ref):
    rows = g_ref.shape[2] // 6
    normed = normed_ref[...]
    put_columns(g_ref, 0, rows, 2, dot_tn(normed, dzf_ref[...]))
    put_columns(g_ref, 2 * rows, rows, 2, dot_tn(normed, dzi_ref[...]))
    put_columns(g_ref, 4 * rows, rows, 2, dot_tn(normed, dzc_ref[...]))


def shape(dims, dtype=F32):
    return jax.ShapeDtypeStruct(dims, dtype)


def call(kernel, grid, ins, outs, scratch, flops, name):
    moved = sum(a.size * a.dtype.itemsize for a, _, _ in ins)
    moved += sum(s.size * s.dtype.itemsize for s, _, _ in outs)
    return pl.pallas_call(
        kernel,
        grid=(grid,),
        in_specs=[pl.BlockSpec(block, index) for _, block, index in ins],
        out_specs=[pl.BlockSpec(block, index) for _, block, index in outs],
        out_shape=[s for s, _, _ in outs],
        scratch_shapes=scratch,
        compiler_params=pltpu.CompilerParams(vmem_limit_bytes=VMEM),
        cost_estimate=pl.CostEstimate(flops=flops, bytes_accessed=moved, transcendentals=0),
        name=name,
    )(*[a for a, _, _ in ins])


def whole(array):
    dims = array.shape
    return (array, dims, lambda i: (0,) * len(dims))


def whole_out(dims, dtype=F32):
    return (shape(dims, dtype), dims, lambda i: (0,) * len(dims))


def first(i):
    return jnp.minimum(i, NB - 1)


def second(i):
    return jnp.maximum(i - NB, 0)


class Sizes:
    def __init__(self, seqs, length, d, h, ff):
        self.seqs, self.steps, self.n = seqs, length // CHUNKS, seqs * length
        self.d, self.h, self.ff = d, h, ff
        self.hb, self.fb = h // NB, ff // NB


def gate_forward(sz, x, gain, bias, wa):
    n, d, h, w, s = sz.n, sz.d, sz.h, sz.hb, sz.seqs
    col = lambda i: (0, i)
    return call(
        functools.partial(gate_kernel, s, sz.steps), NB,
        [whole(x), whole(gain), (bias, (2, w), col), (wa, (NS, 1) + wa.shape[2:], lambda i: (0, i, 0, 0))],
        [whole_out((n, d), BF16)]
        + [(shape((n, h)), (n, w), col)] * 3
        + [(shape((n, h), BF16), (n, w), col)] * 3
        + [(shape((s, CHUNKS, h)), (s, CHUNKS, w), lambda i: (0, 0, i))] * 2
        + [(shape((2 * s, h)), (2 * s, w), col)],
        [pltpu.VMEM((n, w), F32)] * 3, 6 * n * d * h, "gates",
    )


def weights_b(wb):
    r = wb.shape[2]
    tall, short = 2 * r // 5, r // 5
    return (tall, short)


def mix_forward(sz, x, gain, decay, inflow, cp, ch, ent, wb, last):
    n, d, h, ff, w, f, s = sz.n, sz.d, sz.h, sz.ff, sz.hb, sz.fb, sz.seqs
    tall, short = weights_b(wb)
    col = lambda i: (0, first(i))
    late = lambda i: (0, second(i))
    deep = lambda i: (0, 0, first(i))
    return call(
        functools.partial(mix_kernel, s, sz.steps), 2 * NB,
        [
            whole(x), whole(gain), (decay, (n, w), col), (inflow, (n, w), col),
            (cp, (s, CHUNKS, w), deep), (ch, (s, CHUNKS, w), deep), (ent, (s, w), col),
            (wb, (NS // NB, NB, short, LANE), lambda i: (first(i), 0, 4, 0)),
            (wb, (NS, 1, tall, LANE), lambda i: (0, second(i), 0, 0)),
            (wb, (NS // NB, NB, tall, LANE), lambda i: (second(i), 0, 1, 0)),
        ],
        [
            (shape((n, h)), (n, w), col), (shape((n, h), BF16), (n, w), col),
            (shape((s, CHUNKS, h)), (s, CHUNKS, w), deep),
            whole_out((n, d)), whole_out((n, d), BF16),
            (shape((n, ff), BF16), (n, f), late), (shape((n, ff), BF16), (n, f), late),
            whole_out((n, d), BF16 if last else F32),
        ],
        [pltpu.VMEM((n, d), F32), pltpu.VMEM((n, f), F32)], 2 * n * d * (h + 2 * ff), "mix",
    )


def mlp_backward(sz, g, gain, mid, slope, decay, wb):
    n, d, h, ff, w, f, s = sz.n, sz.d, sz.h, sz.ff, sz.hb, sz.fb, sz.seqs
    tall, short = weights_b(wb)
    col = lambda i: (0, second(i))
    early = lambda i: (0, first(i))
    deep = lambda i: (0, 0, second(i))
    return call(
        functools.partial(mlp_back_kernel, s, sz.steps), 2 * NB,
        [
            whole(g), whole(gain), whole(mid), (slope, (n, f), early), (decay, (n, w), col),
            (wb, (NS // NB, NB, short, LANE), lambda i: (second(i), 0, 4, 0)),
            (wb, (NS, 1, tall, LANE), lambda i: (0, first(i), 0, 0)),
            (wb, (NS // NB, NB, tall, LANE), lambda i: (first(i), 0, 1, 0)),
        ],
        [
            whole_out((n, d), BF16), (shape((n, ff), BF16), (n, f), early), whole_out((n, d)), whole_out((n, d), BF16),
            whole_out((1, d)), (shape((n, h)), (n, w), col),
            (shape((s, CHUNKS, h)), (s, CHUNKS, w), deep), (shape((s, CHUNKS, h)), (s, CHUNKS, w), deep),
            (shape((2 * s, h)), (2 * s, w), col),
        ],
        [pltpu.VMEM((n, d), F32)], 2 * n * d * (h + 2 * ff), "mlp_back",
    )


def gate_backward(sz, x, gain, gmid, gh, decay, hidden, e, cand, ff_, fi_, fc_, cp, ca, ent, wa, last):
    n, d, h, w, s = sz.n, sz.d, sz.h, sz.hb, sz.seqs
    col = lambda i: (0, i)
    deep = lambda i: (0, 0, i)
    wide = lambda a: (a, (n, w), col)
    return call(
        functools.partial(gate_back_kernel, s, sz.steps), NB,
        [
            whole(x), whole(gain), whole(gmid), wide(gh), wide(decay), wide(hidden), (e, (s, CHUNKS, w), deep),
            wide(cand), wide(ff_), wide(fi_), wide(fc_), (cp, (s, CHUNKS, w), deep), (ca, (s, CHUNKS, w), deep),
            (ent, (s, w), col), (wa, (NS, 1) + wa.shape[2:], lambda i: (0, i, 0, 0)),
        ],
        [(shape((n, h), BF16), (n, w), col)] * 3
        + [(shape((2, h)), (2, w), col), whole_out((n, d), BF16 if last else F32), whole_out((1, d))],
        [pltpu.VMEM((n, d), F32), pltpu.VMEM((s, CHUNKS, w), F32)], 6 * n * d * h, "gate_back",
    )


def mlp_weights(sz, act, gr, n2, gpre, hb, go):
    n, d, h, ff, w, f = sz.n, sz.d, sz.h, sz.ff, sz.hb, sz.fb
    col = lambda i: (0, i)
    return call(
        mlp_weight_kernel, NB,
        [(act, (n, f), col), whole(gr), whole(n2), (gpre, (n, f), col), (hb, (n, w), col), whole(go)],
        [
            (shape((NS, NB, d * ff // (32 * LANE), LANE), BF16), (NS, 1, d * ff // (32 * LANE), LANE), lambda i: (0, i, 0, 0)),
            (shape((NS, NB, ff // NS, LANE), BF16), (NS // NB, NB, ff // NS, LANE), lambda i: (i, 0, 0, 0)),
            (shape((NS, NB, h // NS, LANE), BF16), (NS // NB, NB, h // NS, LANE), lambda i: (i, 0, 0, 0)),
        ],
        [], 2 * n * d * (h + 2 * ff), "mlp_weights",
    )


def gate_weights(sz, normed, dzf, dzi, dzc):
    n, d, h, w = sz.n, sz.d, sz.h, sz.hb
    col = lambda i: (0, i)
    rows = 3 * d * h // (32 * LANE)
    return call(
        gate_weight_kernel, NB,
        [whole(normed), (dzf, (n, w), col), (dzi, (n, w), col), (dzc, (n, w), col)],
        [(shape((NS, NB, rows, LANE), BF16), (NS, 1, rows, LANE), lambda i: (0, i, 0, 0))],
        [], 6 * n * d * h, "gate_weights",
    )[0]


def enter(fin, seqs, backward):
    count, mine = lax.axis_size("seq"), lax.axis_index("seq")
    prod, state = fin[:seqs], fin[seqs:]
    pre_p, pre_s = jnp.ones_like(prod), jnp.zeros_like(state)
    bit = 1
    while bit < count:
        other = lax.ppermute(jnp.concatenate([prod, state]), "seq", [(i, i ^ bit) for i in range(count)])
        o_p, o_s = other[:seqs], other[seqs:]
        upper = ((mine // bit) % 2 == 1) ^ backward
        pre_p, pre_s = jnp.where(upper, o_p * pre_p, pre_p), jnp.where(upper, pre_p * o_s + pre_s, pre_s)
        state = jnp.where(upper, prod * o_s + state, o_p * state + o_s)
        prod = prod * o_p
        bit *= 2
    return pre_s


def slabs(matrix, seq_count, batch_count):
    rows, cols = matrix.shape[0] // NS, matrix.shape[1] // NB
    cut = matrix.reshape(NS, rows, NB, cols // LANE, LANE).transpose(0, 2, 3, 1, 4)
    return cut.reshape(NS, NB, rows * cols // LANE, LANE)


def unslab(blocks, rows, cols):
    r, c = rows // NS, cols // NB
    cut = blocks.reshape(NS, NB, c // LANE, r, LANE).transpose(0, 3, 1, 2, 4)
    return cut.reshape(rows, cols)


def own_slab(shard):
    rows, cols = shard.shape
    return shard.reshape(rows, cols // LANE, LANE).transpose(1, 0, 2).reshape(-1, LANE)


def body(
    tokens, norm_gain, w_forget, w_input, w_cand, forget_bias, input_bias, w_out, mlp_gain, w_up, w_down, cotangent
):
    seqs, length, d = tokens.shape
    seq_count, batch_count = lax.axis_size("seq"), lax.axis_size("batch")
    h, ff = w_forget.shape[2] * batch_count, w_up.shape[2] * batch_count
    sz = Sizes(seqs, length, d, h, ff)
    both = ("seq", "batch")
    standard = (seq_count, batch_count) == (NS, NB)

    widest = max(v.shape[1] for v in (norm_gain, forget_bias, input_bias, mlp_gain))
    vec = jnp.concatenate(
        [
            jnp.pad(v[l : l + 1], ((0, 0), (0, widest - v.shape[1])))
            for l in range(LAYERS)
            for v in (norm_gain, forget_bias, input_bias, mlp_gain)
        ]
    )
    if standard:
        parts = []
        for l in range(LAYERS):
            parts += [own_slab(m[l]) for m in (w_forget, w_input, w_cand, w_up, w_down, w_out)]
        pack = jnp.concatenate(parts + [jnp.pad(vec, ((0, 8), (0, LANE - widest)))])
        got = lax.all_gather(pack, both, axis=0, tiled=False).reshape(NS, NB, -1, LANE)
        gate_rows, mlp_rows = 3 * d * h // (32 * LANE), (h + 2 * ff) * d // (32 * LANE)
        layer_rows = gate_rows + mlp_rows
        was = [got[:, :, l * layer_rows : l * layer_rows + gate_rows] for l in range(LAYERS)]
        wbs = [got[:, :, l * layer_rows + gate_rows : (l + 1) * layer_rows] for l in range(LAYERS)]
        vecs = got[:, 0, LAYERS * layer_rows : LAYERS * layer_rows + 4 * LAYERS, :widest]
        vecs = vecs.transpose(1, 0, 2)
    else:
        was, wbs = [], []

        def full(m):
            m = lax.all_gather(m, "batch", axis=1, tiled=True)
            return lax.all_gather(m, "seq", axis=0, tiled=True)

        for l in range(LAYERS):
            cut = [slabs(full(m[l]), NS, NB) for m in (w_forget, w_input, w_cand, w_up, w_down, w_out)]
            was.append(jnp.concatenate(cut[:3], axis=2))
            wbs.append(jnp.concatenate(cut[3:], axis=2))
        vecs = lax.all_gather(vec, "seq", axis=1, tiled=False)

    def vector(l, which, size):
        return vecs[4 * l + which][:, : size // seq_count].reshape(1, size).astype(F32)

    def to_rows(v):
        return v.reshape(seqs, CHUNKS, sz.steps, d).transpose(0, 2, 1, 3).reshape(sz.n, d)

    def from_rows(v):
        return v.reshape(seqs, sz.steps, CHUNKS, d).transpose(0, 2, 1, 3).reshape(seqs, length, d)

    stream, grad = to_rows(tokens), to_rows(cotangent)
    kept = []
    for l in range(LAYERS):
        gain_one, gain_two = vector(l, 0, d), vector(l, 3, d)
        bias = jnp.concatenate([vector(l, 1, h), vector(l, 2, h)])
        normed, decay, inflow, cand, f_f, f_i, f_c, cp, ch, fin = gate_forward(sz, stream, gain_one, bias, was[l])
        ent = enter(fin, seqs, False)
        hidden, hb, e, mid, n2, act, slope, result = mix_forward(
            sz, stream, gain_two, decay, inflow, cp, ch, ent, wbs[l], l == LAYERS - 1
        )
        kept.append((stream, gain_one, gain_two, normed, decay, cand, f_f, f_i, f_c, hidden, hb, e, mid, n2, act, slope))
        stream = result
    output = from_rows(stream)

    grads = [None] * LAYERS
    for l in reversed(range(LAYERS)):
        x, gain_one, gain_two, normed, decay, cand, f_f, f_i, f_c, hidden, hb, e, mid, n2, act, slope = kept[l]
        gr, gpre, gmid, go, ggain_two, gh, cp, ca, fin = mlp_backward(sz, grad, gain_two, mid, slope, decay, wbs[l])
        ent = enter(fin, seqs, True)
        gu, gd, gwo = mlp_weights(sz, act, gr, n2, gpre, hb, go)
        dzf, dzi, dzc, gbias, grad, ggain_one = gate_backward(
            sz, x, gain_one, gmid, gh, decay, hidden, e, cand, f_f, f_i, f_c, cp, ca, ent, was[l], l == 0
        )
        gg = gate_weights(sz, normed, dzf, dzi, dzc)
        grads[l] = (gg, gu, gd, gwo, ggain_one, gbias, ggain_two)
    grad_tokens = from_rows(grad)

    third = d * h // (32 * LANE)
    shard_shapes = (w_forget, w_input, w_cand, w_up, w_down, w_out)
    if standard:
        sent = [g for l in range(LAYERS) for g in grads[l][:4]]
        sent = jnp.concatenate([g.reshape(NS * NB, -1, LANE) for g in sent], axis=1)
        mine = lax.psum_scatter(sent, both, scatter_dimension=0, tiled=False)
        at, found = 0, []
        for l in range(LAYERS):
            layer = []
            for m in shard_shapes:
                r, c = m.shape[1:]
                part = mine[at : at + r * c // LANE].reshape(c // LANE, r, LANE)
                layer.append(part.transpose(1, 0, 2).reshape(r, c).astype(F32))
                at += r * c // LANE
            found.append(layer)
    else:
        found = []
        for l in range(LAYERS):
            gg, gu, gd, gwo = grads[l][:4]
            blocks = [gg[:, :, :third], gg[:, :, third : 2 * third], gg[:, :, 2 * third :], gu, gd, gwo]
            layer = []
            for m, g in zip(shard_shapes, blocks):
                v = unslab(g, m.shape[1] * seq_count, m.shape[2] * batch_count)
                v = lax.psum_scatter(v, "seq", scatter_dimension=0, tiled=True)
                layer.append(lax.psum_scatter(v, "batch", scatter_dimension=1, tiled=True).astype(F32))
            found.append(layer)
    found = [jnp.stack([found[l][m] for l in range(LAYERS)]) for m in range(6)]

    small = jnp.concatenate(
        [v.reshape(seq_count, -1) for l in range(LAYERS) for v in (grads[l][4], grads[l][5][0], grads[l][5][1], grads[l][6])],
        axis=1,
    )
    small = lax.psum(lax.psum_scatter(small, "seq", scatter_dimension=0, tiled=True), "batch")
    sizes = (d // seq_count, h // seq_count, h // seq_count, d // seq_count)
    vector_grads, at = [], 0
    for l in range(LAYERS):
        layer = []
        for size in sizes:
            layer.append(small[0, at : at + size])
            at += size
        vector_grads.append(layer)
    g_norm, g_fb, g_ib, g_mlp = [jnp.stack([vector_grads[l][m] for l in range(LAYERS)]) for m in range(4)]
    g_f, g_i, g_c, g_up, g_down, g_out = found
    return output, grad_tokens, g_norm, g_f, g_i, g_c, g_fb, g_ib, g_out, g_mlp, g_up, g_down


def solution(mesh):
    split, vector, matrix = P("batch", "seq", None), P(None, "seq"), P(None, "seq", "batch")
    order = (vector, matrix, matrix, matrix, vector, vector, matrix, vector, matrix, matrix)
    return jax.shard_map(
        body,
        mesh=mesh,
        in_specs=(split,) + order + (split,),
        out_specs=(split, split) + order,
        check_vma=False,
    )
```

time: 3130 us -> 535 us (0.17); the launches traced: 3090 us -> 533 us
  local copies, waits for them, and re-layouts: 1150 us -> 56.1 us
  blocking collectives: 789 us -> 41.9 us
  other arithmetic: 463 us -> 15.4 us
  waiting for transfers between devices: 541 us -> 270 us
  matrix products: 127 us -> 0 us
  Pallas kernels: 0 us -> 120 us
    all_gather x24 -> x0, blocking collectives: 789 us -> none  [the longest x16 487 us: entering_2(): pieces = jax.tree.map(lambda part: lax.all_gather(part, axis), value)]
    slice x434 -> x15, local copies, waits for them, and re-layouts: 627 us -> 22.9 us  [the longest x1 9.2 us: body(): got[:, :, l * layer_rows + gate_rows:(l + 1) * layer_rows]]
    unnamed x16 -> x2, waiting for transfers between devices: 541 us -> 0.03 us
    pad x224 -> x4, local copies, waits for them, and re-layouts: 204 us -> 0.03 us  [body(): jnp.pad(v[l:l + 1], ((0, 0), (0, widest - v.shape[1])))]
    add x195 -> x0, other arithmetic: 159 us -> none  [the longest x52 64.8 us: link(): return (earlier[0] * latter[0], latter[0] * earlier[1] + latter[1])]
    reduce_scatter x0 -> x1, waiting for transfers between devices: none -> 131 us  [body(): mine = lax.psum_scatter(sent, both, scatter_dimension=0, tiled=False)]
    dot_general x72 -> x0, matrix products: 127 us -> none  [matmul(): return jnp.einsum(form, left, right, preferred_element_type=jnp.float32)]
    pallas_call x0 -> x12, Pallas kernels: none -> 120 us  [call(): pl.pallas_call(kernel, grid=(grid,), in_specs=[pl.BlockSpec(block, index)...]
  transfers between devices with their start and end apart: 14 -> 14, of which waited for: 2 -> 11; matrix products, arithmetic and copies ran while one was open for 28% -> 3% of each run, Pallas kernels for 0% -> 4%
where the time goes in v1:
time: 535 us; the launch traced here: 533 us
  waiting for transfers between devices  270 us (50%)
  Pallas kernels  120 us (22%)
  local copies, waits for them, and re-layouts  56.1 us (10%)
  blocking collectives  41.9 us (8%)
  other arithmetic  15.4 us (3%)
  between operations  14.7 us (3%)
  starting transfers between devices  14.3 us (3%)
    reduce_scatter x1, waiting for transfers between devices, body(): mine = lax.psum_scatter(sent, both, scatter_dimension=0, tiled=False)  131 us
    pallas_call x12, Pallas kernels, call(): pl.pallas_call(kernel, grid=(grid,), in_specs=[pl.BlockSpec(block, index)...  120 us
    all_gather x1, waiting for transfers between devices, body(): lax.all_gather(pack, both, axis=0, tiled=False).reshape(NS, NB, -1, LANE)  116 us
    unnamed x1, blocking collectives  35.5 us
    ppermute x12, waiting for transfers between devices, enter(): lax.ppermute(jnp.concatenate([prod, state]), 'seq', [(i, i ^ bit) for i i...  23.2 us
    unnamed x63, local copies, waits for them, and re-layouts  21.8 us
    ppermute x12, starting transfers between devices, enter(): lax.ppermute(jnp.concatenate([prod, state]), 'seq', [(i, i ^ bit) for i i...  14.3 us
  transfers between devices with their start and end apart: 14, of which 11 were waited for; matrix products, arithmetic and copies ran while one was open for 3% of the time, Pallas kernels for 4%

profile of v1, /device:TPU:0, one launch (start us, length us, event | category | flops | bytes accessed | tf_op | source)
XLA Modules:
  0.0 533.0 jit_solution(4720025865113931351)
XLA Ops:
  19.5 116.3 %all-gather.3.cloned.1.call-done = bf16[66048,128]{1,0:T(8,128)(2,1)} async-done(((bf16[2064,128]{1,0:T(8,128)(2,1)}), bf16[66048,128]{1,0:T(8,128)(2,1)}) %all-gather.3.cloned.1.call-update) | async-done | bytes 16908304 | tf_op jit(solution)/shard_map/all_gather | solution.py:548
  136.5 6.2 %fusion.5 = (bf16[8,4,384,128]{3,2,1,0:T(8,128)(2,1)}, bf16[8,4,384,128]{3,2,1,0:T(8,128)(2,1)}) fusion(bf16[8,4,2064,128]{3,2,1,0:T(8,128)(2,1)} %bitcast.111), kind=kLoop, calls=%fused_computation.88 | loop fusion | bytes 12582912 | tf_op jit(solution)/shard_map/slice | solution.py:551
  142.8 9.2 %fusion.4 = (bf16[8,4,640,128]{3,2,1,0:T(8,128)(2,1)}, bf16[8,4,640,128]{3,2,1,0:T(8,128)(2,1)}) fusion(bf16[8,4,2064,128]{3,2,1,0:T(8,128)(2,1)} %bitcast.112), kind=kLoop, calls=%fused_computation.87 | loop fusion | bytes 20971520 | tf_op jit(solution)/shard_map/slice | solution.py:552
  153.3 9.7 %gates.2 = (bf16[512,512]{1,0:T(8,128)(2,1)}, f32[512,1024]{1,0:T(8,128)}, f32[512,1024]{1,0:T(8,128)}, f32[512,1024]{1,0:T(8,128)}, bf16[512,1024]{1,0:T(8,128)...) custom-call(bf16[512,512]{1,0:T(8,128)(2,1)} %bitcast.115, ...), custom_call_target="tpu_custom_call" | custom-call | flops 1610612736 | bytes 13789184 | tf_op jit(solution)/shard_map/gates/pallas_call | solution.py:339
  168.3 3.4 collective-permute-done.1
  177.0 14.7 %mix.2 = (f32[512,1024]{1,0:T(8,128)}, bf16[512,1024]{1,0:T(8,128)(2,1)}, f32[2,8,1024]{2,1,0:T(8,128)}, f32[512,512]{1,0:T(8,128)}, bf16[512,512]{1,0:T(8,128)(...) custom-call(bf16[512,512]{1,0:T(8,128)(2,1)} %bitcast.116, ...), custom_call_target="tpu_custom_call" | custom-call | flops 2684354560 | bytes 30615552 | tf_op jit(solution)/shard_map/mix/pallas_call | solution.py:339
  191.7 9.7 %gates.3 = (bf16[512,512]{1,0:T(8,128)(2,1)}, f32[512,1024]{1,0:T(8,128)}, f32[512,1024]{1,0:T(8,128)}, f32[512,1024]{1,0:T(8,128)}, bf16[512,1024]{1,0:T(8,128)...) custom-call(f32[512,512]{1,0:T(8,128)} %get-tuple-element.89.x_ref, ...), custom_call_target="tpu_custom_call" | custom-call | flops 1610612736 | bytes 14313472 | tf_op jit(solution)/shard_map/gates/pallas_call | solution.py:339
  212.4 2.5 collective-permute-done.5
  215.5 14.7 %mix.3 = (f32[512,1024]{1,0:T(8,128)}, bf16[512,1024]{1,0:T(8,128)(2,1)}, f32[2,8,1024]{2,1,0:T(8,128)}, f32[512,512]{1,0:T(8,128)}, bf16[512,512]{1,0:T(8,128)(...) custom-call(f32[512,512]{1,0:T(8,128)} %get-tuple-element.89.x_ref, ...), custom_call_target="tpu_custom_call" | custom-call | flops 2684354560 | bytes 30615552 | tf_op jit(solution)/shard_map/mix/pallas_call | solution.py:339
  230.2 12.1 %mlp_back.2 = (bf16[512,512]{1,0:T(8,128)(2,1)}, bf16[512,2048]{1,0:T(8,128)(2,1)}, f32[512,512]{1,0:T(8,128)}, bf16[512,512]{1,0:T(8,128)(2,1)}, f32[1,512]{1,0...) custom-call(bf16[512,512]{1,0:T(8,128)(2,1)} %bitcast.118, ...), custom_call_target="tpu_custom_call" | custom-call | flops 2684354560 | bytes 27938816 | tf_op jit(solution)/shard_map/mlp_back/pallas_call | solution.py:339
  247.6 3.4 collective-permute-done.7
  252.5 3.1 collective-permute-done.8
  256.3 10.6 %gate_back.2 = (bf16[512,1024]{1,0:T(8,128)(2,1)}, bf16[512,1024]{1,0:T(8,128)(2,1)}, bf16[512,1024]{1,0:T(8,128)(2,1)}, f32[2,1024]{1,0:T(2,128)}, f32[512,512]{1,0:T(8,128)}, /*index=5*/f32[1,512]{1,0:T(1,128)}) custom-call(f32[512,512]{1,0:T(8,128)} %get-tuple-element.89.x_ref, f32[1,512]{1,0:T(1,128)} %reshape.407.gain_ref, ...), custom_call_target="tpu_custom_call" | custom-call | flops 1610612736 | bytes 21188608 | tf_op jit(solution)/shard_map/gate_back/pallas_call | solution.py:339
  266.9 12.2 %mlp_back.3 = (bf16[512,512]{1,0:T(8,128)(2,1)}, bf16[512,2048]{1,0:T(8,128)(2,1)}, f32[512,512]{1,0:T(8,128)}, bf16[512,512]{1,0:T(8,128)(2,1)}, f32[1,512]{1,0...) custom-call(f32[512,512]{1,0:T(8,128)} %get-tuple-element.109.g_ref, ...), custom_call_target="tpu_custom_call" | custom-call | flops 2684354560 | bytes 28463104 | tf_op jit(solution)/shard_map/mlp_back/pallas_call | solution.py:339
  280.7 7.6 %mlp_weights.3 = (bf16[8,4,256,128]{3,2,1,0:T(8,128)(2,1)}, bf16[8,4,256,128]{3,2,1,0:T(8,128)(2,1)}, bf16[8,4,128,128]{3,2,1,0:T(8,128)(2,1)}) custom-call(bf16[512,2048]{1,0:T(8,128)(2,1)} %get-tuple-element.147.act_ref, bf16[512,512]{1,0:T(8,128)(2,1)} %get-tuple-element.148.gr_ref, bf16[512,512]{1,0:T(8,128)(2,1)} %get-tuple-element.149.n2_ref, ...), custom_call_target="tpu_custom_call" | custom-call | flops 2684354560 | bytes 12058624 | tf_op jit(solution)/shard_map/mlp_weights/pallas_call | solution.py:339
  288.7 7.5 %mlp_weights.2 = (bf16[8,4,256,128]{3,2,1,0:T(8,128)(2,1)}, bf16[8,4,256,128]{3,2,1,0:T(8,128)(2,1)}, bf16[8,4,128,128]{3,2,1,0:T(8,128)(2,1)}) custom-call(bf16[512,2048]{1,0:T(8,128)(2,1)} %get-tuple-element.134.act_ref, bf16[512,512]{1,0:T(8,128)(2,1)} %get-tuple-element.135.gr_ref, bf16[512,512]{1,0:T(8,128)(2,1)} %get-tuple-element.136.n2_ref, ...), custom_call_target="tpu_custom_call" | custom-call | flops 2684354560 | bytes 12058624 | tf_op jit(solution)/shard_map/mlp_weights/pallas_call | solution.py:339
  298.0 5.6 %gate_weights.3 = bf16[8,4,384,128]{3,2,1,0:T(8,128)(2,1)} custom-call(bf16[512,512]{1,0:T(8,128)(2,1)} %get-tuple-element.143.normed_ref, bf16[512,1024]{1,0:T(8,128)(2,1)} %get-tuple-element.144.dzf_ref, bf16[512,1024]{1,0:T(8,128)(2,1)} %get-tuple-element.145.dzi_ref, bf16[512,1024]{1,0:T(8,128)(2,1)} %get-tuple-element.146.dzc_ref), custom_call_target="tpu_custom_call" | custom-call | flops 1610612736 | bytes 6815744 | tf_op jit(solution)/shard_map/gate_weights/pallas_call | solution.py:339
  304.2 10.2 %gate_back.3 = (bf16[512,1024]{1,0:T(8,128)(2,1)}, bf16[512,1024]{1,0:T(8,128)(2,1)}, bf16[512,1024]{1,0:T(8,128)(2,1)}, f32[2,1024]{1,0:T(2,128)}, bf16[512,512]{1,0:T(8,128)(2,1)}, /*index=5*/f32[1,512]{1,0:T(1,128)}) custom-call(bf16[512,512]{1,0:T(8,128)(2,1)} %bitcast.117, f32[1,512]{1,0:T(1,128)} %reshape.405.gain_ref, ...), custom_call_target="tpu_custom_call" | custom-call | flops 1610612736 | bytes 20140032 | tf_op jit(solution)/shard_map/gate_back/pallas_call | solution.py:339
  314.5 5.8 %gate_weights.2 = bf16[8,4,384,128]{3,2,1,0:T(8,128)(2,1)} custom-call(bf16[512,512]{1,0:T(8,128)(2,1)} %get-tuple-element.130.normed_ref, bf16[512,1024]{1,0:T(8,128)(2,1)} %get-tuple-element.131.dzf_ref, bf16[512,1024]{1,0:T(8,128)(2,1)} %get-tuple-element.132.dzi_ref, bf16[512,1024]{1,0:T(8,128)(2,1)} %get-tuple-element.133.dzc_ref), custom_call_target="tpu_custom_call" | custom-call | flops 1610612736 | bytes 6815744 | tf_op jit(solution)/shard_map/gate_weights/pallas_call | solution.py:339
  320.3 4.6 constant_dynamic-update-slice_fusion.18
  329.8 2.5 constant_dynamic-update-slice_fusion.14
  344.0 35.5 %all-reduce.5 = f32[8,768]{1,0:T(8,128)S(1)} all-reduce(f32[8,768]{1,0:T(8,128)S(1)} %concatenate.64), channel_id=3, replica_groups=mesh['seq'=8,'batch'=4] {'seq'}, use_global_device_ids=true, to_apply=%region_0.1.clone | all-reduce | flops 6144 | bytes 49152
  380.1 6.4 %psum.7 = f32[1,768]{1,0:T(1,128)S(1)} all-reduce(f32[1,768]{1,0:T(1,128)S(1)} %constant_dynamic-slice_fusion), channel_id=1, replica_groups=mesh['seq'=8,'batch'=4] {'batch'}, use_global_device_ids=true, to_apply=%region_1.2 | all-reduce | flops 768 | bytes 6144 | tf_op jit(solution)/shard_map/psum | solution.py:636
  389.0 130.6 %reduce-scatter.2.cloned.1.call-done = bf16[1,2048,128]{2,1,0:T(8,128)(2,1)} async-done(((bf16[32,2048,128]{2,1,0:T(8,128)(2,1)}), bf16[1,2048,128]{2,1,0:T(8,128)(2,1)}) %reduce-scatter.2.cloned.1.call-update) | async-done | bytes 524304 | tf_op jit(solution)/shard_map/reduce_scatter | solution.py:609
  (193 shorter events, 74.2 us)
Async XLA Ops:
  7.2 128.6 %all-gather.3.cloned.1.call-start = ((), (), s32[]{:S(2)}) async-start(), calls=%async_computation.2 | async-start | bytes 17436672 | tf_op jit(solution)/shard_map/all_gather | solution.py:548
  17.3 502.3 %reduce-scatter.2.cloned.1.call-start = ((), (), s32[]{:S(2)}) async-start(), calls=%async_computation.1 | async-start | bytes 17301504 | tf_op jit(solution)/shard_map/reduce_scatter | solution.py:609
  163.0 4.0 collective-permute-start
  167.8 3.8 collective-permute-start.1
  171.7 4.7 collective-permute-start.2
  191.7 15.0 %copy-start.8 = (bf16[2,256,512]{2,1,0:T(8,128)(2,1)S(1)}, bf16[2,256,512]{2,1,0:T(8,128)(2,1)}, u32[]{:S(2)}) copy-start(bf16[2,256,512]{2,1,0:T(8,128)(2,1)} %param.23) | copy-start | bytes 1572868
  201.5 4.0 collective-permute-start.3
  206.3 3.8 collective-permute-start.4
  210.1 4.7 collective-permute-start.5
  242.3 4.0 collective-permute-start.6
  247.1 3.8 collective-permute-start.7
  251.0 4.7 collective-permute-start.8
  279.1 9.1 %copy-start.11 = (f32[4,1024]{1,0:T(4,128)S(1)}, f32[4,1024]{1,0:T(4,128)}, u32[]{:S(2)}) copy-start(f32[4,1024]{1,0:T(4,128)} %get-tuple-element.122) | copy-start | bytes 49156
  279.1 9.1 %collective-permute-start.9 = (f32[4,1024]{1,0:T(4,128)}, f32[4,1024]{1,0:T(4,128)S(1)}, u32[]{:S(2)}, u32[]{:S(2)}) collective-permute-start(f32[4,1024]{1,0:T(4,128)} %get-tuple-element.122), channel_id=1, source_target_pairs={{0,4},{4,0},{8,12},{12,8},{16,20},{20,16},{24,28},{28,24},{1,5},{5... | collective-permute-start | bytes 49160 | tf_op jit(solution)/shard_map/ppermute | solution.py:498
  288.3 7.9 %collective-permute-start.10 = (f32[4,1024]{1,0:T(4,128)S(1)}, f32[4,1024]{1,0:T(4,128)S(1)}, u32[]{:S(2)}, u32[]{:S(2)}) collective-permute-start(f32[4,1024]{1,0:T(4,128)S(1)} %pad_maximum_fusion.6), channel_id=1, source_target_pairs={{0,8},{4,12},{8,0},{12,4},{16,24},{20,28},{24,16},{28,20},{1,9},{5... | collective-permute-start | bytes 49160 | tf_op jit(solution)/shard_map/ppermute | solution.py:498
  296.3 7.3 %collective-permute-start.11 = (f32[4,1024]{1,0:T(4,128)S(1)}, f32[4,1024]{1,0:T(4,128)S(1)}, u32[]{:S(2)}, u32[]{:S(2)}) collective-permute-start(f32[4,1024]{1,0:T(4,128)S(1)} %pad_maximum_fusion.7), channel_id=1, source_target_pairs={{0,16},{4,20},{8,24},{12,28},{16,0},{20,4},{24,8},{28,12},{1,17},{... | collective-permute-start | bytes 49160 | tf_op jit(solution)/shard_map/ppermute | solution.py:498
  314.4 10.4 %copy-start.4 = (bf16[8,4,256,128]{3,2,1,0:T(8,128)(2,1)S(1)}, bf16[8,4,256,128]{3,2,1,0:T(8,128)(2,1)}, u32[]{:S(2)}) copy-start(bf16[8,4,256,128]{3,2,1,0:T(8,128)(2,1)} %get-tuple-element.140) | copy-start | bytes 6291460
  320.3 6.5 %copy-start.3 = (bf16[8,4,256,128]{3,2,1,0:T(8,128)(2,1)S(1)}, bf16[8,4,256,128]{3,2,1,0:T(8,128)(2,1)}, u32[]{:S(2)}) copy-start(bf16[8,4,256,128]{3,2,1,0:T(8,128)(2,1)} %get-tuple-element.141) | copy-start | bytes 6291460
  324.9 4.9 copy-start
  329.8 4.4 copy-start.1
  337.3 4.9 copy-start.12
  337.3 4.9 copy-start.17
  337.3 5.7 %copy-start.10 = (bf16[512,512]{1,0:T(8,128)(2,1)S(1)}, bf16[512,512]{1,0:T(8,128)(2,1)}, u32[]{:S(2)}) copy-start(bf16[512,512]{1,0:T(8,128)(2,1)} %get-tuple-element.123) | copy-start | bytes 1572868
  337.3 6.6 %copy-start.13 = (f32[2,1024]{1,0:T(2,128)S(1)}, f32[2,1024]{1,0:T(2,128)}, u32[]{:S(2)}) copy-start(f32[2,1024]{1,0:T(2,128)} %get-tuple-element.125) | copy-start | bytes 24580
  (9 other events, 24.6 us)
Sparse Core Ops, SparseCore 0:
  17.4 118.3 all-gather.2
  337.4 182.0 reduce-scatter.1

commit v2 on v1

v2 whole, which is shorter than its diff:
```python
import functools

import jax
import jax.numpy as jnp
from jax import lax
from jax.experimental import pallas as pl
from jax.experimental.pallas import tpu as pltpu
from jax.sharding import PartitionSpec as P

LAYERS = 2
EPS = 1e-05
NS, NB, LANE = 8, 4, 128
CHUNKS = 8
VMEM = 56 * 1024 * 1024
F32, BF16 = jnp.float32, jnp.bfloat16


def dot(left, right):
    return lax.dot_general(left, right, (((1,), (0,)), ((), ())), preferred_element_type=F32)


def dot_nt(left, right):
    return lax.dot_general(left, right, (((1,), (1,)), ((), ())), preferred_element_type=F32)


def dot_tn(left, right):
    return lax.dot_general(left, right, (((0,), (0,)), ((), ())), preferred_element_type=F32)


def columns_of(ref, slabs=2):
    rows = ref.shape[2] // slabs
    parts = [ref[:, 0, j * rows : (j + 1) * rows, :].reshape(NS * rows, LANE) for j in range(slabs)]
    return jnp.concatenate(parts, axis=1)


def rows_of(ref):
    parts = [ref[:, j].reshape(-1, LANE) for j in range(NB)]
    return jnp.concatenate(parts, axis=1)


def rms_scale(values):
    return lax.rsqrt(jnp.mean(values * values, axis=-1, keepdims=True) + EPS)


def rms_back(values, gain, grad):
    scale = rms_scale(values)
    unit = values * scale
    inner = grad * gain
    back = scale * (inner - unit * jnp.mean(inner * unit, axis=-1, keepdims=True))
    return back, jnp.sum(grad * unit, axis=0, keepdims=True)


def gate_kernel(
    seqs, steps, x_ref, gain_ref, bias_ref, wf_ref, wi_ref, wc_ref,
    normed_ref, decay_ref, inflow_ref, cand_ref, ff_ref, fi_ref, fc_ref, cp_ref, ch_ref, fin_ref,
    zf, zi, zc,
):
    width = 2 * LANE

    @pl.when(pl.program_id(0) == 0)
    def _():
        x = x_ref[...].astype(F32)
        normed_ref[...] = (x * rms_scale(x) * gain_ref[0:1, :]).astype(BF16)

    normed = normed_ref[...]
    zf[...] = dot(normed, columns_of(wf_ref)) + bias_ref[0:1, :]
    zi[...] = dot(normed, columns_of(wi_ref)) + bias_ref[1:2, :]
    zc[...] = dot(normed, columns_of(wc_ref))

    block = 4 * CHUNKS

    def turn(at, carry):
        carry = list(carry)
        for seq in range(seqs):
            span = pl.ds(pl.multiple_of(seq * steps * CHUNKS + at * block, block), block)
            f, i, c = zf[span, :], zi[span, :], zc[span, :]
            low = jnp.minimum(jnp.minimum(f, i), 0.0)
            e0, ef, ei = jnp.exp(low), jnp.exp(low - f), jnp.exp(low - i)
            a, b = e0 + ef, e0 + ei
            inv = 1.0 / (a + b)
            decay, other = b * inv, a * inv
            ec = jnp.exp(-jnp.abs(c))
            cand = jnp.maximum(c, 0.0) + jnp.log1p(ec)
            slope = jnp.where(c >= 0.0, 1.0, ec) / (1.0 + ec)
            inflow = other * cand
            decay_ref[span, :] = decay
            inflow_ref[span, :] = inflow
            cand_ref[span, :] = cand
            ff_ref[span, :] = (ef * inv * decay).astype(BF16)
            fi_ref[span, :] = (ei * inv * other).astype(BF16)
            fc_ref[span, :] = (other * slope).astype(BF16)
            prod, state = carry[2 * seq], carry[2 * seq + 1]
            for k in range(4):
                d = decay[k * CHUNKS : (k + 1) * CHUNKS]
                prod = prod * d
                state = state * d + inflow[k * CHUNKS : (k + 1) * CHUNKS]
            carry[2 * seq], carry[2 * seq + 1] = prod, state
        return tuple(carry)

    one, zero = jnp.ones((CHUNKS, width), F32), jnp.zeros((CHUNKS, width), F32)
    carry = lax.fori_loop(0, steps // 4, turn, (one, zero) * seqs)
    for seq in range(seqs):
        prod, state = carry[2 * seq], carry[2 * seq + 1]
        cp_ref[seq], ch_ref[seq] = prod, state
        whole, last = prod[0:1], state[0:1]
        for c in range(1, CHUNKS):
            whole, last = whole * prod[c : c + 1], last * prod[c : c + 1] + state[c : c + 1]
        fin_ref[seq : seq + 1, :] = whole
        fin_ref[seqs + seq : seqs + seq + 1, :] = last


def mix_kernel(
    seqs, steps, x_ref, gain_ref, decay_ref, inflow_ref, cp_ref, ch_ref, ent_ref, wo_ref, wu_ref, wd_ref,
    hidden_ref, hb_ref, e_ref, mid_ref, n2_ref, act_ref, slope_ref, out_ref,
    acc, pre,
):
    at_step = pl.program_id(0)
    block = 4 * CHUNKS

    @pl.when(at_step == 0)
    def _():
        acc[...] = x_ref[...].astype(F32)

    @pl.when(at_step < NB)
    def _():
        for seq in range(seqs):
            state = ent_ref[seq : seq + 1, :]
            for c in range(CHUNKS):
                e_ref[seq, c : c + 1, :] = state
                state = state * cp_ref[seq, c : c + 1, :] + ch_ref[seq, c : c + 1, :]

        def turn(at, carry):
            carry = list(carry)
            for seq in range(seqs):
                span = pl.ds(pl.multiple_of(seq * steps * CHUNKS + at * block, block), block)
                d, u = decay_ref[span, :], inflow_ref[span, :]
                state, found = carry[seq], []
                for k in range(4):
                    state = state * d[k * CHUNKS : (k + 1) * CHUNKS] + u[k * CHUNKS : (k + 1) * CHUNKS]
                    found.append(state)
                carry[seq] = state
                hidden = jnp.concatenate(found, axis=0)
                hidden_ref[span, :] = hidden
                hb_ref[span, :] = hidden.astype(BF16)
            return tuple(carry)

        lax.fori_loop(0, steps // 4, turn, tuple(e_ref[seq] for seq in range(seqs)))
        acc[...] += dot(hb_ref[...], rows_of(wo_ref))

    @pl.when(at_step == NB - 1)
    def _():
        middle = acc[...]
        mid_ref[...] = middle
        n2_ref[...] = (middle * rms_scale(middle) * gain_ref[1:2, :]).astype(BF16)

    @pl.when(at_step >= NB)
    def _():
        pre[...] = dot(n2_ref[...], columns_of(wu_ref, 4))

        def turn(at, _):
            span = pl.ds(pl.multiple_of(at * 16, 16), 16)
            v = pre[span, :]
            phi = 0.5 + 0.5 * lax.erf(v * 0.7071067811865476)
            act_ref[span, :] = (v * phi).astype(BF16)
            slope_ref[span, :] = (phi + v * (0.3989422804014327 * jnp.exp(v * v * -0.5))).astype(BF16)
            return 0

        lax.fori_loop(0, pre.shape[0] // 16, turn, 0)
        acc[...] += dot(act_ref[...], rows_of(wd_ref))

    @pl.when(at_step == 2 * NB - 1)
    def _():
        out_ref[...] = acc[...].astype(out_ref.dtype)


def mlp_back_kernel(
    seqs, steps, g_ref, gain_ref, mid_ref, slope_ref, decay_ref, wo_ref, wu_ref, wd_ref,
    gr_ref, gpre_ref, gmid_ref, go_ref, ggain_ref, gh_ref, cp_ref, ca_ref, fin_ref,
    acc,
):
    at_step = pl.program_id(0)
    block = 4 * CHUNKS
    width = decay_ref.shape[1]

    @pl.when(at_step == 0)
    def _():
        gr_ref[...] = g_ref[...].astype(BF16)
        acc[...] = jnp.zeros_like(acc)

    @pl.when(at_step < NB)
    def _():
        gact = dot_nt(gr_ref[...], rows_of(wd_ref))
        gpre_ref[...] = (gact * slope_ref[...].astype(F32)).astype(BF16)
        acc[...] += dot_nt(gpre_ref[...], columns_of(wu_ref, 4))

    @pl.when(at_step == NB - 1)
    def _():
        back, ggain = rms_back(mid_ref[...], gain_ref[1:2, :], acc[...])
        ggain_ref[...] = ggain
        gmid = g_ref[...].astype(F32) + back
        gmid_ref[...] = gmid
        go_ref[...] = gmid.astype(BF16)

    @pl.when(at_step >= NB)
    def _():
        gh_ref[...] = dot_nt(go_ref[...], rows_of(wo_ref))

        def turn(turn_at, carry):
            at = steps // 4 - 1 - turn_at
            carry = list(carry)
            for seq in range(seqs):
                span = pl.ds(pl.multiple_of(seq * steps * CHUNKS + at * block, block), block)
                d, g = decay_ref[span, :], gh_ref[span, :]
                prod, state = carry[2 * seq], carry[2 * seq + 1]
                for k in reversed(range(4)):
                    dk = d[k * CHUNKS : (k + 1) * CHUNKS]
                    prod = prod * dk
                    state = dk * (g[k * CHUNKS : (k + 1) * CHUNKS] + state)
                carry[2 * seq], carry[2 * seq + 1] = prod, state
            return tuple(carry)

        one, zero = jnp.ones((CHUNKS, width), F32), jnp.zeros((CHUNKS, width), F32)
        carry = lax.fori_loop(0, steps // 4, turn, (one, zero) * seqs)
        for seq in range(seqs):
            prod, state = carry[2 * seq], carry[2 * seq + 1]
            cp_ref[seq], ca_ref[seq] = prod, state
            whole, last = prod[CHUNKS - 1 :], state[CHUNKS - 1 :]
            for c in reversed(range(CHUNKS - 1)):
                whole, last = whole * prod[c : c + 1], last * prod[c : c + 1] + state[c : c + 1]
            fin_ref[seq : seq + 1, :] = whole
            fin_ref[seqs + seq : seqs + seq + 1, :] = last


def gate_back_kernel(
    seqs, steps, x_ref, gain_ref, gmid_ref, gh_ref, decay_ref, hidden_ref, e_ref, cand_ref, ff_ref, fi_ref, fc_ref,
    cp_ref, ca_ref, ent_ref, wf_ref, wi_ref, wc_ref,
    dzf_ref, dzi_ref, dzc_ref, gbias_ref, gstream_ref, ggain_ref,
    acc, start,
):
    at_step = pl.program_id(0)
    block = 4 * CHUNKS
    width = decay_ref.shape[1]

    @pl.when(at_step == 0)
    def _():
        acc[...] = jnp.zeros_like(acc)

    for seq in range(seqs):
        state = ent_ref[seq : seq + 1, :]
        for c in reversed(range(CHUNKS)):
            start[seq, c : c + 1, :] = state
            state = state * cp_ref[seq, c : c + 1, :] + ca_ref[seq, c : c + 1, :]

    def turn(turn_at, carry):
        at = steps // 4 - 1 - turn_at
        carry = list(carry)
        sum_f, sum_i = carry[seqs], carry[seqs + 1]
        for seq in range(seqs):
            base = seq * steps * CHUNKS + at * block
            span = pl.ds(pl.multiple_of(base, block), block)
            before = hidden_ref[pl.ds(pl.multiple_of(jnp.maximum(base - CHUNKS, 0), CHUNKS), CHUNKS), :]
            before = jnp.where(at == 0, e_ref[seq], before)
            d, g = decay_ref[span, :], gh_ref[span, :]
            previous = jnp.concatenate([before, hidden_ref[span, :][: block - CHUNKS]], axis=0)
            state, found = carry[seq], []
            for k in reversed(range(4)):
                now = g[k * CHUNKS : (k + 1) * CHUNKS] + state
                found.append(now)
                state = d[k * CHUNKS : (k + 1) * CHUNKS] * now
            carry[seq] = state
            gstate = jnp.concatenate(found[::-1], axis=0)
            both = gstate * (cand_ref[span, :] - previous)
            dzf = (-ff_ref[span, :].astype(F32) * both).astype(BF16)
            dzi = (fi_ref[span, :].astype(F32) * both).astype(BF16)
            dzf_ref[span, :] = dzf
            dzi_ref[span, :] = dzi
            dzc_ref[span, :] = (fc_ref[span, :].astype(F32) * gstate).astype(BF16)
            wide_f, wide_i = dzf.astype(F32), dzi.astype(F32)
            for k in range(4):
                sum_f = sum_f + wide_f[k * CHUNKS : (k + 1) * CHUNKS]
                sum_i = sum_i + wide_i[k * CHUNKS : (k + 1) * CHUNKS]
        carry[seqs], carry[seqs + 1] = sum_f, sum_i
        return tuple(carry)

    zero = jnp.zeros((CHUNKS, width), F32)
    carry = lax.fori_loop(0, steps // 4, turn, tuple(start[seq] for seq in range(seqs)) + (zero, zero))
    gbias_ref[0:1, :] = jnp.sum(carry[seqs], axis=0, keepdims=True)
    gbias_ref[1:2, :] = jnp.sum(carry[seqs + 1], axis=0, keepdims=True)
    acc[...] += (
        dot_nt(dzf_ref[...], columns_of(wf_ref))
        + dot_nt(dzi_ref[...], columns_of(wi_ref))
        + dot_nt(dzc_ref[...], columns_of(wc_ref))
    )

    @pl.when(at_step == NB - 1)
    def _():
        back, ggain = rms_back(x_ref[...].astype(F32), gain_ref[0:1, :], acc[...])
        ggain_ref[...] = ggain
        gstream_ref[...] = (gmid_ref[...] + back).astype(gstream_ref.dtype)


def send_or_keep(mine, keep_ref, send_ref, put):
    @pl.when(mine)
    def _():
        put(keep_ref)

    @pl.when(jnp.logical_not(mine))
    def _():
        put(send_ref)


def put_columns(pos_ref, keep_ref, send_ref, start, value):
    at = pl.program_id(0)
    x, core = at // 2, at % 2
    rows = value.shape[0] // NS

    def put(ref):
        for j in range(value.shape[1] // LANE):
            part = value[:, j * LANE : (j + 1) * LANE].astype(BF16).reshape(NS, rows, LANE)
            ref[:, x, start + j * rows : start + (j + 1) * rows, :] = part

    send_or_keep(core == pos_ref[0], keep_ref, send_ref, put)


def put_rows(pos_ref, keep_ref, send_ref, value):
    count = NS // NB
    for j in range(NB):
        part = value[:, j * LANE : (j + 1) * LANE].astype(BF16).reshape(count, -1, LANE)

        def put(ref):
            ref[pl.ds(pl.program_id(0) * count, count), j // 2] = part

        send_or_keep(pos_ref[0] == j % 2, keep_ref, send_ref, put)


def up_weight_kernel(pos_ref, n2_ref, gpre_ref, keep_ref, send_ref):
    put_columns(pos_ref, keep_ref, send_ref, 0, dot_tn(n2_ref[...], gpre_ref[...]))


def row_weight_kernel(pos_ref, left_ref, right_ref, keep_ref, send_ref):
    put_rows(pos_ref, keep_ref, send_ref, dot_tn(left_ref[...], right_ref[...]))


def gate_weight_kernel(vectors, pos_ref, normed_ref, dzf_ref, dzi_ref, dzc_ref, *refs):
    keep_ref, send_ref = refs[-3:-1] if vectors else refs[-2:]
    normed = normed_ref[...]
    rows = normed.shape[1] // NS * dzf_ref.shape[1] // LANE
    for m, dz in enumerate((dzf_ref, dzi_ref, dzc_ref)):
        put_columns(pos_ref, keep_ref, send_ref, m * rows, dot_tn(normed, dz[...]))
    if vectors:
        scratch = refs[-1]

        @pl.when(pl.program_id(0) == 0)
        def _():
            scratch[...] = jnp.zeros_like(scratch)
            row = 0
            for ref in refs[:-3]:
                wide = ref.shape[1] // NS
                for r in range(ref.shape[0]):
                    for s in range(NS):
                        scratch[s, row : row + 1, :wide] = ref[r : r + 1, s * wide : (s + 1) * wide]
                    row += 1
            found = scratch[...].astype(BF16)
            for x in range(2):
                keep_ref[:, x, 3 * rows :, :] = found
                send_ref[:, x, 3 * rows :, :] = found


def add(*parts):
    total = parts[0].astype(F32)
    for part in parts[1:]:
        total = total + part.astype(F32)
    return total


def pair_sum_kernel(rows, cut, pos_ref, *refs):
    count = len(rows)
    keeps, gots = refs[:count], refs[count : 2 * count]
    send_a, keep_a, send_b, keep_b = refs[2 * count :]
    x, y = pos_ref[1], pos_ref[2]
    at = 0
    for keep, got, r in zip(keeps, gots, rows):
        mid = min(max(cut - at, 0), r)
        if mid:
            for v in range(2):
                for out, ix in ((send_a, 1 - x), (keep_a, x)):
                    out[0, v, at : at + mid] = add(keep[0, v, ix, :mid], got[0, v, ix, :mid]).astype(BF16)
        if mid < r:
            low = at + mid - cut
            for v in range(2):
                for out, iy in ((send_b, 1 - y), (keep_b, y)):
                    out[0, v, low : low + r - mid] = add(keep[0, iy, v, mid:], got[0, iy, v, mid:]).astype(BF16)
        at += r


def plane_sum_kernel(pos_ref, keep_a, got_a, keep_b, got_b, send2_a, keep2_a, send2_b, keep2_b):
    x, y = pos_ref[1], pos_ref[2]
    for keep, got, send2, keep2, mine in ((keep_a, got_a, send2_a, keep2_a, y), (keep_b, got_b, send2_b, keep2_b, x)):
        send2[0] = add(keep[0, 1 - mine], got[0, 1 - mine]).astype(BF16)
        keep2[0] = add(keep[0, mine], got[0, mine]).astype(BF16)


def line_sum_kernel(pos_ref, keep_a, got_a, keep_b, got_b, *outs):
    cut = keep_a.shape[1]
    for k, out in enumerate(outs):
        z = pos_ref[3] ^ k
        out[:cut] = add(keep_a[z], got_a[z]).astype(BF16)
        out[cut:] = add(keep_b[z], got_b[z]).astype(BF16)


def line_total_kernel(*refs):
    refs[-1][...] = add(*[ref[...] for ref in refs[:-1]])


def finish_kernel(layout, *refs):
    at = 0
    ins = sum(parts for parts, _ in layout)
    outs = refs[ins:]
    for parts, pieces in layout:
        got = refs[at : at + parts]
        at += parts
        row = 0
        for out, layer, vectors in pieces:
            ref = outs[out]
            if vectors:
                ref[layer : layer + 1, :] = add(*[g[...] for g in got])[row : row + 1, : ref.shape[1]]
                row += 1
                continue
            r = ref.shape[1]
            for j in range(ref.shape[2] // LANE):
                ref[layer, :, j * LANE : (j + 1) * LANE] = add(*[g[row : row + r] for g in got])
                row += r


def pack_kernel(groups, *refs):
    ins = refs[: len(refs) - len(groups) - 1]
    outs, scratch = refs[len(ins) : -1], refs[-1]
    for out, group in zip(outs, groups):
        row = 0
        vec = 0
        for which, layer, vector in group:
            ref = ins[which]
            if vector:
                if vec == 0:
                    scratch[...] = jnp.zeros_like(scratch)
                scratch[vec : vec + 1, : ref.shape[1]] = ref[...].astype(F32)[layer : layer + 1]
                vec += 1
                continue
            r = ref.shape[1]
            for j in range(ref.shape[2] // LANE):
                out[row : row + r, :] = ref[layer, :, j * LANE : (j + 1) * LANE]
                row += r
        if vec:
            out[row:, :] = scratch[...].astype(BF16)


def line_gather_kernel(pos_ref, *refs):
    out = refs[-1]
    for k, part in enumerate(refs[:-1]):
        out[pos_ref[3] ^ k] = part[...]


def plane_gather_kernel(pos_ref, *refs):
    at, half, out = pl.program_id(0), pl.num_programs(0) // 2, refs[-1]
    core, x, y = pos_ref[0], pos_ref[1], pos_ref[2]
    count = len(refs) // 2
    for c in range(2):
        own, from_x, from_y, low = refs[count * c : count * c + 4]
        out[0, y, x, core ^ c] = own[0]
        out[0, y, x ^ 1, core ^ c] = from_x[0]
        out[0, y ^ 1, x, core ^ c] = from_y[0]

        if count == 4:
            out[0, y ^ 1, x ^ 1, core ^ c] = low[0]
            continue
        high = refs[count * c + 4]

        @pl.when(at < half)
        def _():
            out[0, y ^ 1, x ^ 1, core ^ c] = low[0]

        @pl.when(at >= half)
        def _():
            out[0, y ^ 1, x ^ 1, core ^ c] = high[0]


def vector_kernel(gained, w_ref, *refs):
    outs, scratch = refs[:-1], refs[-1]
    scratch[...] = w_ref[:, 0].astype(F32)
    for l in range(LAYERS):
        for which in range(4):
            out, row = ((outs[2 * l], which // 3) if which in (0, 3) else (outs[2 * l + 1], which - 1))
            wide = out.shape[1] // NS
            for s in range(NS):
                out[row : row + 1, s * wide : (s + 1) * wide] = scratch[s, 4 * l + which : 4 * l + which + 1, :wide]


def shape(dims, dtype=F32):
    return jax.ShapeDtypeStruct(dims, dtype)


def call(kernel, grid, ins, outs, scratch, us, name):
    moved = sum(a.size * a.dtype.itemsize for a, _, _ in ins)
    moved += sum(s.size * s.dtype.itemsize for s, _, _ in outs)

    def spec(a, block, index):
        if a.dtype == jnp.int32:
            return pl.BlockSpec(memory_space=pltpu.SMEM)
        return pl.BlockSpec(block, index)

    found = pl.pallas_call(
        kernel,
        grid=(grid,),
        in_specs=[spec(*one) for one in ins],
        out_specs=[spec(*one) for one in outs],
        out_shape=[s for s, _, _ in outs],
        scratch_shapes=scratch,
        compiler_params=pltpu.CompilerParams(vmem_limit_bytes=VMEM),
        cost_estimate=pl.CostEstimate(flops=int(us * 1.1e9) + 1, bytes_accessed=1024, transcendentals=0),
        name=name,
    )(*[a for a, _, _ in ins])
    return found if len(found) > 1 else found[0]


def whole(array):
    dims = array.shape
    return (array, dims, lambda i: (0,) * len(dims))


def whole_out(dims, dtype=F32):
    return (shape(dims, dtype), dims, lambda i: (0,) * len(dims))


def first(i):
    return jnp.minimum(i, NB - 1)


def second(i):
    return jnp.maximum(i - NB, 0)


class Sizes:
    def __init__(self, seqs, length, d, h, ff):
        self.seqs, self.steps, self.n = seqs, length // CHUNKS, seqs * length
        self.d, self.h, self.ff = d, h, ff
        self.hb, self.fb = h // NB, ff // NB


def column_weight(view, at):
    array, rows, place = view
    return (array, (NS, 1, rows, LANE), lambda i: (0, at(i), place, 0))


def row_weight(view, at):
    array, rows, place = view
    return (array, (NS // NB, NB, rows, LANE), lambda i: (at(i), 0, place, 0))


def same(i):
    return i


def gate_forward(sz, x, gain, bias, w):
    n, d, h, wide, s = sz.n, sz.d, sz.h, sz.hb, sz.seqs
    col = lambda i: (0, i)
    return call(
        functools.partial(gate_kernel, s, sz.steps), NB,
        [whole(x), whole(gain), (bias, (2, wide), col)] + [column_weight(w[m], same) for m in "fic"],
        [whole_out((n, d), BF16)]
        + [(shape((n, h)), (n, wide), col)] * 3
        + [(shape((n, h), BF16), (n, wide), col)] * 3
        + [(shape((s, CHUNKS, h)), (s, CHUNKS, wide), lambda i: (0, 0, i))] * 2
        + [(shape((2 * s, h)), (2 * s, wide), col)],
        [pltpu.VMEM((n, wide), F32)] * 3, 9, "gates",
    )


def mix_forward(sz, x, gain, decay, inflow, cp, ch, ent, wt, last):
    n, d, h, ff, w, f, s = sz.n, sz.d, sz.h, sz.ff, sz.hb, sz.fb, sz.seqs
    col = lambda i: (0, first(i))
    late = lambda i: (0, second(i))
    deep = lambda i: (0, 0, first(i))
    return call(
        functools.partial(mix_kernel, s, sz.steps), 2 * NB,
        [
            whole(x), whole(gain), (decay, (n, w), col), (inflow, (n, w), col),
            (cp, (s, CHUNKS, w), deep), (ch, (s, CHUNKS, w), deep), (ent, (s, w), col),
            row_weight(wt["o"], first), column_weight(wt["u"], second), row_weight(wt["d"], second),
        ],
        [
            (shape((n, h)), (n, w), col), (shape((n, h), BF16), (n, w), col),
            (shape((s, CHUNKS, h)), (s, CHUNKS, w), deep),
            whole_out((n, d)), whole_out((n, d), BF16),
            (shape((n, ff), BF16), (n, f), late), (shape((n, ff), BF16), (n, f), late),
            whole_out((n, d), BF16 if last else F32),
        ],
        [pltpu.VMEM((n, d), F32), pltpu.VMEM((n, f), F32)], 14, "mix",
    )


def mlp_backward(sz, g, gain, mid, slope, decay, wt):
    n, d, h, ff, w, f, s = sz.n, sz.d, sz.h, sz.ff, sz.hb, sz.fb, sz.seqs
    col = lambda i: (0, second(i))
    early = lambda i: (0, first(i))
    deep = lambda i: (0, 0, second(i))
    return call(
        functools.partial(mlp_back_kernel, s, sz.steps), 2 * NB,
        [
            whole(g), whole(gain), whole(mid), (slope, (n, f), early), (decay, (n, w), col),
            row_weight(wt["o"], second), column_weight(wt["u"], first), row_weight(wt["d"], first),
        ],
        [
            whole_out((n, d), BF16), (shape((n, ff), BF16), (n, f), early), whole_out((n, d)), whole_out((n, d), BF16),
            whole_out((1, d)), (shape((n, h)), (n, w), col),
            (shape((s, CHUNKS, h)), (s, CHUNKS, w), deep), (shape((s, CHUNKS, h)), (s, CHUNKS, w), deep),
            (shape((2 * s, h)), (2 * s, w), col),
        ],
        [pltpu.VMEM((n, d), F32)], 12, "mlp_back",
    )


def gate_backward(sz, x, gain, gmid, gh, decay, hidden, e, cand, ff_, fi_, fc_, cp, ca, ent, wt, last):
    n, d, h, w, s = sz.n, sz.d, sz.h, sz.hb, sz.seqs
    col = lambda i: (0, i)
    deep = lambda i: (0, 0, i)
    wide = lambda a: (a, (n, w), col)
    return call(
        functools.partial(gate_back_kernel, s, sz.steps), NB,
        [
            whole(x), whole(gain), whole(gmid), wide(gh), wide(decay), wide(hidden), (e, (s, CHUNKS, w), deep),
            wide(cand), wide(ff_), wide(fi_), wide(fc_), (cp, (s, CHUNKS, w), deep), (ca, (s, CHUNKS, w), deep),
            (ent, (s, w), col),
        ] + [column_weight(wt[m], same) for m in "fic"],
        [(shape((n, h), BF16), (n, w), col)] * 3
        + [(shape((2, h)), (2, w), col), whole_out((n, d), BF16 if last else F32), whole_out((1, d))],
        [pltpu.VMEM((n, d), F32), pltpu.VMEM((s, CHUNKS, w), F32)], 10, "gate_back",
    )


def up_weights(sz, pos, n2, gpre):
    n, d, ff, f = sz.n, sz.d, sz.ff, sz.fb
    dims = (NS, 2, d * ff // (32 * LANE), LANE)
    return call(
        up_weight_kernel, NB, [whole(pos), whole(n2), (gpre, (n, f), lambda i: (0, i))],
        [whole_out(dims, BF16)] * 2, [], 5, "up_weights",
    )


def row_weights(sz, pos, left, right, name):
    n, k, d = sz.n, left.shape[1], sz.d
    dims = (NS, 2, k // NS, LANE)
    return call(
        row_weight_kernel, NB, [whole(pos), (left, (n, k // NB), lambda i: (0, i)), whole(right)],
        [whole_out(dims, BF16)] * 2, [], 5, name,
    )


def gate_weights(sz, pos, normed, dzf, dzi, dzc, vectors):
    n, d, h, w = sz.n, sz.d, sz.h, sz.hb
    col = lambda i: (0, i)
    rows = 3 * d * h // (32 * LANE) + (16 if vectors else 0)
    return call(
        functools.partial(gate_weight_kernel, bool(vectors)), NB,
        [whole(pos), whole(normed), (dzf, (n, w), col), (dzi, (n, w), col), (dzc, (n, w), col)]
        + [whole(v) for v in vectors],
        [whole_out((NS, 2, rows, LANE), BF16)] * 2,
        [pltpu.VMEM((NS, 16, LANE), F32)] if vectors else [], 0, "gate_weights",
    )


def swap(array, axes, bits):
    count = lax.axis_size(axes)
    return lax.ppermute(array, axes, [(i, i ^ bits) for i in range(count)])


BOTH = ("seq", "batch")


def after(array, *others):
    return lax.optimization_barrier((array,) + others)[0]


def sum_cut(rows):
    total = sum(rows)
    if len(rows) == 1:
        return total // 2 // 16 * 16
    return rows[0] if rows[0] * 5 >= total * 2 else rows[0] + rows[1]


def by_line(a):
    return (a, (1,) + a.shape[1:], lambda i: (i,) + (0,) * (len(a.shape) - 1))


def by_line_out(*dims):
    return (shape(dims, BF16), (1,) + dims[1:], lambda i: (i,) + (0,) * (len(dims) - 1))


def core_exchange(pairs):
    return [(keep, swap(send, "batch", 1)) for keep, send in pairs]


def pair_sum(pos, pairs):
    rows = tuple(keep.shape[2] for keep, _ in pairs)
    cut, total = sum_cut(rows), sum(rows)
    view = lambda a: by_line(a.reshape((4, 2, 2) + a.shape[2:]))
    two = [by_line_out(4, 2, cut, LANE)] * 2 + [by_line_out(4, 2, total - cut, LANE)] * 2
    return call(
        functools.partial(pair_sum_kernel, rows, cut), 4,
        [whole(pos)] + [view(keep) for keep, _ in pairs] + [view(got) for _, got in pairs], two, [], 0, "pair_sum",
    )


def plane_exchange(parts, first, second):
    send_a, keep_a, send_b, keep_b = parts
    return keep_a, swap(send_a, *first), keep_b, swap(send_b, *second)


X_AXIS, Y_AXIS = ("batch", 2), ("seq", 1)


def plane_sum(pos, parts):
    cut, rest = parts[0].shape[2], parts[2].shape[2]
    one = [by_line_out(4, cut, LANE)] * 2 + [by_line_out(4, rest, LANE)] * 2
    return call(plane_sum_kernel, 4, [whole(pos)] + [by_line(a) for a in parts], one, [], 0, "plane_sum")


def line_sum(pos, parts):
    total = parts[0].shape[1] + parts[2].shape[1]
    return call(
        line_sum_kernel, 1, [whole(pos)] + [whole(a) for a in parts], [whole_out((total, LANE), BF16)] * 4, [], 0, "line_sum",
    )


def line_exchange(parts):
    return [parts[0]] + [swap(part, "seq", 2 * (k + 1)) for k, part in enumerate(parts[1:])]


def reduce_rest(pos, parts):
    parts = plane_sum(pos, plane_exchange(parts, X_AXIS, Y_AXIS))
    return line_exchange(line_sum(pos, plane_exchange(parts, Y_AXIS, X_AXIS)))


def gather(pos, owns, direct):
    lines = []
    for own in owns:
        if lines:
            own = after(own, *lines[:2])
        parts = [own] + [swap(own, "seq", 2 * k) for k in range(1, 4)]
        lines.append(
            call(
                line_gather_kernel, 1, [whole(pos)] + [whole(p) for p in parts],
                [whole_out((4,) + own.shape, BF16)], [], 2, "line_gather",
            )
        )
    found, last = [], ()
    for at, line in enumerate(lines):
        rows = line.shape[1]
        sent = after(line, *last) if last else line
        from_x, from_y = swap(sent, *X_AXIS), swap(sent, *Y_AXIS)
        if at in direct:
            diagonal = swap(sent, BOTH, 6)
            last = (from_x, from_y, diagonal)
            parts = [line, from_x, from_y, diagonal]
        else:
            low, high = swap(from_x[:2], *Y_AXIS), swap(from_y[2:], *X_AXIS)
            last = (from_x, from_y) if at == 0 else (low, high)
            parts = [line, from_x, from_y, low, high]
        parts += [swap(p, "batch", 1) for p in parts]
        maps = [lambda i: (i, 0, 0)] * 3
        maps += maps[:1] if at in direct else [lambda i: (jnp.minimum(i, 1), 0, 0), lambda i: (jnp.maximum(i - 2, 0), 0, 0)]
        place = lambda i: (i, 0, 0, 0, 0, 0)
        got = call(
            plane_gather_kernel, 4, [whole(pos)] + [(p, (1, rows, LANE), m) for p, m in zip(parts, maps * 2)],
            [(shape((4, 2, 2, 2, rows, LANE), BF16), (1, 2, 2, 2, rows, LANE), place)], [], 5, "plane_gather",
        )
        found.append(got.reshape(NS, NB, rows, LANE))
    return found, lines


def enter(fin, seqs, backward, fill=()):
    count, mine = lax.axis_size("seq"), lax.axis_index("seq")
    prod, state = fin[:seqs], fin[seqs:]
    pre_p, pre_s = jnp.ones_like(prod), jnp.zeros_like(state)
    bit, message, done = 1, fin, []
    for step in range(int(count).bit_length() - 1):
        other = lax.ppermute(message, "seq", [(i, i ^ bit) for i in range(count)])
        if step < len(fill):
            done.append(fill[step](message))
        o_p, o_s = other[:seqs], other[seqs:]
        upper = ((mine // bit) % 2 == 1) ^ backward
        pre_p, pre_s = jnp.where(upper, o_p * pre_p, pre_p), jnp.where(upper, pre_p * o_s + pre_s, pre_s)
        state = jnp.where(upper, prod * o_s + state, o_p * state + o_s)
        prod = prod * o_p
        message = jnp.concatenate([prod, state])
        if step < len(fill):
            message = after(message, *done[-1])
        bit *= 2
    return pre_s, done


def slabs(matrix, seq_count, batch_count):
    rows, cols = matrix.shape[0] // NS, matrix.shape[1] // NB
    cut = matrix.reshape(NS, rows, NB, cols // LANE, LANE).transpose(0, 2, 3, 1, 4)
    return cut.reshape(NS, NB, rows * cols // LANE, LANE)


def unslab(blocks, rows, cols):
    r, c = rows // NS, cols // NB
    cut = blocks.reshape(NS, NB, c // LANE, r, LANE).transpose(0, 3, 1, 2, 4)
    return cut.reshape(rows, cols)


def body(
    tokens, norm_gain, w_forget, w_input, w_cand, forget_bias, input_bias, w_out, mlp_gain, w_up, w_down, cotangent
):
    seqs, length, d = tokens.shape
    seq_count, batch_count = lax.axis_size("seq"), lax.axis_size("batch")
    h, ff = w_forget.shape[2] * batch_count, w_up.shape[2] * batch_count
    sz = Sizes(seqs, length, d, h, ff)
    standard = (seq_count, batch_count) == (NS, NB)
    matrices = {"u": w_up, "d": w_down, "o": w_out, "f": w_forget, "i": w_input, "c": w_cand}
    vectors = (norm_gain, forget_bias, input_bias, mlp_gain)
    slab_rows = {"u": d * ff // (32 * LANE), "d": ff // NS, "o": h // NS}
    slab_rows.update({m: d * h // (32 * LANE) for m in "fic"})
    order = {name: k for k, name in enumerate(matrices)}

    if standard:
        s_at, b_at = lax.axis_index("seq"), lax.axis_index("batch")
        pos = jnp.stack([b_at % 2, b_at // 2, s_at % 2, s_at // 2]).astype(jnp.int32)
        groups = []
        for l in range(LAYERS):
            vecs = [(6 + k, at, True) for at in range(LAYERS) for k in range(4)] if l == 0 else []
            groups += [[(order[m], l, False) for m in "fic"] + vecs, [(order[m], l, False) for m in "udo"]]
        rows = [sum(slab_rows["udofic"[which]] for which, _, vec in g if not vec) for g in groups]
        rows[0] += 16
        packs = call(
            functools.partial(pack_kernel, groups), 1, [whole(m) for m in matrices.values()] + [whole(v) for v in vectors],
            [whole_out((r, LANE), BF16) for r in rows], [pltpu.VMEM((16, LANE), F32)], 2, "pack",
        )
        got, lines = gather(pos, packs, (2,))
        places = {"f": 0, "i": 1, "c": 2, "u": 0, "d": 1, "o": 4}
        weights = [{m: (got[2 * l + (m in "udo")], slab_rows[m], places[m]) for m in "udofic"} for l in range(LAYERS)]
        vecs = call(
            functools.partial(vector_kernel, None), 1,
            [(got[0], (NS, 1, 16, LANE), lambda i: (0, 0, 3 * slab_rows["f"] // 16, 0))],
            [whole_out((2, size)) for l in range(LAYERS) for size in (d, h)],
            [pltpu.VMEM((NS, 16, LANE), F32)], 1, "vectors",
        )
        gains, biases = vecs[0::2], vecs[1::2]
    else:
        pos = jnp.zeros((4,), jnp.int32)

        def full(m):
            m = lax.all_gather(m, "batch", axis=1, tiled=True)
            return lax.all_gather(m, "seq", axis=0, tiled=True)

        weights = [
            {m: (slabs(full(matrices[m][l]), NS, NB), slab_rows[m], 0) for m in "udofic"} for l in range(LAYERS)
        ]
        whole_vectors = [lax.all_gather(v, "seq", axis=1, tiled=True).astype(F32) for v in vectors]
        gains = [jnp.stack([whole_vectors[0][l], whole_vectors[3][l]]) for l in range(LAYERS)]
        biases = [jnp.stack([whole_vectors[1][l], whole_vectors[2][l]]) for l in range(LAYERS)]

    def to_rows(v):
        return v.reshape(seqs, CHUNKS, sz.steps, d).transpose(0, 2, 1, 3).reshape(sz.n, d)

    def from_rows(v):
        return v.reshape(seqs, sz.steps, CHUNKS, d).transpose(0, 2, 1, 3).reshape(seqs, length, d)

    stream, grad = to_rows(tokens), to_rows(cotangent)
    kept = []
    for l in range(LAYERS):
        normed, decay, inflow, cand, f_f, f_i, f_c, cp, ch, fin = gate_forward(sz, stream, gains[l], biases[l], weights[l])
        ent, _ = enter(fin, seqs, False)
        if standard and l + 1 < LAYERS:
            ent = after(ent, lines[2 * l + 3])
        hidden, hb, e, mid, n2, act, slope, result = mix_forward(
            sz, stream, gains[l], decay, inflow, cp, ch, ent, weights[l], l == LAYERS - 1
        )
        kept.append((stream, normed, decay, cand, f_f, f_i, f_c, hidden, hb, e, mid, n2, act, slope))
        stream = result
    output = from_rows(stream)

    vector_grads, sums, pending = [None] * LAYERS, [], []
    waiting, held = None, []
    for l in reversed(range(LAYERS)):
        x, normed, decay, cand, f_f, f_i, f_c, hidden, hb, e, mid, n2, act, slope = kept[l]
        gr, gpre, gmid, go, ggain_two, gh, cp, ca, fin = mlp_backward(sz, grad, gains[l], mid, slope, decay, weights[l])
        if waiting:
            names, parts = waiting
            parts = line_sum(pos, [after(parts[0], fin), *parts[1:]])
            gpre = after(gpre, parts[0])
            waiting = (names, line_exchange(parts))
        fill = [
            lambda m: up_weights(sz, pos, after(n2, m), gpre),
            lambda m: row_weights(sz, pos, after(act, m), gr, "down_weights"),
            lambda m: row_weights(sz, pos, after(hb, m), go, "out_weights"),
        ]
        ent, pairs = enter(fin, seqs, True, fill)
        if standard:
            names = [(l, m) for m in "udo"] + (held[0] if held else [])
            early = pair_sum(pos, core_exchange(pairs) + held[1:])
            gmid = after(gmid, early[0])
        dzf, dzi, dzc, gbias, grad, ggain_one = gate_backward(
            sz, x, gains[l], gmid, gh, decay, hidden, e, cand, f_f, f_i, f_c, cp, ca, ent, weights[l], l == 0
        )
        vector_grads[l] = (ggain_one, gbias, ggain_two)
        final = [v for each in vector_grads for v in each] if l == 0 and standard else []
        gate_pair = gate_weights(sz, pos, normed, dzf, dzi, dzc, final)
        if not standard:
            pending.append((l, pairs + [gate_pair]))
            continue
        parts = list(plane_exchange(early, X_AXIS, Y_AXIS))
        parts[0] = after(parts[0], gate_pair[0])
        parts = plane_sum(pos, parts)
        if l > 0:
            held = [[(l, m) for m in "fic"]] + core_exchange([gate_pair])
            grad = after(grad, parts[0])
            waiting = (names, plane_exchange(parts, Y_AXIS, X_AXIS))
        else:
            done = parts[0]
            if waiting:
                names_1, parts_1 = waiting
                parts_1[0] = after(parts_1[0], gate_pair[0])
                done = call(line_total_kernel, 1, [whole(p) for p in parts_1], [whole_out(parts_1[0].shape)], [], 0, "line_total")
                sums.append((names_1, [done]))
            late = pair_sum(pos, core_exchange([(gate_pair[0], after(gate_pair[1], parts[0], done))]))
            sums.append((names, line_exchange(line_sum(pos, plane_exchange(parts, Y_AXIS, X_AXIS)))))
            sums.append(([(l, m) for m in "fic"] + [(at, k) for at in range(LAYERS) for k in range(4)], reduce_rest(pos, late)))
    grad_tokens = from_rows(grad)

    if standard:
        layout, ins = [], []
        for names, parts in sums:
            pieces = [(order[m], l, False) if m in order else (6 + m, l, True) for l, m in names]
            layout.append((len(parts), pieces))
            ins += [whole(p) for p in parts]
        found = call(
            functools.partial(finish_kernel, layout), 1, ins,
            [whole_out(m.shape) for m in matrices.values()] + [whole_out(v.shape) for v in vectors], [], 3, "finish",
        )
        g_up, g_down, g_out, g_f, g_i, g_c, g_norm, g_fb, g_ib, g_mlp = found
    else:
        per_layer = {}
        for l, pairs in pending:
            blocks = [jnp.stack([keep, send], axis=2).reshape(NS, NB, -1, LANE) for keep, send in pairs]
            gates = jnp.split(blocks[3], 3, axis=2)
            for m, g in zip("udofic", blocks[:3] + gates):
                v = unslab(g, matrices[m].shape[1] * seq_count, matrices[m].shape[2] * batch_count)
                v = lax.psum_scatter(v, "seq", scatter_dimension=0, tiled=True)
                per_layer[m, l] = lax.psum_scatter(v, "batch", scatter_dimension=1, tiled=True).astype(F32)
        g_up, g_down, g_out, g_f, g_i, g_c = [
            jnp.stack([per_layer[m, l] for l in range(LAYERS)]) for m in matrices
        ]
        rows = [
            (ggain_one[0], gbias[0], gbias[1], ggain_two[0]) for ggain_one, gbias, ggain_two in vector_grads
        ]
        g_norm, g_fb, g_ib, g_mlp = [
            lax.psum(lax.psum_scatter(jnp.stack([r[k] for r in rows]), "seq", scatter_dimension=1, tiled=True), "batch")
            for k in range(4)
        ]
    return output, grad_tokens, g_norm, g_f, g_i, g_c, g_fb, g_ib, g_out, g_mlp, g_up, g_down


def solution(mesh):
    split, vector, matrix = P("batch", "seq", None), P(None, "seq"), P(None, "seq", "batch")
    order = (vector, matrix, matrix, matrix, vector, vector, matrix, vector, matrix, matrix)
    return jax.shard_map(
        body,
        mesh=mesh,
        in_specs=(split,) + order + (split,),
        out_specs=(split, split) + order,
        check_vma=False,
    )
```

time: 535 us -> 417 us (0.78)
  waiting for transfers between devices: 270 us -> 93.2 us
  Pallas kernels: 120 us -> 209 us
  starting transfers between devices: 14.3 us -> 83.7 us
  blocking collectives: 41.9 us -> 0 us
  local copies, waits for them, and re-layouts: 56.1 us -> 21.5 us
  between operations: 14.7 us -> 1.57 us
  other arithmetic: 15.4 us -> 5.7 us
    reduce_scatter x1 -> x0, waiting for transfers between devices: 131 us -> none  [body(): mine = lax.psum_scatter(sent, both, scatter_dimension=0, tiled=False)]
    all_gather x1 -> x0, waiting for transfers between devices: 116 us -> none  [body(): lax.all_gather(pack, both, axis=0, tiled=False).reshape(NS, NB, -1, LANE)]
    pallas_call x12 -> x37, Pallas kernels: 120 us -> 209 us  [call(): pl.pallas_call(kernel, grid=(grid,), in_specs=[spec(*one) for one in ins]...]
    ppermute x12 -> x87, waiting for transfers between devices: 23.2 us -> 93.2 us  [the longest x75 83.8 us: swap(): return lax.ppermute(array, axes, [(i, i ^ bits) for i in range(count)])]
    ppermute x12 -> x87, starting transfers between devices: 14.3 us -> 83.7 us  [the longest x75 65.5 us: swap(): return lax.ppermute(array, axes, [(i, i ^ bits) for i in range(count)])]
    unnamed x1 -> x0, blocking collectives: 35.5 us -> none
    slice x15 -> x6, local copies, waits for them, and re-layouts: 22.9 us -> 0.12 us  [gather(): low, high = (swap(from_x[:2], *Y_AXIS), swap(from_y[2:], *X_AXIS))]
    psum x1 -> x0, blocking collectives: 6.45 us -> none  [body(): lax.psum(lax.psum_scatter(small, 'seq', scatter_dimension=0, tiled=True),...]
  transfers between devices with their start and end apart: 14 -> 87, of which waited for: 11 -> 30; matrix products, arithmetic and copies ran while one was open for 3% -> 2% of each run, Pallas kernels for 4% -> 35%
where the time goes in v2:
time: 417 us; the launch traced here: 414 us
  Pallas kernels  209 us (50%)
  waiting for transfers between devices  93.2 us (22%)
  starting transfers between devices  83.7 us (20%)
  local copies, waits for them, and re-layouts  21.5 us (5%)
  other arithmetic  5.7 us (1%)
    pallas_call x37, Pallas kernels, call(): pl.pallas_call(kernel, grid=(grid,), in_specs=[spec(*one) for one in ins]...  209 us
    ppermute x75, waiting for transfers between devices, swap(): return lax.ppermute(array, axes, [(i, i ^ bits) for i in range(count)])  83.8 us
    ppermute x75, starting transfers between devices, swap(): return lax.ppermute(array, axes, [(i, i ^ bits) for i in range(count)])  65.5 us
    ppermute x12, starting transfers between devices, enter(): other = lax.ppermute(message, 'seq', [(i, i ^ bit) for i in range(count)])  18.2 us
    unnamed x164, local copies, waits for them, and re-layouts  17.3 us
    ppermute x12, waiting for transfers between devices, enter(): other = lax.ppermute(message, 'seq', [(i, i ^ bit) for i in range(count)])  9.49 us
  transfers between devices with their start and end apart: 87, of which 30 were waited for; matrix products, arithmetic and copies ran while one was open for 2% of the time, Pallas kernels for 35%

profile of v2, /device:TPU:0, one launch (start us, length us, event | category | flops | bytes accessed | tf_op | source)
XLA Modules:
  0.0 414.4 jit_solution(7702414084762407873)
XLA Ops:
  50.5 9.6 %gates.2 = (bf16[512,512]{1,0:T(8,128)(2,1)}, f32[512,1024]{1,0:T(8,128)}, f32[512,1024]{1,0:T(8,128)}, f32[512,1024]{1,0:T(8,128)}, bf16[512,1024]{1,0:T(8,128)...) custom-call(bf16[512,512]{1,0:T(8,128)(2,1)} %bitcast.56, ...), custom_call_target="tpu_custom_call" | custom-call | flops 9900000256 | bytes 1024 | tf_op jit(solution)/shard_map/gates/pallas_call | solution.py:511
  78.4 6.2 %collective-permute-start.14 = (f32[4,1024]{1,0:T(4,128)S(1)}, f32[4,1024]{1,0:T(4,128)S(1)}, u32[]{:S(2)}, u32[]{:S(2)}) collective-permute-start(f32[4,1024]{1,0:T(4,128)S(1)} %pad_maximum_fusion.1), channel_id=1, source_target_pairs={{0,16},{4,20},{8,24},{12,28},{16,0},{20,4},{24,8},{28,12},{1,17},{... | collective-permute-start | bytes 49160 | tf_op jit(solution)/shard_map/ppermute | solution.py:786
  97.0 5.4 %plane_gather.5 = bf16[4,2,2,2,640,128]{5,4,3,2,1,0:T(8,128)(2,1)} custom-call(s32[4]{0:T(128)} %pad_add_fusion.pos_ref, bf16[4,640,128]{2,1,0:T(8,128)(2,1)} %line_gather.5.refs_0_, bf16[4,640,128]{2,1,0:T(8,128)(2,1)} %copy-done.25, bf16[4,640,128]{2,1,0:T(8,128)(2,1)} %copy-done.24, bf16[2,640,128]{2,1,0:T(8,128)(2,1)} %collective-permute-done.23.refs_3_, ...), custom_call_target="tpu_custom_call" | custom-call | flops 5500000256 | bytes 1024 | tf_op jit(solution)/shard_map/plane_gather/pallas_call | solution.py:511
  106.2 7.9 %collective-permute-done.34.refs_2_ = bf16[4,384,128]{2,1,0:T(8,128)(2,1)S(1)} collective-permute-done((bf16[4,384,128]{2,1,0:T(8,128)(2,1)S(1)}, bf16[4,384,128]{2,1,0:T(8,128)(2,1)S(1)}, u32[]{:S(2)}, u32[]{:S(2)}) %collective-permute-start.34) | collective-permute-done | bytes 393248 | tf_op jit(solution)/shard_map/ppermute | solution.py:673
  114.6 14.8 %mix.2 = (f32[512,1024]{1,0:T(8,128)}, bf16[512,1024]{1,0:T(8,128)(2,1)}, f32[2,8,1024]{2,1,0:T(8,128)}, f32[512,512]{1,0:T(8,128)}, bf16[512,512]{1,0:T(8,128)(...) custom-call(bf16[512,512]{1,0:T(8,128)(2,1)} %bitcast.57, ...), custom_call_target="tpu_custom_call" | custom-call | flops 15400000512 | bytes 1024 | tf_op jit(solution)/shard_map/mix/pallas_call | solution.py:511
  135.5 9.7 %gates.3 = (bf16[512,512]{1,0:T(8,128)(2,1)}, f32[512,1024]{1,0:T(8,128)}, f32[512,1024]{1,0:T(8,128)}, f32[512,1024]{1,0:T(8,128)}, bf16[512,1024]{1,0:T(8,128)...) custom-call(f32[512,512]{1,0:T(8,128)} %get-tuple-element.188.x_ref,, ...), custom_call_target="tpu_custom_call" | custom-call | flops 9900000256 | bytes 1024 | tf_op jit(solution)/shard_map/gates/pallas_call | solution.py:511
  155.3 7.3 %collective-permute-done.44.refs_2_ = bf16[4,640,128]{2,1,0:T(8,128)(2,1)S(1)} collective-permute-done((bf16[4,640,128]{2,1,0:T(8,128)(2,1)S(1)}, bf16[4,640,128]{2,1,0:T(8,128)(2,1)S(1)}, u32[]{:S(2)}, u32[]{:S(2)}) %collective-permute-start.44) | collective-permute-done | bytes 655392 | tf_op jit(solution)/shard_map/ppermute | solution.py:673
  165.6 5.8 %collective-permute-done.46.refs_4_ = bf16[2,640,128]{2,1,0:T(8,128)(2,1)S(1)} collective-permute-done((bf16[2,640,128]{2,1,0:T(8,128)(2,1)S(1)}, bf16[2,640,128]{2,1,0:T(8,128)(2,1)S(1)}, u32[]{:S(2)}, u32[]{:S(2)}) %collective-permute-start.46) | collective-permute-done | bytes 327712 | tf_op jit(solution)/shard_map/ppermute | solution.py:673
  175.4 5.5 %plane_gather.7 = bf16[4,2,2,2,640,128]{5,4,3,2,1,0:T(8,128)(2,1)} custom-call(s32[4]{0:T(128)} %pad_add_fusion.pos_ref, bf16[4,640,128]{2,1,0:T(8,128)(2,1)} %line_gather.6.refs_0_, bf16[4,640,128]{2,1,0:T(8,128)(2,1)} %copy-done.27, bf16[4,640,128]{2,1,0:T(8,128)(2,1)} %copy-done.26, bf16[2,640,128]{2,1,0:T(8,128)(2,1)} %collective-permute-done.45.refs_3_, ...), custom_call_target="tpu_custom_call" | custom-call | flops 5500000256 | bytes 1024 | tf_op jit(solution)/shard_map/plane_gather/pallas_call | solution.py:511
  180.8 14.7 %mix.3 = (f32[512,1024]{1,0:T(8,128)}, bf16[512,1024]{1,0:T(8,128)(2,1)}, f32[2,8,1024]{2,1,0:T(8,128)}, f32[512,512]{1,0:T(8,128)}, bf16[512,512]{1,0:T(8,128)(...) custom-call(f32[512,512]{1,0:T(8,128)} %get-tuple-element.188.x_ref, ...), custom_call_target="tpu_custom_call" | custom-call | flops 15400000512 | bytes 1024 | tf_op jit(solution)/shard_map/mix/pallas_call | solution.py:511
  195.6 12.1 %mlp_back.2 = (bf16[512,512]{1,0:T(8,128)(2,1)}, bf16[512,2048]{1,0:T(8,128)(2,1)}, f32[512,512]{1,0:T(8,128)}, bf16[512,512]{1,0:T(8,128)(2,1)}, f32[1,512]{1,0...) custom-call(bf16[512,512]{1,0:T(8,128)(2,1)} %bitcast.63, ...), custom_call_target="tpu_custom_call" | custom-call | flops 13200000000 | bytes 1024 | tf_op jit(solution)/shard_map/mlp_back/pallas_call | solution.py:511
  208.5 5.3 %up_weights.2 = (bf16[8,2,256,128]{3,2,1,0:T(8,128)(2,1)}, bf16[8,2,256,128]{3,2,1,0:T(8,128)(2,1)}) custom-call(s32[4]{0:T(128)} %pad_add_fusion.pos_ref, bf16[512,512]{1,0:T(8,128)(2,1)} %get-tuple-element.206.n2_ref, bf16[512,2048]{1,0:T(8,128)(2,1)} %get-tuple-element.207.gpre_ref), custom_call_target="tpu_custom_call" | custom-call | flops 5500000256 | bytes 1024 | tf_op jit(solution)/shard_map/up_weights/pallas_call | solution.py:511
  215.4 5.4 %down_weights.2 = (bf16[8,2,256,128]{3,2,1,0:T(8,128)(2,1)}, bf16[8,2,256,128]{3,2,1,0:T(8,128)(2,1)}) custom-call(s32[4]{0:T(128)} %pad_add_fusion.pos_ref, bf16[512,2048]{1,0:T(8,128)(2,1)} %get-tuple-element.212.left_ref, bf16[512,512]{1,0:T(8,128)(2,1)} %get-tuple-element.213.right_ref), custom_call_target="tpu_custom_call" | custom-call | flops 5500000256 | bytes 1024 | tf_op jit(solution)/shard_map/down_weights/pallas_call | solution.py:511
  238.9 10.5 %gate_back.2 = (bf16[512,1024]{1,0:T(8,128)(2,1)}, bf16[512,1024]{1,0:T(8,128)(2,1)}, bf16[512,1024]{1,0:T(8,128)(2,1)}, f32[2,1024]{1,0:T(2,128)}, f32[512,512]{1,0:T(8,128)}, /*index=5*/f32[1,512]{1,0:T(1,128)}) custom-call(f32[512,512]{1,0:T(8,128)} %get-tuple-element.188.x_ref, f32[2,512]{1,0:T(2,128)} %get-tuple-element.189.gain_ref, ...), custom_call_target="tpu_custom_call" | custom-call | flops 11000000512 | bytes 1024 | tf_op jit(solution)/shard_map/gate_back/pallas_call | solution.py:511
  249.5 8.3 %gate_weights.2 = (bf16[8,2,384,128]{3,2,1,0:T(8,128)(2,1)}, bf16[8,2,384,128]{3,2,1,0:T(8,128)(2,1)}) custom-call(s32[4]{0:T(128)} %pad_add_fusion.pos_ref, bf16[512,512]{1,0:T(8,128)(2,1)} %get-tuple-element.235.normed_ref, bf16[512,1024]{1,0:T(8,128)(2,1)} %get-tuple-element.236.dzf_ref, bf16[512,1024]{1,0:T(8,128)(2,1)} %get-tuple-element.237.dzi_ref, ...), custom_call_target="tpu_custom_call" | custom-call | flops 1 | bytes 1024 | tf_op jit(solution)/shard_map/gate_weights/pallas_call | solution.py:511
  263.7 12.4 %mlp_back.3 = (bf16[512,512]{1,0:T(8,128)(2,1)}, bf16[512,2048]{1,0:T(8,128)(2,1)}, f32[512,512]{1,0:T(8,128)}, bf16[512,512]{1,0:T(8,128)(2,1)}, f32[1,512]{1,0...) custom-call(f32[512,512]{1,0:T(8,128)} %get-tuple-element.244.g_ref, ...), custom_call_target="tpu_custom_call" | custom-call | flops 13200000000 | bytes 1024 | tf_op jit(solution)/shard_map/mlp_back/pallas_call | solution.py:511
  280.9 5.2 %collective-permute-done.60.got_a = bf16[4,256,128]{2,1,0:T(8,128)(2,1)S(1)} collective-permute-done((bf16[4,256,128]{2,1,0:T(8,128)(2,1)S(1)}, bf16[4,256,128]{2,1,0:T(8,128)(2,1)S(1)}, u32[]{:S(2)}, u32[]{:S(2)}) %collective-permute-start.60) | collective-permute-done | bytes 262176 | tf_op jit(solution)/shard_map/ppermute | solution.py:673
  289.1 5.2 %up_weights.3 = (bf16[8,2,256,128]{3,2,1,0:T(8,128)(2,1)}, bf16[8,2,256,128]{3,2,1,0:T(8,128)(2,1)}) custom-call(s32[4]{0:T(128)} %pad_add_fusion.pos_ref, bf16[512,512]{1,0:T(8,128)(2,1)} %get-tuple-element.250.n2_ref, bf16[512,2048]{1,0:T(8,128)(2,1)} %get-tuple-element.257.gpre_ref), custom_call_target="tpu_custom_call" | custom-call | flops 5500000256 | bytes 1024 | tf_op jit(solution)/shard_map/up_weights/pallas_call | solution.py:511
  295.2 5.3 %down_weights.3 = (bf16[8,2,256,128]{3,2,1,0:T(8,128)(2,1)}, bf16[8,2,256,128]{3,2,1,0:T(8,128)(2,1)}) custom-call(s32[4]{0:T(128)} %pad_add_fusion.pos_ref, bf16[512,2048]{1,0:T(8,128)(2,1)} %get-tuple-element.262.left_ref, bf16[512,512]{1,0:T(8,128)(2,1)} %get-tuple-element.263.right_ref), custom_call_target="tpu_custom_call" | custom-call | flops 5500000256 | bytes 1024 | tf_op jit(solution)/shard_map/down_weights/pallas_call | solution.py:511
  313.0 5.8 %pair_sum.4 = (bf16[4,2,512,128]{3,2,1,0:T(8,128)(2,1)}, bf16[4,2,512,128]{3,2,1,0:T(8,128)(2,1)}, bf16[4,2,512,128]{3,2,1,0:T(8,128)(2,1)}, bf16[4,2,512,128]{3,2,1,0:T(8,128)(2,1)}) custom-call(s32[4]{0:T(128)} %pad_add_fusion.pos_ref, bf16[4,2,2,256,128]{4,3,2,1,0:T(8,128)(2,1)} %bitcast.44, bf16[4,2,2,256,128]{4,3,2,1,0:T(8,128)(2,1)} %bitcast.46, ...), custom_call_target="tpu_custom_call" | custom-call | flops 1 | bytes 1024 | tf_op jit(solution)/shard_map/pair_sum/pallas_call | solution.py:511
  321.1 10.2 %gate_back.3 = (bf16[512,1024]{1,0:T(8,128)(2,1)}, bf16[512,1024]{1,0:T(8,128)(2,1)}, bf16[512,1024]{1,0:T(8,128)(2,1)}, f32[2,1024]{1,0:T(2,128)}, bf16[512,512]{1,0:T(8,128)(2,1)}, /*index=5*/f32[1,512]{1,0:T(1,128)}) custom-call(bf16[512,512]{1,0:T(8,128)(2,1)} %bitcast.58, f32[2,512]{1,0:T(2,128)} %get-tuple-element.175.gain_ref, ...), custom_call_target="tpu_custom_call" | custom-call | flops 11000000512 | bytes 1024 | tf_op jit(solution)/shard_map/gate_back/pallas_call | solution.py:511
  331.4 8.5 %gate_weights.3 = (bf16[8,2,400,128]{3,2,1,0:T(8,128)(2,1)}, bf16[8,2,400,128]{3,2,1,0:T(8,128)(2,1)}) custom-call(s32[4]{0:T(128)} %pad_add_fusion.pos_ref, bf16[512,512]{1,0:T(8,128)(2,1)} %get-tuple-element.285.normed_ref, bf16[512,1024]{1,0:T(8,128)(2,1)} %get-tuple-element.286.dzf_ref, bf16[512,1024]{1,0:T(8,128)(2,1)} %get-tuple-element.287.dzi_ref, ...), custom_call_target="tpu_custom_call" | custom-call | flops 1 | bytes 1024 | tf_op jit(solution)/shard_map/gate_weights/pallas_call | solution.py:511
  394.2 9.2 %collective-permute-done.77.refs_3_ = bf16[1024,128]{1,0:T(8,128)(2,1)S(1)} collective-permute-done((bf16[1024,128]{1,0:T(8,128)(2,1)}, bf16[1024,128]{1,0:T(8,128)(2,1)S(1)}, u32[]{:S(2)}, u32[]{:S(2)}) %collective-permute-start.77) | collective-permute-done | bytes 262176 | tf_op jit(solution)/shard_map/ppermute | solution.py:673
  403.4 7.8 %collective-permute-done.85.refs_7_ = bf16[400,128]{1,0:T(8,128)(2,1)S(1)} collective-permute-done((bf16[400,128]{1,0:T(8,128)(2,1)}, bf16[400,128]{1,0:T(8,128)(2,1)S(1)}, u32[]{:S(2)}, u32[]{:S(2)}) %collective-permute-start.85) | collective-permute-done | bytes 102432 | tf_op jit(solution)/shard_map/ppermute | solution.py:673
  (382 shorter events, 214.9 us)
Async XLA Ops:
  41.9 29.2 %collective-permute-start.22 = (bf16[4,640,128]{2,1,0:T(8,128)(2,1)}, bf16[4,640,128]{2,1,0:T(8,128)(2,1)S(1)}, u32[]{:S(2)}, u32[]{:S(2)}) collective-permute-start(bf16[4,640,128]{2,1,0:T(8,128)(2,1)} %line_gather.5.refs_0_), channel_id=1, source_target_pairs={{0,4},{4,0},{8,12},{12,8},{16,20},{20,16},{24,28},{28,24},{1,5},{5... | collective-permute-start | bytes 1966088 | tf_op jit(solution)/shard_map/ppermute | solution.py:673
  42.5 29.2 %collective-permute-start.21 = (bf16[4,640,128]{2,1,0:T(8,128)(2,1)}, bf16[4,640,128]{2,1,0:T(8,128)(2,1)S(1)}, u32[]{:S(2)}, u32[]{:S(2)}) collective-permute-start(bf16[4,640,128]{2,1,0:T(8,128)(2,1)} %line_gather.5.refs_0_), channel_id=1, source_target_pairs={{0,2},{1,3},{2,0},{3,1},{4,6},{5,7},{6,4},{7,5},{8,10},{9,11},{10,... | collective-permute-start | bytes 1966088 | tf_op jit(solution)/shard_map/ppermute | solution.py:673
  93.1 36.3 %collective-permute-start.36 = (bf16[4,384,128]{2,1,0:T(8,128)(2,1)S(1)}, bf16[4,384,128]{2,1,0:T(8,128)(2,1)S(1)}, u32[]{:S(2)}, u32[]{:S(2)}) collective-permute-start(bf16[4,384,128]{2,1,0:T(8,128)(2,1)S(1)} %copy-done.43), channel_id=1, source_target_pairs={{0,1},{1,0},{2,3},{3,2},{4,5},{5,4},{6,7},{7,6},{8,9},{9,8},{10,11... | collective-permute-start | bytes 1179656 | tf_op jit(solution)/shard_map/ppermute | solution.py:673
  94.9 19.2 %collective-permute-start.34 = (bf16[4,384,128]{2,1,0:T(8,128)(2,1)S(1)}, bf16[4,384,128]{2,1,0:T(8,128)(2,1)S(1)}, u32[]{:S(2)}, u32[]{:S(2)}) collective-permute-start(bf16[4,384,128]{2,1,0:T(8,128)(2,1)S(1)} %copy-done.43), channel_id=1, source_target_pairs={{0,4},{4,0},{8,12},{12,8},{16,20},{20,16},{24,28},{28,24},{1,5},{5... | collective-permute-start | bytes 1179656 | tf_op jit(solution)/shard_map/ppermute | solution.py:673
  96.3 17.9 %collective-permute-start.33 = (bf16[4,384,128]{2,1,0:T(8,128)(2,1)S(1)}, bf16[4,384,128]{2,1,0:T(8,128)(2,1)S(1)}, u32[]{:S(2)}, u32[]{:S(2)}) collective-permute-start(bf16[4,384,128]{2,1,0:T(8,128)(2,1)S(1)} %copy-done.43), channel_id=1, source_target_pairs={{0,2},{1,3},{2,0},{3,1},{4,6},{5,7},{6,4},{7,5},{8,10},{9,11},{10,... | collective-permute-start | bytes 1179656 | tf_op jit(solution)/shard_map/ppermute | solution.py:673
  106.2 23.3 %collective-permute-start.39 = (bf16[4,384,128]{2,1,0:T(8,128)(2,1)S(1)}, bf16[4,384,128]{2,1,0:T(8,128)(2,1)S(1)}, u32[]{:S(2)}, u32[]{:S(2)}) collective-permute-start(bf16[4,384,128]{2,1,0:T(8,128)(2,1)S(1)} %collective-permute-done.35.refs_3_), channel_id=1, source_target_pairs={{0,1},{1,0},{2,3},{3,2},{4,5},{5,4},{6,7},{7,6},{8,9},{9,8},{10,11... | collective-permute-start | bytes 1179656 | tf_op jit(solution)/shard_map/ppermute | solution.py:673
  147.3 16.9 %collective-permute-start.43 = (bf16[4,640,128]{2,1,0:T(8,128)(2,1)S(1)}, bf16[4,640,128]{2,1,0:T(8,128)(2,1)S(1)}, u32[]{:S(2)}, u32[]{:S(2)}) collective-permute-start(bf16[4,640,128]{2,1,0:T(8,128)(2,1)S(1)} %copy-done.37), channel_id=1, source_target_pairs={{0,2},{1,3},{2,0},{3,1},{4,6},{5,7},{6,4},{7,5},{8,10},{9,11},{10,... | collective-permute-start | bytes 1966088 | tf_op jit(solution)/shard_map/ppermute | solution.py:673
  155.3 19.3 %collective-permute-start.47 = (bf16[4,640,128]{2,1,0:T(8,128)(2,1)S(1)}, bf16[4,640,128]{2,1,0:T(8,128)(2,1)S(1)}, u32[]{:S(2)}, u32[]{:S(2)}) collective-permute-start(bf16[4,640,128]{2,1,0:T(8,128)(2,1)S(1)} %copy-done.37), channel_id=1, source_target_pairs={{0,1},{1,0},{2,3},{3,2},{4,5},{5,4},{6,7},{7,6},{8,9},{9,8},{10,11... | collective-permute-start | bytes 1966088 | tf_op jit(solution)/shard_map/ppermute | solution.py:673
  213.8 17.2 %collective-permute-start.54 = (bf16[8,2,256,128]{3,2,1,0:T(8,128)(2,1)}, bf16[8,2,256,128]{3,2,1,0:T(8,128)(2,1)S(1)}, u32[]{:S(2)}, u32[]{:S(2)}) collective-permute-start(bf16[8,2,256,128]{3,2,1,0:T(8,128)(2,1)} %get-tuple-element.210), channel_id=1, source_target_pairs={{0,1},{1,0},{2,3},{3,2},{4,5},{5,4},{6,7},{7,6},{8,9},{9,8},{10,11... | collective-permute-start | bytes 3145736 | tf_op jit(solution)/shard_map/ppermute | solution.py:673
  237.0 20.8 %collective-permute-start.58 = (bf16[4,2,256,128]{3,2,1,0:T(8,128)(2,1)}, bf16[4,2,256,128]{3,2,1,0:T(8,128)(2,1)S(1)}, u32[]{:S(2)}, u32[]{:S(2)}) collective-permute-start(bf16[4,2,256,128]{3,2,1,0:T(8,128)(2,1)} %get-tuple-element.222), channel_id=1, source_target_pairs={{0,2},{1,3},{2,0},{3,1},{4,6},{5,7},{6,4},{7,5},{8,10},{9,11},{10,... | collective-permute-start | bytes 1572872 | tf_op jit(solution)/shard_map/ppermute | solution.py:673
  237.6 20.2 %collective-permute-start.59 = (bf16[4,2,384,128]{3,2,1,0:T(8,128)(2,1)}, bf16[4,2,384,128]{3,2,1,0:T(8,128)(2,1)S(1)}, u32[]{:S(2)}, u32[]{:S(2)}) collective-permute-start(bf16[4,2,384,128]{3,2,1,0:T(8,128)(2,1)} %get-tuple-element.242), channel_id=1, source_target_pairs={{0,4},{4,0},{8,12},{12,8},{16,20},{20,16},{24,28},{28,24},{1,5},{5... | collective-permute-start | bytes 2359304 | tf_op jit(solution)/shard_map/ppermute | solution.py:673
  262.7 23.4 %collective-permute-start.61 = (bf16[4,384,128]{2,1,0:T(8,128)(2,1)}, bf16[4,384,128]{2,1,0:T(8,128)(2,1)S(1)}, u32[]{:S(2)}, u32[]{:S(2)}) collective-permute-start(bf16[4,384,128]{2,1,0:T(8,128)(2,1)} %get-tuple-element.255), channel_id=1, source_target_pairs={{0,2},{1,3},{2,0},{3,1},{4,6},{5,7},{6,4},{7,5},{8,10},{9,11},{10,... | collective-permute-start | bytes 1179656 | tf_op jit(solution)/shard_map/ppermute | solution.py:673
  277.3 30.0 %collective-permute-start.67 = (bf16[8,2,384,128]{3,2,1,0:T(8,128)(2,1)S(1)}, bf16[8,2,384,128]{3,2,1,0:T(8,128)(2,1)S(1)}, u32[]{:S(2)}, u32[]{:S(2)}) collective-permute-start(bf16[8,2,384,128]{3,2,1,0:T(8,128)(2,1)S(1)} %copy-done.35), channel_id=1, source_target_pairs={{0,1},{1,0},{2,3},{3,2},{4,5},{5,4},{6,7},{7,6},{8,9},{9,8},{10,11... | collective-permute-start | bytes 4718600 | tf_op jit(solution)/shard_map/ppermute | solution.py:673
  294.4 17.6 %collective-permute-start.64 = (bf16[8,2,256,128]{3,2,1,0:T(8,128)(2,1)}, bf16[8,2,256,128]{3,2,1,0:T(8,128)(2,1)S(1)}, u32[]{:S(2)}, u32[]{:S(2)}) collective-permute-start(bf16[8,2,256,128]{3,2,1,0:T(8,128)(2,1)} %get-tuple-element.260), channel_id=1, source_target_pairs={{0,1},{1,0},{2,3},{3,2},{4,5},{5,4},{6,7},{7,6},{8,9},{9,8},{10,11... | collective-permute-start | bytes 3145736 | tf_op jit(solution)/shard_map/ppermute | solution.py:673
  307.4 32.5 %collective-permute-start.69 = (bf16[640,128]{1,0:T(8,128)(2,1)S(1)}, bf16[640,128]{1,0:T(8,128)(2,1)S(1)}, u32[]{:S(2)}, u32[]{:S(2)}) collective-permute-start(bf16[640,128]{1,0:T(8,128)(2,1)S(1)} %copy-done.66), channel_id=1, source_target_pairs={{0,8},{4,12},{8,0},{12,4},{16,24},{20,28},{24,16},{28,20},{1,9},{5... | collective-permute-start | bytes 491528 | tf_op jit(solution)/shard_map/ppermute | solution.py:673
  308.2 31.7 %collective-permute-start.70 = (bf16[640,128]{1,0:T(8,128)(2,1)S(1)}, bf16[640,128]{1,0:T(8,128)(2,1)S(1)}, u32[]{:S(2)}, u32[]{:S(2)}) collective-permute-start(bf16[640,128]{1,0:T(8,128)(2,1)S(1)} %copy-done.65), channel_id=1, source_target_pairs={{0,16},{4,20},{8,24},{12,28},{16,0},{20,4},{24,8},{28,12},{1,17},{... | collective-permute-start | bytes 491528 | tf_op jit(solution)/shard_map/ppermute | solution.py:673
  309.7 30.2 %collective-permute-start.71 = (bf16[640,128]{1,0:T(8,128)(2,1)S(1)}, bf16[640,128]{1,0:T(8,128)(2,1)S(1)}, u32[]{:S(2)}, u32[]{:S(2)}) collective-permute-start(bf16[640,128]{1,0:T(8,128)(2,1)S(1)} %copy-done.64), channel_id=1, source_target_pairs={{0,24},{4,28},{8,16},{12,20},{16,8},{20,12},{24,0},{28,4},{1,25},{... | collective-permute-start | bytes 491528 | tf_op jit(solution)/shard_map/ppermute | solution.py:673
  318.8 24.4 %collective-permute-start.73 = (bf16[4,2,512,128]{3,2,1,0:T(8,128)(2,1)}, bf16[4,2,512,128]{3,2,1,0:T(8,128)(2,1)S(1)}, u32[]{:S(2)}, u32[]{:S(2)}) collective-permute-start(bf16[4,2,512,128]{3,2,1,0:T(8,128)(2,1)} %get-tuple-element.303), channel_id=1, source_target_pairs={{0,4},{4,0},{8,12},{12,8},{16,20},{20,16},{24,28},{28,24},{1,5},{5... | collective-permute-start | bytes 3145736 | tf_op jit(solution)/shard_map/ppermute | solution.py:673
  319.7 24.1 %collective-permute-start.72 = (bf16[4,2,512,128]{3,2,1,0:T(8,128)(2,1)}, bf16[4,2,512,128]{3,2,1,0:T(8,128)(2,1)S(1)}, u32[]{:S(2)}, u32[]{:S(2)}) collective-permute-start(bf16[4,2,512,128]{3,2,1,0:T(8,128)(2,1)} %get-tuple-element.273), channel_id=1, source_target_pairs={{0,2},{1,3},{2,0},{3,1},{4,6},{5,7},{6,4},{7,5},{8,10},{9,11},{10,... | collective-permute-start | bytes 3145736 | tf_op jit(solution)/shard_map/ppermute | solution.py:673
  368.8 21.4 %collective-permute-start.76 = (bf16[1024,128]{1,0:T(8,128)(2,1)}, bf16[1024,128]{1,0:T(8,128)(2,1)S(1)}, u32[]{:S(2)}, u32[]{:S(2)}) collective-permute-start(bf16[1024,128]{1,0:T(8,128)(2,1)} %get-tuple-element.309), channel_id=1, source_target_pairs={{0,8},{4,12},{8,0},{12,4},{16,24},{20,28},{24,16},{28,20},{1,9},{5... | collective-permute-start | bytes 786440 | tf_op jit(solution)/shard_map/ppermute | solution.py:673
  380.2 23.1 %collective-permute-start.77 = (bf16[1024,128]{1,0:T(8,128)(2,1)}, bf16[1024,128]{1,0:T(8,128)(2,1)S(1)}, u32[]{:S(2)}, u32[]{:S(2)}) collective-permute-start(bf16[1024,128]{1,0:T(8,128)(2,1)} %get-tuple-element.310), channel_id=1, source_target_pairs={{0,16},{4,20},{8,24},{12,28},{16,0},{20,4},{24,8},{28,12},{1,17},{... | collective-permute-start | bytes 786440 | tf_op jit(solution)/shard_map/ppermute | solution.py:673
  380.4 23.0 %collective-permute-start.78 = (bf16[1024,128]{1,0:T(8,128)(2,1)}, bf16[1024,128]{1,0:T(8,128)(2,1)S(1)}, u32[]{:S(2)}, u32[]{:S(2)}) collective-permute-start(bf16[1024,128]{1,0:T(8,128)(2,1)} %get-tuple-element.311), channel_id=1, source_target_pairs={{0,24},{4,28},{8,16},{12,20},{16,8},{20,12},{24,0},{28,4},{1,25},{... | collective-permute-start | bytes 786440 | tf_op jit(solution)/shard_map/ppermute | solution.py:673
  388.0 23.2 %collective-permute-start.85 = (bf16[400,128]{1,0:T(8,128)(2,1)}, bf16[400,128]{1,0:T(8,128)(2,1)S(1)}, u32[]{:S(2)}, u32[]{:S(2)}) collective-permute-start(bf16[400,128]{1,0:T(8,128)(2,1)} %get-tuple-element.324), channel_id=1, source_target_pairs={{0,16},{4,20},{8,24},{12,28},{16,0},{20,4},{24,8},{28,12},{1,17},{... | collective-permute-start | bytes 307208 | tf_op jit(solution)/shard_map/ppermute | solution.py:673
  390.2 21.0 %collective-permute-start.86 = (bf16[400,128]{1,0:T(8,128)(2,1)}, bf16[400,128]{1,0:T(8,128)(2,1)S(1)}, u32[]{:S(2)}, u32[]{:S(2)}) collective-permute-start(bf16[400,128]{1,0:T(8,128)(2,1)} %get-tuple-element.325), channel_id=1, source_target_pairs={{0,24},{4,28},{8,16},{12,20},{16,8},{20,12},{24,0},{28,4},{1,25},{... | collective-permute-start | bytes 307208 | tf_op jit(solution)/shard_map/ppermute | solution.py:673
  (145 other events, 1110.2 us)

commit v3 on v2

--- a/solution.py
+++ b/solution.py
@@ -11,7 +11,7 @@
 EPS = 1e-05
 NS, NB, LANE = 8, 4, 128
 CHUNKS = 8
-VMEM = 56 * 1024 * 1024
+VMEM = 20 * 1024 * 1024
 F32, BF16 = jnp.float32, jnp.bfloat16
 
 
@@ -455,33 +455,32 @@
 
 
 def line_gather_kernel(pos_ref, *refs):
-    out = refs[-1]
-    for k, part in enumerate(refs[:-1]):
-        out[pos_ref[3] ^ k] = part[...]
+    row = 0
+    for out in refs[4:]:
+        rows = out.shape[1]
+        for k, part in enumerate(refs[:4]):
+            out[pos_ref[3] ^ k] = part[row : row + rows, :]
+        row += rows
 
 
 def plane_gather_kernel(pos_ref, *refs):
     at, half, out = pl.program_id(0), pl.num_programs(0) // 2, refs[-1]
     core, x, y = pos_ref[0], pos_ref[1], pos_ref[2]
     count = len(refs) // 2
+
+    def put(step_y, step_x, c, part):
+        out[0, y ^ step_y, x ^ step_x, core ^ c] = part[0]
+
     for c in range(2):
-        own, from_x, from_y, low = refs[count * c : count * c + 4]
-        out[0, y, x, core ^ c] = own[0]
-        out[0, y, x ^ 1, core ^ c] = from_x[0]
-        out[0, y ^ 1, x, core ^ c] = from_y[0]
-
-        if count == 4:
-            out[0, y ^ 1, x ^ 1, core ^ c] = low[0]
+        own, from_x, from_y, *diagonal = refs[count * c : count * (c + 1)]
+        put(0, 0, c, own)
+        put(0, 1, c, from_x)
+        put(1, 0, c, from_y)
+        if len(diagonal) == 1:
+            put(1, 1, c, diagonal[0])
             continue
-        high = refs[count * c + 4]
-
-        @pl.when(at < half)
-        def _():
-            out[0, y ^ 1, x ^ 1, core ^ c] = low[0]
-
-        @pl.when(at >= half)
-        def _():
-            out[0, y ^ 1, x ^ 1, core ^ c] = high[0]
+        pl.when(at < half)(functools.partial(put, 1, 1, c, diagonal[0]))
+        pl.when(at >= half)(functools.partial(put, 1, 1, c, diagonal[1]))
 
 
 def vector_kernel(gained, w_ref, *refs):
@@ -500,9 +499,6 @@
 
 
 def call(kernel, grid, ins, outs, scratch, us, name):
-    moved = sum(a.size * a.dtype.itemsize for a, _, _ in ins)
-    moved += sum(s.size * s.dtype.itemsize for s, _, _ in outs)
-
     def spec(a, block, index):
         if a.dtype == jnp.int32:
             return pl.BlockSpec(memory_space=pltpu.SMEM)
@@ -512,8 +508,8 @@
         kernel,
         grid=(grid,),
         in_specs=[spec(*one) for one in ins],
-        out_specs=[spec(*one) for one in outs],
-        out_shape=[s for s, _, _ in outs],
+        out_specs=[pl.BlockSpec(block, index) for _, block, index, *_ in outs],
+        out_shape=[pltpu.HBM(one[0].shape, one[0].dtype) if one[3:] else one[0] for one in outs],
         scratch_shapes=scratch,
         compiler_params=pltpu.CompilerParams(vmem_limit_bytes=VMEM),
         cost_estimate=pl.CostEstimate(flops=int(us * 1.1e9) + 1, bytes_accessed=1024, transcendentals=0),
@@ -522,6 +518,10 @@
     return found if len(found) > 1 else found[0]
 
 
+def far(array):
+    return pltpu.with_memory_space_constraint(array, pltpu.HBM)
+
+
 def whole(array):
     dims = array.shape
     return (array, dims, lambda i: (0,) * len(dims))
@@ -546,9 +546,9 @@
         self.hb, self.fb = h // NB, ff // NB
 
 
-def column_weight(view, at):
+def column_weight(view, at, late=False):
     array, rows, place = view
-    return (array, (NS, 1, rows, LANE), lambda i: (0, at(i), place, 0))
+    return (far(array) if late else array, (NS, 1, rows, LANE), lambda i: (0, at(i), place, 0))
 
 
 def row_weight(view, at):
@@ -560,22 +560,22 @@
     return i
 
 
-def gate_forward(sz, x, gain, bias, w):
+def gate_forward(sz, x, gain, bias, w, save):
     n, d, h, wide, s = sz.n, sz.d, sz.h, sz.hb, sz.seqs
     col = lambda i: (0, i)
     return call(
         functools.partial(gate_kernel, s, sz.steps), NB,
         [whole(x), whole(gain), (bias, (2, wide), col)] + [column_weight(w[m], same) for m in "fic"],
-        [whole_out((n, d), BF16)]
-        + [(shape((n, h)), (n, wide), col)] * 3
-        + [(shape((n, h), BF16), (n, wide), col)] * 3
+        [whole_out((n, d), BF16) + save]
+        + [(shape((n, h)), (n, wide), col) + save, (shape((n, h)), (n, wide), col), (shape((n, h)), (n, wide), col) + save]
+        + [(shape((n, h), BF16), (n, wide), col) + save] * 3
         + [(shape((s, CHUNKS, h)), (s, CHUNKS, wide), lambda i: (0, 0, i))] * 2
         + [(shape((2 * s, h)), (2 * s, wide), col)],
         [pltpu.VMEM((n, wide), F32)] * 3, 9, "gates",
     )
 
 
-def mix_forward(sz, x, gain, decay, inflow, cp, ch, ent, wt, last):
+def mix_forward(sz, x, gain, decay, inflow, cp, ch, ent, wt, last, save):
     n, d, h, ff, w, f, s = sz.n, sz.d, sz.h, sz.ff, sz.hb, sz.fb, sz.seqs
     col = lambda i: (0, first(i))
     late = lambda i: (0, second(i))
@@ -588,10 +588,10 @@
             row_weight(wt["o"], first), column_weight(wt["u"], second), row_weight(wt["d"], second),
         ],
         [
-            (shape((n, h)), (n, w), col), (shape((n, h), BF16), (n, w), col),
-            (shape((s, CHUNKS, h)), (s, CHUNKS, w), deep),
-            whole_out((n, d)), whole_out((n, d), BF16),
-            (shape((n, ff), BF16), (n, f), late), (shape((n, ff), BF16), (n, f), late),
+            (shape((n, h)), (n, w), col, True), (shape((n, h), BF16), (n, w), col) + save,
+            (shape((s, CHUNKS, h)), (s, CHUNKS, w), deep) + save,
+            whole_out((n, d)) + save, whole_out((n, d), BF16) + save,
+            (shape((n, ff), BF16), (n, f), late) + save, (shape((n, ff), BF16), (n, f), late) + save,
             whole_out((n, d), BF16 if last else F32),
         ],
         [pltpu.VMEM((n, d), F32), pltpu.VMEM((n, f), F32)], 14, "mix",
@@ -630,7 +630,7 @@
             whole(x), whole(gain), whole(gmid), wide(gh), wide(decay), wide(hidden), (e, (s, CHUNKS, w), deep),
             wide(cand), wide(ff_), wide(fi_), wide(fc_), (cp, (s, CHUNKS, w), deep), (ca, (s, CHUNKS, w), deep),
             (ent, (s, w), col),
-        ] + [column_weight(wt[m], same) for m in "fic"],
+        ] + [column_weight(wt[m], same, True) for m in "fic"],
         [(shape((n, h), BF16), (n, w), col)] * 3
         + [(shape((2, h)), (2, w), col), whole_out((n, d), BF16 if last else F32), whole_out((1, d))],
         [pltpu.VMEM((n, d), F32), pltpu.VMEM((s, CHUNKS, w), F32)], 10, "gate_back",
@@ -740,49 +740,45 @@
     return line_exchange(line_sum(pos, plane_exchange(parts, Y_AXIS, X_AXIS)))
 
 
-def gather(pos, owns, direct):
-    lines = []
-    for own in owns:
-        if lines:
-            own = after(own, *lines[:2])
-        parts = [own] + [swap(own, "seq", 2 * k) for k in range(1, 4)]
-        lines.append(
-            call(
-                line_gather_kernel, 1, [whole(pos)] + [whole(p) for p in parts],
-                [whole_out((4,) + own.shape, BF16)], [], 2, "line_gather",
-            )
-        )
-    found, last = [], ()
-    for at, line in enumerate(lines):
-        rows = line.shape[1]
-        sent = after(line, *last) if last else line
-        from_x, from_y = swap(sent, *X_AXIS), swap(sent, *Y_AXIS)
-        if at in direct:
-            diagonal = swap(sent, BOTH, 6)
-            last = (from_x, from_y, diagonal)
-            parts = [line, from_x, from_y, diagonal]
-        else:
-            low, high = swap(from_x[:2], *Y_AXIS), swap(from_y[2:], *X_AXIS)
-            last = (from_x, from_y) if at == 0 else (low, high)
-            parts = [line, from_x, from_y, low, high]
-        parts += [swap(p, "batch", 1) for p in parts]
-        maps = [lambda i: (i, 0, 0)] * 3
-        maps += maps[:1] if at in direct else [lambda i: (jnp.minimum(i, 1), 0, 0), lambda i: (jnp.maximum(i - 2, 0), 0, 0)]
-        place = lambda i: (i, 0, 0, 0, 0, 0)
-        got = call(
-            plane_gather_kernel, 4, [whole(pos)] + [(p, (1, rows, LANE), m) for p, m in zip(parts, maps * 2)],
-            [(shape((4, 2, 2, 2, rows, LANE), BF16), (1, 2, 2, 2, rows, LANE), place)], [], 5, "plane_gather",
-        )
-        found.append(got.reshape(NS, NB, rows, LANE))
-    return found, lines
-
-
-def enter(fin, seqs, backward, fill=()):
+def line_parts(own):
+    return [own] + [swap(own, "seq", 2 * k) for k in range(1, 4)]
+
+
+def line_gather(pos, parts, rows):
+    return call(
+        line_gather_kernel, 1, [whole(pos)] + [whole(far(p)) for p in parts],
+        [whole_out((4, r, LANE), BF16) for r in rows], [], 2, "line_gather",
+    )
+
+
+def plane_parts(line, direct):
+    from_x, from_y = swap(line, *X_AXIS), swap(line, *Y_AXIS)
+    if direct:
+        return [from_x, from_y, swap(line, BOTH, 6)]
+    return [from_x, from_y, swap(from_x[:2], *Y_AXIS), swap(from_y[2:], *X_AXIS)]
+
+
+def plane_gather(pos, line, parts, behind=()):
+    rows = line.shape[1]
+    parts = [line, *parts]
+    parts += [swap(after(p, *behind) if behind else p, "batch", 1) for p in parts]
+    maps = [lambda i: (i, 0, 0)] * 3
+    maps += maps[:1] if len(parts) == 8 else [lambda i: (jnp.minimum(i, 1), 0, 0), lambda i: (jnp.maximum(i - 2, 0), 0, 0)]
+    got = call(
+        plane_gather_kernel, 4, [whole(pos)] + [(far(p), (1, rows, LANE), m) for p, m in zip(parts, maps * 2)],
+        [(shape((4, 2, 2, 2, rows, LANE), BF16), (1, 2, 2, 2, rows, LANE), lambda i: (i, 0, 0, 0, 0, 0))], [], 5, "plane_gather",
+    )
+    return got.reshape(NS, NB, rows, LANE)
+
+
+def enter(fin, seqs, backward, fill=(), hold=None):
     count, mine = lax.axis_size("seq"), lax.axis_index("seq")
     prod, state = fin[:seqs], fin[seqs:]
     pre_p, pre_s = jnp.ones_like(prod), jnp.zeros_like(state)
     bit, message, done = 1, fin, []
     for step in range(int(count).bit_length() - 1):
+        if hold and step in hold:
+            message = after(message, *hold[step])
         other = lax.ppermute(message, "seq", [(i, i ^ bit) for i in range(count)])
         if step < len(fill):
             done.append(fill[step](message))
@@ -827,19 +823,25 @@
     if standard:
         s_at, b_at = lax.axis_index("seq"), lax.axis_index("batch")
         pos = jnp.stack([b_at % 2, b_at // 2, s_at % 2, s_at // 2]).astype(jnp.int32)
-        groups = []
-        for l in range(LAYERS):
-            vecs = [(6 + k, at, True) for at in range(LAYERS) for k in range(4)] if l == 0 else []
-            groups += [[(order[m], l, False) for m in "fic"] + vecs, [(order[m], l, False) for m in "udo"]]
+        vecs = [(6 + k, at, True) for at in range(LAYERS) for k in range(4)]
+        groups = [[(order[m], 0, False) for m in "fic"] + vecs, [(order[m], 0, False) for m in "udo"]]
+        groups += [[(order[m], l, False) for m in "ficudo"] for l in range(1, LAYERS)]
         rows = [sum(slab_rows["udofic"[which]] for which, _, vec in g if not vec) for g in groups]
         rows[0] += 16
         packs = call(
-            functools.partial(pack_kernel, groups), 1, [whole(m) for m in matrices.values()] + [whole(v) for v in vectors],
+            functools.partial(pack_kernel, groups), 1,
+            [whole(far(m)) for m in matrices.values()] + [whole(far(v)) for v in vectors],
             [whole_out((r, LANE), BF16) for r in rows], [pltpu.VMEM((16, LANE), F32)], 2, "pack",
         )
-        got, lines = gather(pos, packs, (2,))
+        line_g0 = line_gather(pos, line_parts(packs[0]), rows[:1])
+        parts_g0 = plane_parts(line_g0, False)
+        line_r0 = line_gather(pos, line_parts(after(packs[1], line_g0)), rows[1:2])
+        parts_r0 = plane_parts(after(line_r0, *parts_g0[:2]), False)
+        lines = line_gather(pos, line_parts(after(packs[2], line_r0)), (rows[2] - rows[1], rows[1]))
+        got = [plane_gather(pos, line_g0, parts_g0), plane_gather(pos, line_r0, parts_r0)]
         places = {"f": 0, "i": 1, "c": 2, "u": 0, "d": 1, "o": 4}
-        weights = [{m: (got[2 * l + (m in "udo")], slab_rows[m], places[m]) for m in "udofic"} for l in range(LAYERS)]
+        view = lambda got: {m: (got[m in "udo"], slab_rows[m], places[m]) for m in "udofic"}
+        weights = [view(got)]
         vecs = call(
             functools.partial(vector_kernel, None), 1,
             [(got[0], (NS, 1, 16, LANE), lambda i: (0, 0, 3 * slab_rows["f"] // 16, 0))],
@@ -870,13 +872,23 @@
     stream, grad = to_rows(tokens), to_rows(cotangent)
     kept = []
     for l in range(LAYERS):
-        normed, decay, inflow, cand, f_f, f_i, f_c, cp, ch, fin = gate_forward(sz, stream, gains[l], biases[l], weights[l])
-        ent, _ = enter(fin, seqs, False)
+        save = (True,) if l + 1 < LAYERS else ()
+        normed, decay, inflow, cand, f_f, f_i, f_c, cp, ch, fin = gate_forward(
+            sz, stream, gains[l], biases[l], weights[l], (True,)
+        )
         if standard and l + 1 < LAYERS:
-            ent = after(ent, lines[2 * l + 3])
+            ent, _ = enter(fin, seqs, False, (), {1: lines[:1], 2: parts_r0[2:]})
+        else:
+            ent, _ = enter(fin, seqs, False, (), {1: parts_r1[:2]} if standard and l else None)
         hidden, hb, e, mid, n2, act, slope, result = mix_forward(
-            sz, stream, gains[l], decay, inflow, cp, ch, ent, weights[l], l == LAYERS - 1
+            sz, stream, gains[l], decay, inflow, cp, ch, ent, weights[l], l == LAYERS - 1, save
         )
+        if standard and l + 1 < LAYERS:
+            line_g1, line_r1 = lines
+            parts_g1 = plane_parts(after(line_g1, *parts_r0[2:]), True)
+            parts_r1 = plane_parts(after(line_r1, *parts_g1), False)
+            got = [plane_gather(pos, line_g1, parts_g1, (result,)), plane_gather(pos, line_r1, parts_r1)]
+            weights.append(view(got))
         kept.append((stream, normed, decay, cand, f_f, f_i, f_c, hidden, hb, e, mid, n2, act, slope))
         stream = result
     output = from_rows(stream)
@@ -885,18 +897,26 @@
     waiting, held = None, []
     for l in reversed(range(LAYERS)):
         x, normed, decay, cand, f_f, f_i, f_c, hidden, hb, e, mid, n2, act, slope = kept[l]
+        place = far if l + 1 < LAYERS else lambda a: a
+        decay, cand, f_f, f_i, f_c, hidden = map(far, (decay, cand, f_f, f_i, f_c, hidden))
+        mid, slope = place(mid), place(slope)
         gr, gpre, gmid, go, ggain_two, gh, cp, ca, fin = mlp_backward(sz, grad, gains[l], mid, slope, decay, weights[l])
-        if waiting:
-            names, parts = waiting
-            parts = line_sum(pos, [after(parts[0], fin), *parts[1:]])
-            gpre = after(gpre, parts[0])
-            waiting = (names, line_exchange(parts))
-        fill = [
-            lambda m: up_weights(sz, pos, after(n2, m), gpre),
-            lambda m: row_weights(sz, pos, after(act, m), gr, "down_weights"),
-            lambda m: row_weights(sz, pos, after(hb, m), go, "out_weights"),
-        ]
-        ent, pairs = enter(fin, seqs, True, fill)
+        def up(message):
+            return up_weights(sz, pos, place(after(n2, message)), gpre)
+
+        def down(message):
+            left = after(act, message)
+            if waiting:
+                names, parts = waiting
+                parts = line_sum(pos, [after(parts[0], message), *parts[1:]])
+                left = after(left, parts[0])
+                waiting[1] = line_exchange(parts)
+            return row_weights(sz, pos, place(left), gr, "down_weights")
+
+        def out(message):
+            return row_weights(sz, pos, place(after(hb, message)), go, "out_weights")
+
+        ent, pairs = enter(fin, seqs, True, (up, down, out))
         if standard:
             names = [(l, m) for m in "udo"] + (held[0] if held else [])
             early = pair_sum(pos, core_exchange(pairs) + held[1:])
@@ -906,7 +926,7 @@
         )
         vector_grads[l] = (ggain_one, gbias, ggain_two)
         final = [v for each in vector_grads for v in each] if l == 0 and standard else []
-        gate_pair = gate_weights(sz, pos, normed, dzf, dzi, dzc, final)
+        gate_pair = gate_weights(sz, pos, far(normed), dzf, dzi, dzc, final)
         if not standard:
             pending.append((l, pairs + [gate_pair]))
             continue
@@ -916,7 +936,7 @@
         if l > 0:
             held = [[(l, m) for m in "fic"]] + core_exchange([gate_pair])
             grad = after(grad, parts[0])
-            waiting = (names, plane_exchange(parts, Y_AXIS, X_AXIS))
+            waiting = [names, plane_exchange(parts, Y_AXIS, X_AXIS)]
         else:
             done = parts[0]
             if waiting:

time: 417 us -> 336 us (0.81)
  Pallas kernels: 209 us -> 138 us
  starting transfers between devices: 83.7 us -> 77.2 us
  waiting for transfers between devices: 93.2 us -> 98.9 us
  other arithmetic: 5.7 us -> 0.39 us
    pallas_call x37 -> x36, Pallas kernels: 209 us -> 138 us  [call(): pl.pallas_call(kernel, grid=(grid,), in_specs=[spec(*one) for one in ins]...]
    unnamed x164 -> x120, local copies, waits for them, and re-layouts: 17.3 us -> 11.2 us
    ppermute x75 -> x72, starting transfers between devices: 65.5 us -> 60.4 us  [swap(): return lax.ppermute(array, axes, [(i, i ^ bits) for i in range(count)])]
    slice x6, local copies, waits for them, and re-layouts: 0.12 us -> 5 us  [the longest x3 3.03 us: plane_parts(): from_y[2:]]
    ppermute x75 -> x72, waiting for transfers between devices: 83.8 us -> 88.4 us  [swap(): return lax.ppermute(array, axes, [(i, i ^ bits) for i in range(count)])]
  transfers between devices with their start and end apart: 87 -> 84, of which waited for: 30 -> 31; matrix products, arithmetic and copies ran while one was open for 2% -> 2% of each run, Pallas kernels for 35% -> 32%
where the time goes in v3:
time: 336 us; the launch traced here: 335 us
  Pallas kernels  138 us (41%)
  waiting for transfers between devices  98.9 us (29%)
  starting transfers between devices  77.2 us (23%)
  local copies, waits for them, and re-layouts  18.7 us (6%)
    pallas_call x36, Pallas kernels, call(): pl.pallas_call(kernel, grid=(grid,), in_specs=[spec(*one) for one in ins]...  138 us
    ppermute x72, waiting for transfers between devices, swap(): return lax.ppermute(array, axes, [(i, i ^ bits) for i in range(count)])  88.4 us
    ppermute x72, starting transfers between devices, swap(): return lax.ppermute(array, axes, [(i, i ^ bits) for i in range(count)])  60.4 us
    ppermute x12, starting transfers between devices, enter(): other = lax.ppermute(message, 'seq', [(i, i ^ bit) for i in range(count)])  16.9 us
    unnamed x120, local copies, waits for them, and re-layouts  11.2 us
    ppermute x12, waiting for transfers between devices, enter(): other = lax.ppermute(message, 'seq', [(i, i ^ bit) for i in range(count)])  10.5 us
  transfers between devices with their start and end apart: 84, of which 31 were waited for; matrix products, arithmetic and copies ran while one was open for 2% of the time, Pallas kernels for 32%

profile of v3, /device:TPU:0, one launch (start us, length us, event | category | flops | bytes accessed | tf_op | source)
XLA Modules:
  0.0 335.2 jit_solution(18066625042973057159)
XLA Ops:
  1.8 5.1 %collective-permute-start.2 = (bf16[400,128]{1,0:T(8,128)(2,1)S(1)}, bf16[400,128]{1,0:T(8,128)(2,1)S(1)}, u32[]{:S(2)}, u32[]{:S(2)}) collective-permute-start(bf16[400,128]{1,0:T(8,128)(2,1)S(1)} %get-tuple-element.180.refs_0_), channel_id=1, source_target_pairs={{0,24},{4,28},{8,16},{12,20},{16,8},{20,12},{24,0},{28,4},{1,25},{... | collective-permute-start | bytes 307208 | tf_op jit(solution)/shard_map/ppermute | solution.py:673
  10.8 4.8 %collective-permute-done.1.refs_2_ = bf16[400,128]{1,0:T(8,128)(2,1)S(1)} collective-permute-done((bf16[400,128]{1,0:T(8,128)(2,1)S(1)}, bf16[400,128]{1,0:T(8,128)(2,1)S(1)}, u32[]{:S(2)}, u32[]{:S(2)}) %collective-permute-start.1) | collective-permute-done | bytes 102432 | tf_op jit(solution)/shard_map/ppermute | solution.py:673
  49.1 8.1 %gates.2 = (bf16[512,512]{1,0:T(8,128)(2,1)}, f32[512,1024]{1,0:T(8,128)}, f32[512,1024]{1,0:T(8,128)S(1)}, f32[512,1024]{1,0:T(8,128)}, bf16[512,1024]{1,0:T(8,...) custom-call(bf16[512,512]{1,0:T(8,128)(2,1)S(1)} %bitcast.53, ...), custom_call_target="tpu_custom_call" | custom-call | flops 9900000256 | bytes 1024 | tf_op jit(solution)/shard_map/gates/pallas_call | solution.py:507
  57.8 6.2 %collective-permute-done.17.refs_2_ = bf16[1024,128]{1,0:T(8,128)(2,1)S(1)} collective-permute-done((bf16[1024,128]{1,0:T(8,128)(2,1)S(1)}, bf16[1024,128]{1,0:T(8,128)(2,1)S(1)}, u32[]{:S(2)}, u32[]{:S(2)}) %collective-permute-start.17) | collective-permute-done | bytes 262176 | tf_op jit(solution)/shard_map/ppermute | solution.py:673
  71.8 6.3 %collective-permute-done.23.refs_4_ = bf16[2,640,128]{2,1,0:T(8,128)(2,1)S(1)} collective-permute-done((bf16[2,640,128]{2,1,0:T(8,128)(2,1)S(1)}, bf16[2,640,128]{2,1,0:T(8,128)(2,1)S(1)}, u32[]{:S(2)}, u32[]{:S(2)}) %collective-permute-start.23) | collective-permute-done | bytes 327712 | tf_op jit(solution)/shard_map/ppermute | solution.py:673
  87.8 3.5 %plane_gather.5 = bf16[4,2,2,2,640,128]{5,4,3,2,1,0:T(8,128)(2,1)S(1)} custom-call(s32[4]{0:T(128)S(1)} %pad_add_fusion.pos_ref, bf16[4,640,128]{2,1,0:T(8,128)(2,1)} %copy-done.7, bf16[4,640,128]{2,1,0:T(8,128)(2,1)} %collective-permute-done.20.refs_1_, bf16[4,640,128]{2,1,0:T(8,128)(2,1)} %collective-permute-done.22.refs_2_, ...), custom_call_target="tpu_custom_call" | custom-call | flops 5500000256 | bytes 1024 | tf_op jit(solution)/shard_map/plane_gather/pallas_call | solution.py:507
  91.4 12.6 %mix.2 = (f32[512,1024]{1,0:T(8,128)}, bf16[512,1024]{1,0:T(8,128)(2,1)}, f32[2,8,1024]{2,1,0:T(8,128)}, f32[512,512]{1,0:T(8,128)}, bf16[512,512]{1,0:T(8,128)(...) custom-call(bf16[512,512]{1,0:T(8,128)(2,1)S(1)} %bitcast.54, ...), custom_call_target="tpu_custom_call" | custom-call | flops 15400000512 | bytes 1024 | tf_op jit(solution)/shard_map/mix/pallas_call | solution.py:507
  112.8 8.2 %gates.3 = (bf16[512,512]{1,0:T(8,128)(2,1)}, f32[512,1024]{1,0:T(8,128)}, f32[512,1024]{1,0:T(8,128)S(1)}, f32[512,1024]{1,0:T(8,128)}, bf16[512,1024]{1,0:T(8,...) custom-call(f32[512,512]{1,0:T(8,128)S(1)} %get-tuple-element.196.x_, ...), custom_call_target="tpu_custom_call" | custom-call | flops 9900000256 | bytes 1024 | tf_op jit(solution)/shard_map/gates/pallas_call | solution.py:507
  135.2 7.9 %collective-permute-done.43.refs_4_ = bf16[2,640,128]{2,1,0:T(8,128)(2,1)S(1)} collective-permute-done((bf16[2,640,128]{2,1,0:T(8,128)(2,1)S(1)}, bf16[2,640,128]{2,1,0:T(8,128)(2,1)S(1)}, u32[]{:S(2)}, u32[]{:S(2)}) %collective-permute-start.43) | collective-permute-done | bytes 327712 | tf_op jit(solution)/shard_map/ppermute | solution.py:673
  149.9 11.1 %mix.3 = (f32[512,1024]{1,0:T(8,128)}, bf16[512,1024]{1,0:T(8,128)(2,1)S(1)}, f32[2,8,1024]{2,1,0:T(8,128)S(1)}, f32[512,512]{1,0:T(8,128)S(1)}, bf16[512,512]{1...) custom-call(f32[512,512]{1,0:T(8,128)S(1)} %copy-done.21, ...), custom_call_target="tpu_custom_call" | custom-call | flops 15400000512 | bytes 1024 | tf_op jit(solution)/shard_map/mix/pallas_call | solution.py:507
  161.1 8.7 %mlp_back.2 = (bf16[512,512]{1,0:T(8,128)(2,1)S(1)}, bf16[512,2048]{1,0:T(8,128)(2,1)S(1)}, f32[512,512]{1,0:T(8,128)S(1)}, bf16[512,512]{1,0:T(8,128)(2,1)S(1)}...) custom-call(bf16[512,512]{1,0:T(8,128)(2,1)S(1)} %bitcast.58, ...), custom_call_target="tpu_custom_call" | custom-call | flops 13200000000 | bytes 1024 | tf_op jit(solution)/shard_map/mlp_back/pallas_call | solution.py:507
  170.5 3.8 %up_weights.2 = (bf16[8,2,256,128]{3,2,1,0:T(8,128)(2,1)S(1)}, bf16[8,2,256,128]{3,2,1,0:T(8,128)(2,1)}) custom-call(s32[4]{0:T(128)S(1)} %pad_add_fusion.pos_ref, bf16[512,512]{1,0:T(8,128)(2,1)S(1)} %get-tuple-element.218.n2_ref, bf16[512,2048]{1,0:T(8,128)(2,1)S(1)} %get-tuple-element.219.gpre_ref), custom_call_target="tpu_custom_call" | custom-call | flops 5500000256 | bytes 1024 | tf_op jit(solution)/shard_map/up_weights/pallas_call | solution.py:507
  174.6 3.9 %down_weights.2 = (bf16[8,2,256,128]{3,2,1,0:T(8,128)(2,1)S(1)}, bf16[8,2,256,128]{3,2,1,0:T(8,128)(2,1)}) custom-call(s32[4]{0:T(128)S(1)} %pad_add_fusion.pos_ref, bf16[512,2048]{1,0:T(8,128)(2,1)S(1)} %get-tuple-element.224.left_ref, bf16[512,512]{1,0:T(8,128)(2,1)S(1)} %get-tuple-element.225.right_ref), custom_call_target="tpu_custom_call" | custom-call | flops 5500000256 | bytes 1024 | tf_op jit(solution)/shard_map/down_weights/pallas_call | solution.py:507
  197.3 8.0 %gate_back.2 = (bf16[512,1024]{1,0:T(8,128)(2,1)S(1)}, bf16[512,1024]{1,0:T(8,128)(2,1)S(1)}, bf16[512,1024]{1,0:T(8,128)(2,1)S(1)}, f32[2,1024]{1,0:T(2,128)S(1...) custom-call(f32[512,512]{1,0:T(8,128)S(1)} %copy-done.22, f32[2,512]{1,0:T(2,128)S(1)} %get-tuple-element.197.gain_ref, ...), custom_call_target="tpu_custom_call" | custom-call | flops 11000000512 | bytes 1024 | tf_op jit(solution)/shard_map/gate_back/pallas_call | solution.py:507
  205.3 6.5 %gate_weights.2 = (bf16[8,2,384,128]{3,2,1,0:T(8,128)(2,1)S(1)}, bf16[8,2,384,128]{3,2,1,0:T(8,128)(2,1)S(1)}) custom-call(s32[4]{0:T(128)S(1)} %pad_add_fusion.pos_ref, bf16[512,512]{1,0:T(8,128)(2,1)} %get-tuple-element.247.normed_ref, bf16[512,1024]{1,0:T(8,128)(2,1)S(1)} %get-tuple-element.248.dzf_ref, bf16[512,1024]{1,0:T(8,128)(2,1)S(1)} %get-tuple-element.249.dzi_ref, ...), custom_call_target="tpu_custom_call" | custom-call | flops 1 | bytes 1024 | tf_op jit(solution)/shard_map/gate_weights/pallas_call | solution.py:507
  214.0 9.2 %mlp_back.3 = (bf16[512,512]{1,0:T(8,128)(2,1)S(1)}, bf16[512,2048]{1,0:T(8,128)(2,1)S(1)}, f32[512,512]{1,0:T(8,128)S(1)}, bf16[512,512]{1,0:T(8,128)(2,1)S(1)}...) custom-call(f32[512,512]{1,0:T(8,128)S(1)} %get-tuple-element.256.g_, ...), custom_call_target="tpu_custom_call" | custom-call | flops 13200000000 | bytes 1024 | tf_op jit(solution)/shard_map/mlp_back/pallas_call | solution.py:507
  234.0 3.9 %down_weights.3 = (bf16[8,2,256,128]{3,2,1,0:T(8,128)(2,1)S(1)}, bf16[8,2,256,128]{3,2,1,0:T(8,128)(2,1)S(1)}) custom-call(s32[4]{0:T(128)S(1)} %pad_add_fusion.pos_ref, bf16[512,2048]{1,0:T(8,128)(2,1)} %get-tuple-element.274.left_ref, bf16[512,512]{1,0:T(8,128)(2,1)S(1)} %get-tuple-element.275.right_ref), custom_call_target="tpu_custom_call" | custom-call | flops 5500000256 | bytes 1024 | tf_op jit(solution)/shard_map/down_weights/pallas_call | solution.py:507
  252.2 8.0 %gate_back.3 = (bf16[512,1024]{1,0:T(8,128)(2,1)S(1)}, bf16[512,1024]{1,0:T(8,128)(2,1)S(1)}, bf16[512,1024]{1,0:T(8,128)(2,1)S(1)}, f32[2,1024]{1,0:T(2,128)S(1...) custom-call(bf16[512,512]{1,0:T(8,128)(2,1)S(1)} %bitcast.55, f32[2,512]{1,0:T(2,128)S(1)} %get-tuple-element.181.gain_ref, ...), custom_call_target="tpu_custom_call" | custom-call | flops 11000000512 | bytes 1024 | tf_op jit(solution)/shard_map/gate_back/pallas_call | solution.py:507
  260.2 6.6 %gate_weights.3 = (bf16[8,2,400,128]{3,2,1,0:T(8,128)(2,1)S(1)}, bf16[8,2,400,128]{3,2,1,0:T(8,128)(2,1)S(1)}) custom-call(s32[4]{0:T(128)S(1)} %pad_add_fusion.pos_ref, bf16[512,512]{1,0:T(8,128)(2,1)} %get-tuple-element.297.normed_ref, bf16[512,1024]{1,0:T(8,128)(2,1)S(1)} %get-tuple-element.298.dzf_ref, bf16[512,1024]{1,0:T(8,128)(2,1)S(1)} %get-tuple-element.299.dzi_ref, ...), custom_call_target="tpu_custom_call" | custom-call | flops 1 | bytes 1024 | tf_op jit(solution)/shard_map/gate_weights/pallas_call | solution.py:507
  266.9 7.5 %collective-permute-done.70.got_b = bf16[4,2,512,128]{3,2,1,0:T(8,128)(2,1)S(1)} collective-permute-done((bf16[4,2,512,128]{3,2,1,0:T(8,128)(2,1)S(1)}, bf16[4,2,512,128]{3,2,1,0:T(8,128)(2,1)S(1)}, u32[]{:S(2)}, u32[]{:S(2)}) %collective-permute-start.70) | collective-permute-done | bytes 1048608 | tf_op jit(solution)/shard_map/ppermute | solution.py:673
  283.1 8.2 %collective-permute-done.72.got_b = bf16[4,512,128]{2,1,0:T(8,128)(2,1)S(1)} collective-permute-done((bf16[4,512,128]{2,1,0:T(8,128)(2,1)S(1)}, bf16[4,512,128]{2,1,0:T(8,128)(2,1)S(1)}, u32[]{:S(2)}, u32[]{:S(2)}) %collective-permute-start.72) | collective-permute-done | bytes 524320 | tf_op jit(solution)/shard_map/ppermute | solution.py:673
  292.8 6.4 %collective-permute-done.77.got_a = bf16[4,2,192,128]{3,2,1,0:T(8,128)(2,1)S(1)} collective-permute-done((bf16[4,2,192,128]{3,2,1,0:T(8,128)(2,1)S(1)}, bf16[4,2,192,128]{3,2,1,0:T(8,128)(2,1)S(1)}, u32[]{:S(2)}, u32[]{:S(2)}) %collective-permute-start.77) | collective-permute-done | bytes 393248 | tf_op jit(solution)/shard_map/ppermute | solution.py:673
  315.4 10.9 %collective-permute-done.74.refs_3_ = bf16[1024,128]{1,0:T(8,128)(2,1)S(1)} collective-permute-done((bf16[1024,128]{1,0:T(8,128)(2,1)S(1)}, bf16[1024,128]{1,0:T(8,128)(2,1)S(1)}, u32[]{:S(2)}, u32[]{:S(2)}) %collective-permute-start.74) | collective-permute-done | bytes 262176 | tf_op jit(solution)/shard_map/ppermute | solution.py:673
  326.3 7.8 %collective-permute-done.82.refs_7_ = bf16[400,128]{1,0:T(8,128)(2,1)S(1)} collective-permute-done((bf16[400,128]{1,0:T(8,128)(2,1)S(1)}, bf16[400,128]{1,0:T(8,128)(2,1)S(1)}, u32[]{:S(2)}, u32[]{:S(2)}) %collective-permute-start.82) | collective-permute-done | bytes 102432 | tf_op jit(solution)/shard_map/ppermute | solution.py:673
  (332 shorter events, 160.3 us)
Async XLA Ops:
  39.3 17.9 %collective-permute-start.18 = (bf16[1024,128]{1,0:T(8,128)(2,1)S(1)}, bf16[1024,128]{1,0:T(8,128)(2,1)S(1)}, u32[]{:S(2)}, u32[]{:S(2)}) collective-permute-start(bf16[1024,128]{1,0:T(8,128)(2,1)S(1)} %get-tuple-element.191.refs_0_), channel_id=1, source_target_pairs={{0,24},{4,28},{8,16},{12,20},{16,8},{20,12},{24,0},{28,4},{1,25},{... | collective-permute-start | bytes 786440 | tf_op jit(solution)/shard_map/ppermute | solution.py:673
  41.4 22.6 %collective-permute-start.17 = (bf16[1024,128]{1,0:T(8,128)(2,1)S(1)}, bf16[1024,128]{1,0:T(8,128)(2,1)S(1)}, u32[]{:S(2)}, u32[]{:S(2)}) collective-permute-start(bf16[1024,128]{1,0:T(8,128)(2,1)S(1)} %get-tuple-element.191.refs_0_), channel_id=1, source_target_pairs={{0,16},{4,20},{8,24},{12,28},{16,0},{20,4},{24,8},{28,12},{1,17},{... | collective-permute-start | bytes 786440 | tf_op jit(solution)/shard_map/ppermute | solution.py:673
  41.4 22.6 %collective-permute-start.16 = (bf16[1024,128]{1,0:T(8,128)(2,1)S(1)}, bf16[1024,128]{1,0:T(8,128)(2,1)S(1)}, u32[]{:S(2)}, u32[]{:S(2)}) collective-permute-start(bf16[1024,128]{1,0:T(8,128)(2,1)S(1)} %get-tuple-element.191.refs_0_), channel_id=1, source_target_pairs={{0,8},{4,12},{8,0},{12,4},{16,24},{20,28},{24,16},{28,20},{1,9},{5... | collective-permute-start | bytes 786440 | tf_op jit(solution)/shard_map/ppermute | solution.py:673
  43.8 23.2 %collective-permute-start.22 = (bf16[4,640,128]{2,1,0:T(8,128)(2,1)S(1)}, bf16[4,640,128]{2,1,0:T(8,128)(2,1)}, u32[]{:S(2)}, u32[]{:S(2)}) collective-permute-start(bf16[4,640,128]{2,1,0:T(8,128)(2,1)S(1)} %line_gather.4.refs_0_), channel_id=1, source_target_pairs={{0,4},{4,0},{8,12},{12,8},{16,20},{20,16},{24,28},{28,24},{1,5},{5... | collective-permute-start | bytes 1966088 | tf_op jit(solution)/shard_map/ppermute | solution.py:673
  45.3 23.4 %collective-permute-start.20 = (bf16[4,640,128]{2,1,0:T(8,128)(2,1)S(1)}, bf16[4,640,128]{2,1,0:T(8,128)(2,1)}, u32[]{:S(2)}, u32[]{:S(2)}) collective-permute-start(bf16[4,640,128]{2,1,0:T(8,128)(2,1)S(1)} %line_gather.4.refs_0_), channel_id=1, source_target_pairs={{0,2},{1,3},{2,0},{3,1},{4,6},{5,7},{6,4},{7,5},{8,10},{9,11},{10,... | collective-permute-start | bytes 1966088 | tf_op jit(solution)/shard_map/ppermute | solution.py:673
  84.2 19.8 %collective-permute-start.32 = (bf16[4,384,128]{2,1,0:T(8,128)(2,1)S(1)}, bf16[4,384,128]{2,1,0:T(8,128)(2,1)S(1)}, u32[]{:S(2)}, u32[]{:S(2)}) collective-permute-start(bf16[4,384,128]{2,1,0:T(8,128)(2,1)S(1)} %get-tuple-element.200.refs_0_), channel_id=1, source_target_pairs={{0,6},{1,7},{2,4},{3,5},{4,2},{5,3},{6,0},{7,1},{8,14},{9,15},{10,... | collective-permute-start | bytes 1179656 | tf_op jit(solution)/shard_map/ppermute | solution.py:673
  86.7 18.4 %collective-permute-start.31 = (bf16[4,384,128]{2,1,0:T(8,128)(2,1)S(1)}, bf16[4,384,128]{2,1,0:T(8,128)(2,1)S(1)}, u32[]{:S(2)}, u32[]{:S(2)}) collective-permute-start(bf16[4,384,128]{2,1,0:T(8,128)(2,1)S(1)} %get-tuple-element.200.refs_0_), channel_id=1, source_target_pairs={{0,4},{4,0},{8,12},{12,8},{16,20},{20,16},{24,28},{28,24},{1,5},{5... | collective-permute-start | bytes 1179656 | tf_op jit(solution)/shard_map/ppermute | solution.py:673
  87.3 18.0 %collective-permute-start.30 = (bf16[4,384,128]{2,1,0:T(8,128)(2,1)S(1)}, bf16[4,384,128]{2,1,0:T(8,128)(2,1)S(1)}, u32[]{:S(2)}, u32[]{:S(2)}) collective-permute-start(bf16[4,384,128]{2,1,0:T(8,128)(2,1)S(1)} %get-tuple-element.200.refs_0_), channel_id=1, source_target_pairs={{0,2},{1,3},{2,0},{3,1},{4,6},{5,7},{6,4},{7,5},{8,10},{9,11},{10,... | collective-permute-start | bytes 1179656 | tf_op jit(solution)/shard_map/ppermute | solution.py:673
  105.8 20.3 %collective-permute-start.39 = (bf16[4,640,128]{2,1,0:T(8,128)(2,1)S(1)}, bf16[4,640,128]{2,1,0:T(8,128)(2,1)}, u32[]{:S(2)}, u32[]{:S(2)}) collective-permute-start(bf16[4,640,128]{2,1,0:T(8,128)(2,1)S(1)} %get-tuple-element.210.refs_0_), channel_id=1, source_target_pairs={{0,4},{4,0},{8,12},{12,8},{16,20},{20,16},{24,28},{28,24},{1,5},{5... | collective-permute-start | bytes 1966088 | tf_op jit(solution)/shard_map/ppermute | solution.py:673
  107.3 18.8 %collective-permute-start.38 = (bf16[4,640,128]{2,1,0:T(8,128)(2,1)S(1)}, bf16[4,640,128]{2,1,0:T(8,128)(2,1)S(1)}, u32[]{:S(2)}, u32[]{:S(2)}) collective-permute-start(bf16[4,640,128]{2,1,0:T(8,128)(2,1)S(1)} %get-tuple-element.210.refs_0_), channel_id=1, source_target_pairs={{0,2},{1,3},{2,0},{3,1},{4,6},{5,7},{6,4},{7,5},{8,10},{9,11},{10,... | collective-permute-start | bytes 1966088 | tf_op jit(solution)/shard_map/ppermute | solution.py:673
  192.1 19.7 %collective-permute-start.55 = (bf16[4,2,256,128]{3,2,1,0:T(8,128)(2,1)S(1)}, bf16[4,2,256,128]{3,2,1,0:T(8,128)(2,1)S(1)}, u32[]{:S(2)}, u32[]{:S(2)}) collective-permute-start(bf16[4,2,256,128]{3,2,1,0:T(8,128)(2,1)S(1)} %get-tuple-element.234), channel_id=1, source_target_pairs={{0,2},{1,3},{2,0},{3,1},{4,6},{5,7},{6,4},{7,5},{8,10},{9,11},{10,... | collective-permute-start | bytes 1572872 | tf_op jit(solution)/shard_map/ppermute | solution.py:673
  193.6 18.4 %collective-permute-start.56 = (bf16[4,2,384,128]{3,2,1,0:T(8,128)(2,1)S(1)}, bf16[4,2,384,128]{3,2,1,0:T(8,128)(2,1)S(1)}, u32[]{:S(2)}, u32[]{:S(2)}) collective-permute-start(bf16[4,2,384,128]{3,2,1,0:T(8,128)(2,1)S(1)} %get-tuple-element.254), channel_id=1, source_target_pairs={{0,4},{4,0},{8,12},{12,8},{16,20},{20,16},{24,28},{28,24},{1,5},{5... | collective-permute-start | bytes 2359304 | tf_op jit(solution)/shard_map/ppermute | solution.py:673
  212.9 19.5 %collective-permute-start.58 = (bf16[4,256,128]{2,1,0:T(8,128)(2,1)S(1)}, bf16[4,256,128]{2,1,0:T(8,128)(2,1)S(1)}, u32[]{:S(2)}, u32[]{:S(2)}) collective-permute-start(bf16[4,256,128]{2,1,0:T(8,128)(2,1)S(1)} %get-tuple-element.255), channel_id=1, source_target_pairs={{0,4},{4,0},{8,12},{12,8},{16,20},{20,16},{24,28},{28,24},{1,5},{5... | collective-permute-start | bytes 786440 | tf_op jit(solution)/shard_map/ppermute | solution.py:673
  244.3 22.5 %collective-permute-start.66 = (bf16[640,128]{1,0:T(8,128)(2,1)S(1)}, bf16[640,128]{1,0:T(8,128)(2,1)S(1)}, u32[]{:S(2)}, u32[]{:S(2)}) collective-permute-start(bf16[640,128]{1,0:T(8,128)(2,1)S(1)} %get-tuple-element.309), channel_id=1, source_target_pairs={{0,8},{4,12},{8,0},{12,4},{16,24},{20,28},{24,16},{28,20},{1,9},{5... | collective-permute-start | bytes 491528 | tf_op jit(solution)/shard_map/ppermute | solution.py:673
  244.6 22.2 %collective-permute-start.67 = (bf16[640,128]{1,0:T(8,128)(2,1)S(1)}, bf16[640,128]{1,0:T(8,128)(2,1)S(1)}, u32[]{:S(2)}, u32[]{:S(2)}) collective-permute-start(bf16[640,128]{1,0:T(8,128)(2,1)S(1)} %get-tuple-element.310), channel_id=1, source_target_pairs={{0,16},{4,20},{8,24},{12,28},{16,0},{20,4},{24,8},{28,12},{1,17},{... | collective-permute-start | bytes 491528 | tf_op jit(solution)/shard_map/ppermute | solution.py:673
  246.2 20.6 %collective-permute-start.68 = (bf16[640,128]{1,0:T(8,128)(2,1)S(1)}, bf16[640,128]{1,0:T(8,128)(2,1)S(1)}, u32[]{:S(2)}, u32[]{:S(2)}) collective-permute-start(bf16[640,128]{1,0:T(8,128)(2,1)S(1)} %get-tuple-element.311), channel_id=1, source_target_pairs={{0,24},{4,28},{8,16},{12,20},{16,8},{20,12},{24,0},{28,4},{1,25},{... | collective-permute-start | bytes 491528 | tf_op jit(solution)/shard_map/ppermute | solution.py:673
  250.3 24.1 %collective-permute-start.70 = (bf16[4,2,512,128]{3,2,1,0:T(8,128)(2,1)S(1)}, bf16[4,2,512,128]{3,2,1,0:T(8,128)(2,1)S(1)}, u32[]{:S(2)}, u32[]{:S(2)}) collective-permute-start(bf16[4,2,512,128]{3,2,1,0:T(8,128)(2,1)S(1)} %get-tuple-element.315), channel_id=1, source_target_pairs={{0,4},{4,0},{8,12},{12,8},{16,20},{20,16},{24,28},{28,24},{1,5},{5... | collective-permute-start | bytes 3145736 | tf_op jit(solution)/shard_map/ppermute | solution.py:673
  251.5 23.7 %collective-permute-start.69 = (bf16[4,2,512,128]{3,2,1,0:T(8,128)(2,1)S(1)}, bf16[4,2,512,128]{3,2,1,0:T(8,128)(2,1)S(1)}, u32[]{:S(2)}, u32[]{:S(2)}) collective-permute-start(bf16[4,2,512,128]{3,2,1,0:T(8,128)(2,1)S(1)} %get-tuple-element.285), channel_id=1, source_target_pairs={{0,2},{1,3},{2,0},{3,1},{4,6},{5,7},{6,4},{7,5},{8,10},{9,11},{10,... | collective-permute-start | bytes 3145736 | tf_op jit(solution)/shard_map/ppermute | solution.py:673
  281.0 19.3 %collective-permute-start.78 = (bf16[4,2,208,128]{3,2,1,0:T(8,128)(2,1)S(1)}, bf16[4,2,208,128]{3,2,1,0:T(8,128)(2,1)S(1)}, u32[]{:S(2)}, u32[]{:S(2)}) collective-permute-start(bf16[4,2,208,128]{3,2,1,0:T(8,128)(2,1)S(1)} %get-tuple-element.329), channel_id=1, source_target_pairs={{0,4},{4,0},{8,12},{12,8},{16,20},{20,16},{24,28},{28,24},{1,5},{5... | collective-permute-start | bytes 1277960 | tf_op jit(solution)/shard_map/ppermute | solution.py:673
  292.7 18.8 %collective-permute-start.73 = (bf16[1024,128]{1,0:T(8,128)(2,1)S(1)}, bf16[1024,128]{1,0:T(8,128)(2,1)S(1)}, u32[]{:S(2)}, u32[]{:S(2)}) collective-permute-start(bf16[1024,128]{1,0:T(8,128)(2,1)S(1)} %get-tuple-element.321), channel_id=1, source_target_pairs={{0,8},{4,12},{8,0},{12,4},{16,24},{20,28},{24,16},{28,20},{1,9},{5... | collective-permute-start | bytes 786440 | tf_op jit(solution)/shard_map/ppermute | solution.py:673
  303.5 22.8 %collective-permute-start.74 = (bf16[1024,128]{1,0:T(8,128)(2,1)S(1)}, bf16[1024,128]{1,0:T(8,128)(2,1)S(1)}, u32[]{:S(2)}, u32[]{:S(2)}) collective-permute-start(bf16[1024,128]{1,0:T(8,128)(2,1)S(1)} %get-tuple-element.322), channel_id=1, source_target_pairs={{0,16},{4,20},{8,24},{12,28},{16,0},{20,4},{24,8},{28,12},{1,17},{... | collective-permute-start | bytes 786440 | tf_op jit(solution)/shard_map/ppermute | solution.py:673
  303.5 22.8 %collective-permute-start.75 = (bf16[1024,128]{1,0:T(8,128)(2,1)S(1)}, bf16[1024,128]{1,0:T(8,128)(2,1)S(1)}, u32[]{:S(2)}, u32[]{:S(2)}) collective-permute-start(bf16[1024,128]{1,0:T(8,128)(2,1)S(1)} %get-tuple-element.323), channel_id=1, source_target_pairs={{0,24},{4,28},{8,16},{12,20},{16,8},{20,12},{24,0},{28,4},{1,25},{... | collective-permute-start | bytes 786440 | tf_op jit(solution)/shard_map/ppermute | solution.py:673
  309.2 24.9 %collective-permute-start.82 = (bf16[400,128]{1,0:T(8,128)(2,1)S(1)}, bf16[400,128]{1,0:T(8,128)(2,1)S(1)}, u32[]{:S(2)}, u32[]{:S(2)}) collective-permute-start(bf16[400,128]{1,0:T(8,128)(2,1)S(1)} %get-tuple-element.336), channel_id=1, source_target_pairs={{0,16},{4,20},{8,24},{12,28},{16,0},{20,4},{24,8},{28,12},{1,17},{... | collective-permute-start | bytes 307208 | tf_op jit(solution)/shard_map/ppermute | solution.py:673
  311.5 22.6 %collective-permute-start.83 = (bf16[400,128]{1,0:T(8,128)(2,1)S(1)}, bf16[400,128]{1,0:T(8,128)(2,1)S(1)}, u32[]{:S(2)}, u32[]{:S(2)}) collective-permute-start(bf16[400,128]{1,0:T(8,128)(2,1)S(1)} %get-tuple-element.337), channel_id=1, source_target_pairs={{0,24},{4,28},{8,16},{12,20},{16,8},{20,12},{24,0},{28,4},{1,25},{... | collective-permute-start | bytes 307208 | tf_op jit(solution)/shard_map/ppermute | solution.py:673
  (120 other events, 1102.3 us)

commit v4 on v3

v4 whole, which is shorter than its diff:
```python
import functools

import jax
import jax.numpy as jnp
from jax import lax
from jax.experimental import pallas as pl
from jax.experimental.pallas import tpu as pltpu
from jax.sharding import PartitionSpec as P

LAYERS = 2
EPS = 1e-05
NS, NB, LANE = 8, 4, 128
CHUNKS = 8
STEPS = 2
GATE_STEPS = 4
TURN, WIDE = 2, 256
VMEM = 28 * 1024 * 1024
F32, BF16 = jnp.float32, jnp.bfloat16


def dot(left, right):
    return lax.dot_general(left, right, (((1,), (0,)), ((), ())), preferred_element_type=F32)


def dot_nt(left, right):
    return lax.dot_general(left, right, (((1,), (1,)), ((), ())), preferred_element_type=F32)


def dot_tn(left, right):
    return lax.dot_general(left, right, (((0,), (0,)), ((), ())), preferred_element_type=F32)


def columns_of(ref, slabs=2):
    rows = ref.shape[2] // slabs
    parts = [
        ref[:, b, j * rows : (j + 1) * rows, :].reshape(NS * rows, LANE) for b in range(ref.shape[1]) for j in range(slabs)
    ]
    return jnp.concatenate(parts, axis=1)


def rows_of(ref):
    parts = [ref[:, j].reshape(-1, LANE) for j in range(NB)]
    return jnp.concatenate(parts, axis=1)


def rms_scale(values):
    return lax.rsqrt(jnp.mean(values * values, axis=-1, keepdims=True) + EPS)


def rms_back(values, gain, grad):
    scale = rms_scale(values)
    unit = values * scale
    inner = grad * gain
    back = scale * (inner - unit * jnp.mean(inner * unit, axis=-1, keepdims=True))
    return back, jnp.sum(grad * unit, axis=0, keepdims=True)


def gate_kernel(
    seqs, steps, x_ref, gain_ref, bias_ref, wf_ref, wi_ref, wc_ref,
    normed_ref, decay_ref, inflow_ref, cand_ref, ff_ref, fi_ref, fc_ref, cp_ref, ch_ref, fin_ref,
    z,
):
    width = decay_ref.shape[1]

    @pl.when(pl.program_id(0) == 0)
    def _():
        x = x_ref[...].astype(F32)
        normed_ref[...] = (x * rms_scale(x) * gain_ref[0:1, :]).astype(BF16)

    weights = jnp.concatenate([columns_of(ref) for ref in (wf_ref, wi_ref, wc_ref)], axis=1)
    block = TURN * CHUNKS
    places = [(seq, left) for seq in range(seqs) for left in range(0, width, WIDE)]

    def turn(of, at, carry):
        carry = list(carry)
        for k, (seq, left) in enumerate(places):
            if seq != of:
                continue
            span = slice(seq * steps * CHUNKS + at * block, seq * steps * CHUNKS + (at + 1) * block)
            cols = slice(left, left + WIDE)
            f = z[span, cols] + bias_ref[0:1, cols]
            i = z[span, width + left : width + left + WIDE] + bias_ref[1:2, cols]
            c = z[span, 2 * width + left : 2 * width + left + WIDE]
            low = jnp.minimum(jnp.minimum(f, i), 0.0)
            e0, ef, ei = jnp.exp(low), jnp.exp(low - f), jnp.exp(low - i)
            a, b = e0 + ef, e0 + ei
            inv = 1.0 / (a + b)
            decay, other = b * inv, a * inv
            ec = jnp.exp(-jnp.abs(c))
            cand = jnp.maximum(c, 0.0) + jnp.log1p(ec)
            slope = jnp.where(c >= 0.0, 1.0, ec) / (1.0 + ec)
            inflow = other * cand
            decay_ref[span, cols] = decay
            inflow_ref[span, cols] = inflow
            cand_ref[span, cols] = cand
            ff_ref[span, cols] = (ef * inv * decay).astype(BF16)
            fi_ref[span, cols] = (ei * inv * other).astype(BF16)
            fc_ref[span, cols] = (other * slope).astype(BF16)
            prod, state = carry[2 * k], carry[2 * k + 1]
            for t in range(TURN):
                d = decay[t * CHUNKS : (t + 1) * CHUNKS]
                prod = prod * d
                state = state * d + inflow[t * CHUNKS : (t + 1) * CHUNKS]
            carry[2 * k], carry[2 * k + 1] = prod, state
        return tuple(carry)

    one, zero = jnp.ones((CHUNKS, WIDE), F32), jnp.zeros((CHUNKS, WIDE), F32)
    carry = (one, zero) * len(places)
    for seq in range(seqs):
        rows = slice(seq * steps * CHUNKS, (seq + 1) * steps * CHUNKS)
        z[rows, :] = dot(normed_ref[rows, :], weights)
        for at in range(steps // TURN):
            carry = turn(seq, at, carry)
    for k, (seq, left) in enumerate(places):
        prod, state = carry[2 * k], carry[2 * k + 1]
        cols = slice(left, left + WIDE)
        cp_ref[seq, :, cols], ch_ref[seq, :, cols] = prod, state
        whole, last = prod[0:1], state[0:1]
        for c in range(1, CHUNKS):
            whole, last = whole * prod[c : c + 1], last * prod[c : c + 1] + state[c : c + 1]
        fin_ref[seq : seq + 1, cols] = whole
        fin_ref[seqs + seq : seqs + seq + 1, cols] = last


def mix_kernel(
    seqs, steps, x_ref, gain_ref, decay_ref, inflow_ref, cp_ref, ch_ref, ent_ref, wo_ref, wu_ref, wd_ref,
    hidden_ref, hb_ref, e_ref, mid_ref, n2_ref, act_ref, slope_ref, out_ref,
    acc,
):
    at_step = pl.program_id(0)
    block = TURN * CHUNKS
    width = decay_ref.shape[1]
    places = [(seq, left) for seq in range(seqs) for left in range(0, width, WIDE)]

    @pl.when(at_step == 0)
    def _():
        acc[...] = x_ref[...].astype(F32)

    @pl.when(at_step < STEPS)
    def _():
        for seq in range(seqs):
            state = ent_ref[seq : seq + 1, :]
            for c in range(CHUNKS):
                e_ref[seq, c : c + 1, :] = state
                state = state * cp_ref[seq, c : c + 1, :] + ch_ref[seq, c : c + 1, :]

        def turn(at, carry):
            carry = list(carry)
            for k, (seq, left) in enumerate(places):
                span = pl.ds(pl.multiple_of(seq * steps * CHUNKS + at * block, block), block)
                cols = slice(left, left + WIDE)
                d, u = decay_ref[span, cols], inflow_ref[span, cols]
                state, found = carry[k], []
                for t in range(TURN):
                    state = state * d[t * CHUNKS : (t + 1) * CHUNKS] + u[t * CHUNKS : (t + 1) * CHUNKS]
                    found.append(state)
                carry[k] = state
                hidden = jnp.concatenate(found, axis=0)
                hidden_ref[span, cols] = hidden
                hb_ref[span, cols] = hidden.astype(BF16)
            return tuple(carry)

        lax.fori_loop(0, steps // TURN, turn, tuple(e_ref[seq, :, left : left + WIDE] for seq, left in places))
        acc[...] += dot(hb_ref[...], rows_of(wo_ref))

    @pl.when(at_step == STEPS - 1)
    def _():
        middle = acc[...]
        mid_ref[...] = middle
        n2_ref[...] = (middle * rms_scale(middle) * gain_ref[1:2, :]).astype(BF16)

    @pl.when(at_step >= STEPS)
    def _():
        w_up, w_down = columns_of(wu_ref, 4), rows_of(wd_ref)
        size = acc.shape[0] // 2
        for k in range(2):
            span = slice(k * size, (k + 1) * size)
            v = dot(n2_ref[span, :], w_up)
            phi = 0.5 + 0.5 * lax.erf(v * 0.7071067811865476)
            act = (v * phi).astype(BF16)
            act_ref[span, :] = act
            slope_ref[span, :] = (phi + v * (0.3989422804014327 * jnp.exp(v * v * -0.5))).astype(BF16)
            acc[span, :] += dot(act, w_down)

    @pl.when(at_step == 2 * STEPS - 1)
    def _():
        out_ref[...] = acc[...].astype(out_ref.dtype)


def mlp_back_kernel(
    seqs, steps, g_ref, gain_ref, mid_ref, slope_ref, decay_ref, wo_ref, wu_ref, wd_ref,
    gr_ref, gpre_ref, gmid_ref, go_ref, ggain_ref, gh_ref, cp_ref, ca_ref, fin_ref,
    acc,
):
    at_step = pl.program_id(0)
    block = TURN * CHUNKS
    width = decay_ref.shape[1]
    places = [(seq, left) for seq in range(seqs) for left in range(0, width, WIDE)]

    @pl.when(at_step == 0)
    def _():
        gr_ref[...] = g_ref[...].astype(BF16)
        acc[...] = jnp.zeros_like(acc)

    @pl.when(at_step < STEPS)
    def _():
        gact = dot_nt(gr_ref[...], rows_of(wd_ref))
        gpre_ref[...] = (gact * slope_ref[...].astype(F32)).astype(BF16)
        acc[...] += dot_nt(gpre_ref[...], columns_of(wu_ref, 4))

    @pl.when(at_step == STEPS - 1)
    def _():
        back, ggain = rms_back(mid_ref[...], gain_ref[1:2, :], acc[...])
        ggain_ref[...] = ggain
        gmid = g_ref[...].astype(F32) + back
        gmid_ref[...] = gmid
        go_ref[...] = gmid.astype(BF16)

    @pl.when(at_step >= STEPS)
    def _():
        gh_ref[...] = dot_nt(go_ref[...], rows_of(wo_ref))

        def turn(turn_at, carry):
            at = steps // TURN - 1 - turn_at
            carry = list(carry)
            for k, (seq, left) in enumerate(places):
                span = pl.ds(pl.multiple_of(seq * steps * CHUNKS + at * block, block), block)
                cols = slice(left, left + WIDE)
                d, g = decay_ref[span, cols], gh_ref[span, cols]
                prod, state = carry[2 * k], carry[2 * k + 1]
                for t in reversed(range(TURN)):
                    dk = d[t * CHUNKS : (t + 1) * CHUNKS]
                    prod = prod * dk
                    state = dk * (g[t * CHUNKS : (t + 1) * CHUNKS] + state)
                carry[2 * k], carry[2 * k + 1] = prod, state
            return tuple(carry)

        one, zero = jnp.ones((CHUNKS, WIDE), F32), jnp.zeros((CHUNKS, WIDE), F32)
        carry = lax.fori_loop(0, steps // TURN, turn, (one, zero) * len(places))
        for k, (seq, left) in enumerate(places):
            prod, state = carry[2 * k], carry[2 * k + 1]
            cols = slice(left, left + WIDE)
            cp_ref[seq, :, cols], ca_ref[seq, :, cols] = prod, state
            whole, last = prod[CHUNKS - 1 :], state[CHUNKS - 1 :]
            for c in reversed(range(CHUNKS - 1)):
                whole, last = whole * prod[c : c + 1], last * prod[c : c + 1] + state[c : c + 1]
            fin_ref[seq : seq + 1, cols] = whole
            fin_ref[seqs + seq : seqs + seq + 1, cols] = last


def gate_back_kernel(
    seqs, steps, others, pos_ref, x_ref, gain_ref, gmid_ref, gh_ref, decay_ref, hidden_ref, e_ref, cand_ref,
    ff_ref, fi_ref, fc_ref, cp_ref, ca_ref, ent_ref, normed_ref, wf_ref, wi_ref, wc_ref, *refs,
):
    given = refs[: len(others)]
    keep_ref, send_ref, gbias_ref, gstream_ref, ggain_ref, acc, start, dz, rest = refs[len(others) :]
    at_step = pl.program_id(0)
    block = TURN * CHUNKS
    width = decay_ref.shape[1]
    places = [(seq, left) for seq in range(seqs) for left in range(0, width, WIDE)]

    @pl.when(at_step == 0)
    def _():
        acc[...] = jnp.zeros_like(acc)

    for seq in range(seqs):
        state = ent_ref[seq : seq + 1, :]
        for c in reversed(range(CHUNKS)):
            start[seq, c : c + 1, :] = state
            state = state * cp_ref[seq, c : c + 1, :] + ca_ref[seq, c : c + 1, :]

    def turn(of, at, carry):
        carry = list(carry)
        for k, (seq, left) in enumerate(places):
            if seq != of:
                continue
            cols = slice(left, left + WIDE)
            state, sum_f, sum_i = carry[3 * k : 3 * k + 3]
            base = seq * steps * CHUNKS + at * block
            span = slice(base, base + block)
            before = hidden_ref[base - CHUNKS : base, cols] if at else e_ref[seq, :, cols]
            d, g = decay_ref[span, cols], gh_ref[span, cols]
            previous = jnp.concatenate([before, hidden_ref[span, cols][: block - CHUNKS]], axis=0)
            found = []
            for t in reversed(range(TURN)):
                now = g[t * CHUNKS : (t + 1) * CHUNKS] + state
                found.append(now)
                state = d[t * CHUNKS : (t + 1) * CHUNKS] * now
            gstate = jnp.concatenate(found[::-1], axis=0)
            both = gstate * (cand_ref[span, cols] - previous)
            dzf = (-ff_ref[span, cols].astype(F32) * both).astype(BF16)
            dzi = (fi_ref[span, cols].astype(F32) * both).astype(BF16)
            dz[span, left : left + WIDE] = dzf
            dz[span, width + left : width + left + WIDE] = dzi
            dz[span, 2 * width + left : 2 * width + left + WIDE] = (fc_ref[span, cols].astype(F32) * gstate).astype(BF16)
            wide_f, wide_i = dzf.astype(F32), dzi.astype(F32)
            for t in range(TURN):
                sum_f = sum_f + wide_f[t * CHUNKS : (t + 1) * CHUNKS]
                sum_i = sum_i + wide_i[t * CHUNKS : (t + 1) * CHUNKS]
            carry[3 * k : 3 * k + 3] = state, sum_f, sum_i
        return tuple(carry)

    zero = jnp.zeros((CHUNKS, WIDE), F32)
    first_carry = [v for seq, left in places for v in (start[seq, :, left : left + WIDE], zero, zero)]
    carry = tuple(first_carry)
    weights = jnp.concatenate([columns_of(ref) for ref in (wf_ref, wi_ref, wc_ref)], axis=1)
    grad = None
    for seq in range(seqs):
        rows = slice(seq * steps * CHUNKS, (seq + 1) * steps * CHUNKS)
        for at in reversed(range(steps // TURN)):
            carry = turn(seq, at, carry)
        acc[rows, :] += dot_nt(dz[rows, :], weights)
        part = dot_tn(normed_ref[rows, :], dz[rows, :])
        grad = part if grad is None else grad + part
    for row in range(2):
        for left in range(0, width, WIDE):
            total = sum(carry[3 * k + 1 + row] for k, place in enumerate(places) if place[1] == left)
            gbias_ref[row : row + 1, left : left + WIDE] = jnp.sum(total, axis=0, keepdims=True)
    rows = wf_ref.shape[2]
    for m in range(3):
        put_columns(pos_ref, keep_ref, send_ref, m * rows, grad[:, m * width : (m + 1) * width])

    @pl.when(at_step == STEPS - 1)
    def _():
        back, ggain = rms_back(x_ref[...].astype(F32), gain_ref[0:1, :], acc[...])
        ggain_ref[...] = ggain
        gstream_ref[...] = (gmid_ref[...] + back).astype(gstream_ref.dtype)

    if others:

        def rows_to(ref, first_row):
            wide = ref.shape[1] // NS
            for r in range(ref.shape[0]):
                for s in range(NS):
                    rest[s, first_row + r : first_row + r + 1, :wide] = ref[r : r + 1, s * wide : (s + 1) * wide]

        @pl.when(at_step == 0)
        def _():
            rest[...] = jnp.zeros_like(rest)
            for ref, first_row in zip(given, others):
                rows_to(ref, first_row)

        wide = width * STEPS // NS
        for row in range(2):
            for s in range(width // wide):
                rest[at_step * (width // wide) + s, 1 + row : 2 + row, :wide] = gbias_ref[row : row + 1, s * wide : (s + 1) * wide]

        @pl.when(at_step == STEPS - 1)
        def _():
            rows_to(ggain_ref, 0)
            found = rest[...].astype(BF16)
            for x in range(2):
                keep_ref[:, x, 3 * rows :, :] = found
                send_ref[:, x, 3 * rows :, :] = found


def send_or_keep(mine, keep_ref, send_ref, put):
    @pl.when(mine)
    def _():
        put(keep_ref)

    @pl.when(jnp.logical_not(mine))
    def _():
        put(send_ref)


def put_columns(pos_ref, keep_ref, send_ref, start, value):
    rows, width = value.shape[0] // NS, value.shape[1] // 2
    x = pl.program_id(0)
    for core in range(2):
        parts = [
            value[:, left : left + LANE].astype(BF16).reshape(NS, rows, LANE)
            for left in range(core * width, (core + 1) * width, LANE)
        ]

        def put(ref):
            for j, part in enumerate(parts):
                ref[:, x, start + j * rows : start + (j + 1) * rows, :] = part

        send_or_keep(pos_ref[0] == core, keep_ref, send_ref, put)


def put_rows(pos_ref, keep_ref, send_ref, value):
    count = NS // STEPS
    for j in range(NB):
        part = value[:, j * LANE : (j + 1) * LANE].astype(BF16).reshape(count, -1, LANE)

        def put(ref):
            ref[pl.ds(pl.program_id(0) * count, count), j // 2] = part

        send_or_keep(pos_ref[0] == j % 2, keep_ref, send_ref, put)


def up_weight_kernel(pos_ref, n2_ref, gpre_ref, keep_ref, send_ref):
    put_columns(pos_ref, keep_ref, send_ref, 0, dot_tn(n2_ref[...], gpre_ref[...]))


def row_weight_kernel(pos_ref, left_ref, right_ref, keep_ref, send_ref):
    put_rows(pos_ref, keep_ref, send_ref, dot_tn(left_ref[...], right_ref[...]))


def add(*parts):
    total = parts[0].astype(F32)
    for part in parts[1:]:
        total = total + part.astype(F32)
    return total


def pair_sum_kernel(rows, pos_ref, *refs):
    count = len(rows)
    send, stay = refs[2 * count :]
    core, x, y, step = pos_ref[0], pos_ref[1], pos_ref[2], pos_ref[4]
    at = 0
    for keep, got, r in zip(refs[:count], refs[count : 2 * count], rows):
        for v in range(2):
            for out, first in ((send, 1 - step), (stay, step)):
                iy, ix = jnp.where(core == 0, v, first), jnp.where(core == 0, first, v)
                out[0, v, at : at + r] = add(keep[0, iy, ix], got[0, iy, ix]).astype(BF16)
        at += r


def plane_sum_kernel(pos_ref, keep, got, send, stay):
    second = pos_ref[5]
    send[0] = add(keep[0, 1 - second], got[0, 1 - second]).astype(BF16)
    stay[0] = add(keep[0, second], got[0, second]).astype(BF16)


def line_sum_kernel(pos_ref, keep, got, send, stay):
    core, first = pos_ref[0], pos_ref[6]
    for v in range(2):
        for out, f in ((send, 1 - first), (stay, first)):
            z = jnp.where(core == 0, f + 2 * v, 2 * f + v)
            out[v] = add(keep[z], got[z]).astype(BF16)


def last_sum_kernel(pos_ref, keep, got, send, stay):
    second = pos_ref[7]
    send[...] = add(keep[1 - second], got[1 - second]).astype(BF16)
    stay[...] = add(keep[second], got[second]).astype(BF16)


def total_kernel(keep, got, out):
    out[...] = add(keep[...], got[...])


def finish_kernel(layout, *refs):
    at = 0
    ins = sum(parts for parts, _ in layout)
    outs = refs[ins:]
    for parts, pieces in layout:
        got = refs[at : at + parts]
        at += parts
        row = 0
        for out, layer, vectors in pieces:
            ref = outs[out]
            if vectors:
                ref[layer : layer + 1, :] = add(*[g[...] for g in got])[row : row + 1, : ref.shape[1]]
                row += 1
                continue
            r = ref.shape[1]
            for j in range(ref.shape[2] // LANE):
                ref[layer, :, j * LANE : (j + 1) * LANE] = add(*[g[row : row + r] for g in got])
                row += r


def pack_kernel(groups, *refs):
    ins = refs[: len(refs) - len(groups) - 1]
    outs, scratch = refs[len(ins) : -1], refs[-1]
    for out, group in zip(outs, groups):
        row = 0
        vec = 0
        for which, layer, vector in group:
            ref = ins[which]
            if vector:
                if vec == 0:
                    scratch[...] = jnp.zeros_like(scratch)
                scratch[vec : vec + 1, : ref.shape[1]] = ref[...].astype(F32)[layer : layer + 1]
                vec += 1
                continue
            r = ref.shape[1]
            for j in range(ref.shape[2] // LANE):
                out[row : row + r, :] = ref[layer, :, j * LANE : (j + 1) * LANE]
                row += r
        if vec:
            out[row:, :] = scratch[...].astype(BF16)


def line_gather_kernel(pos_ref, *refs):
    row = 0
    for out in refs[4:]:
        rows = out.shape[1]
        for k, part in enumerate(refs[:4]):
            out[pos_ref[3] ^ k] = part[row : row + rows, :]
        row += rows


def plane_gather_kernel(pos_ref, *refs):
    out = refs[-1]
    at, half = pl.program_id(0), pl.num_programs(0) // 2
    core, x, y = pos_ref[0], pos_ref[1], pos_ref[2]
    count = len(refs) // 2
    for c in range(2):
        own, first, second, *diagonal = refs[count * c : count * (c + 1)]
        other = core ^ c
        turn = other if count == 4 else 0
        out[0, y, x, other] = own[0]
        out[0, y ^ turn, x ^ (1 - turn), other] = first[0]
        out[0, y ^ (1 - turn), x ^ turn, other] = second[0]
        if count == 4:
            out[0, y ^ 1, x ^ 1, other] = diagonal[0][0]
            continue

        @pl.when(at < half)
        def _():
            out[0, y ^ 1, x ^ 1, other] = diagonal[0][0]

        @pl.when(at >= half)
        def _():
            out[0, y ^ 1, x ^ 1, other] = diagonal[1][0]


def vector_kernel(gained, w_ref, *refs):
    outs, scratch = refs[:-1], refs[-1]
    scratch[...] = w_ref[:, 0].astype(F32)
    for l in range(LAYERS):
        for which in range(4):
            out, row = ((outs[2 * l], which // 3) if which in (0, 3) else (outs[2 * l + 1], which - 1))
            wide = out.shape[1] // NS
            for s in range(NS):
                out[row : row + 1, s * wide : (s + 1) * wide] = scratch[s, 4 * l + which : 4 * l + which + 1, :wide]


def shape(dims, dtype=F32):
    return jax.ShapeDtypeStruct(dims, dtype)


def call(kernel, grid, ins, outs, scratch, us, name):
    def spec(a, block, index):
        if a.dtype == jnp.int32:
            return pl.BlockSpec(memory_space=pltpu.SMEM)
        return pl.BlockSpec(block, index)

    found = pl.pallas_call(
        kernel,
        grid=(grid,),
        in_specs=[spec(*one) for one in ins],
        out_specs=[pl.BlockSpec(block, index) for _, block, index, *_ in outs],
        out_shape=[pltpu.HBM(one[0].shape, one[0].dtype) if one[3:] else one[0] for one in outs],
        scratch_shapes=scratch,
        compiler_params=pltpu.CompilerParams(vmem_limit_bytes=VMEM),
        cost_estimate=pl.CostEstimate(flops=int(us * 1.1e9) + 1, bytes_accessed=1024, transcendentals=0),
        name=name,
    )(*[a for a, _, _ in ins])
    return found if len(found) > 1 else found[0]


def far(array):
    return pltpu.with_memory_space_constraint(array, pltpu.HBM)


def whole(array):
    dims = array.shape
    return (array, dims, lambda i: (0,) * len(dims))


def whole_out(dims, dtype=F32):
    return (shape(dims, dtype), dims, lambda i: (0,) * len(dims))


def first(i):
    return jnp.minimum(i, STEPS - 1)


def second(i):
    return jnp.maximum(i - STEPS, 0)


class Sizes:
    def __init__(self, seqs, length, d, h, ff):
        self.seqs, self.steps, self.n = seqs, length // CHUNKS, seqs * length
        self.d, self.h, self.ff = d, h, ff
        self.hb, self.fb = h // STEPS, ff // STEPS


def column_weight(view, at, late=False, steps=STEPS):
    array, rows, place = view
    return (far(array) if late else array, (NS, NB // steps, rows, LANE), lambda i: (0, at(i), place, 0))


def row_weight(view, at):
    array, rows, place = view
    return (array, (NS // STEPS, NB, rows, LANE), lambda i: (at(i), 0, place, 0))


def same(i):
    return i


def gate_forward(sz, x, gain, bias, w, save):
    n, d, h, wide, s = sz.n, sz.d, sz.h, sz.h // GATE_STEPS, sz.seqs
    col = lambda i: (0, i)
    return call(
        functools.partial(gate_kernel, s, sz.steps), GATE_STEPS,
        [whole(x), whole(gain), (bias, (2, wide), col)] + [column_weight(w[m], same, False, GATE_STEPS) for m in "fic"],
        [whole_out((n, d), BF16) + save]
        + [(shape((n, h)), (n, wide), col) + save, (shape((n, h)), (n, wide), col), (shape((n, h)), (n, wide), col) + save]
        + [(shape((n, h), BF16), (n, wide), col) + save] * 3
        + [(shape((s, CHUNKS, h)), (s, CHUNKS, wide), lambda i: (0, 0, i))] * 2
        + [(shape((2 * s, h)), (2 * s, wide), col)],
        [pltpu.VMEM((n, 3 * wide), F32)], 9, "gates",
    )


def mix_forward(sz, x, gain, decay, inflow, cp, ch, ent, wt, last, save):
    n, d, h, ff, w, f, s = sz.n, sz.d, sz.h, sz.ff, sz.hb, sz.fb, sz.seqs
    col = lambda i: (0, first(i))
    late = lambda i: (0, second(i))
    deep = lambda i: (0, 0, first(i))
    return call(
        functools.partial(mix_kernel, s, sz.steps), 2 * STEPS,
        [
            whole(x), whole(gain), (decay, (n, w), col), (inflow, (n, w), col),
            (cp, (s, CHUNKS, w), deep), (ch, (s, CHUNKS, w), deep), (ent, (s, w), col),
            row_weight(wt["o"], first), column_weight(wt["u"], second), row_weight(wt["d"], second),
        ],
        [
            (shape((n, h)), (n, w), col, True), (shape((n, h), BF16), (n, w), col) + save,
            (shape((s, CHUNKS, h)), (s, CHUNKS, w), deep) + save,
            whole_out((n, d)) + save, whole_out((n, d), BF16) + save,
            (shape((n, ff), BF16), (n, f), late) + save, (shape((n, ff), BF16), (n, f), late) + save,
            whole_out((n, d), BF16 if last else F32),
        ],
        [pltpu.VMEM((n, d), F32)], 14, "mix",
    )


def mlp_backward(sz, g, gain, mid, slope, decay, wt):
    n, d, h, ff, w, f, s = sz.n, sz.d, sz.h, sz.ff, sz.hb, sz.fb, sz.seqs
    col = lambda i: (0, second(i))
    early = lambda i: (0, first(i))
    deep = lambda i: (0, 0, second(i))
    return call(
        functools.partial(mlp_back_kernel, s, sz.steps), 2 * STEPS,
        [
            whole(g), whole(gain), whole(mid), (slope, (n, f), early), (decay, (n, w), col),
            row_weight(wt["o"], second), column_weight(wt["u"], first), row_weight(wt["d"], first),
        ],
        [
            whole_out((n, d), BF16), (shape((n, ff), BF16), (n, f), early), whole_out((n, d)), whole_out((n, d), BF16),
            whole_out((1, d)), (shape((n, h)), (n, w), col),
            (shape((s, CHUNKS, h)), (s, CHUNKS, w), deep), (shape((s, CHUNKS, h)), (s, CHUNKS, w), deep),
            (shape((2 * s, h)), (2 * s, w), col),
        ],
        [pltpu.VMEM((n, d), F32)], 12, "mlp_back",
    )


def gate_backward(sz, pos, x, gain, gmid, gh, decay, hidden, e, cand, ff_, fi_, fc_, cp, ca, ent, normed, wt, last, vectors):
    n, d, h, w, s = sz.n, sz.d, sz.h, sz.hb, sz.seqs
    col = lambda i: (0, i)
    deep = lambda i: (0, 0, i)
    wide = lambda a: (a, (n, w), col)
    rows = 3 * d * h // (32 * LANE) + (16 if vectors else 0)
    return call(
        functools.partial(gate_back_kernel, s, sz.steps, tuple(row for _, row in vectors)), STEPS,
        [
            whole(pos), whole(x), whole(gain), whole(gmid), wide(gh), wide(decay), wide(hidden), (e, (s, CHUNKS, w), deep),
            wide(cand), wide(ff_), wide(fi_), wide(fc_), (cp, (s, CHUNKS, w), deep), (ca, (s, CHUNKS, w), deep),
            (ent, (s, w), col), whole(normed),
        ] + [column_weight(wt[m], same, True) for m in "fic"] + [whole(v) for v, _ in vectors],
        [whole_out((NS, 2, rows, LANE), BF16)] * 2
        + [(shape((2, h)), (2, w), col), whole_out((n, d), BF16 if last else F32), whole_out((1, d))],
        [
            pltpu.VMEM((n, d), F32), pltpu.VMEM((s, CHUNKS, w), F32), pltpu.VMEM((n, 3 * w), BF16),
            pltpu.VMEM((NS, 16, LANE), F32),
        ], 16, "gate_back",
    )


def up_weights(sz, pos, n2, gpre):
    n, d, ff, f = sz.n, sz.d, sz.ff, sz.fb
    dims = (NS, 2, d * ff // (32 * LANE), LANE)
    return call(
        up_weight_kernel, STEPS, [whole(pos), whole(n2), (gpre, (n, f), lambda i: (0, i))],
        [whole_out(dims, BF16)] * 2, [], 5, "up_weights",
    )


def row_weights(sz, pos, left, right, name):
    n, k, d = sz.n, left.shape[1], sz.d
    dims = (NS, 2, k // NS, LANE)
    return call(
        row_weight_kernel, STEPS, [whole(pos), (left, (n, k // STEPS), lambda i: (0, i)), whole(right)],
        [whole_out(dims, BF16)] * 2, [], 5, name,
    )


def swap(array, axes, bits):
    count = lax.axis_size(axes)
    return lax.ppermute(array, axes, [(i, i ^ bits) for i in range(count)])


BOTH = ("seq", "batch")


def after(array, *others):
    return lax.optimization_barrier((array,) + others)[0]


def by_line(a):
    return (a, (1,) + a.shape[1:], lambda i: (i,) + (0,) * (len(a.shape) - 1))


def by_line_out(*dims):
    return (shape(dims, BF16), (1,) + dims[1:], lambda i: (i,) + (0,) * (len(dims) - 1))


def core_exchange(pairs):
    return [(keep, swap(send, "batch", 1)) for keep, send in pairs]


FIRST, SECOND, FIRST_Z, SECOND_Z = (2, 4), (4, 2), (8, 16), (16, 8)


def cross(array, bits):
    count = lax.axis_size(BOTH)
    return lax.ppermute(array, BOTH, [(i, i ^ bits[i % 2]) for i in range(count)])


def pair_sum(pos, pairs):
    rows = tuple(keep.shape[2] for keep, _ in pairs)
    view = lambda a: by_line(a.reshape((4, 2, 2) + a.shape[2:]))
    return call(
        functools.partial(pair_sum_kernel, rows), 4,
        [whole(pos)] + [view(keep) for keep, _ in pairs] + [view(got) for _, got in pairs],
        [by_line_out(4, 2, sum(rows), LANE)] * 2, [], 0, "pair_sum",
    )


def onward(parts, bits):
    return [parts[1], cross(parts[0], bits)]


def plane_sum(pos, parts):
    rows = parts[0].shape[2]
    return call(
        plane_sum_kernel, 4, [whole(pos)] + [by_line(a) for a in parts], [by_line_out(4, rows, LANE)] * 2, [], 0, "plane_sum",
    )


def line_sum(pos, parts):
    rows = parts[0].shape[1]
    return call(
        line_sum_kernel, 1, [whole(pos)] + [whole(a) for a in parts], [whole_out((2, rows, LANE), BF16)] * 2, [], 0, "line_sum",
    )


def last_sum(pos, parts):
    rows = parts[0].shape[1]
    return call(
        last_sum_kernel, 1, [whole(pos)] + [whole(a) for a in parts], [whole_out((rows, LANE), BF16)] * 2, [], 0, "last_sum",
    )


SUMS = ((plane_sum, SECOND), (line_sum, FIRST_Z), (last_sum, SECOND_Z))


class Reduction:
    def __init__(self, pos, names, pairs):
        self.pos, self.names, self.stage = pos, names, 0
        self.parts = pair_sum(pos, pairs)
        self.seen = self.parts[0]
        self.parts = onward(self.parts, FIRST)

    def step(self, *others):
        work, bits = SUMS[self.stage]
        if others:
            self.parts[0] = after(self.parts[0], *others)
        parts = work(self.pos, self.parts)
        self.stage, self.seen, self.parts = self.stage + 1, parts[0], onward(parts, bits)
        return self.seen

    def total(self, *others):
        keep, got = self.parts
        keep = after(keep, *others)
        total = call(total_kernel, 1, [whole(keep), whole(got)], [whole_out(keep.shape)], [], 0, "total")
        self.parts = [total]
        return total


def line_parts(own):
    return [own] + [swap(own, "seq", 2 * k) for k in range(1, 4)]


def line_gather(pos, parts, rows):
    return call(
        line_gather_kernel, 1, [whole(pos)] + [whole(far(p)) for p in parts],
        [whole_out((4, r, LANE), BF16) for r in rows], [], 2, "line_gather",
    )


X_AXIS, Y_AXIS = ("batch", 2), ("seq", 1)


def plane_gather(pos, line, parts, behind=()):
    rows = line.shape[1]
    parts = [line, *parts]
    parts += [swap(after(p, *behind) if behind else p, "batch", 1) for p in parts]
    each, low, high = (lambda i: (i, 0, 0)), (lambda i: (jnp.minimum(i, 1), 0, 0)), (lambda i: (jnp.maximum(i - 2, 0), 0, 0))
    maps = [each] * 4 if len(parts) == 8 else [each, each, each, low, high]
    got = call(
        plane_gather_kernel, 4, [whole(pos)] + [(far(p), (1, rows, LANE), m) for p, m in zip(parts, maps * 2)],
        [(shape((4, 2, 2, 2, rows, LANE), BF16), (1, 2, 2, 2, rows, LANE), lambda i: (i, 0, 0, 0, 0, 0))], [], 5, "plane_gather",
    )
    return got.reshape(NS, NB, rows, LANE)


def enter(fin, seqs, backward, fill=(), hold=None):
    count, mine = lax.axis_size("seq"), lax.axis_index("seq")
    prod, state = fin[:seqs], fin[seqs:]
    pre_p, pre_s = jnp.ones_like(prod), jnp.zeros_like(state)
    bit, message, done = 1, fin, []
    for step in range(int(count).bit_length() - 1):
        if hold and step in hold:
            message = after(message, *hold[step])
        other = lax.ppermute(message, "seq", [(i, i ^ bit) for i in range(count)])
        if step < len(fill):
            done.append(fill[step](message))
        o_p, o_s = other[:seqs], other[seqs:]
        upper = ((mine // bit) % 2 == 1) ^ backward
        pre_p, pre_s = jnp.where(upper, o_p * pre_p, pre_p), jnp.where(upper, pre_p * o_s + pre_s, pre_s)
        state = jnp.where(upper, prod * o_s + state, o_p * state + o_s)
        prod = prod * o_p
        message = jnp.concatenate([prod, state])
        if step < len(fill):
            message = after(message, *done[-1])
        bit *= 2
    return pre_s, done


def slabs(matrix, seq_count, batch_count):
    rows, cols = matrix.shape[0] // NS, matrix.shape[1] // NB
    cut = matrix.reshape(NS, rows, NB, cols // LANE, LANE).transpose(0, 2, 3, 1, 4)
    return cut.reshape(NS, NB, rows * cols // LANE, LANE)


def unslab(blocks, rows, cols):
    r, c = rows // NS, cols // NB
    cut = blocks.reshape(NS, NB, c // LANE, r, LANE).transpose(0, 3, 1, 2, 4)
    return cut.reshape(rows, cols)


def body(
    tokens, norm_gain, w_forget, w_input, w_cand, forget_bias, input_bias, w_out, mlp_gain, w_up, w_down, cotangent
):
    seqs, length, d = tokens.shape
    seq_count, batch_count = lax.axis_size("seq"), lax.axis_size("batch")
    h, ff = w_forget.shape[2] * batch_count, w_up.shape[2] * batch_count
    sz = Sizes(seqs, length, d, h, ff)
    standard = (seq_count, batch_count) == (NS, NB)
    matrices = {"u": w_up, "d": w_down, "o": w_out, "f": w_forget, "i": w_input, "c": w_cand}
    vectors = (norm_gain, forget_bias, input_bias, mlp_gain)
    slab_rows = {"u": d * ff // (32 * LANE), "d": ff // NS, "o": h // NS}
    slab_rows.update({m: d * h // (32 * LANE) for m in "fic"})
    order = {name: k for k, name in enumerate(matrices)}

    if standard:
        s_at, b_at = lax.axis_index("seq"), lax.axis_index("batch")
        core, x, y, z = b_at % 2, b_at // 2, s_at % 2, s_at // 2
        turned = [jnp.where(core == 0, a, b) for a, b in ((x, y), (y, x), (z % 2, z // 2), (z // 2, z % 2))]
        pos = jnp.stack([core, x, y, z, *turned]).astype(jnp.int32)
        vecs = [(6 + k, at, True) for at in range(LAYERS) for k in range(4)]
        groups = []
        for l in range(LAYERS):
            groups += [[(order[m], l, False) for m in "fic"] + vecs * (l == 0), [(order[m], l, False) for m in "udo"]]
        gate_rows, rest_rows = sum(slab_rows[m] for m in "fic"), sum(slab_rows[m] for m in "udo")
        rows = [gate_rows + 16, rest_rows] + [gate_rows, rest_rows] * (LAYERS - 1)
        packs = call(
            functools.partial(pack_kernel, groups), 1,
            [whole(far(m)) for m in matrices.values()] + [whole(far(v)) for v in vectors],
            [whole_out((r, LANE), BF16) for r in rows], [pltpu.VMEM((16, LANE), F32)], 2, "pack",
        )
        line_g0 = line_gather(pos, line_parts(packs[0]), rows[:1])
        parts_g0 = [swap(line_g0, *X_AXIS), swap(line_g0, *Y_AXIS)]
        parts_g0 += [swap(parts_g0[0][:2], *Y_AXIS), swap(parts_g0[1][2:], *X_AXIS)]
        line_r0 = line_gather(pos, line_parts(after(packs[1], line_g0)), rows[1:2])
        sent_r0 = after(line_r0, *parts_g0[:2])
        parts_r0 = [cross(sent_r0, FIRST), cross(sent_r0, SECOND)]
        line_g1 = line_gather(pos, line_parts(after(packs[2], line_r0)), rows[2:3])
        got = [plane_gather(pos, line_g0, parts_g0), None]
        places = {"f": 0, "i": 1, "c": 2, "u": 0, "d": 1, "o": 4}
        view = lambda got: {m: (got[m in "udo"], slab_rows[m], places[m]) for m in "udofic"}
        weights, lines_at, parts_at = [view(got)], [line_r0], [parts_r0]
        vecs = call(
            functools.partial(vector_kernel, None), 1,
            [(got[0], (NS, 1, 16, LANE), lambda i: (0, 0, 3 * slab_rows["f"] // 16, 0))],
            [whole_out((2, size)) for l in range(LAYERS) for size in (d, h)],
            [pltpu.VMEM((NS, 16, LANE), F32)], 1, "vectors",
        )
        gains, biases = vecs[0::2], vecs[1::2]
    else:
        pos = jnp.zeros((8,), jnp.int32)

        def full(m):
            m = lax.all_gather(m, "batch", axis=1, tiled=True)
            return lax.all_gather(m, "seq", axis=0, tiled=True)

        weights = [
            {m: (slabs(full(matrices[m][l]), NS, NB), slab_rows[m], 0) for m in "udofic"} for l in range(LAYERS)
        ]
        whole_vectors = [lax.all_gather(v, "seq", axis=1, tiled=True).astype(F32) for v in vectors]
        gains = [jnp.stack([whole_vectors[0][l], whole_vectors[3][l]]) for l in range(LAYERS)]
        biases = [jnp.stack([whole_vectors[1][l], whole_vectors[2][l]]) for l in range(LAYERS)]

    def to_rows(v):
        return v.reshape(seqs, CHUNKS, sz.steps, d).transpose(0, 2, 1, 3).reshape(sz.n, d)

    def from_rows(v):
        return v.reshape(seqs, sz.steps, CHUNKS, d).transpose(0, 2, 1, 3).reshape(seqs, length, d)

    stream, grad = to_rows(tokens), to_rows(cotangent)
    kept = []
    for l in range(LAYERS):
        save = (True,) if l + 1 < LAYERS else ()
        normed, decay, inflow, cand, f_f, f_i, f_c, cp, ch, fin = gate_forward(
            sz, stream, gains[l], biases[l], weights[l], (True,)
        )
        if standard:
            near, beside = parts_at[l]
            diagonal = cross(after(near, fin), SECOND)
            hold = {1: [line_g1] if l + 1 < LAYERS else [near], 2: [diagonal]}
            ent, _ = enter(fin, seqs, False, (), hold)
            rest = plane_gather(pos, lines_at[l], [near, beside, diagonal])
            weights[l] = view([weights[l]["f"][0], rest])
        else:
            ent, _ = enter(fin, seqs, False)
        hidden, hb, e, mid, n2, act, slope, result = mix_forward(
            sz, stream, gains[l], decay, inflow, cp, ch, ent, weights[l], l == LAYERS - 1, save
        )
        if standard and l + 1 < LAYERS:
            own, *others = line_parts(after(packs[2 * l + 3], ent))
            line_r = line_gather(pos, [after(own, result), *others], rows[2 * l + 3 : 2 * l + 4])
            sent_g = after(line_g1, diagonal)
            parts_g = [cross(sent_g, FIRST), cross(sent_g, SECOND), swap(sent_g, BOTH, 6)]
            sent_r = after(line_r, *parts_g)
            weights.append(view([plane_gather(pos, line_g1, parts_g, (result,)), None]))
            lines_at.append(line_r)
            parts_at.append([cross(sent_r, FIRST), cross(sent_r, SECOND)])
        kept.append((stream, normed, decay, cand, f_f, f_i, f_c, hidden, hb, e, mid, n2, act, slope))
        stream = result
    output = from_rows(stream)

    vector_grads, sums, pending = [None] * LAYERS, [], []
    above = None
    for l in reversed(range(LAYERS)):
        x, normed, decay, cand, f_f, f_i, f_c, hidden, hb, e, mid, n2, act, slope = kept[l]
        place = far if l + 1 < LAYERS else lambda a: a
        decay, cand, f_f, f_i, f_c, hidden = map(far, (decay, cand, f_f, f_i, f_c, hidden))
        mid, slope = place(mid), place(slope)
        gr, gpre, gmid, go, ggain_two, gh, cp, ca, fin = mlp_backward(sz, grad, gains[l], mid, slope, decay, weights[l])

        def up(message):
            if above:
                message = above[0].step(message)
            return up_weights(sz, pos, place(after(n2, message)), gpre)

        def down(message):
            if above:
                message = above[1].step(message)
            return row_weights(sz, pos, place(after(act, message)), gr, "down_weights")

        def out(message):
            if above:
                message = above[0].step(message)
            return row_weights(sz, pos, place(after(hb, message)), go, "out_weights")

        ent, pairs = enter(fin, seqs, True, (up, down, out))
        if standard:
            mlp = Reduction(pos, [(l, m) for m in "udo"], core_exchange(pairs))
            gmid = after(gmid, mlp.seen)
        final = []
        if l == 0 and standard:
            final = [(ggain_two, 3)]
            for at in range(1, LAYERS):
                final += [(v, 4 * at + row) for v, row in zip(vector_grads[at], (0, 1, 3))]
        *gate_pair, gbias, grad, ggain_one = gate_backward(
            sz, pos, x, gains[l], gmid, gh, decay, hidden, e, cand, f_f, f_i, f_c, cp, ca, ent, far(normed), weights[l],
            l == 0, final,
        )
        vector_grads[l] = (ggain_one, gbias, ggain_two)
        if not standard:
            pending.append((l, pairs + [gate_pair]))
            continue
        if above:
            above[1].step(gate_pair[0])
            above[0].step(above[1].seen)
            mlp.step(above[0].seen)
            gate_pair[1] = after(gate_pair[1], mlp.seen)
        names = [(l, m) for m in "fic"]
        if l == 0:
            names += [(at, k) for at in range(LAYERS) for k in range(4)]
        gates = Reduction(pos, names, core_exchange([gate_pair]))
        if l > 0:
            grad, above = after(grad, gates.seen), [mlp, gates]
            continue
        gates.step(above[1].step(gates.seen))
        gates.step(above[0].total(gates.seen))
        mlp.step()
        gates.step(above[1].total(gates.seen))
        mlp.step()
        sums = [(one.names, one.parts) for one in (*above, mlp, gates)]
    grad_tokens = from_rows(grad)

    if standard:
        layout, ins = [], []
        for names, parts in sums:
            pieces = [(order[m], l, False) if m in order else (6 + m, l, True) for l, m in names]
            layout.append((len(parts), pieces))
            ins += [whole(p) for p in parts]
        found = call(
            functools.partial(finish_kernel, layout), 1, ins,
            [whole_out(m.shape) for m in matrices.values()] + [whole_out(v.shape) for v in vectors], [], 3, "finish",
        )
        g_up, g_down, g_out, g_f, g_i, g_c, g_norm, g_fb, g_ib, g_mlp = found
    else:
        per_layer = {}
        for l, pairs in pending:
            blocks = [jnp.stack([keep, send], axis=2).reshape(NS, NB, -1, LANE) for keep, send in pairs]
            gates = jnp.split(blocks[3], 3, axis=2)
            for m, g in zip("udofic", blocks[:3] + gates):
                v = unslab(g, matrices[m].shape[1] * seq_count, matrices[m].shape[2] * batch_count)
                v = lax.psum_scatter(v, "seq", scatter_dimension=0, tiled=True)
                per_layer[m, l] = lax.psum_scatter(v, "batch", scatter_dimension=1, tiled=True).astype(F32)
        g_up, g_down, g_out, g_f, g_i, g_c = [
            jnp.stack([per_layer[m, l] for l in range(LAYERS)]) for m in matrices
        ]
        rows = [
            (ggain_one[0], gbias[0], gbias[1], ggain_two[0]) for ggain_one, gbias, ggain_two in vector_grads
        ]
        g_norm, g_fb, g_ib, g_mlp = [
            lax.psum(lax.psum_scatter(jnp.stack([r[k] for r in rows]), "seq", scatter_dimension=1, tiled=True), "batch")
            for k in range(4)
        ]
    return output, grad_tokens, g_norm, g_f, g_i, g_c, g_fb, g_ib, g_out, g_mlp, g_up, g_down


def solution(mesh):
    split, vector, matrix = P("batch", "seq", None), P(None, "seq"), P(None, "seq", "batch")
    order = (vector, matrix, matrix, matrix, vector, vector, matrix, vector, matrix, matrix)
    return jax.shard_map(
        body,
        mesh=mesh,
        in_specs=(split,) + order + (split,),
        out_specs=(split, split) + order,
        check_vma=False,
    )
```

time: 336 us -> 320 us (0.952)
  Pallas kernels: 138 us -> 114 us
  waiting for transfers between devices: 98.9 us -> 110 us
  local copies, waits for them, and re-layouts: 18.7 us -> 13.4 us
    ppermute x72 -> x42, waiting for transfers between devices: 88.4 us -> 32.7 us  [swap(): return lax.ppermute(array, axes, [(i, i ^ bits) for i in range(count)])]
    ppermute x0 -> x24, waiting for transfers between devices: none -> 49.2 us  [cross(): lax.ppermute(array, BOTH, [(i, i ^ bits[i % 2]) for i in range(count)])]
    ppermute x0 -> x24, starting transfers between devices: none -> 27.3 us  [cross(): lax.ppermute(array, BOTH, [(i, i ^ bits[i % 2]) for i in range(count)])]
    pallas_call x36 -> x43, Pallas kernels: 138 us -> 114 us  [call(): pl.pallas_call(kernel, grid=(grid,), in_specs=[spec(*one) for one in ins]...]
    ppermute x72 -> x42, starting transfers between devices: 60.4 us -> 38.3 us  [swap(): return lax.ppermute(array, axes, [(i, i ^ bits) for i in range(count)])]
    ppermute x12, waiting for transfers between devices: 10.5 us -> 28.2 us  [enter(): other = lax.ppermute(message, 'seq', [(i, i ^ bit) for i in range(count)])]
    slice x6 -> x2, local copies, waits for them, and re-layouts: 5 us -> 0.03 us  [body(): parts_g0 += [swap(parts_g0[0][:2], *Y_AXIS), swap(parts_g0[1][2:], *X_AXIS)]]
    unnamed x120 -> x126, local copies, waits for them, and re-layouts: 11.2 us -> 10.8 us
  transfers between devices with their start and end apart: 84 -> 78, of which waited for: 31 -> 28; matrix products, arithmetic and copies ran while one was open for 2% -> 1% of each run, Pallas kernels for 32% -> 25%
where the time goes in v4:
time: 320 us; the launch traced here: 319 us
  Pallas kernels  114 us (36%)
  waiting for transfers between devices  110 us (34%)
  starting transfers between devices  79.9 us (25%)
  local copies, waits for them, and re-layouts  13.4 us (4%)
    pallas_call x43, Pallas kernels, call(): pl.pallas_call(kernel, grid=(grid,), in_specs=[spec(*one) for one in ins]...  114 us
    ppermute x24, waiting for transfers between devices, cross(): lax.ppermute(array, BOTH, [(i, i ^ bits[i % 2]) for i in range(count)])  49.2 us
    ppermute x42, starting transfers between devices, swap(): return lax.ppermute(array, axes, [(i, i ^ bits) for i in range(count)])  38.3 us
    ppermute x42, waiting for transfers between devices, swap(): return lax.ppermute(array, axes, [(i, i ^ bits) for i in range(count)])  32.7 us
    ppermute x12, waiting for transfers between devices, enter(): other = lax.ppermute(message, 'seq', [(i, i ^ bit) for i in range(count)])  28.2 us
    ppermute x24, starting transfers between devices, cross(): lax.ppermute(array, BOTH, [(i, i ^ bits[i % 2]) for i in range(count)])  27.3 us
    ppermute x12, starting transfers between devices, enter(): other = lax.ppermute(message, 'seq', [(i, i ^ bit) for i in range(count)])  14.3 us
    unnamed x126, local copies, waits for them, and re-layouts  10.8 us
  transfers between devices with their start and end apart: 78, of which 28 were waited for; matrix products, arithmetic and copies ran while one was open for 1% of the time, Pallas kernels for 25%

profile of v4, /device:TPU:0, one launch (start us, length us, event | category | flops | bytes accessed | tf_op | source)
XLA Modules:
  0.0 319.3 jit_solution(10949642794586271376)
XLA Ops:
  1.8 5.1 %collective-permute-start.2 = (bf16[400,128]{1,0:T(8,128)(2,1)S(1)}, bf16[400,128]{1,0:T(8,128)(2,1)S(1)}, u32[]{:S(2)}, u32[]{:S(2)}) collective-permute-start(bf16[400,128]{1,0:T(8,128)(2,1)S(1)} %get-tuple-element.179.refs_0_), channel_id=1, source_target_pairs={{0,24},{4,28},{8,16},{12,20},{16,8},{20,12},{24,0},{28,4},{1,25},{... | collective-permute-start | bytes 307208 | tf_op jit(solution)/shard_map/ppermute | solution.py:700
  10.8 4.8 %collective-permute-done.1.refs_2_ = bf16[400,128]{1,0:T(8,128)(2,1)S(1)} collective-permute-done((bf16[400,128]{1,0:T(8,128)(2,1)S(1)}, bf16[400,128]{1,0:T(8,128)(2,1)S(1)}, u32[]{:S(2)}, u32[]{:S(2)}) %collective-permute-start.1) | collective-permute-done | bytes 102432 | tf_op jit(solution)/shard_map/ppermute | solution.py:700
  31.8 4.4 %collective-permute-done.14.refs_2_ = bf16[640,128]{1,0:T(8,128)(2,1)S(1)} collective-permute-done((bf16[640,128]{1,0:T(8,128)(2,1)S(1)}, bf16[640,128]{1,0:T(8,128)(2,1)S(1)}, u32[]{:S(2)}, u32[]{:S(2)}) %collective-permute-start.14) | collective-permute-done | bytes 163872 | tf_op jit(solution)/shard_map/ppermute | solution.py:700
  44.7 6.4 %gates.2 = (bf16[512,512]{1,0:T(8,128)(2,1)}, f32[512,1024]{1,0:T(8,128)}, f32[512,1024]{1,0:T(8,128)S(1)}, f32[512,1024]{1,0:T(8,128)}, bf16[512,1024]{1,0:T(8,...) custom-call(bf16[512,512]{1,0:T(8,128)(2,1)S(1)} %bitcast.55, ...), custom_call_target="tpu_custom_call" | custom-call | flops 9900000256 | bytes 1024 | tf_op jit(solution)/shard_map/gates/pallas_call | solution.py:543
  63.8 3.7 %collective-permute-done.17.refs_2_ = bf16[384,128]{1,0:T(8,128)(2,1)S(1)} collective-permute-done((bf16[384,128]{1,0:T(8,128)(2,1)S(1)}, bf16[384,128]{1,0:T(8,128)(2,1)S(1)}, u32[]{:S(2)}, u32[]{:S(2)}) %collective-permute-start.17) | collective-permute-done | bytes 98336 | tf_op jit(solution)/shard_map/ppermute | solution.py:700
  72.0 3.7 %collective-permute-done.19 = f32[4,1024]{1,0:T(4,128)S(1)} collective-permute-done((f32[4,1024]{1,0:T(4,128)S(1)}, f32[4,1024]{1,0:T(4,128)S(1)}, u32[]{:S(2)}, u32[]{:S(2)}) %collective-permute-start.19) | collective-permute-done | bytes 16416 | tf_op jit(solution)/shard_map/ppermute | solution.py:826
  76.5 3.9 %collective-permute-done.22 = f32[4,1024]{1,0:T(4,128)S(1)} collective-permute-done((f32[4,1024]{1,0:T(4,128)S(1)}, f32[4,1024]{1,0:T(4,128)S(1)}, u32[]{:S(2)}, u32[]{:S(2)}) %collective-permute-start.22) | collective-permute-done | bytes 16416 | tf_op jit(solution)/shard_map/ppermute | solution.py:826
  89.7 8.8 %mix.2 = (f32[512,1024]{1,0:T(8,128)}, bf16[512,1024]{1,0:T(8,128)(2,1)}, f32[2,8,1024]{2,1,0:T(8,128)}, f32[512,512]{1,0:T(8,128)}, bf16[512,512]{1,0:T(8,128)(...) custom-call(bf16[512,512]{1,0:T(8,128)(2,1)S(1)} %bitcast.56, ...), custom_call_target="tpu_custom_call" | custom-call | flops 15400000512 | bytes 1024 | tf_op jit(solution)/shard_map/mix/pallas_call | solution.py:543
  102.0 4.4 %collective-permute-done.36.refs_1_ = bf16[640,128]{1,0:T(8,128)(2,1)S(1)} collective-permute-done((bf16[640,128]{1,0:T(8,128)(2,1)S(1)}, bf16[640,128]{1,0:T(8,128)(2,1)S(1)}, u32[]{:S(2)}, u32[]{:S(2)}) %collective-permute-start.36) | collective-permute-done | bytes 163872 | tf_op jit(solution)/shard_map/ppermute | solution.py:700
  114.1 6.5 %gates.3 = (bf16[512,512]{1,0:T(8,128)(2,1)}, f32[512,1024]{1,0:T(8,128)}, f32[512,1024]{1,0:T(8,128)S(1)}, f32[512,1024]{1,0:T(8,128)}, bf16[512,1024]{1,0:T(8,...) custom-call(f32[512,512]{1,0:T(8,128)S(1)} %get-tuple-element.195.x_, ...), custom_call_target="tpu_custom_call" | custom-call | flops 9900000256 | bytes 1024 | tf_op jit(solution)/shard_map/gates/pallas_call | solution.py:543
  126.6 9.1 %collective-permute-done.35 = f32[4,1024]{1,0:T(4,128)S(1)} collective-permute-done((f32[4,1024]{1,0:T(4,128)S(1)}, f32[4,1024]{1,0:T(4,128)S(1)}, u32[]{:S(2)}, u32[]{:S(2)}) %collective-permute-start.35) | collective-permute-done | bytes 16416 | tf_op jit(solution)/shard_map/ppermute | solution.py:826
  145.1 3.9 %plane_gather.7 = bf16[4,2,2,2,640,128]{5,4,3,2,1,0:T(8,128)(2,1)S(1)} custom-call(s32[8]{0:T(128)S(1)} %stack.35.pos_ref, bf16[4,640,128]{2,1,0:T(8,128)(2,1)} %copy-done.7, bf16[4,640,128]{2,1,0:T(8,128)(2,1)} %collective-permute-done.39.refs_1_, bf16[4,640,128]{2,1,0:T(8,128)(2,1)} %collective-permute-done.43.refs_2_, ...), custom_call_target="tpu_custom_call" | custom-call | flops 5500000256 | bytes 1024 | tf_op jit(solution)/shard_map/plane_gather/pallas_call | solution.py:543
  149.0 7.5 %mix.3 = (f32[512,1024]{1,0:T(8,128)}, bf16[512,1024]{1,0:T(8,128)(2,1)S(1)}, f32[2,8,1024]{2,1,0:T(8,128)S(1)}, f32[512,512]{1,0:T(8,128)S(1)}, bf16[512,512]{1...) custom-call(f32[512,512]{1,0:T(8,128)S(1)} %get-tuple-element.195.x_, ...), custom_call_target="tpu_custom_call" | custom-call | flops 15400000512 | bytes 1024 | tf_op jit(solution)/shard_map/mix/pallas_call | solution.py:543
  156.5 7.0 %mlp_back.2 = (bf16[512,512]{1,0:T(8,128)(2,1)S(1)}, bf16[512,2048]{1,0:T(8,128)(2,1)S(1)}, f32[512,512]{1,0:T(8,128)S(1)}, bf16[512,512]{1,0:T(8,128)(2,1)S(1)}...) custom-call(bf16[512,512]{1,0:T(8,128)(2,1)S(1)} %bitcast.60, ...), custom_call_target="tpu_custom_call" | custom-call | flops 13200000000 | bytes 1024 | tf_op jit(solution)/shard_map/mlp_back/pallas_call | solution.py:543
  169.0 3.5 %down_weights.2 = (bf16[8,2,256,128]{3,2,1,0:T(8,128)(2,1)S(1)}, bf16[8,2,256,128]{3,2,1,0:T(8,128)(2,1)}) custom-call(s32[8]{0:T(128)S(1)} %stack.35.pos_ref, bf16[512,2048]{1,0:T(8,128)(2,1)S(1)} %get-tuple-element.227.left_ref, bf16[512,512]{1,0:T(8,128)(2,1)S(1)} %get-tuple-element.228.right_ref), custom_call_target="tpu_custom_call" | custom-call | flops 5500000256 | bytes 1024 | tf_op jit(solution)/shard_map/down_weights/pallas_call | solution.py:543
  177.7 3.5 %collective-permute-done.53 = f32[4,1024]{1,0:T(4,128)S(1)} collective-permute-done((f32[4,1024]{1,0:T(4,128)S(1)}, f32[4,1024]{1,0:T(4,128)S(1)}, u32[]{:S(2)}, u32[]{:S(2)}) %collective-permute-start.53) | collective-permute-done | bytes 16416 | tf_op jit(solution)/shard_map/ppermute | solution.py:826
  185.3 8.4 %gate_back.2 = (bf16[8,2,384,128]{3,2,1,0:T(8,128)(2,1)S(1)}, bf16[8,2,384,128]{3,2,1,0:T(8,128)(2,1)S(1)}, f32[2,1024]{1,0:T(2,128)S(1)}, f32[512,512]{1,0:T(8,128)S(1)}, f32[1,512]{1,0:T(1,128)S(1)}) custom-call(s32[8]{0:T(128)S(1)} %stack.35.pos_ref, f32[512,512]{1,0:T(8,128)S(1)} %copy-done.26, f32[2,512]{1,0:T(2,128)S(1)} %get-tuple-element.196.gain_ref, ...), custom_call_target="tpu_custom_call" | custom-call | flops 17600000000 | bytes 1024 | tf_op jit(solution)/shard_map/gate_back/pallas_call | solution.py:543
  198.7 7.8 %mlp_back.3 = (bf16[512,512]{1,0:T(8,128)(2,1)S(1)}, bf16[512,2048]{1,0:T(8,128)(2,1)S(1)}, f32[512,512]{1,0:T(8,128)S(1)}, bf16[512,512]{1,0:T(8,128)(2,1)S(1)}...) custom-call(f32[512,512]{1,0:T(8,128)S(1)} %get-tuple-element.253.g_, ...), custom_call_target="tpu_custom_call" | custom-call | flops 13200000000 | bytes 1024 | tf_op jit(solution)/shard_map/mlp_back/pallas_call | solution.py:543
  240.7 8.9 %gate_back.3 = (bf16[8,2,400,128]{3,2,1,0:T(8,128)(2,1)S(1)}, bf16[8,2,400,128]{3,2,1,0:T(8,128)(2,1)S(1)}, f32[2,1024]{1,0:T(2,128)}, bf16[512,512]{1,0:T(8,128)(2,1)S(1)}, f32[1,512]{1,0:T(1,128)}) custom-call(s32[8]{0:T(128)S(1)} %stack.35.pos_ref, bf16[512,512]{1,0:T(8,128)(2,1)S(1)} %bitcast.57, f32[2,512]{1,0:T(2,128)S(1)} %get-tuple-element.180.gain_ref, ...), custom_call_target="tpu_custom_call" | custom-call | flops 17600000000 | bytes 1024 | tf_op jit(solution)/shard_map/gate_back/pallas_call | solution.py:543
  250.9 6.9 %collective-permute-done.66.got = bf16[4,2,640,128]{3,2,1,0:T(8,128)(2,1)S(1)} collective-permute-done((bf16[4,2,640,128]{3,2,1,0:T(8,128)(2,1)S(1)}, bf16[4,2,640,128]{3,2,1,0:T(8,128)(2,1)S(1)}, u32[]{:S(2)}, u32[]{:S(2)}) %collective-permute-start.66) | collective-permute-done | bytes 1310752 | tf_op jit(solution)/shard_map/ppermute | solution.py:727
  268.0 5.7 %collective-permute-done.68.got = bf16[2,384,128]{2,1,0:T(8,128)(2,1)S(1)} collective-permute-done((bf16[2,384,128]{2,1,0:T(8,128)(2,1)S(1)}, bf16[2,384,128]{2,1,0:T(8,128)(2,1)S(1)}, u32[]{:S(2)}, u32[]{:S(2)}) %collective-permute-start.68) | collective-permute-done | bytes 196640 | tf_op jit(solution)/shard_map/ppermute | solution.py:727
  274.3 8.8 %collective-permute-done.69.got = bf16[4,2,400,128]{3,2,1,0:T(8,128)(2,1)S(1)} collective-permute-done((bf16[4,2,400,128]{3,2,1,0:T(8,128)(2,1)S(1)}, bf16[4,2,400,128]{3,2,1,0:T(8,128)(2,1)S(1)}, u32[]{:S(2)}, u32[]{:S(2)}) %collective-permute-start.69) | collective-permute-done | bytes 819232 | tf_op jit(solution)/shard_map/ppermute | solution.py:727
  288.6 9.5 %collective-permute-done.70.got = bf16[640,128]{1,0:T(8,128)(2,1)S(1)} collective-permute-done((bf16[640,128]{1,0:T(8,128)(2,1)S(1)}, bf16[640,128]{1,0:T(8,128)(2,1)S(1)}, u32[]{:S(2)}, u32[]{:S(2)}) %collective-permute-start.70) | collective-permute-done | bytes 163872 | tf_op jit(solution)/shard_map/ppermute | solution.py:727
  305.2 4.0 %collective-permute-done.72.got = bf16[384,128]{1,0:T(8,128)(2,1)S(1)} collective-permute-done((bf16[384,128]{1,0:T(8,128)(2,1)S(1)}, bf16[384,128]{1,0:T(8,128)(2,1)S(1)}, u32[]{:S(2)}, u32[]{:S(2)}) %collective-permute-start.72) | collective-permute-done | bytes 98336 | tf_op jit(solution)/shard_map/ppermute | solution.py:727
  (329 shorter events, 171.2 us)
Async XLA Ops:
  38.9 32.4 %collective-permute-start.23 = (bf16[4,640,128]{2,1,0:T(8,128)(2,1)S(1)}, bf16[4,640,128]{2,1,0:T(8,128)(2,1)}, u32[]{:S(2)}, u32[]{:S(2)}) collective-permute-start(bf16[4,640,128]{2,1,0:T(8,128)(2,1)S(1)} %line_gather.5.refs_0_), channel_id=1, source_target_pairs={{0,4},{1,3},{2,6},{3,1},{4,0},{5,7},{6,2},{7,5},{8,12},{9,11},{10,... | collective-permute-start | bytes 1966088 | tf_op jit(solution)/shard_map/ppermute | solution.py:727
  39.5 16.3 %collective-permute-start.20 = (bf16[4,640,128]{2,1,0:T(8,128)(2,1)S(1)}, bf16[4,640,128]{2,1,0:T(8,128)(2,1)}, u32[]{:S(2)}, u32[]{:S(2)}) collective-permute-start(bf16[4,640,128]{2,1,0:T(8,128)(2,1)S(1)} %line_gather.5.refs_0_), channel_id=1, source_target_pairs={{0,2},{1,5},{2,0},{3,7},{4,6},{5,1},{6,4},{7,3},{8,10},{9,13},{10,... | collective-permute-start | bytes 1966088 | tf_op jit(solution)/shard_map/ppermute | solution.py:727
  55.8 16.0 %collective-permute-start.21 = (bf16[4,640,128]{2,1,0:T(8,128)(2,1)}, bf16[4,640,128]{2,1,0:T(8,128)(2,1)S(1)}, u32[]{:S(2)}, u32[]{:S(2)}) collective-permute-start(bf16[4,640,128]{2,1,0:T(8,128)(2,1)} %collective-permute-done.20.refs_1_), channel_id=1, source_target_pairs={{0,4},{1,3},{2,6},{3,1},{4,0},{5,7},{6,2},{7,5},{8,12},{9,11},{10,... | collective-permute-start | bytes 1966088 | tf_op jit(solution)/shard_map/ppermute | solution.py:727
  63.8 17.2 %collective-permute-start.24 = (bf16[4,640,128]{2,1,0:T(8,128)(2,1)S(1)}, bf16[4,640,128]{2,1,0:T(8,128)(2,1)}, u32[]{:S(2)}, u32[]{:S(2)}) collective-permute-start(bf16[4,640,128]{2,1,0:T(8,128)(2,1)S(1)} %line_gather.5.refs_0_), channel_id=1, source_target_pairs={{0,1},{1,0},{2,3},{3,2},{4,5},{5,4},{6,7},{7,6},{8,9},{9,8},{10,11... | collective-permute-start | bytes 1966088 | tf_op jit(solution)/shard_map/ppermute | solution.py:700
  71.8 14.4 %collective-permute-start.27 = (bf16[4,640,128]{2,1,0:T(8,128)(2,1)S(1)}, bf16[4,640,128]{2,1,0:T(8,128)(2,1)}, u32[]{:S(2)}, u32[]{:S(2)}) collective-permute-start(bf16[4,640,128]{2,1,0:T(8,128)(2,1)S(1)} %collective-permute-done.21.refs_3_), channel_id=1, source_target_pairs={{0,1},{1,0},{2,3},{3,2},{4,5},{5,4},{6,7},{7,6},{8,9},{9,8},{10,11... | collective-permute-start | bytes 1966088 | tf_op jit(solution)/shard_map/ppermute | solution.py:700
  80.5 18.1 %collective-permute-start.30 = (bf16[4,384,128]{2,1,0:T(8,128)(2,1)S(1)}, bf16[4,384,128]{2,1,0:T(8,128)(2,1)S(1)}, u32[]{:S(2)}, u32[]{:S(2)}) collective-permute-start(bf16[4,384,128]{2,1,0:T(8,128)(2,1)S(1)} %line_gather.6.refs_0_), channel_id=1, source_target_pairs={{0,6},{1,7},{2,4},{3,5},{4,2},{5,3},{6,0},{7,1},{8,14},{9,15},{10,... | collective-permute-start | bytes 1179656 | tf_op jit(solution)/shard_map/ppermute | solution.py:700
  81.0 17.9 %collective-permute-start.29 = (bf16[4,384,128]{2,1,0:T(8,128)(2,1)S(1)}, bf16[4,384,128]{2,1,0:T(8,128)(2,1)S(1)}, u32[]{:S(2)}, u32[]{:S(2)}) collective-permute-start(bf16[4,384,128]{2,1,0:T(8,128)(2,1)S(1)} %line_gather.6.refs_0_), channel_id=1, source_target_pairs={{0,4},{1,3},{2,6},{3,1},{4,0},{5,7},{6,2},{7,5},{8,12},{9,11},{10,... | collective-permute-start | bytes 1179656 | tf_op jit(solution)/shard_map/ppermute | solution.py:727
  82.6 16.3 %collective-permute-start.28 = (bf16[4,384,128]{2,1,0:T(8,128)(2,1)S(1)}, bf16[4,384,128]{2,1,0:T(8,128)(2,1)S(1)}, u32[]{:S(2)}, u32[]{:S(2)}) collective-permute-start(bf16[4,384,128]{2,1,0:T(8,128)(2,1)S(1)} %line_gather.6.refs_0_), channel_id=1, source_target_pairs={{0,2},{1,5},{2,0},{3,7},{4,6},{5,1},{6,4},{7,3},{8,10},{9,13},{10,... | collective-permute-start | bytes 1179656 | tf_op jit(solution)/shard_map/ppermute | solution.py:727
  84.1 15.5 %collective-permute-start.38 = (bf16[640,128]{1,0:T(8,128)(2,1)S(1)}, bf16[640,128]{1,0:T(8,128)(2,1)S(1)}, u32[]{:S(2)}, u32[]{:S(2)}) collective-permute-start(bf16[640,128]{1,0:T(8,128)(2,1)S(1)} %get-tuple-element.210.refs_0_), channel_id=1, source_target_pairs={{0,24},{4,28},{8,16},{12,20},{16,8},{20,12},{24,0},{28,4},{1,25},{... | collective-permute-start | bytes 491528 | tf_op jit(solution)/shard_map/ppermute | solution.py:700
  86.2 13.8 %collective-permute-start.37 = (bf16[640,128]{1,0:T(8,128)(2,1)S(1)}, bf16[640,128]{1,0:T(8,128)(2,1)S(1)}, u32[]{:S(2)}, u32[]{:S(2)}) collective-permute-start(bf16[640,128]{1,0:T(8,128)(2,1)S(1)} %get-tuple-element.210.refs_0_), channel_id=1, source_target_pairs={{0,16},{4,20},{8,24},{12,28},{16,0},{20,4},{24,8},{28,12},{1,17},{... | collective-permute-start | bytes 491528 | tf_op jit(solution)/shard_map/ppermute | solution.py:700
  108.4 27.5 %collective-permute-start.43 = (bf16[4,640,128]{2,1,0:T(8,128)(2,1)S(1)}, bf16[4,640,128]{2,1,0:T(8,128)(2,1)}, u32[]{:S(2)}, u32[]{:S(2)}) collective-permute-start(bf16[4,640,128]{2,1,0:T(8,128)(2,1)S(1)} %line_gather.7.refs_0_), channel_id=1, source_target_pairs={{0,4},{1,3},{2,6},{3,1},{4,0},{5,7},{6,2},{7,5},{8,12},{9,11},{10,... | collective-permute-start | bytes 1966088 | tf_op jit(solution)/shard_map/ppermute | solution.py:727
  108.9 15.6 %collective-permute-start.39 = (bf16[4,640,128]{2,1,0:T(8,128)(2,1)S(1)}, bf16[4,640,128]{2,1,0:T(8,128)(2,1)}, u32[]{:S(2)}, u32[]{:S(2)}) collective-permute-start(bf16[4,640,128]{2,1,0:T(8,128)(2,1)S(1)} %line_gather.7.refs_0_), channel_id=1, source_target_pairs={{0,2},{1,5},{2,0},{3,7},{4,6},{5,1},{6,4},{7,3},{8,10},{9,13},{10,... | collective-permute-start | bytes 1966088 | tf_op jit(solution)/shard_map/ppermute | solution.py:727
  126.6 18.4 %collective-permute-start.44 = (bf16[4,640,128]{2,1,0:T(8,128)(2,1)S(1)}, bf16[4,640,128]{2,1,0:T(8,128)(2,1)}, u32[]{:S(2)}, u32[]{:S(2)}) collective-permute-start(bf16[4,640,128]{2,1,0:T(8,128)(2,1)S(1)} %line_gather.7.refs_0_), channel_id=1, source_target_pairs={{0,1},{1,0},{2,3},{3,2},{4,5},{5,4},{6,7},{7,6},{8,9},{9,8},{10,11... | collective-permute-start | bytes 1966088 | tf_op jit(solution)/shard_map/ppermute | solution.py:700
  167.4 13.8 %collective-permute-start.50 = (bf16[8,2,256,128]{3,2,1,0:T(8,128)(2,1)}, bf16[8,2,256,128]{3,2,1,0:T(8,128)(2,1)S(1)}, u32[]{:S(2)}, u32[]{:S(2)}) collective-permute-start(bf16[8,2,256,128]{3,2,1,0:T(8,128)(2,1)} %get-tuple-element.225), channel_id=1, source_target_pairs={{0,1},{1,0},{2,3},{3,2},{4,5},{5,4},{6,7},{7,6},{8,9},{9,8},{10,11... | collective-permute-start | bytes 3145736 | tf_op jit(solution)/shard_map/ppermute | solution.py:700
  193.7 17.7 %collective-permute-start.55 = (bf16[4,2,640,128]{3,2,1,0:T(8,128)(2,1)S(1)}, bf16[4,2,640,128]{3,2,1,0:T(8,128)(2,1)S(1)}, u32[]{:S(2)}, u32[]{:S(2)}) collective-permute-start(bf16[4,2,640,128]{3,2,1,0:T(8,128)(2,1)S(1)} %get-tuple-element.237), channel_id=1, source_target_pairs={{0,2},{1,5},{2,0},{3,7},{4,6},{5,1},{6,4},{7,3},{8,10},{9,13},{10,... | collective-permute-start | bytes 3932168 | tf_op jit(solution)/shard_map/ppermute | solution.py:727
  198.2 22.2 %collective-permute-start.57 = (bf16[4,2,384,128]{3,2,1,0:T(8,128)(2,1)S(1)}, bf16[4,2,384,128]{3,2,1,0:T(8,128)(2,1)S(1)}, u32[]{:S(2)}, u32[]{:S(2)}) collective-permute-start(bf16[4,2,384,128]{3,2,1,0:T(8,128)(2,1)S(1)} %get-tuple-element.252), channel_id=1, source_target_pairs={{0,2},{1,5},{2,0},{3,7},{4,6},{5,1},{6,4},{7,3},{8,10},{9,13},{10,... | collective-permute-start | bytes 2359304 | tf_op jit(solution)/shard_map/ppermute | solution.py:727
  217.5 21.3 %collective-permute-start.60 = (bf16[8,2,256,128]{3,2,1,0:T(8,128)(2,1)S(1)}, bf16[8,2,256,128]{3,2,1,0:T(8,128)(2,1)S(1)}, u32[]{:S(2)}, u32[]{:S(2)}) collective-permute-start(bf16[8,2,256,128]{3,2,1,0:T(8,128)(2,1)S(1)} %get-tuple-element.267), channel_id=1, source_target_pairs={{0,1},{1,0},{2,3},{3,2},{4,5},{5,4},{6,7},{7,6},{8,9},{9,8},{10,11... | collective-permute-start | bytes 3145736 | tf_op jit(solution)/shard_map/ppermute | solution.py:700
  224.4 14.4 %collective-permute-start.61 = (bf16[8,2,256,128]{3,2,1,0:T(8,128)(2,1)S(1)}, bf16[8,2,256,128]{3,2,1,0:T(8,128)(2,1)S(1)}, u32[]{:S(2)}, u32[]{:S(2)}) collective-permute-start(bf16[8,2,256,128]{3,2,1,0:T(8,128)(2,1)S(1)} %get-tuple-element.276), channel_id=1, source_target_pairs={{0,1},{1,0},{2,3},{3,2},{4,5},{5,4},{6,7},{7,6},{8,9},{9,8},{10,11... | collective-permute-start | bytes 3145736 | tf_op jit(solution)/shard_map/ppermute | solution.py:700
  235.0 15.3 %collective-permute-start.65 = (bf16[2,640,128]{2,1,0:T(8,128)(2,1)S(1)}, bf16[2,640,128]{2,1,0:T(8,128)(2,1)S(1)}, u32[]{:S(2)}, u32[]{:S(2)}) collective-permute-start(bf16[2,640,128]{2,1,0:T(8,128)(2,1)S(1)} %get-tuple-element.279), channel_id=1, source_target_pairs={{0,8},{1,17},{2,10},{3,19},{4,12},{5,21},{6,14},{7,23},{8,0},{9,25... | collective-permute-start | bytes 983048 | tf_op jit(solution)/shard_map/ppermute | solution.py:727
  240.1 17.7 %collective-permute-start.66 = (bf16[4,2,640,128]{3,2,1,0:T(8,128)(2,1)S(1)}, bf16[4,2,640,128]{3,2,1,0:T(8,128)(2,1)S(1)}, u32[]{:S(2)}, u32[]{:S(2)}) collective-permute-start(bf16[4,2,640,128]{3,2,1,0:T(8,128)(2,1)S(1)} %get-tuple-element.284), channel_id=1, source_target_pairs={{0,2},{1,5},{2,0},{3,7},{4,6},{5,1},{6,4},{7,3},{8,10},{9,13},{10,... | collective-permute-start | bytes 3932168 | tf_op jit(solution)/shard_map/ppermute | solution.py:727
  263.6 19.4 %collective-permute-start.69 = (bf16[4,2,400,128]{3,2,1,0:T(8,128)(2,1)S(1)}, bf16[4,2,400,128]{3,2,1,0:T(8,128)(2,1)S(1)}, u32[]{:S(2)}, u32[]{:S(2)}) collective-permute-start(bf16[4,2,400,128]{3,2,1,0:T(8,128)(2,1)S(1)} %get-tuple-element.316), channel_id=1, source_target_pairs={{0,2},{1,5},{2,0},{3,7},{4,6},{5,1},{6,4},{7,3},{8,10},{9,13},{10,... | collective-permute-start | bytes 2457608 | tf_op jit(solution)/shard_map/ppermute | solution.py:727
  264.6 20.5 %collective-permute-start.73 = (bf16[4,640,128]{2,1,0:T(8,128)(2,1)S(1)}, bf16[4,640,128]{2,1,0:T(8,128)(2,1)S(1)}, u32[]{:S(2)}, u32[]{:S(2)}) collective-permute-start(bf16[4,640,128]{2,1,0:T(8,128)(2,1)S(1)} %get-tuple-element.312), channel_id=1, source_target_pairs={{0,4},{1,3},{2,6},{3,1},{4,0},{5,7},{6,2},{7,5},{8,12},{9,11},{10,... | collective-permute-start | bytes 1966088 | tf_op jit(solution)/shard_map/ppermute | solution.py:727
  283.9 14.3 %collective-permute-start.71 = (bf16[4,400,128]{2,1,0:T(8,128)(2,1)S(1)}, bf16[4,400,128]{2,1,0:T(8,128)(2,1)S(1)}, u32[]{:S(2)}, u32[]{:S(2)}) collective-permute-start(bf16[4,400,128]{2,1,0:T(8,128)(2,1)S(1)} %get-tuple-element.320), channel_id=1, source_target_pairs={{0,4},{1,3},{2,6},{3,1},{4,0},{5,7},{6,2},{7,5},{8,12},{9,11},{10,... | collective-permute-start | bytes 1228808 | tf_op jit(solution)/shard_map/ppermute | solution.py:727
  285.8 16.5 %collective-permute-start.74 = (bf16[2,640,128]{2,1,0:T(8,128)(2,1)S(1)}, bf16[2,640,128]{2,1,0:T(8,128)(2,1)S(1)}, u32[]{:S(2)}, u32[]{:S(2)}) collective-permute-start(bf16[2,640,128]{2,1,0:T(8,128)(2,1)S(1)} %get-tuple-element.329), channel_id=1, source_target_pairs={{0,8},{1,17},{2,10},{3,19},{4,12},{5,21},{6,14},{7,23},{8,0},{9,25... | collective-permute-start | bytes 983048 | tf_op jit(solution)/shard_map/ppermute | solution.py:727
  (117 other events, 1114.3 us)

commit v5 on v4

--- a/solution.py
+++ b/solution.py
@@ -419,18 +419,28 @@
         at += r
 
 
-def plane_sum_kernel(pos_ref, keep, got, send, stay):
+def plane_sum_kernel(pos_ref, *refs):
     second = pos_ref[5]
-    send[0] = add(keep[0, 1 - second], got[0, 1 - second]).astype(BF16)
-    stay[0] = add(keep[0, second], got[0, second]).astype(BF16)
-
-
-def line_sum_kernel(pos_ref, keep, got, send, stay):
+    *pairs, send, stay = refs
+    at = 0
+    for keep, got in zip(pairs[::2], pairs[1::2]):
+        rows = slice(at, at + keep.shape[2])
+        send[0, rows, :] = add(keep[0, 1 - second], got[0, 1 - second]).astype(BF16)
+        stay[0, rows, :] = add(keep[0, second], got[0, second]).astype(BF16)
+        at += keep.shape[2]
+
+
+def line_sum_kernel(pos_ref, *refs):
     core, first = pos_ref[0], pos_ref[6]
-    for v in range(2):
-        for out, f in ((send, 1 - first), (stay, first)):
-            z = jnp.where(core == 0, f + 2 * v, 2 * f + v)
-            out[v] = add(keep[z], got[z]).astype(BF16)
+    *pairs, send, stay = refs
+    at = 0
+    for keep, got in zip(pairs[::2], pairs[1::2]):
+        rows = slice(at, at + keep.shape[1])
+        for v in range(2):
+            for out, f in ((send, 1 - first), (stay, first)):
+                z = jnp.where(core == 0, f + 2 * v, 2 * f + v)
+                out[v, rows, :] = add(keep[z], got[z]).astype(BF16)
+        at += keep.shape[1]
 
 
 def last_sum_kernel(pos_ref, keep, got, send, stay):
@@ -728,12 +738,12 @@
 
 
 def pair_sum(pos, pairs):
-    rows = tuple(keep.shape[2] for keep, _ in pairs)
-    view = lambda a: by_line(a.reshape((4, 2, 2) + a.shape[2:]))
+    rows, lines = tuple(keep.shape[2] for keep, _ in pairs), pairs[0][0].shape[0] // 2
+    view = lambda a: by_line(a.reshape((lines, 2, 2) + a.shape[2:]))
     return call(
-        functools.partial(pair_sum_kernel, rows), 4,
+        functools.partial(pair_sum_kernel, rows), lines,
         [whole(pos)] + [view(keep) for keep, _ in pairs] + [view(got) for _, got in pairs],
-        [by_line_out(4, 2, sum(rows), LANE)] * 2, [], 0, "pair_sum",
+        [by_line_out(lines, 2, sum(rows), LANE)] * 2, [], 0, "pair_sum",
     )
 
 
@@ -742,14 +752,15 @@
 
 
 def plane_sum(pos, parts):
-    rows = parts[0].shape[2]
+    rows, lines = sum(part.shape[2] for part in parts[::2]), parts[0].shape[0]
     return call(
-        plane_sum_kernel, 4, [whole(pos)] + [by_line(a) for a in parts], [by_line_out(4, rows, LANE)] * 2, [], 0, "plane_sum",
+        plane_sum_kernel, lines, [whole(pos)] + [by_line(a) for a in parts], [by_line_out(lines, rows, LANE)] * 2, [], 0,
+        "plane_sum",
     )
 
 
 def line_sum(pos, parts):
-    rows = parts[0].shape[1]
+    rows = sum(part.shape[1] for part in parts[::2])
     return call(
         line_sum_kernel, 1, [whole(pos)] + [whole(a) for a in parts], [whole_out((2, rows, LANE), BF16)] * 2, [], 0, "line_sum",
     )
@@ -771,6 +782,9 @@
         self.parts = pair_sum(pos, pairs)
         self.seen = self.parts[0]
         self.parts = onward(self.parts, FIRST)
+
+    def join(self, other):
+        self.names, self.parts = self.names + other.names, self.parts + other.parts
 
     def step(self, *others):
         work, bits = SUMS[self.stage]
@@ -780,12 +794,38 @@
         self.stage, self.seen, self.parts = self.stage + 1, parts[0], onward(parts, bits)
         return self.seen
 
+    def one_more(self, others, work, bits):
+        if others:
+            self.parts[0] = after(self.parts[0], *others)
+        parts = work(self.pos, self.parts)
+        self.seen, self.parts = parts[0], onward(parts, bits)
+        return self.seen
+
     def total(self, *others):
         keep, got = self.parts
         keep = after(keep, *others)
         total = call(total_kernel, 1, [whole(keep), whole(got)], [whole_out(keep.shape)], [], 0, "total")
         self.parts = [total]
         return total
+
+
+class UprightReduction(Reduction):
+    def __init__(self, pos, names, pair):
+        self.pos, self.names, self.stage = pos, names, 0
+        self.rows = pair[0].shape[2]
+        self.parts = [part.reshape(4, 4 * self.rows, LANE) for part in pair]
+        self.one_more((), line_sum, FIRST_Z)
+
+    def step(self, *others):
+        self.stage += 1
+        if self.stage == 1:
+            return self.one_more(others, last_sum, SECOND_Z)
+        if self.stage == 2:
+            pairs = lambda pos, parts: pair_sum(pos, [tuple(part.reshape(2, 2, self.rows, LANE) for part in parts)])
+            return self.one_more(others, pairs, FIRST)
+        self.one_more(others, plane_sum, SECOND)
+        self.parts = [part[0] for part in self.parts]
+        return self.seen
 
 
 def line_parts(own):
@@ -961,22 +1001,28 @@
 
         def up(message):
             if above:
-                message = above[0].step(message)
+                message = above_up.step(message)
             return up_weights(sz, pos, place(after(n2, message)), gpre)
 
         def down(message):
             if above:
-                message = above[1].step(message)
+                message = above.step(message)
             return row_weights(sz, pos, place(after(act, message)), gr, "down_weights")
 
         def out(message):
             if above:
-                message = above[0].step(message)
+                message = above_up.step(message)
             return row_weights(sz, pos, place(after(hb, message)), go, "out_weights")
 
         ent, pairs = enter(fin, seqs, True, (up, down, out))
         if standard:
-            mlp = Reduction(pos, [(l, m) for m in "udo"], core_exchange(pairs))
+            if above:
+                pairs[2] = (after(pairs[2][0], above.step(pairs[2][0])), pairs[2][1])
+            exchanged = core_exchange(pairs)
+            if not above:
+                upright = UprightReduction(pos, [(l, "u")], exchanged[0])
+                gmid = after(gmid, upright.seen)
+            mlp = Reduction(pos, [(l, "d"), (l, "o")], exchanged[1:])
             gmid = after(gmid, mlp.seen)
         final = []
         if l == 0 and standard:
@@ -992,23 +1038,23 @@
             pending.append((l, pairs + [gate_pair]))
             continue
         if above:
-            above[1].step(gate_pair[0])
-            above[0].step(above[1].seen)
-            mlp.step(above[0].seen)
-            gate_pair[1] = after(gate_pair[1], mlp.seen)
+            mlp.step(above_up.step(above.step(gate_pair[0])))
+            upright = UprightReduction(pos, [(l, "u")], (after(exchanged[0][0], mlp.seen), exchanged[0][1]))
+            gate_pair[1] = after(gate_pair[1], upright.seen)
         names = [(l, m) for m in "fic"]
         if l == 0:
             names += [(at, k) for at in range(LAYERS) for k in range(4)]
         gates = Reduction(pos, names, core_exchange([gate_pair]))
         if l > 0:
-            grad, above = after(grad, gates.seen), [mlp, gates]
+            grad, above, above_up = after(grad, gates.seen), mlp, upright
+            above.join(gates)
             continue
-        gates.step(above[1].step(gates.seen))
-        gates.step(above[0].total(gates.seen))
-        mlp.step()
-        gates.step(above[1].total(gates.seen))
-        mlp.step()
-        sums = [(one.names, one.parts) for one in (*above, mlp, gates)]
+        gates.step()
+        upright.step(above.total(gates.seen))
+        mlp.join(gates)
+        mlp.step(upright.step(above_up.total(upright.seen)))
+        mlp.step(upright.step(mlp.seen))
+        sums = [(one.names, one.parts) for one in (above, above_up, mlp, upright)]
     grad_tokens = from_rows(grad)
 
     if standard:

time: 320 us -> 311 us (0.972)
  waiting for transfers between devices: 110 us -> 94.3 us
  starting transfers between devices: 79.9 us -> 84.6 us
    ppermute x24 -> x27, waiting for transfers between devices: 49.2 us -> 32 us  [cross(): lax.ppermute(array, BOTH, [(i, i ^ bits[i % 2]) for i in range(count)])]
    ppermute x24 -> x27, starting transfers between devices: 27.3 us -> 38 us  [cross(): lax.ppermute(array, BOTH, [(i, i ^ bits[i % 2]) for i in range(count)])]
    ppermute x42, starting transfers between devices: 38.3 us -> 32.3 us  [swap(): return lax.ppermute(array, axes, [(i, i ^ bits) for i in range(count)])]
    pallas_call x43 -> x46, Pallas kernels: 114 us -> 115 us  [call(): pl.pallas_call(kernel, grid=(grid,), in_specs=[spec(*one) for one in ins]...]
  transfers between devices with their start and end apart: 78 -> 81, of which waited for: 28 -> 31; matrix products, arithmetic and copies ran while one was open for 1% -> 1% of each run, Pallas kernels for 25% -> 26%
where the time goes in v5:
time: 311 us; the launch traced here: 309 us
  Pallas kernels  115 us (37%)
  waiting for transfers between devices  94.3 us (30%)
  starting transfers between devices  84.6 us (27%)
  local copies, waits for them, and re-layouts  12.3 us (4%)
    pallas_call x46, Pallas kernels, call(): pl.pallas_call(kernel, grid=(grid,), in_specs=[spec(*one) for one in ins]...  115 us
    ppermute x27, starting transfers between devices, cross(): lax.ppermute(array, BOTH, [(i, i ^ bits[i % 2]) for i in range(count)])  38 us
    ppermute x42, waiting for transfers between devices, swap(): return lax.ppermute(array, axes, [(i, i ^ bits) for i in range(count)])  32.7 us
    ppermute x42, starting transfers between devices, swap(): return lax.ppermute(array, axes, [(i, i ^ bits) for i in range(count)])  32.3 us
    ppermute x27, waiting for transfers between devices, cross(): lax.ppermute(array, BOTH, [(i, i ^ bits[i % 2]) for i in range(count)])  32 us
    ppermute x12, waiting for transfers between devices, enter(): other = lax.ppermute(message, 'seq', [(i, i ^ bit) for i in range(count)])  29.7 us
    ppermute x12, starting transfers between devices, enter(): other = lax.ppermute(message, 'seq', [(i, i ^ bit) for i in range(count)])  14.3 us
    unnamed x126, local copies, waits for them, and re-layouts  9.69 us
  transfers between devices with their start and end apart: 81, of which 31 were waited for; matrix products, arithmetic and copies ran while one was open for 1% of the time, Pallas kernels for 26%

profile of v5, /device:TPU:0, one launch (start us, length us, event | category | flops | bytes accessed | tf_op | source)
XLA Modules:
  0.0 308.6 jit_solution(12407224002869161894)
XLA Ops:
  1.8 5.1 %collective-permute-start.2 = (bf16[400,128]{1,0:T(8,128)(2,1)S(1)}, bf16[400,128]{1,0:T(8,128)(2,1)S(1)}, u32[]{:S(2)}, u32[]{:S(2)}) collective-permute-start(bf16[400,128]{1,0:T(8,128)(2,1)S(1)} %get-tuple-element.190.refs_0_), channel_id=1, source_target_pairs={{0,24},{4,28},{8,16},{12,20},{16,8},{20,12},{24,0},{28,4},{1,25},{... | collective-permute-start | bytes 307208 | tf_op jit(solution)/shard_map/ppermute | solution.py:710
  10.8 4.8 %collective-permute-done.1.refs_2_ = bf16[400,128]{1,0:T(8,128)(2,1)S(1)} collective-permute-done((bf16[400,128]{1,0:T(8,128)(2,1)S(1)}, bf16[400,128]{1,0:T(8,128)(2,1)S(1)}, u32[]{:S(2)}, u32[]{:S(2)}) %collective-permute-start.1) | collective-permute-done | bytes 102432 | tf_op jit(solution)/shard_map/ppermute | solution.py:710
  31.8 4.4 %collective-permute-done.14.refs_2_ = bf16[640,128]{1,0:T(8,128)(2,1)S(1)} collective-permute-done((bf16[640,128]{1,0:T(8,128)(2,1)S(1)}, bf16[640,128]{1,0:T(8,128)(2,1)S(1)}, u32[]{:S(2)}, u32[]{:S(2)}) %collective-permute-start.14) | collective-permute-done | bytes 163872 | tf_op jit(solution)/shard_map/ppermute | solution.py:710
  44.7 6.4 %gates.2 = (bf16[512,512]{1,0:T(8,128)(2,1)}, f32[512,1024]{1,0:T(8,128)}, f32[512,1024]{1,0:T(8,128)S(1)}, f32[512,1024]{1,0:T(8,128)}, bf16[512,1024]{1,0:T(8,...) custom-call(bf16[512,512]{1,0:T(8,128)(2,1)S(1)} %bitcast.63, ...), custom_call_target="tpu_custom_call" | custom-call | flops 9900000256 | bytes 1024 | tf_op jit(solution)/shard_map/gates/pallas_call | solution.py:553
  63.8 3.7 %collective-permute-done.17.refs_2_ = bf16[384,128]{1,0:T(8,128)(2,1)S(1)} collective-permute-done((bf16[384,128]{1,0:T(8,128)(2,1)S(1)}, bf16[384,128]{1,0:T(8,128)(2,1)S(1)}, u32[]{:S(2)}, u32[]{:S(2)}) %collective-permute-start.17) | collective-permute-done | bytes 98336 | tf_op jit(solution)/shard_map/ppermute | solution.py:710
  72.0 3.7 %collective-permute-done.19 = f32[4,1024]{1,0:T(4,128)S(1)} collective-permute-done((f32[4,1024]{1,0:T(4,128)S(1)}, f32[4,1024]{1,0:T(4,128)S(1)}, u32[]{:S(2)}, u32[]{:S(2)}) %collective-permute-start.19) | collective-permute-done | bytes 16416 | tf_op jit(solution)/shard_map/ppermute | solution.py:866
  76.5 3.9 %collective-permute-done.22 = f32[4,1024]{1,0:T(4,128)S(1)} collective-permute-done((f32[4,1024]{1,0:T(4,128)S(1)}, f32[4,1024]{1,0:T(4,128)S(1)}, u32[]{:S(2)}, u32[]{:S(2)}) %collective-permute-start.22) | collective-permute-done | bytes 16416 | tf_op jit(solution)/shard_map/ppermute | solution.py:866
  89.7 8.8 %mix.2 = (f32[512,1024]{1,0:T(8,128)}, bf16[512,1024]{1,0:T(8,128)(2,1)}, f32[2,8,1024]{2,1,0:T(8,128)}, f32[512,512]{1,0:T(8,128)}, bf16[512,512]{1,0:T(8,128)(...) custom-call(bf16[512,512]{1,0:T(8,128)(2,1)S(1)} %bitcast.64, ...), custom_call_target="tpu_custom_call" | custom-call | flops 15400000512 | bytes 1024 | tf_op jit(solution)/shard_map/mix/pallas_call | solution.py:553
  102.0 4.4 %collective-permute-done.36.refs_1_ = bf16[640,128]{1,0:T(8,128)(2,1)S(1)} collective-permute-done((bf16[640,128]{1,0:T(8,128)(2,1)S(1)}, bf16[640,128]{1,0:T(8,128)(2,1)S(1)}, u32[]{:S(2)}, u32[]{:S(2)}) %collective-permute-start.36) | collective-permute-done | bytes 163872 | tf_op jit(solution)/shard_map/ppermute | solution.py:710
  114.0 6.5 %gates.3 = (bf16[512,512]{1,0:T(8,128)(2,1)}, f32[512,1024]{1,0:T(8,128)}, f32[512,1024]{1,0:T(8,128)S(1)}, f32[512,1024]{1,0:T(8,128)}, bf16[512,1024]{1,0:T(8,...) custom-call(f32[512,512]{1,0:T(8,128)S(1)} %get-tuple-element.206.x_, ...), custom_call_target="tpu_custom_call" | custom-call | flops 9900000256 | bytes 1024 | tf_op jit(solution)/shard_map/gates/pallas_call | solution.py:553
  126.5 9.1 %collective-permute-done.35 = f32[4,1024]{1,0:T(4,128)S(1)} collective-permute-done((f32[4,1024]{1,0:T(4,128)S(1)}, f32[4,1024]{1,0:T(4,128)S(1)}, u32[]{:S(2)}, u32[]{:S(2)}) %collective-permute-start.35) | collective-permute-done | bytes 16416 | tf_op jit(solution)/shard_map/ppermute | solution.py:866
  145.0 3.9 %plane_gather.7 = bf16[4,2,2,2,640,128]{5,4,3,2,1,0:T(8,128)(2,1)S(1)} custom-call(s32[8]{0:T(128)S(1)} %stack.35.pos_ref, bf16[4,640,128]{2,1,0:T(8,128)(2,1)} %copy-done.7, bf16[4,640,128]{2,1,0:T(8,128)(2,1)} %collective-permute-done.39.refs_1_, bf16[4,640,128]{2,1,0:T(8,128)(2,1)} %collective-permute-done.43.refs_2_, ...), custom_call_target="tpu_custom_call" | custom-call | flops 5500000256 | bytes 1024 | tf_op jit(solution)/shard_map/plane_gather/pallas_call | solution.py:553
  148.9 7.5 %mix.3 = (f32[512,1024]{1,0:T(8,128)}, bf16[512,1024]{1,0:T(8,128)(2,1)S(1)}, f32[2,8,1024]{2,1,0:T(8,128)S(1)}, f32[512,512]{1,0:T(8,128)S(1)}, bf16[512,512]{1...) custom-call(f32[512,512]{1,0:T(8,128)S(1)} %get-tuple-element.206.x_, ...), custom_call_target="tpu_custom_call" | custom-call | flops 15400000512 | bytes 1024 | tf_op jit(solution)/shard_map/mix/pallas_call | solution.py:553
  156.4 7.0 %mlp_back.2 = (bf16[512,512]{1,0:T(8,128)(2,1)S(1)}, bf16[512,2048]{1,0:T(8,128)(2,1)S(1)}, f32[512,512]{1,0:T(8,128)S(1)}, bf16[512,512]{1,0:T(8,128)(2,1)S(1)}...) custom-call(bf16[512,512]{1,0:T(8,128)(2,1)S(1)} %bitcast.68, ...), custom_call_target="tpu_custom_call" | custom-call | flops 13200000000 | bytes 1024 | tf_op jit(solution)/shard_map/mlp_back/pallas_call | solution.py:553
  169.1 3.5 %down_weights.2 = (bf16[8,2,256,128]{3,2,1,0:T(8,128)(2,1)S(1)}, bf16[8,2,256,128]{3,2,1,0:T(8,128)(2,1)}) custom-call(s32[8]{0:T(128)S(1)} %stack.35.pos_ref, bf16[512,2048]{1,0:T(8,128)(2,1)S(1)} %get-tuple-element.240.left_ref, bf16[512,512]{1,0:T(8,128)(2,1)S(1)} %get-tuple-element.241.right_ref), custom_call_target="tpu_custom_call" | custom-call | flops 5500000256 | bytes 1024 | tf_op jit(solution)/shard_map/down_weights/pallas_call | solution.py:553
  177.6 3.6 %collective-permute-done.53 = f32[4,1024]{1,0:T(4,128)S(1)} collective-permute-done((f32[4,1024]{1,0:T(4,128)S(1)}, f32[4,1024]{1,0:T(4,128)S(1)}, u32[]{:S(2)}, u32[]{:S(2)}) %collective-permute-start.53) | collective-permute-done | bytes 16416 | tf_op jit(solution)/shard_map/ppermute | solution.py:866
  184.7 8.3 %gate_back.2 = (bf16[8,2,384,128]{3,2,1,0:T(8,128)(2,1)S(1)}, bf16[8,2,384,128]{3,2,1,0:T(8,128)(2,1)S(1)}, f32[2,1024]{1,0:T(2,128)S(1)}, f32[512,512]{1,0:T(8,128)S(1)}, f32[1,512]{1,0:T(1,128)S(1)}) custom-call(s32[8]{0:T(128)S(1)} %stack.35.pos_ref, f32[512,512]{1,0:T(8,128)S(1)} %copy-done.26, f32[2,512]{1,0:T(2,128)S(1)} %get-tuple-element.207.gain_ref, ...), custom_call_target="tpu_custom_call" | custom-call | flops 17600000000 | bytes 1024 | tf_op jit(solution)/shard_map/gate_back/pallas_call | solution.py:553
  198.0 7.7 %mlp_back.3 = (bf16[512,512]{1,0:T(8,128)(2,1)S(1)}, bf16[512,2048]{1,0:T(8,128)(2,1)S(1)}, f32[512,512]{1,0:T(8,128)S(1)}, bf16[512,512]{1,0:T(8,128)(2,1)S(1)}...) custom-call(f32[512,512]{1,0:T(8,128)S(1)} %get-tuple-element.266.g_, ...), custom_call_target="tpu_custom_call" | custom-call | flops 13200000000 | bytes 1024 | tf_op jit(solution)/shard_map/mlp_back/pallas_call | solution.py:553
  238.0 9.0 %gate_back.3 = (bf16[8,2,400,128]{3,2,1,0:T(8,128)(2,1)S(1)}, bf16[8,2,400,128]{3,2,1,0:T(8,128)(2,1)S(1)}, f32[2,1024]{1,0:T(2,128)}, bf16[512,512]{1,0:T(8,128)(2,1)S(1)}, f32[1,512]{1,0:T(1,128)}) custom-call(s32[8]{0:T(128)S(1)} %stack.35.pos_ref, bf16[512,512]{1,0:T(8,128)(2,1)S(1)} %bitcast.65, f32[2,512]{1,0:T(2,128)S(1)} %get-tuple-element.191.gain_ref, ...), custom_call_target="tpu_custom_call" | custom-call | flops 17600000000 | bytes 1024 | tf_op jit(solution)/shard_map/gate_back/pallas_call | solution.py:553
  251.7 3.5 %collective-permute-done.69 = bf16[8,2,400,128]{3,2,1,0:T(8,128)(2,1)S(1)} collective-permute-done((bf16[8,2,400,128]{3,2,1,0:T(8,128)(2,1)S(1)}, bf16[8,2,400,128]{3,2,1,0:T(8,128)(2,1)S(1)}, u32[]{:S(2)}, u32[]{:S(2)}) %collective-permute-start.69) | collective-permute-done | bytes 1638432 | tf_op jit(solution)/shard_map/ppermute | solution.py:710
  259.0 9.6 %collective-permute-done.70.refs_1_ = bf16[4,2,400,128]{3,2,1,0:T(8,128)(2,1)S(1)} collective-permute-done((bf16[4,2,400,128]{3,2,1,0:T(8,128)(2,1)S(1)}, bf16[4,2,400,128]{3,2,1,0:T(8,128)(2,1)S(1)}, u32[]{:S(2)}, u32[]{:S(2)}) %collective-permute-start.70) | collective-permute-done | bytes 819232 | tf_op jit(solution)/shard_map/ppermute | solution.py:737
  276.3 3.5 %collective-permute-start.73 = (bf16[1,256,128]{2,1,0:T(8,128)(2,1)S(1)}, bf16[1,256,128]{2,1,0:T(8,128)(2,1)S(1)}, u32[]{:S(2)}, u32[]{:S(2)}) collective-permute-start(bf16[1,256,128]{2,1,0:T(8,128)(2,1)S(1)} %get-tuple-element.328), channel_id=1, source_target_pairs={{0,4},{1,3},{2,6},{3,1},{4,0},{5,7},{6,2},{7,5},{8,12},{9,11},{10,... | collective-permute-start | bytes 196616 | tf_op jit(solution)/shard_map/ppermute | solution.py:737
  284.0 4.2 %collective-permute-start.78 = (bf16[2,784,128]{2,1,0:T(8,128)(2,1)S(1)}, bf16[2,784,128]{2,1,0:T(8,128)(2,1)S(1)}, u32[]{:S(2)}, u32[]{:S(2)}) collective-permute-start(bf16[2,784,128]{2,1,0:T(8,128)(2,1)S(1)} %get-tuple-element.351), channel_id=1, source_target_pairs={{0,8},{1,17},{2,10},{3,19},{4,12},{5,21},{6,14},{7,23},{8,0},{9,25... | collective-permute-start | bytes 1204232 | tf_op jit(solution)/shard_map/ppermute | solution.py:737
  299.8 5.5 %collective-permute-start.80 = (bf16[1,256,128]{2,1,0:T(8,128)(2,1)S(1)}, bf16[1,256,128]{2,1,0:T(8,128)(2,1)S(1)}, u32[]{:S(2)}, u32[]{:S(2)}) collective-permute-start(bf16[1,256,128]{2,1,0:T(8,128)(2,1)S(1)} %get-tuple-element.353), channel_id=1, source_target_pairs={{0,4},{1,3},{2,6},{3,1},{4,0},{5,7},{6,2},{7,5},{8,12},{9,11},{10,... | collective-permute-start | bytes 196616 | tf_op jit(solution)/shard_map/ppermute | solution.py:737
  (338 shorter events, 169.0 us)
Async XLA Ops:
  38.9 32.4 %collective-permute-start.23 = (bf16[4,640,128]{2,1,0:T(8,128)(2,1)S(1)}, bf16[4,640,128]{2,1,0:T(8,128)(2,1)}, u32[]{:S(2)}, u32[]{:S(2)}) collective-permute-start(bf16[4,640,128]{2,1,0:T(8,128)(2,1)S(1)} %line_gather.5.refs_0_), channel_id=1, source_target_pairs={{0,4},{1,3},{2,6},{3,1},{4,0},{5,7},{6,2},{7,5},{8,12},{9,11},{10,... | collective-permute-start | bytes 1966088 | tf_op jit(solution)/shard_map/ppermute | solution.py:737
  39.5 16.3 %collective-permute-start.20 = (bf16[4,640,128]{2,1,0:T(8,128)(2,1)S(1)}, bf16[4,640,128]{2,1,0:T(8,128)(2,1)}, u32[]{:S(2)}, u32[]{:S(2)}) collective-permute-start(bf16[4,640,128]{2,1,0:T(8,128)(2,1)S(1)} %line_gather.5.refs_0_), channel_id=1, source_target_pairs={{0,2},{1,5},{2,0},{3,7},{4,6},{5,1},{6,4},{7,3},{8,10},{9,13},{10,... | collective-permute-start | bytes 1966088 | tf_op jit(solution)/shard_map/ppermute | solution.py:737
  55.8 16.0 %collective-permute-start.21 = (bf16[4,640,128]{2,1,0:T(8,128)(2,1)}, bf16[4,640,128]{2,1,0:T(8,128)(2,1)S(1)}, u32[]{:S(2)}, u32[]{:S(2)}) collective-permute-start(bf16[4,640,128]{2,1,0:T(8,128)(2,1)} %collective-permute-done.20.refs_1_), channel_id=1, source_target_pairs={{0,4},{1,3},{2,6},{3,1},{4,0},{5,7},{6,2},{7,5},{8,12},{9,11},{10,... | collective-permute-start | bytes 1966088 | tf_op jit(solution)/shard_map/ppermute | solution.py:737
  63.8 17.2 %collective-permute-start.24 = (bf16[4,640,128]{2,1,0:T(8,128)(2,1)S(1)}, bf16[4,640,128]{2,1,0:T(8,128)(2,1)}, u32[]{:S(2)}, u32[]{:S(2)}) collective-permute-start(bf16[4,640,128]{2,1,0:T(8,128)(2,1)S(1)} %line_gather.5.refs_0_), channel_id=1, source_target_pairs={{0,1},{1,0},{2,3},{3,2},{4,5},{5,4},{6,7},{7,6},{8,9},{9,8},{10,11... | collective-permute-start | bytes 1966088 | tf_op jit(solution)/shard_map/ppermute | solution.py:710
  71.8 14.4 %collective-permute-start.27 = (bf16[4,640,128]{2,1,0:T(8,128)(2,1)S(1)}, bf16[4,640,128]{2,1,0:T(8,128)(2,1)}, u32[]{:S(2)}, u32[]{:S(2)}) collective-permute-start(bf16[4,640,128]{2,1,0:T(8,128)(2,1)S(1)} %collective-permute-done.21.refs_3_), channel_id=1, source_target_pairs={{0,1},{1,0},{2,3},{3,2},{4,5},{5,4},{6,7},{7,6},{8,9},{9,8},{10,11... | collective-permute-start | bytes 1966088 | tf_op jit(solution)/shard_map/ppermute | solution.py:710
  80.5 18.1 %collective-permute-start.30 = (bf16[4,384,128]{2,1,0:T(8,128)(2,1)S(1)}, bf16[4,384,128]{2,1,0:T(8,128)(2,1)S(1)}, u32[]{:S(2)}, u32[]{:S(2)}) collective-permute-start(bf16[4,384,128]{2,1,0:T(8,128)(2,1)S(1)} %line_gather.6.refs_0_), channel_id=1, source_target_pairs={{0,6},{1,7},{2,4},{3,5},{4,2},{5,3},{6,0},{7,1},{8,14},{9,15},{10,... | collective-permute-start | bytes 1179656 | tf_op jit(solution)/shard_map/ppermute | solution.py:710
  81.0 17.9 %collective-permute-start.29 = (bf16[4,384,128]{2,1,0:T(8,128)(2,1)S(1)}, bf16[4,384,128]{2,1,0:T(8,128)(2,1)S(1)}, u32[]{:S(2)}, u32[]{:S(2)}) collective-permute-start(bf16[4,384,128]{2,1,0:T(8,128)(2,1)S(1)} %line_gather.6.refs_0_), channel_id=1, source_target_pairs={{0,4},{1,3},{2,6},{3,1},{4,0},{5,7},{6,2},{7,5},{8,12},{9,11},{10,... | collective-permute-start | bytes 1179656 | tf_op jit(solution)/shard_map/ppermute | solution.py:737
  82.6 16.3 %collective-permute-start.28 = (bf16[4,384,128]{2,1,0:T(8,128)(2,1)S(1)}, bf16[4,384,128]{2,1,0:T(8,128)(2,1)S(1)}, u32[]{:S(2)}, u32[]{:S(2)}) collective-permute-start(bf16[4,384,128]{2,1,0:T(8,128)(2,1)S(1)} %line_gather.6.refs_0_), channel_id=1, source_target_pairs={{0,2},{1,5},{2,0},{3,7},{4,6},{5,1},{6,4},{7,3},{8,10},{9,13},{10,... | collective-permute-start | bytes 1179656 | tf_op jit(solution)/shard_map/ppermute | solution.py:737
  84.1 15.5 %collective-permute-start.38 = (bf16[640,128]{1,0:T(8,128)(2,1)S(1)}, bf16[640,128]{1,0:T(8,128)(2,1)S(1)}, u32[]{:S(2)}, u32[]{:S(2)}) collective-permute-start(bf16[640,128]{1,0:T(8,128)(2,1)S(1)} %get-tuple-element.221.refs_0_), channel_id=1, source_target_pairs={{0,24},{4,28},{8,16},{12,20},{16,8},{20,12},{24,0},{28,4},{1,25},{... | collective-permute-start | bytes 491528 | tf_op jit(solution)/shard_map/ppermute | solution.py:710
  86.2 13.8 %collective-permute-start.37 = (bf16[640,128]{1,0:T(8,128)(2,1)S(1)}, bf16[640,128]{1,0:T(8,128)(2,1)S(1)}, u32[]{:S(2)}, u32[]{:S(2)}) collective-permute-start(bf16[640,128]{1,0:T(8,128)(2,1)S(1)} %get-tuple-element.221.refs_0_), channel_id=1, source_target_pairs={{0,16},{4,20},{8,24},{12,28},{16,0},{20,4},{24,8},{28,12},{1,17},{... | collective-permute-start | bytes 491528 | tf_op jit(solution)/shard_map/ppermute | solution.py:710
  108.3 27.4 %collective-permute-start.43 = (bf16[4,640,128]{2,1,0:T(8,128)(2,1)S(1)}, bf16[4,640,128]{2,1,0:T(8,128)(2,1)}, u32[]{:S(2)}, u32[]{:S(2)}) collective-permute-start(bf16[4,640,128]{2,1,0:T(8,128)(2,1)S(1)} %line_gather.7.refs_0_), channel_id=1, source_target_pairs={{0,4},{1,3},{2,6},{3,1},{4,0},{5,7},{6,2},{7,5},{8,12},{9,11},{10,... | collective-permute-start | bytes 1966088 | tf_op jit(solution)/shard_map/ppermute | solution.py:737
  108.9 15.6 %collective-permute-start.39 = (bf16[4,640,128]{2,1,0:T(8,128)(2,1)S(1)}, bf16[4,640,128]{2,1,0:T(8,128)(2,1)}, u32[]{:S(2)}, u32[]{:S(2)}) collective-permute-start(bf16[4,640,128]{2,1,0:T(8,128)(2,1)S(1)} %line_gather.7.refs_0_), channel_id=1, source_target_pairs={{0,2},{1,5},{2,0},{3,7},{4,6},{5,1},{6,4},{7,3},{8,10},{9,13},{10,... | collective-permute-start | bytes 1966088 | tf_op jit(solution)/shard_map/ppermute | solution.py:737
  126.5 18.4 %collective-permute-start.44 = (bf16[4,640,128]{2,1,0:T(8,128)(2,1)S(1)}, bf16[4,640,128]{2,1,0:T(8,128)(2,1)}, u32[]{:S(2)}, u32[]{:S(2)}) collective-permute-start(bf16[4,640,128]{2,1,0:T(8,128)(2,1)S(1)} %line_gather.7.refs_0_), channel_id=1, source_target_pairs={{0,1},{1,0},{2,3},{3,2},{4,5},{5,4},{6,7},{7,6},{8,9},{9,8},{10,11... | collective-permute-start | bytes 1966088 | tf_op jit(solution)/shard_map/ppermute | solution.py:710
  167.4 13.8 %collective-permute-start.48 = (bf16[8,2,256,128]{3,2,1,0:T(8,128)(2,1)}, bf16[8,2,256,128]{3,2,1,0:T(8,128)(2,1)S(1)}, u32[]{:S(2)}, u32[]{:S(2)}) collective-permute-start(bf16[8,2,256,128]{3,2,1,0:T(8,128)(2,1)} %get-tuple-element.235), channel_id=1, source_target_pairs={{0,1},{1,0},{2,3},{3,2},{4,5},{5,4},{6,7},{7,6},{8,9},{9,8},{10,11... | collective-permute-start | bytes 3145736 | tf_op jit(solution)/shard_map/ppermute | solution.py:710
  193.1 14.3 %collective-permute-start.56 = (bf16[2,1024,128]{2,1,0:T(8,128)(2,1)S(1)}, bf16[2,1024,128]{2,1,0:T(8,128)(2,1)S(1)}, u32[]{:S(2)}, u32[]{:S(2)}) collective-permute-start(bf16[2,1024,128]{2,1,0:T(8,128)(2,1)S(1)} %get-tuple-element.236), channel_id=1, source_target_pairs={{0,8},{1,17},{2,10},{3,19},{4,12},{5,21},{6,14},{7,23},{8,0},{9,25... | collective-permute-start | bytes 1572872 | tf_op jit(solution)/shard_map/ppermute | solution.py:737
  193.5 21.4 %collective-permute-start.57 = (bf16[4,2,384,128]{3,2,1,0:T(8,128)(2,1)S(1)}, bf16[4,2,384,128]{3,2,1,0:T(8,128)(2,1)S(1)}, u32[]{:S(2)}, u32[]{:S(2)}) collective-permute-start(bf16[4,2,384,128]{3,2,1,0:T(8,128)(2,1)S(1)} %get-tuple-element.250), channel_id=1, source_target_pairs={{0,2},{1,5},{2,0},{3,7},{4,6},{5,1},{6,4},{7,3},{8,10},{9,13},{10,... | collective-permute-start | bytes 2359304 | tf_op jit(solution)/shard_map/ppermute | solution.py:737
  197.5 17.4 %collective-permute-start.58 = (bf16[4,2,384,128]{3,2,1,0:T(8,128)(2,1)S(1)}, bf16[4,2,384,128]{3,2,1,0:T(8,128)(2,1)S(1)}, u32[]{:S(2)}, u32[]{:S(2)}) collective-permute-start(bf16[4,2,384,128]{3,2,1,0:T(8,128)(2,1)S(1)} %get-tuple-element.265), channel_id=1, source_target_pairs={{0,2},{1,5},{2,0},{3,7},{4,6},{5,1},{6,4},{7,3},{8,10},{9,13},{10,... | collective-permute-start | bytes 2359304 | tf_op jit(solution)/shard_map/ppermute | solution.py:737
  219.2 17.8 %collective-permute-start.62 = (bf16[8,2,256,128]{3,2,1,0:T(8,128)(2,1)S(1)}, bf16[8,2,256,128]{3,2,1,0:T(8,128)(2,1)S(1)}, u32[]{:S(2)}, u32[]{:S(2)}) collective-permute-start(bf16[8,2,256,128]{3,2,1,0:T(8,128)(2,1)S(1)} %get-tuple-element.290), channel_id=1, source_target_pairs={{0,1},{1,0},{2,3},{3,2},{4,5},{5,4},{6,7},{7,6},{8,9},{9,8},{10,11... | collective-permute-start | bytes 3145736 | tf_op jit(solution)/shard_map/ppermute | solution.py:710
  228.2 22.6 %collective-permute-start.68 = (bf16[8,2,256,128]{3,2,1,0:T(8,128)(2,1)S(1)}, bf16[8,2,256,128]{3,2,1,0:T(8,128)(2,1)S(1)}, u32[]{:S(2)}, u32[]{:S(2)}) collective-permute-start(bf16[8,2,256,128]{3,2,1,0:T(8,128)(2,1)S(1)} %get-tuple-element.280), channel_id=1, source_target_pairs={{0,1},{1,0},{2,3},{3,2},{4,5},{5,4},{6,7},{7,6},{8,9},{9,8},{10,11... | collective-permute-start | bytes 3145736 | tf_op jit(solution)/shard_map/ppermute | solution.py:710
  231.1 16.6 %collective-permute-start.66 = (bf16[1,2,256,128]{3,2,1,0:T(8,128)(2,1)S(1)}, bf16[1,2,256,128]{3,2,1,0:T(8,128)(2,1)S(1)}, u32[]{:S(2)}, u32[]{:S(2)}) collective-permute-start(bf16[1,2,256,128]{3,2,1,0:T(8,128)(2,1)S(1)} %get-tuple-element.293), channel_id=1, source_target_pairs={{0,2},{1,5},{2,0},{3,7},{4,6},{5,1},{6,4},{7,3},{8,10},{9,13},{10,... | collective-permute-start | bytes 393224 | tf_op jit(solution)/shard_map/ppermute | solution.py:737
  256.6 16.3 %collective-permute-start.72 = (bf16[2,1024,128]{2,1,0:T(8,128)(2,1)S(1)}, bf16[2,1024,128]{2,1,0:T(8,128)(2,1)S(1)}, u32[]{:S(2)}, u32[]{:S(2)}) collective-permute-start(bf16[2,1024,128]{2,1,0:T(8,128)(2,1)S(1)} %get-tuple-element.332), channel_id=1, source_target_pairs={{0,8},{1,17},{2,10},{3,19},{4,12},{5,21},{6,14},{7,23},{8,0},{9,25... | collective-permute-start | bytes 1572872 | tf_op jit(solution)/shard_map/ppermute | solution.py:737
  257.2 14.9 %collective-permute-start.71 = (bf16[768,128]{1,0:T(8,128)(2,1)S(1)}, bf16[768,128]{1,0:T(8,128)(2,1)S(1)}, u32[]{:S(2)}, u32[]{:S(2)}) collective-permute-start(bf16[768,128]{1,0:T(8,128)(2,1)S(1)} %get-tuple-element.326), channel_id=1, source_target_pairs={{0,16},{1,9},{2,18},{3,11},{4,20},{5,13},{6,22},{7,15},{8,24},{9,1... | collective-permute-start | bytes 589832 | tf_op jit(solution)/shard_map/ppermute | solution.py:737
  269.5 13.7 %collective-permute-start.76 = (bf16[4,400,128]{2,1,0:T(8,128)(2,1)S(1)}, bf16[4,400,128]{2,1,0:T(8,128)(2,1)S(1)}, u32[]{:S(2)}, u32[]{:S(2)}) collective-permute-start(bf16[4,400,128]{2,1,0:T(8,128)(2,1)S(1)} %get-tuple-element.336), channel_id=1, source_target_pairs={{0,4},{1,3},{2,6},{3,1},{4,0},{5,7},{6,2},{7,5},{8,12},{9,11},{10,... | collective-permute-start | bytes 1228808 | tf_op jit(solution)/shard_map/ppermute | solution.py:737
  284.0 13.1 %collective-permute-start.78 = (bf16[2,784,128]{2,1,0:T(8,128)(2,1)S(1)}, bf16[2,784,128]{2,1,0:T(8,128)(2,1)S(1)}, u32[]{:S(2)}, u32[]{:S(2)}) collective-permute-start(bf16[2,784,128]{2,1,0:T(8,128)(2,1)S(1)} %get-tuple-element.351), channel_id=1, source_target_pairs={{0,8},{1,17},{2,10},{3,19},{4,12},{5,21},{6,14},{7,23},{8,0},{9,25... | collective-permute-start | bytes 1204232 | tf_op jit(solution)/shard_map/ppermute | solution.py:737
  (120 other events, 1159.1 us)

commit v6 on v5

--- a/solution.py
+++ b/solution.py
@@ -859,10 +859,11 @@
     count, mine = lax.axis_size("seq"), lax.axis_index("seq")
     prod, state = fin[:seqs], fin[seqs:]
     pre_p, pre_s = jnp.ones_like(prod), jnp.zeros_like(state)
-    bit, message, done = 1, fin, []
+    bit, message, done, other = 1, fin, [], fin
     for step in range(int(count).bit_length() - 1):
-        if hold and step in hold:
-            message = after(message, *hold[step])
+        before = hold(step, other) if hold else ()
+        if before:
+            message = after(message, *before)
         other = lax.ppermute(message, "seq", [(i, i ^ bit) for i in range(count)])
         if step < len(fill):
             done.append(fill[step](message))
@@ -926,7 +927,7 @@
         line_r0 = line_gather(pos, line_parts(after(packs[1], line_g0)), rows[1:2])
         sent_r0 = after(line_r0, *parts_g0[:2])
         parts_r0 = [cross(sent_r0, FIRST), cross(sent_r0, SECOND)]
-        line_g1 = line_gather(pos, line_parts(after(packs[2], line_r0)), rows[2:3])
+        parts_g1 = line_parts(after(packs[2], line_r0, *parts_g0[2:]))
         got = [plane_gather(pos, line_g0, parts_g0), None]
         places = {"f": 0, "i": 1, "c": 2, "u": 0, "d": 1, "o": 4}
         view = lambda got: {m: (got[m in "udo"], slab_rows[m], places[m]) for m in "udofic"}
@@ -959,7 +960,7 @@
         return v.reshape(seqs, sz.steps, CHUNKS, d).transpose(0, 2, 1, 3).reshape(seqs, length, d)
 
     stream, grad = to_rows(tokens), to_rows(cotangent)
-    kept = []
+    kept, diagonals = [], []
     for l in range(LAYERS):
         save = (True,) if l + 1 < LAYERS else ()
         normed, decay, inflow, cand, f_f, f_i, f_c, cp, ch, fin = gate_forward(
@@ -967,9 +968,18 @@
         )
         if standard:
             near, beside = parts_at[l]
-            diagonal = cross(after(near, fin), SECOND)
-            hold = {1: [line_g1] if l + 1 < LAYERS else [near], 2: [diagonal]}
+            if l + 1 < LAYERS:
+                line_g1 = line_gather(pos, [after(parts_g1[0], fin), *parts_g1[1:]], rows[2:3])
+
+            def hold(step, other):
+                if step == 0:
+                    return [line_g1] if l + 1 < LAYERS else []
+                if step == 1:
+                    diagonals.append(cross(after(near, other, beside), SECOND))
+                return []
+
             ent, _ = enter(fin, seqs, False, (), hold)
+            diagonal = diagonals[l] = after(diagonals[l], ent)
             rest = plane_gather(pos, lines_at[l], [near, beside, diagonal])
             weights[l] = view([weights[l]["f"][0], rest])
         else:
@@ -981,8 +991,9 @@
             own, *others = line_parts(after(packs[2 * l + 3], ent))
             line_r = line_gather(pos, [after(own, result), *others], rows[2 * l + 3 : 2 * l + 4])
             sent_g = after(line_g1, diagonal)
-            parts_g = [cross(sent_g, FIRST), cross(sent_g, SECOND), swap(sent_g, BOTH, 6)]
-            sent_r = after(line_r, *parts_g)
+            parts_g = [cross(sent_g, FIRST), cross(sent_g, SECOND)]
+            parts_g.append(cross(after(parts_g[0], line_r), SECOND))
+            sent_r = after(line_r, *parts_g[:2])
             weights.append(view([plane_gather(pos, line_g1, parts_g, (result,)), None]))
             lines_at.append(line_r)
             parts_at.append([cross(sent_r, FIRST), cross(sent_r, SECOND)])

time: 311 us -> 302 us (0.971)
  starting transfers between devices: 84.6 us -> 73.3 us
  waiting for transfers between devices: 94.3 us -> 100 us
    ppermute x27 -> x28, waiting for transfers between devices: 32 us -> 56 us  [cross(): lax.ppermute(array, BOTH, [(i, i ^ bits[i % 2]) for i in range(count)])]
    ppermute x42 -> x41, waiting for transfers between devices: 32.7 us -> 21.6 us  [swap(): return lax.ppermute(array, axes, [(i, i ^ bits) for i in range(count)])]
    ppermute x27 -> x28, starting transfers between devices: 38 us -> 27.6 us  [cross(): lax.ppermute(array, BOTH, [(i, i ^ bits[i % 2]) for i in range(count)])]
    ppermute x12, waiting for transfers between devices: 29.7 us -> 22.5 us  [enter(): other = lax.ppermute(message, 'seq', [(i, i ^ bit) for i in range(count)])]
    unnamed x126 -> x134, local copies, waits for them, and re-layouts: 9.69 us -> 8.24 us
    ppermute x42 -> x41, starting transfers between devices: 32.3 us -> 32.2 us  [swap(): return lax.ppermute(array, axes, [(i, i ^ bits) for i in range(count)])]
  transfers between devices with their start and end apart: 81 -> 81, of which waited for: 31 -> 35; matrix products, arithmetic and copies ran while one was open for 1% -> 1% of each run, Pallas kernels for 26% -> 26%
where the time goes in v6:
time: 302 us; the launch traced here: 301 us
  Pallas kernels  115 us (38%)
  waiting for transfers between devices  100 us (33%)
  starting transfers between devices  73.3 us (24%)
  local copies, waits for them, and re-layouts  10.8 us (4%)
    pallas_call x46, Pallas kernels, call(): pl.pallas_call(kernel, grid=(grid,), in_specs=[spec(*one) for one in ins]...  115 us
    ppermute x28, waiting for transfers between devices, cross(): lax.ppermute(array, BOTH, [(i, i ^ bits[i % 2]) for i in range(count)])  56 us
    ppermute x41, starting transfers between devices, swap(): return lax.ppermute(array, axes, [(i, i ^ bits) for i in range(count)])  32.2 us
    ppermute x28, starting transfers between devices, cross(): lax.ppermute(array, BOTH, [(i, i ^ bits[i % 2]) for i in range(count)])  27.6 us
    ppermute x12, waiting for transfers between devices, enter(): other = lax.ppermute(message, 'seq', [(i, i ^ bit) for i in range(count)])  22.5 us
    ppermute x41, waiting for transfers between devices, swap(): return lax.ppermute(array, axes, [(i, i ^ bits) for i in range(count)])  21.6 us
    ppermute x12, starting transfers between devices, enter(): other = lax.ppermute(message, 'seq', [(i, i ^ bit) for i in range(count)])  13.5 us
    unnamed x134, local copies, waits for them, and re-layouts  8.24 us
  transfers between devices with their start and end apart: 81, of which 35 were waited for; matrix products, arithmetic and copies ran while one was open for 1% of the time, Pallas kernels for 26%

profile of v6, /device:TPU:0, one launch (start us, length us, event | category | flops | bytes accessed | tf_op | source)
XLA Modules:
  0.0 301.2 jit_solution(18196285421381652799)
XLA Ops:
  1.8 5.1 %collective-permute-start.2 = (bf16[400,128]{1,0:T(8,128)(2,1)S(1)}, bf16[400,128]{1,0:T(8,128)(2,1)S(1)}, u32[]{:S(2)}, u32[]{:S(2)}) collective-permute-start(bf16[400,128]{1,0:T(8,128)(2,1)S(1)} %get-tuple-element.191.refs_0_), channel_id=1, source_target_pairs={{0,24},{4,28},{8,16},{12,20},{16,8},{20,12},{24,0},{28,4},{1,25},{... | collective-permute-start | bytes 307208 | tf_op jit(solution)/shard_map/ppermute | solution.py:710
  10.8 4.8 %collective-permute-done.1.refs_2_ = bf16[400,128]{1,0:T(8,128)(2,1)S(1)} collective-permute-done((bf16[400,128]{1,0:T(8,128)(2,1)S(1)}, bf16[400,128]{1,0:T(8,128)(2,1)S(1)}, u32[]{:S(2)}, u32[]{:S(2)}) %collective-permute-start.1) | collective-permute-done | bytes 102432 | tf_op jit(solution)/shard_map/ppermute | solution.py:710
  31.8 4.4 %collective-permute-done.13.refs_2_ = bf16[640,128]{1,0:T(8,128)(2,1)S(1)} collective-permute-done((bf16[640,128]{1,0:T(8,128)(2,1)S(1)}, bf16[640,128]{1,0:T(8,128)(2,1)S(1)}, u32[]{:S(2)}, u32[]{:S(2)}) %collective-permute-start.13) | collective-permute-done | bytes 163872 | tf_op jit(solution)/shard_map/ppermute | solution.py:710
  47.6 6.4 %gates.2 = (bf16[512,512]{1,0:T(8,128)(2,1)}, f32[512,1024]{1,0:T(8,128)}, f32[512,1024]{1,0:T(8,128)S(1)}, f32[512,1024]{1,0:T(8,128)}, bf16[512,1024]{1,0:T(8,...) custom-call(bf16[512,512]{1,0:T(8,128)(2,1)S(1)} %bitcast.63, ...), custom_call_target="tpu_custom_call" | custom-call | flops 9900000256 | bytes 1024 | tf_op jit(solution)/shard_map/gates/pallas_call | solution.py:553
  79.4 3.4 %plane_gather.5 = bf16[4,2,2,2,640,128]{5,4,3,2,1,0:T(8,128)(2,1)S(1)} custom-call(s32[8]{0:T(128)S(1)} %stack.35.pos_ref, bf16[4,640,128]{2,1,0:T(8,128)(2,1)} %copy-done.6, bf16[4,640,128]{2,1,0:T(8,128)(2,1)} %collective-permute-done.21.refs_1_, bf16[4,640,128]{2,1,0:T(8,128)(2,1)} %collective-permute-done.22.refs_2_, bf16[4,640,128]{2,1,0:T(8,128)(2,1)} %copy-done.34, ...), custom_call_target="tpu_custom_call" | custom-call | flops 5500000256 | bytes 1024 | tf_op jit(solution)/shard_map/plane_gather/pallas_call | solution.py:553
  82.8 8.8 %mix.2 = (f32[512,1024]{1,0:T(8,128)}, bf16[512,1024]{1,0:T(8,128)(2,1)}, f32[2,8,1024]{2,1,0:T(8,128)}, f32[512,512]{1,0:T(8,128)}, bf16[512,512]{1,0:T(8,128)(...) custom-call(bf16[512,512]{1,0:T(8,128)(2,1)S(1)} %bitcast.64, ...), custom_call_target="tpu_custom_call" | custom-call | flops 15400000512 | bytes 1024 | tf_op jit(solution)/shard_map/mix/pallas_call | solution.py:553
  95.6 6.6 %collective-permute-done.33.refs_3_ = bf16[4,384,128]{2,1,0:T(8,128)(2,1)S(1)} collective-permute-done((bf16[4,384,128]{2,1,0:T(8,128)(2,1)S(1)}, bf16[4,384,128]{2,1,0:T(8,128)(2,1)S(1)}, u32[]{:S(2)}, u32[]{:S(2)}) %collective-permute-start.33) | collective-permute-done | bytes 393248 | tf_op jit(solution)/shard_map/ppermute | solution.py:737
  108.0 6.5 %gates.3 = (bf16[512,512]{1,0:T(8,128)(2,1)}, f32[512,1024]{1,0:T(8,128)}, f32[512,1024]{1,0:T(8,128)S(1)}, f32[512,1024]{1,0:T(8,128)}, bf16[512,1024]{1,0:T(8,...) custom-call(f32[512,512]{1,0:T(8,128)S(1)} %get-tuple-element.208.x_, ...), custom_call_target="tpu_custom_call" | custom-call | flops 9900000256 | bytes 1024 | tf_op jit(solution)/shard_map/gates/pallas_call | solution.py:553
  121.3 3.6 %collective-permute-done.39 = f32[4,1024]{1,0:T(4,128)S(1)} collective-permute-done((f32[4,1024]{1,0:T(4,128)S(1)}, f32[4,1024]{1,0:T(4,128)S(1)}, u32[]{:S(2)}, u32[]{:S(2)}) %collective-permute-start.39) | collective-permute-done | bytes 16416 | tf_op jit(solution)/shard_map/ppermute | solution.py:867
  136.9 7.5 %mix.3 = (f32[512,1024]{1,0:T(8,128)}, bf16[512,1024]{1,0:T(8,128)(2,1)S(1)}, f32[2,8,1024]{2,1,0:T(8,128)S(1)}, f32[512,512]{1,0:T(8,128)S(1)}, bf16[512,512]{1...) custom-call(f32[512,512]{1,0:T(8,128)S(1)} %get-tuple-element.208.x_, ...), custom_call_target="tpu_custom_call" | custom-call | flops 15400000512 | bytes 1024 | tf_op jit(solution)/shard_map/mix/pallas_call | solution.py:553
  144.4 7.0 %mlp_back.2 = (bf16[512,512]{1,0:T(8,128)(2,1)S(1)}, bf16[512,2048]{1,0:T(8,128)(2,1)S(1)}, f32[512,512]{1,0:T(8,128)S(1)}, bf16[512,512]{1,0:T(8,128)(2,1)S(1)}...) custom-call(bf16[512,512]{1,0:T(8,128)(2,1)S(1)} %bitcast.68, ...), custom_call_target="tpu_custom_call" | custom-call | flops 13200000000 | bytes 1024 | tf_op jit(solution)/shard_map/mlp_back/pallas_call | solution.py:553
  152.4 3.4 %up_weights.2 = (bf16[8,2,256,128]{3,2,1,0:T(8,128)(2,1)S(1)}, bf16[8,2,256,128]{3,2,1,0:T(8,128)(2,1)}) custom-call(s32[8]{0:T(128)S(1)} %stack.35.pos_ref, bf16[512,512]{1,0:T(8,128)(2,1)S(1)} %get-tuple-element.234.n2_ref, bf16[512,2048]{1,0:T(8,128)(2,1)S(1)} %get-tuple-element.235.gpre_ref), custom_call_target="tpu_custom_call" | custom-call | flops 5500000256 | bytes 1024 | tf_op jit(solution)/shard_map/up_weights/pallas_call | solution.py:553
  156.0 3.5 %down_weights.2 = (bf16[8,2,256,128]{3,2,1,0:T(8,128)(2,1)S(1)}, bf16[8,2,256,128]{3,2,1,0:T(8,128)(2,1)}) custom-call(s32[8]{0:T(128)S(1)} %stack.35.pos_ref, bf16[512,2048]{1,0:T(8,128)(2,1)S(1)} %get-tuple-element.242.left_ref, bf16[512,512]{1,0:T(8,128)(2,1)S(1)} %get-tuple-element.243.right_ref), custom_call_target="tpu_custom_call" | custom-call | flops 5500000256 | bytes 1024 | tf_op jit(solution)/shard_map/down_weights/pallas_call | solution.py:553
  171.6 8.4 %gate_back.2 = (bf16[8,2,384,128]{3,2,1,0:T(8,128)(2,1)S(1)}, bf16[8,2,384,128]{3,2,1,0:T(8,128)(2,1)S(1)}, f32[2,1024]{1,0:T(2,128)S(1)}, f32[512,512]{1,0:T(8,128)S(1)}, f32[1,512]{1,0:T(1,128)S(1)}) custom-call(s32[8]{0:T(128)S(1)} %stack.35.pos_ref, f32[512,512]{1,0:T(8,128)S(1)} %copy-done.26, f32[2,512]{1,0:T(2,128)S(1)} %get-tuple-element.209.gain_ref, ...), custom_call_target="tpu_custom_call" | custom-call | flops 17600000000 | bytes 1024 | tf_op jit(solution)/shard_map/gate_back/pallas_call | solution.py:553
  185.8 7.7 %mlp_back.3 = (bf16[512,512]{1,0:T(8,128)(2,1)S(1)}, bf16[512,2048]{1,0:T(8,128)(2,1)S(1)}, f32[512,512]{1,0:T(8,128)S(1)}, bf16[512,512]{1,0:T(8,128)(2,1)S(1)}...) custom-call(f32[512,512]{1,0:T(8,128)S(1)} %get-tuple-element.268.g_, ...), custom_call_target="tpu_custom_call" | custom-call | flops 13200000000 | bytes 1024 | tf_op jit(solution)/shard_map/mlp_back/pallas_call | solution.py:553
  215.0 3.6 %collective-permute-done.64 = f32[4,1024]{1,0:T(4,128)S(1)} collective-permute-done((f32[4,1024]{1,0:T(4,128)S(1)}, f32[4,1024]{1,0:T(4,128)S(1)}, u32[]{:S(2)}, u32[]{:S(2)}) %collective-permute-start.64) | collective-permute-done | bytes 16416 | tf_op jit(solution)/shard_map/ppermute | solution.py:867
  219.7 3.6 %collective-permute-done.61.refs_1_ = bf16[4,768,128]{2,1,0:T(8,128)(2,1)S(1)} collective-permute-done((bf16[4,768,128]{2,1,0:T(8,128)(2,1)S(1)}, bf16[4,768,128]{2,1,0:T(8,128)(2,1)S(1)}, u32[]{:S(2)}, u32[]{:S(2)}) %collective-permute-start.61) | collective-permute-done | bytes 786464 | tf_op jit(solution)/shard_map/ppermute | solution.py:737
  226.9 9.0 %gate_back.3 = (bf16[8,2,400,128]{3,2,1,0:T(8,128)(2,1)S(1)}, bf16[8,2,400,128]{3,2,1,0:T(8,128)(2,1)S(1)}, f32[2,1024]{1,0:T(2,128)}, bf16[512,512]{1,0:T(8,128)(2,1)S(1)}, f32[1,512]{1,0:T(1,128)}) custom-call(s32[8]{0:T(128)S(1)} %stack.35.pos_ref, bf16[512,512]{1,0:T(8,128)(2,1)S(1)} %bitcast.65, f32[2,512]{1,0:T(2,128)S(1)} %get-tuple-element.192.gain_ref, ...), custom_call_target="tpu_custom_call" | custom-call | flops 17600000000 | bytes 1024 | tf_op jit(solution)/shard_map/gate_back/pallas_call | solution.py:553
  239.3 3.5 %collective-permute-done.69 = bf16[8,2,400,128]{3,2,1,0:T(8,128)(2,1)S(1)} collective-permute-done((bf16[8,2,400,128]{3,2,1,0:T(8,128)(2,1)S(1)}, bf16[8,2,400,128]{3,2,1,0:T(8,128)(2,1)S(1)}, u32[]{:S(2)}, u32[]{:S(2)}) %collective-permute-start.69) | collective-permute-done | bytes 1638432 | tf_op jit(solution)/shard_map/ppermute | solution.py:710
  247.7 8.6 %collective-permute-done.70.refs_1_ = bf16[4,2,400,128]{3,2,1,0:T(8,128)(2,1)S(1)} collective-permute-done((bf16[4,2,400,128]{3,2,1,0:T(8,128)(2,1)S(1)}, bf16[4,2,400,128]{3,2,1,0:T(8,128)(2,1)S(1)}, u32[]{:S(2)}, u32[]{:S(2)}) %collective-permute-start.70) | collective-permute-done | bytes 819232 | tf_op jit(solution)/shard_map/ppermute | solution.py:737
  271.0 8.8 %collective-permute-done.74 = bf16[1024,128]{1,0:T(8,128)(2,1)S(1)} collective-permute-done((bf16[1024,128]{1,0:T(8,128)(2,1)S(1)}, bf16[1024,128]{1,0:T(8,128)(2,1)S(1)}, u32[]{:S(2)}, u32[]{:S(2)}) %collective-permute-start.74) | collective-permute-done | bytes 262176 | tf_op jit(solution)/shard_map/ppermute | solution.py:737
  281.3 5.0 %collective-permute-done.77.refs_1_ = bf16[1,2,256,128]{3,2,1,0:T(8,128)(2,1)S(1)} collective-permute-done((bf16[1,2,256,128]{3,2,1,0:T(8,128)(2,1)S(1)}, bf16[1,2,256,128]{3,2,1,0:T(8,128)(2,1)S(1)}, u32[]{:S(2)}, u32[]{:S(2)}) %collective-permute-start.77) | collective-permute-done | bytes 131104 | tf_op jit(solution)/shard_map/ppermute | solution.py:737
  286.9 4.4 %collective-permute-done.78.got = bf16[2,784,128]{2,1,0:T(8,128)(2,1)S(1)} collective-permute-done((bf16[2,784,128]{2,1,0:T(8,128)(2,1)S(1)}, bf16[2,784,128]{2,1,0:T(8,128)(2,1)S(1)}, u32[]{:S(2)}, u32[]{:S(2)}) %collective-permute-start.78) | collective-permute-done | bytes 401440 | tf_op jit(solution)/shard_map/ppermute | solution.py:737
  296.6 3.6 %collective-permute-done.79.refs_3_ = bf16[784,128]{1,0:T(8,128)(2,1)S(1)} collective-permute-done((bf16[784,128]{1,0:T(8,128)(2,1)S(1)}, bf16[784,128]{1,0:T(8,128)(2,1)S(1)}, u32[]{:S(2)}, u32[]{:S(2)}) %collective-permute-start.79) | collective-permute-done | bytes 200736 | tf_op jit(solution)/shard_map/ppermute | solution.py:737
  (346 shorter events, 162.2 us)
Async XLA Ops:
  23.5 12.6 %collective-permute-start.13 = (bf16[640,128]{1,0:T(8,128)(2,1)S(1)}, bf16[640,128]{1,0:T(8,128)(2,1)S(1)}, u32[]{:S(2)}, u32[]{:S(2)}) collective-permute-start(bf16[640,128]{1,0:T(8,128)(2,1)S(1)} %get-tuple-element.201.refs_0_), channel_id=1, source_target_pairs={{0,16},{4,20},{8,24},{12,28},{16,0},{20,4},{24,8},{28,12},{1,17},{... | collective-permute-start | bytes 491528 | tf_op jit(solution)/shard_map/ppermute | solution.py:710
  23.5 12.6 %collective-permute-start.12 = (bf16[640,128]{1,0:T(8,128)(2,1)S(1)}, bf16[640,128]{1,0:T(8,128)(2,1)S(1)}, u32[]{:S(2)}, u32[]{:S(2)}) collective-permute-start(bf16[640,128]{1,0:T(8,128)(2,1)S(1)} %get-tuple-element.201.refs_0_), channel_id=1, source_target_pairs={{0,8},{4,12},{8,0},{12,4},{16,24},{20,28},{24,16},{28,20},{1,9},{5... | collective-permute-start | bytes 491528 | tf_op jit(solution)/shard_map/ppermute | solution.py:710
  38.9 22.0 %collective-permute-start.22 = (bf16[4,640,128]{2,1,0:T(8,128)(2,1)S(1)}, bf16[4,640,128]{2,1,0:T(8,128)(2,1)}, u32[]{:S(2)}, u32[]{:S(2)}) collective-permute-start(bf16[4,640,128]{2,1,0:T(8,128)(2,1)S(1)} %line_gather.5.refs_0_), channel_id=1, source_target_pairs={{0,4},{1,3},{2,6},{3,1},{4,0},{5,7},{6,2},{7,5},{8,12},{9,11},{10,... | collective-permute-start | bytes 1966088 | tf_op jit(solution)/shard_map/ppermute | solution.py:737
  39.5 21.4 %collective-permute-start.21 = (bf16[4,640,128]{2,1,0:T(8,128)(2,1)S(1)}, bf16[4,640,128]{2,1,0:T(8,128)(2,1)}, u32[]{:S(2)}, u32[]{:S(2)}) collective-permute-start(bf16[4,640,128]{2,1,0:T(8,128)(2,1)S(1)} %line_gather.5.refs_0_), channel_id=1, source_target_pairs={{0,2},{1,5},{2,0},{3,7},{4,6},{5,1},{6,4},{7,3},{8,10},{9,13},{10,... | collective-permute-start | bytes 1966088 | tf_op jit(solution)/shard_map/ppermute | solution.py:737
  40.0 13.9 %collective-permute-start.17 = (bf16[384,128]{1,0:T(8,128)(2,1)S(1)}, bf16[384,128]{1,0:T(8,128)(2,1)S(1)}, u32[]{:S(2)}, u32[]{:S(2)}) collective-permute-start(bf16[384,128]{1,0:T(8,128)(2,1)S(1)} %get-tuple-element.203.refs_0_), channel_id=1, source_target_pairs={{0,24},{4,28},{8,16},{12,20},{16,8},{20,12},{24,0},{28,4},{1,25},{... | collective-permute-start | bytes 294920 | tf_op jit(solution)/shard_map/ppermute | solution.py:710
  71.8 19.9 %collective-permute-start.32 = (bf16[640,128]{1,0:T(8,128)(2,1)S(1)}, bf16[640,128]{1,0:T(8,128)(2,1)S(1)}, u32[]{:S(2)}, u32[]{:S(2)}) collective-permute-start(bf16[640,128]{1,0:T(8,128)(2,1)S(1)} %get-tuple-element.214.refs_0_), channel_id=1, source_target_pairs={{0,24},{4,28},{8,16},{12,20},{16,8},{20,12},{24,0},{28,4},{1,25},{... | collective-permute-start | bytes 491528 | tf_op jit(solution)/shard_map/ppermute | solution.py:710
  74.1 17.6 %collective-permute-start.31 = (bf16[640,128]{1,0:T(8,128)(2,1)S(1)}, bf16[640,128]{1,0:T(8,128)(2,1)S(1)}, u32[]{:S(2)}, u32[]{:S(2)}) collective-permute-start(bf16[640,128]{1,0:T(8,128)(2,1)S(1)} %get-tuple-element.214.refs_0_), channel_id=1, source_target_pairs={{0,16},{4,20},{8,24},{12,28},{16,0},{20,4},{24,8},{28,12},{1,17},{... | collective-permute-start | bytes 491528 | tf_op jit(solution)/shard_map/ppermute | solution.py:710
  74.1 17.6 %collective-permute-start.30 = (bf16[640,128]{1,0:T(8,128)(2,1)S(1)}, bf16[640,128]{1,0:T(8,128)(2,1)S(1)}, u32[]{:S(2)}, u32[]{:S(2)}) collective-permute-start(bf16[640,128]{1,0:T(8,128)(2,1)S(1)} %get-tuple-element.214.refs_0_), channel_id=1, source_target_pairs={{0,8},{4,12},{8,0},{12,4},{16,24},{20,28},{24,16},{28,20},{1,9},{5... | collective-permute-start | bytes 491528 | tf_op jit(solution)/shard_map/ppermute | solution.py:710
  76.3 18.6 %collective-permute-start.29 = (bf16[4,384,128]{2,1,0:T(8,128)(2,1)S(1)}, bf16[4,384,128]{2,1,0:T(8,128)(2,1)S(1)}, u32[]{:S(2)}, u32[]{:S(2)}) collective-permute-start(bf16[4,384,128]{2,1,0:T(8,128)(2,1)S(1)} %line_gather.6.refs_0_), channel_id=1, source_target_pairs={{0,4},{1,3},{2,6},{3,1},{4,0},{5,7},{6,2},{7,5},{8,12},{9,11},{10,... | collective-permute-start | bytes 1179656 | tf_op jit(solution)/shard_map/ppermute | solution.py:737
  77.8 16.5 %collective-permute-start.28 = (bf16[4,384,128]{2,1,0:T(8,128)(2,1)S(1)}, bf16[4,384,128]{2,1,0:T(8,128)(2,1)S(1)}, u32[]{:S(2)}, u32[]{:S(2)}) collective-permute-start(bf16[4,384,128]{2,1,0:T(8,128)(2,1)S(1)} %line_gather.6.refs_0_), channel_id=1, source_target_pairs={{0,2},{1,5},{2,0},{3,7},{4,6},{5,1},{6,4},{7,3},{8,10},{9,13},{10,... | collective-permute-start | bytes 1179656 | tf_op jit(solution)/shard_map/ppermute | solution.py:737
  102.2 17.7 %collective-permute-start.42 = (bf16[4,640,128]{2,1,0:T(8,128)(2,1)S(1)}, bf16[4,640,128]{2,1,0:T(8,128)(2,1)}, u32[]{:S(2)}, u32[]{:S(2)}) collective-permute-start(bf16[4,640,128]{2,1,0:T(8,128)(2,1)S(1)} %line_gather.7.refs_0_), channel_id=1, source_target_pairs={{0,4},{1,3},{2,6},{3,1},{4,0},{5,7},{6,2},{7,5},{8,12},{9,11},{10,... | collective-permute-start | bytes 1966088 | tf_op jit(solution)/shard_map/ppermute | solution.py:737
  102.7 17.2 %collective-permute-start.41 = (bf16[4,640,128]{2,1,0:T(8,128)(2,1)S(1)}, bf16[4,640,128]{2,1,0:T(8,128)(2,1)}, u32[]{:S(2)}, u32[]{:S(2)}) collective-permute-start(bf16[4,640,128]{2,1,0:T(8,128)(2,1)S(1)} %line_gather.7.refs_0_), channel_id=1, source_target_pairs={{0,2},{1,5},{2,0},{3,7},{4,6},{5,1},{6,4},{7,3},{8,10},{9,13},{10,... | collective-permute-start | bytes 1966088 | tf_op jit(solution)/shard_map/ppermute | solution.py:737
  180.0 14.9 %collective-permute-start.56 = (bf16[2,1024,128]{2,1,0:T(8,128)(2,1)S(1)}, bf16[2,1024,128]{2,1,0:T(8,128)(2,1)S(1)}, u32[]{:S(2)}, u32[]{:S(2)}) collective-permute-start(bf16[2,1024,128]{2,1,0:T(8,128)(2,1)S(1)} %get-tuple-element.238), channel_id=1, source_target_pairs={{0,8},{1,17},{2,10},{3,19},{4,12},{5,21},{6,14},{7,23},{8,0},{9,25... | collective-permute-start | bytes 1572872 | tf_op jit(solution)/shard_map/ppermute | solution.py:737
  182.1 20.3 %collective-permute-start.57 = (bf16[4,2,384,128]{3,2,1,0:T(8,128)(2,1)S(1)}, bf16[4,2,384,128]{3,2,1,0:T(8,128)(2,1)S(1)}, u32[]{:S(2)}, u32[]{:S(2)}) collective-permute-start(bf16[4,2,384,128]{3,2,1,0:T(8,128)(2,1)S(1)} %get-tuple-element.252), channel_id=1, source_target_pairs={{0,2},{1,5},{2,0},{3,7},{4,6},{5,1},{6,4},{7,3},{8,10},{9,13},{10,... | collective-permute-start | bytes 2359304 | tf_op jit(solution)/shard_map/ppermute | solution.py:737
  184.5 18.0 %collective-permute-start.58 = (bf16[4,2,384,128]{3,2,1,0:T(8,128)(2,1)S(1)}, bf16[4,2,384,128]{3,2,1,0:T(8,128)(2,1)S(1)}, u32[]{:S(2)}, u32[]{:S(2)}) collective-permute-start(bf16[4,2,384,128]{3,2,1,0:T(8,128)(2,1)S(1)} %get-tuple-element.267), channel_id=1, source_target_pairs={{0,2},{1,5},{2,0},{3,7},{4,6},{5,1},{6,4},{7,3},{8,10},{9,13},{10,... | collective-permute-start | bytes 2359304 | tf_op jit(solution)/shard_map/ppermute | solution.py:737
  206.7 17.8 %collective-permute-start.62 = (bf16[8,2,256,128]{3,2,1,0:T(8,128)(2,1)S(1)}, bf16[8,2,256,128]{3,2,1,0:T(8,128)(2,1)S(1)}, u32[]{:S(2)}, u32[]{:S(2)}) collective-permute-start(bf16[8,2,256,128]{3,2,1,0:T(8,128)(2,1)S(1)} %get-tuple-element.292), channel_id=1, source_target_pairs={{0,1},{1,0},{2,3},{3,2},{4,5},{5,4},{6,7},{7,6},{8,9},{9,8},{10,11... | collective-permute-start | bytes 3145736 | tf_op jit(solution)/shard_map/ppermute | solution.py:710
  209.9 13.4 %collective-permute-start.61 = (bf16[4,768,128]{2,1,0:T(8,128)(2,1)S(1)}, bf16[4,768,128]{2,1,0:T(8,128)(2,1)S(1)}, u32[]{:S(2)}, u32[]{:S(2)}) collective-permute-start(bf16[4,768,128]{2,1,0:T(8,128)(2,1)S(1)} %get-tuple-element.286), channel_id=1, source_target_pairs={{0,4},{1,3},{2,6},{3,1},{4,0},{5,7},{6,2},{7,5},{8,12},{9,11},{10,... | collective-permute-start | bytes 2359304 | tf_op jit(solution)/shard_map/ppermute | solution.py:737
  214.9 23.5 %collective-permute-start.68 = (bf16[8,2,256,128]{3,2,1,0:T(8,128)(2,1)S(1)}, bf16[8,2,256,128]{3,2,1,0:T(8,128)(2,1)S(1)}, u32[]{:S(2)}, u32[]{:S(2)}) collective-permute-start(bf16[8,2,256,128]{3,2,1,0:T(8,128)(2,1)S(1)} %get-tuple-element.282), channel_id=1, source_target_pairs={{0,1},{1,0},{2,3},{3,2},{4,5},{5,4},{6,7},{7,6},{8,9},{9,8},{10,11... | collective-permute-start | bytes 3145736 | tf_op jit(solution)/shard_map/ppermute | solution.py:710
  218.7 18.0 %collective-permute-start.66 = (bf16[1,2,256,128]{3,2,1,0:T(8,128)(2,1)S(1)}, bf16[1,2,256,128]{3,2,1,0:T(8,128)(2,1)S(1)}, u32[]{:S(2)}, u32[]{:S(2)}) collective-permute-start(bf16[1,2,256,128]{3,2,1,0:T(8,128)(2,1)S(1)} %get-tuple-element.295), channel_id=1, source_target_pairs={{0,2},{1,5},{2,0},{3,7},{4,6},{5,1},{6,4},{7,3},{8,10},{9,13},{10,... | collective-permute-start | bytes 393224 | tf_op jit(solution)/shard_map/ppermute | solution.py:737
  245.2 18.6 %collective-permute-start.72 = (bf16[2,1024,128]{2,1,0:T(8,128)(2,1)S(1)}, bf16[2,1024,128]{2,1,0:T(8,128)(2,1)S(1)}, u32[]{:S(2)}, u32[]{:S(2)}) collective-permute-start(bf16[2,1024,128]{2,1,0:T(8,128)(2,1)S(1)} %get-tuple-element.334), channel_id=1, source_target_pairs={{0,8},{1,17},{2,10},{3,19},{4,12},{5,21},{6,14},{7,23},{8,0},{9,25... | collective-permute-start | bytes 1572872 | tf_op jit(solution)/shard_map/ppermute | solution.py:737
  246.8 15.6 %collective-permute-start.71 = (bf16[768,128]{1,0:T(8,128)(2,1)S(1)}, bf16[768,128]{1,0:T(8,128)(2,1)S(1)}, u32[]{:S(2)}, u32[]{:S(2)}) collective-permute-start(bf16[768,128]{1,0:T(8,128)(2,1)S(1)} %get-tuple-element.328), channel_id=1, source_target_pairs={{0,16},{1,9},{2,18},{3,11},{4,20},{5,13},{6,22},{7,15},{8,24},{9,1... | collective-permute-start | bytes 589832 | tf_op jit(solution)/shard_map/ppermute | solution.py:737
  257.1 23.3 %collective-permute-start.76 = (bf16[4,400,128]{2,1,0:T(8,128)(2,1)S(1)}, bf16[4,400,128]{2,1,0:T(8,128)(2,1)S(1)}, u32[]{:S(2)}, u32[]{:S(2)}) collective-permute-start(bf16[4,400,128]{2,1,0:T(8,128)(2,1)S(1)} %get-tuple-element.338), channel_id=1, source_target_pairs={{0,4},{1,3},{2,6},{3,1},{4,0},{5,7},{6,2},{7,5},{8,12},{9,11},{10,... | collective-permute-start | bytes 1228808 | tf_op jit(solution)/shard_map/ppermute | solution.py:737
  258.3 22.1 %collective-permute-start.75 = (bf16[4,384,128]{2,1,0:T(8,128)(2,1)S(1)}, bf16[4,384,128]{2,1,0:T(8,128)(2,1)S(1)}, u32[]{:S(2)}, u32[]{:S(2)}) collective-permute-start(bf16[4,384,128]{2,1,0:T(8,128)(2,1)S(1)} %get-tuple-element.332), channel_id=1, source_target_pairs={{0,4},{1,3},{2,6},{3,1},{4,0},{5,7},{6,2},{7,5},{8,12},{9,11},{10,... | collective-permute-start | bytes 1179656 | tf_op jit(solution)/shard_map/ppermute | solution.py:737
  264.5 15.3 %collective-permute-start.74 = (bf16[1024,128]{1,0:T(8,128)(2,1)S(1)}, bf16[1024,128]{1,0:T(8,128)(2,1)S(1)}, u32[]{:S(2)}, u32[]{:S(2)}) collective-permute-start(bf16[1024,128]{1,0:T(8,128)(2,1)S(1)} %get-tuple-element.343), channel_id=1, source_target_pairs={{0,16},{1,9},{2,18},{3,11},{4,20},{5,13},{6,22},{7,15},{8,24},{9,1... | collective-permute-start | bytes 786440 | tf_op jit(solution)/shard_map/ppermute | solution.py:737
  (124 other events, 1071.4 us)

commit v7 on v6

--- a/solution.py
+++ b/solution.py
@@ -743,7 +743,7 @@
     return call(
         functools.partial(pair_sum_kernel, rows), lines,
         [whole(pos)] + [view(keep) for keep, _ in pairs] + [view(got) for _, got in pairs],
-        [by_line_out(lines, 2, sum(rows), LANE)] * 2, [], 0, "pair_sum",
+        [by_line_out(lines, 2, sum(rows), LANE)] * 2, [], 3, "pair_sum",
     )
 
 
@@ -867,6 +867,8 @@
         other = lax.ppermute(message, "seq", [(i, i ^ bit) for i in range(count)])
         if step < len(fill):
             done.append(fill[step](message))
+        if done and bit * 2 == count:
+            other = after(other, *done[-1])
         o_p, o_s = other[:seqs], other[seqs:]
         upper = ((mine // bit) % 2 == 1) ^ backward
         pre_p, pre_s = jnp.where(upper, o_p * pre_p, pre_p), jnp.where(upper, pre_p * o_s + pre_s, pre_s)
@@ -1021,20 +1023,38 @@
             return row_weights(sz, pos, place(after(act, message)), gr, "down_weights")
 
         def out(message):
+            return row_weights(sz, pos, place(after(hb, message)), go, "out_weights")
+
+        def both(message):
+            return [*down(message), *out(message)]
+
+        def begin(message):
             if above:
                 message = above_up.step(message)
-            return row_weights(sz, pos, place(after(hb, message)), go, "out_weights")
-
-        ent, pairs = enter(fin, seqs, True, (up, down, out))
+            exchanged = core_exchange([made[0], made[1][:2], made[1][2:]])
+            upright = None
+            if not above:
+                upright = UprightReduction(pos, [(l, "u")], (after(exchanged[0][0], message), exchanged[0][1]))
+                message = upright.seen
+            (keep, got), *others = exchanged[1:]
+            begun.extend([exchanged, upright, Reduction(pos, [(l, "d"), (l, "o")], [(after(keep, message), got), *others])])
+            return [begun[2].seen]
+
+        made, begun = [], []
+
+        def keep_made(work):
+            def run(message):
+                made.append(work(message))
+                return made[-1]
+
+            return run
+
         if standard:
-            if above:
-                pairs[2] = (after(pairs[2][0], above.step(pairs[2][0])), pairs[2][1])
-            exchanged = core_exchange(pairs)
-            if not above:
-                upright = UprightReduction(pos, [(l, "u")], exchanged[0])
-                gmid = after(gmid, upright.seen)
-            mlp = Reduction(pos, [(l, "d"), (l, "o")], exchanged[1:])
+            ent, _ = enter(fin, seqs, True, (keep_made(up), keep_made(both), begin))
+            exchanged, upright, mlp = begun
             gmid = after(gmid, mlp.seen)
+        else:
+            ent, pairs = enter(fin, seqs, True, (up, down, out))
         final = []
         if l == 0 and standard:
             final = [(ggain_two, 3)]
@@ -1048,23 +1068,26 @@
         if not standard:
             pending.append((l, pairs + [gate_pair]))
             continue
-        if above:
-            mlp.step(above_up.step(above.step(gate_pair[0])))
-            upright = UprightReduction(pos, [(l, "u")], (after(exchanged[0][0], mlp.seen), exchanged[0][1]))
-            gate_pair[1] = after(gate_pair[1], upright.seen)
         names = [(l, m) for m in "fic"]
         if l == 0:
             names += [(at, k) for at in range(LAYERS) for k in range(4)]
-        gates = Reduction(pos, names, core_exchange([gate_pair]))
+        if above:
+            gate_pair[1] = after(gate_pair[1], above.step(gate_pair[0]))
+        ((keep, got),) = core_exchange([gate_pair])
+        gates = Reduction(pos, names, [(keep, got)])
+        if l == 0:
+            upright = UprightReduction(pos, [(l, "u")], (after(exchanged[0][0], gates.seen), exchanged[0][1]))
         if l > 0:
             grad, above, above_up = after(grad, gates.seen), mlp, upright
             above.join(gates)
             continue
-        gates.step()
-        upright.step(above.total(gates.seen))
+        mlp.step(above_up.step(above.step(upright.seen)))
+        gates.step(mlp.seen)
+        above_up.total(upright.step(above.total(gates.seen)))
         mlp.join(gates)
-        mlp.step(upright.step(above_up.total(upright.seen)))
-        mlp.step(upright.step(mlp.seen))
+        mlp.step(above_up.parts[0])
+        upright.step(mlp.seen)
+        mlp.step(upright.step())
         sums = [(one.names, one.parts) for one in (above, above_up, mlp, upright)]
     grad_tokens = from_rows(grad)
 

time: 302 us -> 291 us (0.964)
  waiting for transfers between devices: 100 us -> 87.4 us
    ppermute x28, waiting for transfers between devices: 56 us -> 46.6 us  [cross(): lax.ppermute(array, BOTH, [(i, i ^ bits[i % 2]) for i in range(count)])]
    ppermute x28, starting transfers between devices: 27.6 us -> 31.9 us  [cross(): lax.ppermute(array, BOTH, [(i, i ^ bits[i % 2]) for i in range(count)])]
    unnamed x134 -> x130, local copies, waits for them, and re-layouts: 8.24 us -> 8.2 us
  transfers between devices with their start and end apart: 81 -> 81, of which waited for: 35 -> 31; matrix products, arithmetic and copies ran while one was open for 1% -> 1% of each run, Pallas kernels for 26% -> 29%
where the time goes in v7:
time: 291 us; the launch traced here: 290 us
  Pallas kernels  115 us (40%)
  waiting for transfers between devices  87.4 us (30%)
  starting transfers between devices  73 us (25%)
  local copies, waits for them, and re-layouts  11.8 us (4%)
    pallas_call x46, Pallas kernels, call(): pl.pallas_call(kernel, grid=(grid,), in_specs=[spec(*one) for one in ins]...  115 us
    ppermute x28, waiting for transfers between devices, cross(): lax.ppermute(array, BOTH, [(i, i ^ bits[i % 2]) for i in range(count)])  46.6 us
    ppermute x28, starting transfers between devices, cross(): lax.ppermute(array, BOTH, [(i, i ^ bits[i % 2]) for i in range(count)])  31.9 us
    ppermute x41, starting transfers between devices, swap(): return lax.ppermute(array, axes, [(i, i ^ bits) for i in range(count)])  29.9 us
    ppermute x12, waiting for transfers between devices, enter(): other = lax.ppermute(message, 'seq', [(i, i ^ bit) for i in range(count)])  20.8 us
    ppermute x41, waiting for transfers between devices, swap(): return lax.ppermute(array, axes, [(i, i ^ bits) for i in range(count)])  20.1 us
    ppermute x12, starting transfers between devices, enter(): other = lax.ppermute(message, 'seq', [(i, i ^ bit) for i in range(count)])  11.2 us
    unnamed x130, local copies, waits for them, and re-layouts  8.2 us
  transfers between devices with their start and end apart: 81, of which 31 were waited for; matrix products, arithmetic and copies ran while one was open for 1% of the time, Pallas kernels for 29%

profile of v7, /device:TPU:0, one launch (start us, length us, event | category | flops | bytes accessed | tf_op | source)
XLA Modules:
  0.0 289.7 jit_solution(11880764848926930976)
XLA Ops:
  1.8 5.1 %collective-permute-start.2 = (bf16[400,128]{1,0:T(8,128)(2,1)S(1)}, bf16[400,128]{1,0:T(8,128)(2,1)S(1)}, u32[]{:S(2)}, u32[]{:S(2)}) collective-permute-start(bf16[400,128]{1,0:T(8,128)(2,1)S(1)} %get-tuple-element.194.refs_0_), channel_id=1, source_target_pairs={{0,24},{4,28},{8,16},{12,20},{16,8},{20,12},{24,0},{28,4},{1,25},{... | collective-permute-start | bytes 307208 | tf_op jit(solution)/shard_map/ppermute | solution.py:710
  10.8 4.8 %collective-permute-done.1.refs_2_ = bf16[400,128]{1,0:T(8,128)(2,1)S(1)} collective-permute-done((bf16[400,128]{1,0:T(8,128)(2,1)S(1)}, bf16[400,128]{1,0:T(8,128)(2,1)S(1)}, u32[]{:S(2)}, u32[]{:S(2)}) %collective-permute-start.1) | collective-permute-done | bytes 102432 | tf_op jit(solution)/shard_map/ppermute | solution.py:710
  31.8 4.4 %collective-permute-done.13.refs_2_ = bf16[640,128]{1,0:T(8,128)(2,1)S(1)} collective-permute-done((bf16[640,128]{1,0:T(8,128)(2,1)S(1)}, bf16[640,128]{1,0:T(8,128)(2,1)S(1)}, u32[]{:S(2)}, u32[]{:S(2)}) %collective-permute-start.13) | collective-permute-done | bytes 163872 | tf_op jit(solution)/shard_map/ppermute | solution.py:710
  47.6 6.4 %gates.2 = (bf16[512,512]{1,0:T(8,128)(2,1)}, f32[512,1024]{1,0:T(8,128)}, f32[512,1024]{1,0:T(8,128)S(1)}, f32[512,1024]{1,0:T(8,128)}, bf16[512,1024]{1,0:T(8,...) custom-call(bf16[512,512]{1,0:T(8,128)(2,1)S(1)} %bitcast.56, ...), custom_call_target="tpu_custom_call" | custom-call | flops 9900000256 | bytes 1024 | tf_op jit(solution)/shard_map/gates/pallas_call | solution.py:553
  79.3 3.4 %plane_gather.5 = bf16[4,2,2,2,640,128]{5,4,3,2,1,0:T(8,128)(2,1)S(1)} custom-call(s32[8]{0:T(128)S(1)} %stack.35.pos_ref, bf16[4,640,128]{2,1,0:T(8,128)(2,1)} %copy-done, bf16[4,640,128]{2,1,0:T(8,128)(2,1)} %copy-done.32, bf16[4,640,128]{2,1,0:T(8,128)(2,1)} %copy-done.31, bf16[4,640,128]{2,1,0:T(8,128)(2,1)} %collective-permute-done.23.refs_3_, ...), custom_call_target="tpu_custom_call" | custom-call | flops 5500000256 | bytes 1024 | tf_op jit(solution)/shard_map/plane_gather/pallas_call | solution.py:553
  82.7 8.8 %mix.2 = (f32[512,1024]{1,0:T(8,128)}, bf16[512,1024]{1,0:T(8,128)(2,1)}, f32[2,8,1024]{2,1,0:T(8,128)}, f32[512,512]{1,0:T(8,128)}, bf16[512,512]{1,0:T(8,128)(...) custom-call(bf16[512,512]{1,0:T(8,128)(2,1)S(1)} %bitcast.57, ...), custom_call_target="tpu_custom_call" | custom-call | flops 15400000512 | bytes 1024 | tf_op jit(solution)/shard_map/mix/pallas_call | solution.py:553
  95.5 6.6 %collective-permute-done.33.refs_3_ = bf16[4,384,128]{2,1,0:T(8,128)(2,1)S(1)} collective-permute-done((bf16[4,384,128]{2,1,0:T(8,128)(2,1)S(1)}, bf16[4,384,128]{2,1,0:T(8,128)(2,1)S(1)}, u32[]{:S(2)}, u32[]{:S(2)}) %collective-permute-start.33) | collective-permute-done | bytes 393248 | tf_op jit(solution)/shard_map/ppermute | solution.py:737
  107.9 6.5 %gates.3 = (bf16[512,512]{1,0:T(8,128)(2,1)}, f32[512,1024]{1,0:T(8,128)}, f32[512,1024]{1,0:T(8,128)S(1)}, f32[512,1024]{1,0:T(8,128)}, bf16[512,1024]{1,0:T(8,...) custom-call(f32[512,512]{1,0:T(8,128)S(1)} %get-tuple-element.211.x_, ...), custom_call_target="tpu_custom_call" | custom-call | flops 9900000256 | bytes 1024 | tf_op jit(solution)/shard_map/gates/pallas_call | solution.py:553
  121.1 3.6 %collective-permute-done.39 = f32[4,1024]{1,0:T(4,128)S(1)} collective-permute-done((f32[4,1024]{1,0:T(4,128)S(1)}, f32[4,1024]{1,0:T(4,128)S(1)}, u32[]{:S(2)}, u32[]{:S(2)}) %collective-permute-start.39) | collective-permute-done | bytes 16416 | tf_op jit(solution)/shard_map/ppermute | solution.py:867
  133.4 3.5 %plane_gather.7 = bf16[4,2,2,2,640,128]{5,4,3,2,1,0:T(8,128)(2,1)S(1)} custom-call(s32[8]{0:T(128)S(1)} %stack.35.pos_ref, bf16[4,640,128]{2,1,0:T(8,128)(2,1)} %copy-done.1, bf16[4,640,128]{2,1,0:T(8,128)(2,1)} %collective-permute-done.41.refs_1_, bf16[4,640,128]{2,1,0:T(8,128)(2,1)} %collective-permute-done.42.refs_2_, ...), custom_call_target="tpu_custom_call" | custom-call | flops 5500000256 | bytes 1024 | tf_op jit(solution)/shard_map/plane_gather/pallas_call | solution.py:553
  136.9 7.4 %mix.3 = (f32[512,1024]{1,0:T(8,128)}, bf16[512,1024]{1,0:T(8,128)(2,1)S(1)}, f32[2,8,1024]{2,1,0:T(8,128)S(1)}, f32[512,512]{1,0:T(8,128)S(1)}, bf16[512,512]{1...) custom-call(f32[512,512]{1,0:T(8,128)S(1)} %get-tuple-element.211.x_, ...), custom_call_target="tpu_custom_call" | custom-call | flops 15400000512 | bytes 1024 | tf_op jit(solution)/shard_map/mix/pallas_call | solution.py:553
  144.3 6.9 %mlp_back.2 = (bf16[512,512]{1,0:T(8,128)(2,1)S(1)}, bf16[512,2048]{1,0:T(8,128)(2,1)S(1)}, f32[512,512]{1,0:T(8,128)S(1)}, bf16[512,512]{1,0:T(8,128)(2,1)S(1)}...) custom-call(bf16[512,512]{1,0:T(8,128)(2,1)S(1)} %bitcast.61, ...), custom_call_target="tpu_custom_call" | custom-call | flops 13200000000 | bytes 1024 | tf_op jit(solution)/shard_map/mlp_back/pallas_call | solution.py:553
  152.2 3.4 %up_weights.2 = (bf16[8,2,256,128]{3,2,1,0:T(8,128)(2,1)S(1)}, bf16[8,2,256,128]{3,2,1,0:T(8,128)(2,1)}) custom-call(s32[8]{0:T(128)S(1)} %stack.35.pos_ref, bf16[512,512]{1,0:T(8,128)(2,1)S(1)} %get-tuple-element.238.n2_ref, bf16[512,2048]{1,0:T(8,128)(2,1)S(1)} %get-tuple-element.239.gpre_ref), custom_call_target="tpu_custom_call" | custom-call | flops 5500000256 | bytes 1024 | tf_op jit(solution)/shard_map/up_weights/pallas_call | solution.py:553
  155.7 3.5 %down_weights.2 = (bf16[8,2,256,128]{3,2,1,0:T(8,128)(2,1)S(1)}, bf16[8,2,256,128]{3,2,1,0:T(8,128)(2,1)}) custom-call(s32[8]{0:T(128)S(1)} %stack.35.pos_ref, bf16[512,2048]{1,0:T(8,128)(2,1)S(1)} %get-tuple-element.243.left_ref, bf16[512,512]{1,0:T(8,128)(2,1)S(1)} %get-tuple-element.244.right_ref), custom_call_target="tpu_custom_call" | custom-call | flops 5500000256 | bytes 1024 | tf_op jit(solution)/shard_map/down_weights/pallas_call | solution.py:553
  163.1 3.6 %collective-permute-done.49 = f32[4,1024]{1,0:T(4,128)S(1)} collective-permute-done((f32[4,1024]{1,0:T(4,128)S(1)}, f32[4,1024]{1,0:T(4,128)S(1)}, u32[]{:S(2)}, u32[]{:S(2)}) %collective-permute-start.49) | collective-permute-done | bytes 16416 | tf_op jit(solution)/shard_map/ppermute | solution.py:867
  171.8 8.3 %gate_back.2 = (bf16[8,2,384,128]{3,2,1,0:T(8,128)(2,1)S(1)}, bf16[8,2,384,128]{3,2,1,0:T(8,128)(2,1)S(1)}, f32[2,1024]{1,0:T(2,128)S(1)}, f32[512,512]{1,0:T(8,128)S(1)}, f32[1,512]{1,0:T(1,128)S(1)}) custom-call(s32[8]{0:T(128)S(1)} %stack.35.pos_ref, f32[512,512]{1,0:T(8,128)S(1)} %copy-done.24, f32[2,512]{1,0:T(2,128)S(1)} %get-tuple-element.212.gain_ref, ...), custom_call_target="tpu_custom_call" | custom-call | flops 17600000000 | bytes 1024 | tf_op jit(solution)/shard_map/gate_back/pallas_call | solution.py:553
  185.9 7.8 %mlp_back.3 = (bf16[512,512]{1,0:T(8,128)(2,1)S(1)}, bf16[512,2048]{1,0:T(8,128)(2,1)S(1)}, f32[512,512]{1,0:T(8,128)S(1)}, bf16[512,512]{1,0:T(8,128)(2,1)S(1)}...) custom-call(f32[512,512]{1,0:T(8,128)S(1)} %get-tuple-element.273.g_, ...), custom_call_target="tpu_custom_call" | custom-call | flops 13200000000 | bytes 1024 | tf_op jit(solution)/shard_map/mlp_back/pallas_call | solution.py:553
  215.7 9.0 %gate_back.3 = (bf16[8,2,400,128]{3,2,1,0:T(8,128)(2,1)S(1)}, bf16[8,2,400,128]{3,2,1,0:T(8,128)(2,1)S(1)}, f32[2,1024]{1,0:T(2,128)}, bf16[512,512]{1,0:T(8,128)(2,1)S(1)}, f32[1,512]{1,0:T(1,128)}) custom-call(s32[8]{0:T(128)S(1)} %stack.35.pos_ref, bf16[512,512]{1,0:T(8,128)(2,1)S(1)} %bitcast.58, f32[2,512]{1,0:T(2,128)S(1)} %get-tuple-element.195.gain_ref, ...), custom_call_target="tpu_custom_call" | custom-call | flops 17600000000 | bytes 1024 | tf_op jit(solution)/shard_map/gate_back/pallas_call | solution.py:553
  235.8 7.2 %collective-permute-done.67.got = bf16[2,768,128]{2,1,0:T(8,128)(2,1)S(1)} collective-permute-done((bf16[2,768,128]{2,1,0:T(8,128)(2,1)S(1)}, bf16[2,768,128]{2,1,0:T(8,128)(2,1)S(1)}, u32[]{:S(2)}, u32[]{:S(2)}) %collective-permute-start.67) | collective-permute-done | bytes 393248 | tf_op jit(solution)/shard_map/ppermute | solution.py:737
  246.6 5.7 %collective-permute-done.68.refs_1_ = bf16[1,2,256,128]{3,2,1,0:T(8,128)(2,1)S(1)} collective-permute-done((bf16[1,2,256,128]{3,2,1,0:T(8,128)(2,1)S(1)}, bf16[1,2,256,128]{3,2,1,0:T(8,128)(2,1)S(1)}, u32[]{:S(2)}, u32[]{:S(2)}) %collective-permute-start.68) | collective-permute-done | bytes 131104 | tf_op jit(solution)/shard_map/ppermute | solution.py:737
  262.5 5.0 %collective-permute-done.73 = bf16[1,256,128]{2,1,0:T(8,128)(2,1)S(1)} collective-permute-done((bf16[1,256,128]{2,1,0:T(8,128)(2,1)S(1)}, bf16[1,256,128]{2,1,0:T(8,128)(2,1)S(1)}, u32[]{:S(2)}, u32[]{:S(2)}) %collective-permute-start.73) | collective-permute-done | bytes 65568 | tf_op jit(solution)/shard_map/ppermute | solution.py:737
  271.3 4.2 %collective-permute-done.77.refs_1_ = bf16[1,2,256,128]{3,2,1,0:T(8,128)(2,1)S(1)} collective-permute-done((bf16[1,2,256,128]{3,2,1,0:T(8,128)(2,1)S(1)}, bf16[1,2,256,128]{3,2,1,0:T(8,128)(2,1)S(1)}, u32[]{:S(2)}, u32[]{:S(2)}) %collective-permute-start.77) | collective-permute-done | bytes 131104 | tf_op jit(solution)/shard_map/ppermute | solution.py:737
  276.1 3.8 %collective-permute-done.78.got = bf16[2,784,128]{2,1,0:T(8,128)(2,1)S(1)} collective-permute-done((bf16[2,784,128]{2,1,0:T(8,128)(2,1)S(1)}, bf16[2,784,128]{2,1,0:T(8,128)(2,1)S(1)}, u32[]{:S(2)}, u32[]{:S(2)}) %collective-permute-start.78) | collective-permute-done | bytes 401440 | tf_op jit(solution)/shard_map/ppermute | solution.py:737
  285.0 3.7 %collective-permute-done.79.refs_3_ = bf16[784,128]{1,0:T(8,128)(2,1)S(1)} collective-permute-done((bf16[784,128]{1,0:T(8,128)(2,1)S(1)}, bf16[784,128]{1,0:T(8,128)(2,1)S(1)}, u32[]{:S(2)}, u32[]{:S(2)}) %collective-permute-start.79) | collective-permute-done | bytes 200736 | tf_op jit(solution)/shard_map/ppermute | solution.py:737
  (342 shorter events, 155.3 us)
Async XLA Ops:
  23.5 12.6 %collective-permute-start.13 = (bf16[640,128]{1,0:T(8,128)(2,1)S(1)}, bf16[640,128]{1,0:T(8,128)(2,1)S(1)}, u32[]{:S(2)}, u32[]{:S(2)}) collective-permute-start(bf16[640,128]{1,0:T(8,128)(2,1)S(1)} %get-tuple-element.204.refs_0_), channel_id=1, source_target_pairs={{0,16},{4,20},{8,24},{12,28},{16,0},{20,4},{24,8},{28,12},{1,17},{... | collective-permute-start | bytes 491528 | tf_op jit(solution)/shard_map/ppermute | solution.py:710
  23.5 12.6 %collective-permute-start.12 = (bf16[640,128]{1,0:T(8,128)(2,1)S(1)}, bf16[640,128]{1,0:T(8,128)(2,1)S(1)}, u32[]{:S(2)}, u32[]{:S(2)}) collective-permute-start(bf16[640,128]{1,0:T(8,128)(2,1)S(1)} %get-tuple-element.204.refs_0_), channel_id=1, source_target_pairs={{0,8},{4,12},{8,0},{12,4},{16,24},{20,28},{24,16},{28,20},{1,9},{5... | collective-permute-start | bytes 491528 | tf_op jit(solution)/shard_map/ppermute | solution.py:710
  38.9 22.0 %collective-permute-start.22 = (bf16[4,640,128]{2,1,0:T(8,128)(2,1)S(1)}, bf16[4,640,128]{2,1,0:T(8,128)(2,1)S(1)}, u32[]{:S(2)}, u32[]{:S(2)}) collective-permute-start(bf16[4,640,128]{2,1,0:T(8,128)(2,1)S(1)} %line_gather.5.refs_0_), channel_id=1, source_target_pairs={{0,4},{1,3},{2,6},{3,1},{4,0},{5,7},{6,2},{7,5},{8,12},{9,11},{10,... | collective-permute-start | bytes 1966088 | tf_op jit(solution)/shard_map/ppermute | solution.py:737
  39.5 21.4 %collective-permute-start.21 = (bf16[4,640,128]{2,1,0:T(8,128)(2,1)S(1)}, bf16[4,640,128]{2,1,0:T(8,128)(2,1)S(1)}, u32[]{:S(2)}, u32[]{:S(2)}) collective-permute-start(bf16[4,640,128]{2,1,0:T(8,128)(2,1)S(1)} %line_gather.5.refs_0_), channel_id=1, source_target_pairs={{0,2},{1,5},{2,0},{3,7},{4,6},{5,1},{6,4},{7,3},{8,10},{9,13},{10,... | collective-permute-start | bytes 1966088 | tf_op jit(solution)/shard_map/ppermute | solution.py:737
  40.0 13.9 %collective-permute-start.17 = (bf16[384,128]{1,0:T(8,128)(2,1)S(1)}, bf16[384,128]{1,0:T(8,128)(2,1)S(1)}, u32[]{:S(2)}, u32[]{:S(2)}) collective-permute-start(bf16[384,128]{1,0:T(8,128)(2,1)S(1)} %get-tuple-element.206.refs_0_), channel_id=1, source_target_pairs={{0,24},{4,28},{8,16},{12,20},{16,8},{20,12},{24,0},{28,4},{1,25},{... | collective-permute-start | bytes 294920 | tf_op jit(solution)/shard_map/ppermute | solution.py:710
  71.8 19.8 %collective-permute-start.32 = (bf16[640,128]{1,0:T(8,128)(2,1)S(1)}, bf16[640,128]{1,0:T(8,128)(2,1)S(1)}, u32[]{:S(2)}, u32[]{:S(2)}) collective-permute-start(bf16[640,128]{1,0:T(8,128)(2,1)S(1)} %get-tuple-element.217.refs_0_), channel_id=1, source_target_pairs={{0,24},{4,28},{8,16},{12,20},{16,8},{20,12},{24,0},{28,4},{1,25},{... | collective-permute-start | bytes 491528 | tf_op jit(solution)/shard_map/ppermute | solution.py:710
  74.1 17.5 %collective-permute-start.31 = (bf16[640,128]{1,0:T(8,128)(2,1)S(1)}, bf16[640,128]{1,0:T(8,128)(2,1)S(1)}, u32[]{:S(2)}, u32[]{:S(2)}) collective-permute-start(bf16[640,128]{1,0:T(8,128)(2,1)S(1)} %get-tuple-element.217.refs_0_), channel_id=1, source_target_pairs={{0,16},{4,20},{8,24},{12,28},{16,0},{20,4},{24,8},{28,12},{1,17},{... | collective-permute-start | bytes 491528 | tf_op jit(solution)/shard_map/ppermute | solution.py:710
  74.1 17.4 %collective-permute-start.30 = (bf16[640,128]{1,0:T(8,128)(2,1)S(1)}, bf16[640,128]{1,0:T(8,128)(2,1)S(1)}, u32[]{:S(2)}, u32[]{:S(2)}) collective-permute-start(bf16[640,128]{1,0:T(8,128)(2,1)S(1)} %get-tuple-element.217.refs_0_), channel_id=1, source_target_pairs={{0,8},{4,12},{8,0},{12,4},{16,24},{20,28},{24,16},{28,20},{1,9},{5... | collective-permute-start | bytes 491528 | tf_op jit(solution)/shard_map/ppermute | solution.py:710
  76.3 18.6 %collective-permute-start.29 = (bf16[4,384,128]{2,1,0:T(8,128)(2,1)S(1)}, bf16[4,384,128]{2,1,0:T(8,128)(2,1)S(1)}, u32[]{:S(2)}, u32[]{:S(2)}) collective-permute-start(bf16[4,384,128]{2,1,0:T(8,128)(2,1)S(1)} %line_gather.6.refs_0_), channel_id=1, source_target_pairs={{0,4},{1,3},{2,6},{3,1},{4,0},{5,7},{6,2},{7,5},{8,12},{9,11},{10,... | collective-permute-start | bytes 1179656 | tf_op jit(solution)/shard_map/ppermute | solution.py:737
  77.7 16.5 %collective-permute-start.28 = (bf16[4,384,128]{2,1,0:T(8,128)(2,1)S(1)}, bf16[4,384,128]{2,1,0:T(8,128)(2,1)S(1)}, u32[]{:S(2)}, u32[]{:S(2)}) collective-permute-start(bf16[4,384,128]{2,1,0:T(8,128)(2,1)S(1)} %line_gather.6.refs_0_), channel_id=1, source_target_pairs={{0,2},{1,5},{2,0},{3,7},{4,6},{5,1},{6,4},{7,3},{8,10},{9,13},{10,... | collective-permute-start | bytes 1179656 | tf_op jit(solution)/shard_map/ppermute | solution.py:737
  102.1 17.7 %collective-permute-start.42 = (bf16[4,640,128]{2,1,0:T(8,128)(2,1)S(1)}, bf16[4,640,128]{2,1,0:T(8,128)(2,1)}, u32[]{:S(2)}, u32[]{:S(2)}) collective-permute-start(bf16[4,640,128]{2,1,0:T(8,128)(2,1)S(1)} %line_gather.7.refs_0_), channel_id=1, source_target_pairs={{0,4},{1,3},{2,6},{3,1},{4,0},{5,7},{6,2},{7,5},{8,12},{9,11},{10,... | collective-permute-start | bytes 1966088 | tf_op jit(solution)/shard_map/ppermute | solution.py:737
  102.6 17.2 %collective-permute-start.41 = (bf16[4,640,128]{2,1,0:T(8,128)(2,1)S(1)}, bf16[4,640,128]{2,1,0:T(8,128)(2,1)}, u32[]{:S(2)}, u32[]{:S(2)}) collective-permute-start(bf16[4,640,128]{2,1,0:T(8,128)(2,1)S(1)} %line_gather.7.refs_0_), channel_id=1, source_target_pairs={{0,2},{1,5},{2,0},{3,7},{4,6},{5,1},{6,4},{7,3},{8,10},{9,13},{10,... | collective-permute-start | bytes 1966088 | tf_op jit(solution)/shard_map/ppermute | solution.py:737
  180.2 14.9 %collective-permute-start.56 = (bf16[2,1024,128]{2,1,0:T(8,128)(2,1)S(1)}, bf16[2,1024,128]{2,1,0:T(8,128)(2,1)S(1)}, u32[]{:S(2)}, u32[]{:S(2)}) collective-permute-start(bf16[2,1024,128]{2,1,0:T(8,128)(2,1)S(1)} %get-tuple-element.254), channel_id=1, source_target_pairs={{0,8},{1,17},{2,10},{3,19},{4,12},{5,21},{6,14},{7,23},{8,0},{9,25... | collective-permute-start | bytes 1572872 | tf_op jit(solution)/shard_map/ppermute | solution.py:737
  182.2 19.1 %collective-permute-start.57 = (bf16[4,2,384,128]{3,2,1,0:T(8,128)(2,1)S(1)}, bf16[4,2,384,128]{3,2,1,0:T(8,128)(2,1)S(1)}, u32[]{:S(2)}, u32[]{:S(2)}) collective-permute-start(bf16[4,2,384,128]{3,2,1,0:T(8,128)(2,1)S(1)} %get-tuple-element.256), channel_id=1, source_target_pairs={{0,2},{1,5},{2,0},{3,7},{4,6},{5,1},{6,4},{7,3},{8,10},{9,13},{10,... | collective-permute-start | bytes 2359304 | tf_op jit(solution)/shard_map/ppermute | solution.py:737
  184.6 18.0 %collective-permute-start.58 = (bf16[4,2,384,128]{3,2,1,0:T(8,128)(2,1)S(1)}, bf16[4,2,384,128]{3,2,1,0:T(8,128)(2,1)S(1)}, u32[]{:S(2)}, u32[]{:S(2)}) collective-permute-start(bf16[4,2,384,128]{3,2,1,0:T(8,128)(2,1)S(1)} %get-tuple-element.272), channel_id=1, source_target_pairs={{0,2},{1,5},{2,0},{3,7},{4,6},{5,1},{6,4},{7,3},{8,10},{9,13},{10,... | collective-permute-start | bytes 2359304 | tf_op jit(solution)/shard_map/ppermute | solution.py:737
  195.7 17.1 %collective-permute-start.60 = (bf16[1024,128]{1,0:T(8,128)(2,1)S(1)}, bf16[1024,128]{1,0:T(8,128)(2,1)S(1)}, u32[]{:S(2)}, u32[]{:S(2)}) collective-permute-start(bf16[1024,128]{1,0:T(8,128)(2,1)S(1)} %get-tuple-element.283), channel_id=1, source_target_pairs={{0,16},{1,9},{2,18},{3,11},{4,20},{5,13},{6,22},{7,15},{8,24},{9,1... | collective-permute-start | bytes 786440 | tf_op jit(solution)/shard_map/ppermute | solution.py:737
  209.7 15.0 %collective-permute-start.64 = (bf16[4,768,128]{2,1,0:T(8,128)(2,1)S(1)}, bf16[4,768,128]{2,1,0:T(8,128)(2,1)S(1)}, u32[]{:S(2)}, u32[]{:S(2)}) collective-permute-start(bf16[4,768,128]{2,1,0:T(8,128)(2,1)S(1)} %get-tuple-element.291), channel_id=1, source_target_pairs={{0,4},{1,3},{2,6},{3,1},{4,0},{5,7},{6,2},{7,5},{8,12},{9,11},{10,... | collective-permute-start | bytes 2359304 | tf_op jit(solution)/shard_map/ppermute | solution.py:737
  230.0 23.7 %collective-permute-start.70 = (bf16[4,2,400,128]{3,2,1,0:T(8,128)(2,1)S(1)}, bf16[4,2,400,128]{3,2,1,0:T(8,128)(2,1)S(1)}, u32[]{:S(2)}, u32[]{:S(2)}) collective-permute-start(bf16[4,2,400,128]{3,2,1,0:T(8,128)(2,1)S(1)} %get-tuple-element.331), channel_id=1, source_target_pairs={{0,2},{1,5},{2,0},{3,7},{4,6},{5,1},{6,4},{7,3},{8,10},{9,13},{10,... | collective-permute-start | bytes 2457608 | tf_op jit(solution)/shard_map/ppermute | solution.py:737
  230.9 22.0 %collective-permute-start.69 = (bf16[4,2,384,128]{3,2,1,0:T(8,128)(2,1)S(1)}, bf16[4,2,384,128]{3,2,1,0:T(8,128)(2,1)S(1)}, u32[]{:S(2)}, u32[]{:S(2)}) collective-permute-start(bf16[4,2,384,128]{3,2,1,0:T(8,128)(2,1)S(1)} %get-tuple-element.306), channel_id=1, source_target_pairs={{0,2},{1,5},{2,0},{3,7},{4,6},{5,1},{6,4},{7,3},{8,10},{9,13},{10,... | collective-permute-start | bytes 2359304 | tf_op jit(solution)/shard_map/ppermute | solution.py:737
  234.0 25.1 %collective-permute-start.72 = (bf16[2,1024,128]{2,1,0:T(8,128)(2,1)S(1)}, bf16[2,1024,128]{2,1,0:T(8,128)(2,1)S(1)}, u32[]{:S(2)}, u32[]{:S(2)}) collective-permute-start(bf16[2,1024,128]{2,1,0:T(8,128)(2,1)S(1)} %get-tuple-element.333), channel_id=1, source_target_pairs={{0,8},{1,17},{2,10},{3,19},{4,12},{5,21},{6,14},{7,23},{8,0},{9,25... | collective-permute-start | bytes 1572872 | tf_op jit(solution)/shard_map/ppermute | solution.py:737
  235.0 17.3 %collective-permute-start.68 = (bf16[1,2,256,128]{3,2,1,0:T(8,128)(2,1)S(1)}, bf16[1,2,256,128]{3,2,1,0:T(8,128)(2,1)S(1)}, u32[]{:S(2)}, u32[]{:S(2)}) collective-permute-start(bf16[1,2,256,128]{3,2,1,0:T(8,128)(2,1)S(1)} %get-tuple-element.304), channel_id=1, source_target_pairs={{0,2},{1,5},{2,0},{3,7},{4,6},{5,1},{6,4},{7,3},{8,10},{9,13},{10,... | collective-permute-start | bytes 393224 | tf_op jit(solution)/shard_map/ppermute | solution.py:737
  243.6 13.8 %collective-permute-start.71 = (bf16[768,128]{1,0:T(8,128)(2,1)S(1)}, bf16[768,128]{1,0:T(8,128)(2,1)S(1)}, u32[]{:S(2)}, u32[]{:S(2)}) collective-permute-start(bf16[768,128]{1,0:T(8,128)(2,1)S(1)} %get-tuple-element.339), channel_id=1, source_target_pairs={{0,16},{1,9},{2,18},{3,11},{4,20},{5,13},{6,22},{7,15},{8,24},{9,1... | collective-permute-start | bytes 589832 | tf_op jit(solution)/shard_map/ppermute | solution.py:737
  254.6 13.0 %collective-permute-start.75 = (bf16[4,400,128]{2,1,0:T(8,128)(2,1)S(1)}, bf16[4,400,128]{2,1,0:T(8,128)(2,1)S(1)}, u32[]{:S(2)}, u32[]{:S(2)}) collective-permute-start(bf16[4,400,128]{2,1,0:T(8,128)(2,1)S(1)} %get-tuple-element.345), channel_id=1, source_target_pairs={{0,4},{1,3},{2,6},{3,1},{4,0},{5,7},{6,2},{7,5},{8,12},{9,11},{10,... | collective-permute-start | bytes 1228808 | tf_op jit(solution)/shard_map/ppermute | solution.py:737
  255.4 12.2 %collective-permute-start.74 = (bf16[4,384,128]{2,1,0:T(8,128)(2,1)S(1)}, bf16[4,384,128]{2,1,0:T(8,128)(2,1)S(1)}, u32[]{:S(2)}, u32[]{:S(2)}) collective-permute-start(bf16[4,384,128]{2,1,0:T(8,128)(2,1)S(1)} %get-tuple-element.343), channel_id=1, source_target_pairs={{0,4},{1,3},{2,6},{3,1},{4,0},{5,7},{6,2},{7,5},{8,12},{9,11},{10,... | collective-permute-start | bytes 1179656 | tf_op jit(solution)/shard_map/ppermute | solution.py:737
  (122 other events, 990.3 us)

commit v8 on v7

--- a/solution.py
+++ b/solution.py
@@ -568,6 +568,10 @@
     return pltpu.with_memory_space_constraint(array, pltpu.HBM)
 
 
+def anywhere(array):
+    return array
+
+
 def whole(array):
     dims = array.shape
     return (array, dims, lambda i: (0,) * len(dims))
@@ -832,9 +836,9 @@
     return [own] + [swap(own, "seq", 2 * k) for k in range(1, 4)]
 
 
-def line_gather(pos, parts, rows):
+def line_gather(pos, parts, rows, place=anywhere):
     return call(
-        line_gather_kernel, 1, [whole(pos)] + [whole(far(p)) for p in parts],
+        line_gather_kernel, 1, [whole(pos)] + [whole(place(p)) for p in parts],
         [whole_out((4, r, LANE), BF16) for r in rows], [], 2, "line_gather",
     )
 
@@ -842,14 +846,14 @@
 X_AXIS, Y_AXIS = ("batch", 2), ("seq", 1)
 
 
-def plane_gather(pos, line, parts, behind=()):
+def plane_gather(pos, line, parts, behind=(), place=anywhere):
     rows = line.shape[1]
     parts = [line, *parts]
     parts += [swap(after(p, *behind) if behind else p, "batch", 1) for p in parts]
     each, low, high = (lambda i: (i, 0, 0)), (lambda i: (jnp.minimum(i, 1), 0, 0)), (lambda i: (jnp.maximum(i - 2, 0), 0, 0))
     maps = [each] * 4 if len(parts) == 8 else [each, each, each, low, high]
     got = call(
-        plane_gather_kernel, 4, [whole(pos)] + [(far(p), (1, rows, LANE), m) for p, m in zip(parts, maps * 2)],
+        plane_gather_kernel, 4, [whole(pos)] + [(place(p), (1, rows, LANE), m) for p, m in zip(parts, maps * 2)],
         [(shape((4, 2, 2, 2, rows, LANE), BF16), (1, 2, 2, 2, rows, LANE), lambda i: (i, 0, 0, 0, 0, 0))], [], 5, "plane_gather",
     )
     return got.reshape(NS, NB, rows, LANE)
@@ -923,14 +927,14 @@
             [whole(far(m)) for m in matrices.values()] + [whole(far(v)) for v in vectors],
             [whole_out((r, LANE), BF16) for r in rows], [pltpu.VMEM((16, LANE), F32)], 2, "pack",
         )
-        line_g0 = line_gather(pos, line_parts(packs[0]), rows[:1])
+        line_g0 = line_gather(pos, line_parts(packs[0]), rows[:1], anywhere)
         parts_g0 = [swap(line_g0, *X_AXIS), swap(line_g0, *Y_AXIS)]
         parts_g0 += [swap(parts_g0[0][:2], *Y_AXIS), swap(parts_g0[1][2:], *X_AXIS)]
         line_r0 = line_gather(pos, line_parts(after(packs[1], line_g0)), rows[1:2])
         sent_r0 = after(line_r0, *parts_g0[:2])
         parts_r0 = [cross(sent_r0, FIRST), cross(sent_r0, SECOND)]
         parts_g1 = line_parts(after(packs[2], line_r0, *parts_g0[2:]))
-        got = [plane_gather(pos, line_g0, parts_g0), None]
+        got = [plane_gather(pos, line_g0, parts_g0, (), anywhere), None]
         places = {"f": 0, "i": 1, "c": 2, "u": 0, "d": 1, "o": 4}
         view = lambda got: {m: (got[m in "udo"], slab_rows[m], places[m]) for m in "udofic"}
         weights, lines_at, parts_at = [view(got)], [line_r0], [parts_r0]
@@ -1081,13 +1085,13 @@
             grad, above, above_up = after(grad, gates.seen), mlp, upright
             above.join(gates)
             continue
-        mlp.step(above_up.step(above.step(upright.seen)))
+        mlp.step(above.step(upright.seen))
         gates.step(mlp.seen)
-        above_up.total(upright.step(above.total(gates.seen)))
+        above_up.step(upright.step(above.total(gates.seen)))
         mlp.join(gates)
-        mlp.step(above_up.parts[0])
+        mlp.step(above_up.seen)
         upright.step(mlp.seen)
-        mlp.step(upright.step())
+        mlp.step(above_up.total(upright.step()))
         sums = [(one.names, one.parts) for one in (above, above_up, mlp, upright)]
     grad_tokens = from_rows(grad)
 

time: 291 us -> 279 us (0.959)
  waiting for transfers between devices: 87.4 us -> 97.2 us
  Pallas kernels: 115 us -> 107 us
  starting transfers between devices: 73 us -> 65.9 us
  local copies, waits for them, and re-layouts: 11.8 us -> 6.7 us
    pallas_call x46, Pallas kernels: 115 us -> 107 us  [call(): pl.pallas_call(kernel, grid=(grid,), in_specs=[spec(*one) for one in ins]...]
    ppermute x28, waiting for transfers between devices: 46.6 us -> 53.2 us  [cross(): lax.ppermute(array, BOTH, [(i, i ^ bits[i % 2]) for i in range(count)])]
    unnamed x130 -> x48, local copies, waits for them, and re-layouts: 8.2 us -> 3.06 us
    ppermute x28, starting transfers between devices: 31.9 us -> 27.5 us  [cross(): lax.ppermute(array, BOTH, [(i, i ^ bits[i % 2]) for i in range(count)])]
  transfers between devices with their start and end apart: 81 -> 81, of which waited for: 31 -> 32; matrix products, arithmetic and copies ran while one was open for 1% -> 1% of each run, Pallas kernels for 29% -> 28%
where the time goes in v8:
time: 279 us
  Pallas kernels  107 us (38%)
  waiting for transfers between devices  97.2 us (35%)
  starting transfers between devices  65.9 us (24%)
  local copies, waits for them, and re-layouts  6.7 us (2%)
    pallas_call x46, Pallas kernels, call(): pl.pallas_call(kernel, grid=(grid,), in_specs=[spec(*one) for one in ins]...  107 us
    ppermute x28, waiting for transfers between devices, cross(): lax.ppermute(array, BOTH, [(i, i ^ bits[i % 2]) for i in range(count)])  53.2 us
    ppermute x41, starting transfers between devices, swap(): return lax.ppermute(array, axes, [(i, i ^ bits) for i in range(count)])  29.7 us
    ppermute x28, starting transfers between devices, cross(): lax.ppermute(array, BOTH, [(i, i ^ bits[i % 2]) for i in range(count)])  27.5 us
    ppermute x12, waiting for transfers between devices, enter(): other = lax.ppermute(message, 'seq', [(i, i ^ bit) for i in range(count)])  22.2 us
    ppermute x41, waiting for transfers between devices, swap(): return lax.ppermute(array, axes, [(i, i ^ bits) for i in range(count)])  21.7 us
    ppermute x12, starting transfers between devices, enter(): other = lax.ppermute(message, 'seq', [(i, i ^ bit) for i in range(count)])  8.73 us
  transfers between devices with their start and end apart: 81, of which 32 were waited for; matrix products, arithmetic and copies ran while one was open for 1% of the time, Pallas kernels for 28%

profile of v8, /device:TPU:0, one launch (start us, length us, event | category | flops | bytes accessed | tf_op | source)
XLA Modules:
  0.0 279.0 jit_solution(5456946014529707975)
XLA Ops:
  1.8 5.1 %collective-permute-start.2 = (bf16[400,128]{1,0:T(8,128)(2,1)S(1)}, bf16[400,128]{1,0:T(8,128)(2,1)S(1)}, u32[]{:S(2)}, u32[]{:S(2)}) collective-permute-start(bf16[400,128]{1,0:T(8,128)(2,1)S(1)} %get-tuple-element.194.refs_0_), channel_id=1, source_target_pairs={{0,24},{4,28},{8,16},{12,20},{16,8},{20,12},{24,0},{28,4},{1,25},{... | collective-permute-start | bytes 307208 | tf_op jit(solution)/shard_map/ppermute | solution.py:714
  10.7 4.8 %collective-permute-done.1.refs_2_ = bf16[400,128]{1,0:T(8,128)(2,1)S(1)} collective-permute-done((bf16[400,128]{1,0:T(8,128)(2,1)S(1)}, bf16[400,128]{1,0:T(8,128)(2,1)S(1)}, u32[]{:S(2)}, u32[]{:S(2)}) %collective-permute-start.1) | collective-permute-done | bytes 102432 | tf_op jit(solution)/shard_map/ppermute | solution.py:714
  29.9 4.6 %collective-permute-done.13.refs_2_ = bf16[640,128]{1,0:T(8,128)(2,1)S(1)} collective-permute-done((bf16[640,128]{1,0:T(8,128)(2,1)S(1)}, bf16[640,128]{1,0:T(8,128)(2,1)S(1)}, u32[]{:S(2)}, u32[]{:S(2)}) %collective-permute-start.13) | collective-permute-done | bytes 163872 | tf_op jit(solution)/shard_map/ppermute | solution.py:714
  43.1 6.4 %gates.2 = (bf16[512,512]{1,0:T(8,128)(2,1)}, f32[512,1024]{1,0:T(8,128)}, f32[512,1024]{1,0:T(8,128)S(1)}, f32[512,1024]{1,0:T(8,128)}, bf16[512,1024]{1,0:T(8,...) custom-call(bf16[512,512]{1,0:T(8,128)(2,1)S(1)} %bitcast.56, ...), custom_call_target="tpu_custom_call" | custom-call | flops 9900000256 | bytes 1024 | tf_op jit(solution)/shard_map/gates/pallas_call | solution.py:553
  56.2 3.7 %collective-permute-done.19 = f32[4,1024]{1,0:T(4,128)S(1)} collective-permute-done((f32[4,1024]{1,0:T(4,128)S(1)}, f32[4,1024]{1,0:T(4,128)S(1)}, u32[]{:S(2)}, u32[]{:S(2)}) %collective-permute-start.19) | collective-permute-done | bytes 16416 | tf_op jit(solution)/shard_map/ppermute | solution.py:871
  60.6 4.1 %collective-permute-done.20 = f32[4,1024]{1,0:T(4,128)S(1)} collective-permute-done((f32[4,1024]{1,0:T(4,128)S(1)}, f32[4,1024]{1,0:T(4,128)S(1)}, u32[]{:S(2)}, u32[]{:S(2)}) %collective-permute-start.20) | collective-permute-done | bytes 16416 | tf_op jit(solution)/shard_map/ppermute | solution.py:871
  75.0 8.9 %mix.2 = (f32[512,1024]{1,0:T(8,128)}, bf16[512,1024]{1,0:T(8,128)(2,1)}, f32[2,8,1024]{2,1,0:T(8,128)}, f32[512,512]{1,0:T(8,128)}, bf16[512,512]{1,0:T(8,128)(...) custom-call(bf16[512,512]{1,0:T(8,128)(2,1)S(1)} %bitcast.57, ...), custom_call_target="tpu_custom_call" | custom-call | flops 15400000512 | bytes 1024 | tf_op jit(solution)/shard_map/mix/pallas_call | solution.py:553
  85.7 6.7 %collective-permute-done.33.refs_3_ = bf16[4,384,128]{2,1,0:T(8,128)(2,1)S(1)} collective-permute-done((bf16[4,384,128]{2,1,0:T(8,128)(2,1)S(1)}, bf16[4,384,128]{2,1,0:T(8,128)(2,1)S(1)}, u32[]{:S(2)}, u32[]{:S(2)}) %collective-permute-start.33) | collective-permute-done | bytes 393248 | tf_op jit(solution)/shard_map/ppermute | solution.py:741
  95.0 6.5 %gates.3 = (bf16[512,512]{1,0:T(8,128)(2,1)}, f32[512,1024]{1,0:T(8,128)}, f32[512,1024]{1,0:T(8,128)S(1)}, f32[512,1024]{1,0:T(8,128)}, bf16[512,1024]{1,0:T(8,...) custom-call(f32[512,512]{1,0:T(8,128)S(1)} %get-tuple-element.211.x_, ...), custom_call_target="tpu_custom_call" | custom-call | flops 9900000256 | bytes 1024 | tf_op jit(solution)/shard_map/gates/pallas_call | solution.py:553
  103.8 6.2 %collective-permute-done.42.refs_2_ = bf16[4,640,128]{2,1,0:T(8,128)(2,1)S(1)} collective-permute-done((bf16[4,640,128]{2,1,0:T(8,128)(2,1)S(1)}, bf16[4,640,128]{2,1,0:T(8,128)(2,1)S(1)}, u32[]{:S(2)}, u32[]{:S(2)}) %collective-permute-start.42) | collective-permute-done | bytes 655392 | tf_op jit(solution)/shard_map/ppermute | solution.py:741
  110.9 3.7 %collective-permute-done.39 = f32[4,1024]{1,0:T(4,128)S(1)} collective-permute-done((f32[4,1024]{1,0:T(4,128)S(1)}, f32[4,1024]{1,0:T(4,128)S(1)}, u32[]{:S(2)}, u32[]{:S(2)}) %collective-permute-start.39) | collective-permute-done | bytes 16416 | tf_op jit(solution)/shard_map/ppermute | solution.py:871
  115.8 3.5 %collective-permute-done.40 = f32[4,1024]{1,0:T(4,128)S(1)} collective-permute-done((f32[4,1024]{1,0:T(4,128)S(1)}, f32[4,1024]{1,0:T(4,128)S(1)}, u32[]{:S(2)}, u32[]{:S(2)}) %collective-permute-start.40) | collective-permute-done | bytes 16416 | tf_op jit(solution)/shard_map/ppermute | solution.py:871
  126.7 7.3 %mix.3 = (f32[512,1024]{1,0:T(8,128)}, bf16[512,1024]{1,0:T(8,128)(2,1)S(1)}, f32[2,8,1024]{2,1,0:T(8,128)S(1)}, f32[512,512]{1,0:T(8,128)S(1)}, bf16[512,512]{1...) custom-call(f32[512,512]{1,0:T(8,128)S(1)} %copy-done.16, ...), custom_call_target="tpu_custom_call" | custom-call | flops 15400000512 | bytes 1024 | tf_op jit(solution)/shard_map/mix/pallas_call | solution.py:553
  134.0 6.9 %mlp_back.2 = (bf16[512,512]{1,0:T(8,128)(2,1)S(1)}, bf16[512,2048]{1,0:T(8,128)(2,1)S(1)}, f32[512,512]{1,0:T(8,128)S(1)}, bf16[512,512]{1,0:T(8,128)(2,1)S(1)}...) custom-call(bf16[512,512]{1,0:T(8,128)(2,1)S(1)} %bitcast.61, ...), custom_call_target="tpu_custom_call" | custom-call | flops 13200000000 | bytes 1024 | tf_op jit(solution)/shard_map/mlp_back/pallas_call | solution.py:553
  145.0 3.5 %down_weights.2 = (bf16[8,2,256,128]{3,2,1,0:T(8,128)(2,1)S(1)}, bf16[8,2,256,128]{3,2,1,0:T(8,128)(2,1)}) custom-call(s32[8]{0:T(128)S(1)} %stack.35.pos_ref, bf16[512,2048]{1,0:T(8,128)(2,1)S(1)} %get-tuple-element.243.left_ref, bf16[512,512]{1,0:T(8,128)(2,1)S(1)} %get-tuple-element.244.right_ref), custom_call_target="tpu_custom_call" | custom-call | flops 5500000256 | bytes 1024 | tf_op jit(solution)/shard_map/down_weights/pallas_call | solution.py:553
  152.3 3.7 %collective-permute-done.49 = f32[4,1024]{1,0:T(4,128)S(1)} collective-permute-done((f32[4,1024]{1,0:T(4,128)S(1)}, f32[4,1024]{1,0:T(4,128)S(1)}, u32[]{:S(2)}, u32[]{:S(2)}) %collective-permute-start.49) | collective-permute-done | bytes 16416 | tf_op jit(solution)/shard_map/ppermute | solution.py:871
  160.9 8.3 %gate_back.2 = (bf16[8,2,384,128]{3,2,1,0:T(8,128)(2,1)S(1)}, bf16[8,2,384,128]{3,2,1,0:T(8,128)(2,1)S(1)}, f32[2,1024]{1,0:T(2,128)S(1)}, f32[512,512]{1,0:T(8,128)S(1)}, f32[1,512]{1,0:T(1,128)S(1)}) custom-call(s32[8]{0:T(128)S(1)} %stack.35.pos_ref, f32[512,512]{1,0:T(8,128)S(1)} %copy-done.17, f32[2,512]{1,0:T(2,128)S(1)} %get-tuple-element.212.gain_ref, ...), custom_call_target="tpu_custom_call" | custom-call | flops 17600000000 | bytes 1024 | tf_op jit(solution)/shard_map/gate_back/pallas_call | solution.py:553
  174.4 7.6 %mlp_back.3 = (bf16[512,512]{1,0:T(8,128)(2,1)S(1)}, bf16[512,2048]{1,0:T(8,128)(2,1)S(1)}, f32[512,512]{1,0:T(8,128)S(1)}, bf16[512,512]{1,0:T(8,128)(2,1)S(1)}...) custom-call(f32[512,512]{1,0:T(8,128)S(1)} %get-tuple-element.273.g_, ...), custom_call_target="tpu_custom_call" | custom-call | flops 13200000000 | bytes 1024 | tf_op jit(solution)/shard_map/mlp_back/pallas_call | solution.py:553
  205.0 9.0 %gate_back.3 = (bf16[8,2,400,128]{3,2,1,0:T(8,128)(2,1)S(1)}, bf16[8,2,400,128]{3,2,1,0:T(8,128)(2,1)S(1)}, f32[2,1024]{1,0:T(2,128)}, bf16[512,512]{1,0:T(8,128)(2,1)S(1)}, f32[1,512]{1,0:T(1,128)}) custom-call(s32[8]{0:T(128)S(1)} %stack.35.pos_ref, bf16[512,512]{1,0:T(8,128)(2,1)S(1)} %bitcast.58, f32[2,512]{1,0:T(2,128)S(1)} %get-tuple-element.195.gain_ref, ...), custom_call_target="tpu_custom_call" | custom-call | flops 17600000000 | bytes 1024 | tf_op jit(solution)/shard_map/gate_back/pallas_call | solution.py:553
  224.3 8.5 %collective-permute-done.67.got = bf16[2,768,128]{2,1,0:T(8,128)(2,1)S(1)} collective-permute-done((bf16[2,768,128]{2,1,0:T(8,128)(2,1)S(1)}, bf16[2,768,128]{2,1,0:T(8,128)(2,1)S(1)}, u32[]{:S(2)}, u32[]{:S(2)}) %collective-permute-start.67) | collective-permute-done | bytes 393248 | tf_op jit(solution)/shard_map/ppermute | solution.py:741
  236.0 4.2 %collective-permute-done.68.refs_1_ = bf16[4,2,384,128]{3,2,1,0:T(8,128)(2,1)S(1)} collective-permute-done((bf16[4,2,384,128]{3,2,1,0:T(8,128)(2,1)S(1)}, bf16[4,2,384,128]{3,2,1,0:T(8,128)(2,1)S(1)}, u32[]{:S(2)}, u32[]{:S(2)}) %collective-permute-start.68) | collective-permute-done | bytes 786464 | tf_op jit(solution)/shard_map/ppermute | solution.py:741
  251.1 4.9 %collective-permute-done.72.refs_1_ = bf16[1,2,256,128]{3,2,1,0:T(8,128)(2,1)S(1)} collective-permute-done((bf16[1,2,256,128]{3,2,1,0:T(8,128)(2,1)S(1)}, bf16[1,2,256,128]{3,2,1,0:T(8,128)(2,1)S(1)}, u32[]{:S(2)}, u32[]{:S(2)}) %collective-permute-start.72) | collective-permute-done | bytes 131104 | tf_op jit(solution)/shard_map/ppermute | solution.py:741
  260.6 4.2 %collective-permute-done.76.refs_1_ = bf16[1,2,256,128]{3,2,1,0:T(8,128)(2,1)S(1)} collective-permute-done((bf16[1,2,256,128]{3,2,1,0:T(8,128)(2,1)S(1)}, bf16[1,2,256,128]{3,2,1,0:T(8,128)(2,1)S(1)}, u32[]{:S(2)}, u32[]{:S(2)}) %collective-permute-start.76) | collective-permute-done | bytes 131104 | tf_op jit(solution)/shard_map/ppermute | solution.py:741
  265.4 4.0 %collective-permute-done.78.got = bf16[2,784,128]{2,1,0:T(8,128)(2,1)S(1)} collective-permute-done((bf16[2,784,128]{2,1,0:T(8,128)(2,1)S(1)}, bf16[2,784,128]{2,1,0:T(8,128)(2,1)S(1)}, u32[]{:S(2)}, u32[]{:S(2)}) %collective-permute-start.78) | collective-permute-done | bytes 401440 | tf_op jit(solution)/shard_map/ppermute | solution.py:741
  (260 shorter events, 141.3 us)
Async XLA Ops:
  21.7 12.8 %collective-permute-start.13 = (bf16[640,128]{1,0:T(8,128)(2,1)S(1)}, bf16[640,128]{1,0:T(8,128)(2,1)S(1)}, u32[]{:S(2)}, u32[]{:S(2)}) collective-permute-start(bf16[640,128]{1,0:T(8,128)(2,1)S(1)} %get-tuple-element.204.refs_0_), channel_id=1, source_target_pairs={{0,16},{4,20},{8,24},{12,28},{16,0},{20,4},{24,8},{28,12},{1,17},{... | collective-permute-start | bytes 491528 | tf_op jit(solution)/shard_map/ppermute | solution.py:714
  21.7 12.8 %collective-permute-start.12 = (bf16[640,128]{1,0:T(8,128)(2,1)S(1)}, bf16[640,128]{1,0:T(8,128)(2,1)S(1)}, u32[]{:S(2)}, u32[]{:S(2)}) collective-permute-start(bf16[640,128]{1,0:T(8,128)(2,1)S(1)} %get-tuple-element.204.refs_0_), channel_id=1, source_target_pairs={{0,8},{4,12},{8,0},{12,4},{16,24},{20,28},{24,16},{28,20},{1,9},{5... | collective-permute-start | bytes 491528 | tf_op jit(solution)/shard_map/ppermute | solution.py:714
  36.5 18.1 %collective-permute-start.22 = (bf16[4,640,128]{2,1,0:T(8,128)(2,1)S(1)}, bf16[4,640,128]{2,1,0:T(8,128)(2,1)S(1)}, u32[]{:S(2)}, u32[]{:S(2)}) collective-permute-start(bf16[4,640,128]{2,1,0:T(8,128)(2,1)S(1)} %line_gather.5.refs_0_), channel_id=1, source_target_pairs={{0,4},{1,3},{2,6},{3,1},{4,0},{5,7},{6,2},{7,5},{8,12},{9,11},{10,... | collective-permute-start | bytes 1966088 | tf_op jit(solution)/shard_map/ppermute | solution.py:741
  37.1 17.5 %collective-permute-start.21 = (bf16[4,640,128]{2,1,0:T(8,128)(2,1)S(1)}, bf16[4,640,128]{2,1,0:T(8,128)(2,1)S(1)}, u32[]{:S(2)}, u32[]{:S(2)}) collective-permute-start(bf16[4,640,128]{2,1,0:T(8,128)(2,1)S(1)} %line_gather.5.refs_0_), channel_id=1, source_target_pairs={{0,2},{1,5},{2,0},{3,7},{4,6},{5,1},{6,4},{7,3},{8,10},{9,13},{10,... | collective-permute-start | bytes 1966088 | tf_op jit(solution)/shard_map/ppermute | solution.py:741
  37.6 11.8 %collective-permute-start.17 = (bf16[384,128]{1,0:T(8,128)(2,1)S(1)}, bf16[384,128]{1,0:T(8,128)(2,1)S(1)}, u32[]{:S(2)}, u32[]{:S(2)}) collective-permute-start(bf16[384,128]{1,0:T(8,128)(2,1)S(1)} %get-tuple-element.206.refs_0_), channel_id=1, source_target_pairs={{0,24},{4,28},{8,16},{12,20},{16,8},{20,12},{24,0},{28,4},{1,25},{... | collective-permute-start | bytes 294920 | tf_op jit(solution)/shard_map/ppermute | solution.py:714
  65.4 18.5 %collective-permute-start.32 = (bf16[640,128]{1,0:T(8,128)(2,1)S(1)}, bf16[640,128]{1,0:T(8,128)(2,1)S(1)}, u32[]{:S(2)}, u32[]{:S(2)}) collective-permute-start(bf16[640,128]{1,0:T(8,128)(2,1)S(1)} %get-tuple-element.217.refs_0_), channel_id=1, source_target_pairs={{0,24},{4,28},{8,16},{12,20},{16,8},{20,12},{24,0},{28,4},{1,25},{... | collective-permute-start | bytes 491528 | tf_op jit(solution)/shard_map/ppermute | solution.py:714
  67.4 16.5 %collective-permute-start.31 = (bf16[640,128]{1,0:T(8,128)(2,1)S(1)}, bf16[640,128]{1,0:T(8,128)(2,1)S(1)}, u32[]{:S(2)}, u32[]{:S(2)}) collective-permute-start(bf16[640,128]{1,0:T(8,128)(2,1)S(1)} %get-tuple-element.217.refs_0_), channel_id=1, source_target_pairs={{0,16},{4,20},{8,24},{12,28},{16,0},{20,4},{24,8},{28,12},{1,17},{... | collective-permute-start | bytes 491528 | tf_op jit(solution)/shard_map/ppermute | solution.py:714
  67.4 16.5 %collective-permute-start.30 = (bf16[640,128]{1,0:T(8,128)(2,1)S(1)}, bf16[640,128]{1,0:T(8,128)(2,1)S(1)}, u32[]{:S(2)}, u32[]{:S(2)}) collective-permute-start(bf16[640,128]{1,0:T(8,128)(2,1)S(1)} %get-tuple-element.217.refs_0_), channel_id=1, source_target_pairs={{0,8},{4,12},{8,0},{12,4},{16,24},{20,28},{24,16},{28,20},{1,9},{5... | collective-permute-start | bytes 491528 | tf_op jit(solution)/shard_map/ppermute | solution.py:714
  69.8 15.4 %collective-permute-start.29 = (bf16[4,384,128]{2,1,0:T(8,128)(2,1)S(1)}, bf16[4,384,128]{2,1,0:T(8,128)(2,1)S(1)}, u32[]{:S(2)}, u32[]{:S(2)}) collective-permute-start(bf16[4,384,128]{2,1,0:T(8,128)(2,1)S(1)} %line_gather.6.refs_0_), channel_id=1, source_target_pairs={{0,4},{1,3},{2,6},{3,1},{4,0},{5,7},{6,2},{7,5},{8,12},{9,11},{10,... | collective-permute-start | bytes 1179656 | tf_op jit(solution)/shard_map/ppermute | solution.py:741
  71.3 13.2 %collective-permute-start.28 = (bf16[4,384,128]{2,1,0:T(8,128)(2,1)S(1)}, bf16[4,384,128]{2,1,0:T(8,128)(2,1)S(1)}, u32[]{:S(2)}, u32[]{:S(2)}) collective-permute-start(bf16[4,384,128]{2,1,0:T(8,128)(2,1)S(1)} %line_gather.6.refs_0_), channel_id=1, source_target_pairs={{0,2},{1,5},{2,0},{3,7},{4,6},{5,1},{6,4},{7,3},{8,10},{9,13},{10,... | collective-permute-start | bytes 1179656 | tf_op jit(solution)/shard_map/ppermute | solution.py:741
  92.4 17.6 %collective-permute-start.42 = (bf16[4,640,128]{2,1,0:T(8,128)(2,1)S(1)}, bf16[4,640,128]{2,1,0:T(8,128)(2,1)S(1)}, u32[]{:S(2)}, u32[]{:S(2)}) collective-permute-start(bf16[4,640,128]{2,1,0:T(8,128)(2,1)S(1)} %line_gather.7.refs_0_), channel_id=1, source_target_pairs={{0,4},{1,3},{2,6},{3,1},{4,0},{5,7},{6,2},{7,5},{8,12},{9,11},{10,... | collective-permute-start | bytes 1966088 | tf_op jit(solution)/shard_map/ppermute | solution.py:741
  93.0 17.0 %collective-permute-start.41 = (bf16[4,640,128]{2,1,0:T(8,128)(2,1)S(1)}, bf16[4,640,128]{2,1,0:T(8,128)(2,1)S(1)}, u32[]{:S(2)}, u32[]{:S(2)}) collective-permute-start(bf16[4,640,128]{2,1,0:T(8,128)(2,1)S(1)} %line_gather.7.refs_0_), channel_id=1, source_target_pairs={{0,2},{1,5},{2,0},{3,7},{4,6},{5,1},{6,4},{7,3},{8,10},{9,13},{10,... | collective-permute-start | bytes 1966088 | tf_op jit(solution)/shard_map/ppermute | solution.py:741
  169.3 14.9 %collective-permute-start.56 = (bf16[2,1024,128]{2,1,0:T(8,128)(2,1)S(1)}, bf16[2,1024,128]{2,1,0:T(8,128)(2,1)S(1)}, u32[]{:S(2)}, u32[]{:S(2)}) collective-permute-start(bf16[2,1024,128]{2,1,0:T(8,128)(2,1)S(1)} %get-tuple-element.254), channel_id=1, source_target_pairs={{0,8},{1,17},{2,10},{3,19},{4,12},{5,21},{6,14},{7,23},{8,0},{9,25... | collective-permute-start | bytes 1572872 | tf_op jit(solution)/shard_map/ppermute | solution.py:741
  171.3 19.0 %collective-permute-start.57 = (bf16[4,2,384,128]{3,2,1,0:T(8,128)(2,1)S(1)}, bf16[4,2,384,128]{3,2,1,0:T(8,128)(2,1)S(1)}, u32[]{:S(2)}, u32[]{:S(2)}) collective-permute-start(bf16[4,2,384,128]{3,2,1,0:T(8,128)(2,1)S(1)} %get-tuple-element.256), channel_id=1, source_target_pairs={{0,2},{1,5},{2,0},{3,7},{4,6},{5,1},{6,4},{7,3},{8,10},{9,13},{10,... | collective-permute-start | bytes 2359304 | tf_op jit(solution)/shard_map/ppermute | solution.py:741
  173.7 18.0 %collective-permute-start.58 = (bf16[4,2,384,128]{3,2,1,0:T(8,128)(2,1)S(1)}, bf16[4,2,384,128]{3,2,1,0:T(8,128)(2,1)S(1)}, u32[]{:S(2)}, u32[]{:S(2)}) collective-permute-start(bf16[4,2,384,128]{3,2,1,0:T(8,128)(2,1)S(1)} %get-tuple-element.272), channel_id=1, source_target_pairs={{0,2},{1,5},{2,0},{3,7},{4,6},{5,1},{6,4},{7,3},{8,10},{9,13},{10,... | collective-permute-start | bytes 2359304 | tf_op jit(solution)/shard_map/ppermute | solution.py:741
  184.8 17.4 %collective-permute-start.60 = (bf16[1024,128]{1,0:T(8,128)(2,1)S(1)}, bf16[1024,128]{1,0:T(8,128)(2,1)S(1)}, u32[]{:S(2)}, u32[]{:S(2)}) collective-permute-start(bf16[1024,128]{1,0:T(8,128)(2,1)S(1)} %get-tuple-element.283), channel_id=1, source_target_pairs={{0,16},{1,9},{2,18},{3,11},{4,20},{5,13},{6,22},{7,15},{8,24},{9,1... | collective-permute-start | bytes 786440 | tf_op jit(solution)/shard_map/ppermute | solution.py:741
  198.8 15.2 %collective-permute-start.64 = (bf16[4,768,128]{2,1,0:T(8,128)(2,1)S(1)}, bf16[4,768,128]{2,1,0:T(8,128)(2,1)S(1)}, u32[]{:S(2)}, u32[]{:S(2)}) collective-permute-start(bf16[4,768,128]{2,1,0:T(8,128)(2,1)S(1)} %get-tuple-element.291), channel_id=1, source_target_pairs={{0,4},{1,3},{2,6},{3,1},{4,0},{5,7},{6,2},{7,5},{8,12},{9,11},{10,... | collective-permute-start | bytes 2359304 | tf_op jit(solution)/shard_map/ppermute | solution.py:741
  219.3 21.7 %collective-permute-start.69 = (bf16[4,2,400,128]{3,2,1,0:T(8,128)(2,1)S(1)}, bf16[4,2,400,128]{3,2,1,0:T(8,128)(2,1)S(1)}, u32[]{:S(2)}, u32[]{:S(2)}) collective-permute-start(bf16[4,2,400,128]{3,2,1,0:T(8,128)(2,1)S(1)} %get-tuple-element.331), channel_id=1, source_target_pairs={{0,2},{1,5},{2,0},{3,7},{4,6},{5,1},{6,4},{7,3},{8,10},{9,13},{10,... | collective-permute-start | bytes 2457608 | tf_op jit(solution)/shard_map/ppermute | solution.py:741
  219.4 20.7 %collective-permute-start.68 = (bf16[4,2,384,128]{3,2,1,0:T(8,128)(2,1)S(1)}, bf16[4,2,384,128]{3,2,1,0:T(8,128)(2,1)S(1)}, u32[]{:S(2)}, u32[]{:S(2)}) collective-permute-start(bf16[4,2,384,128]{3,2,1,0:T(8,128)(2,1)S(1)} %get-tuple-element.306), channel_id=1, source_target_pairs={{0,2},{1,5},{2,0},{3,7},{4,6},{5,1},{6,4},{7,3},{8,10},{9,13},{10,... | collective-permute-start | bytes 2359304 | tf_op jit(solution)/shard_map/ppermute | solution.py:741
  223.6 24.8 %collective-permute-start.71 = (bf16[2,1024,128]{2,1,0:T(8,128)(2,1)S(1)}, bf16[2,1024,128]{2,1,0:T(8,128)(2,1)S(1)}, u32[]{:S(2)}, u32[]{:S(2)}) collective-permute-start(bf16[2,1024,128]{2,1,0:T(8,128)(2,1)S(1)} %get-tuple-element.333), channel_id=1, source_target_pairs={{0,8},{1,17},{2,10},{3,19},{4,12},{5,21},{6,14},{7,23},{8,0},{9,25... | collective-permute-start | bytes 1572872 | tf_op jit(solution)/shard_map/ppermute | solution.py:741
  233.5 13.4 %collective-permute-start.70 = (bf16[768,128]{1,0:T(8,128)(2,1)S(1)}, bf16[768,128]{1,0:T(8,128)(2,1)S(1)}, u32[]{:S(2)}, u32[]{:S(2)}) collective-permute-start(bf16[768,128]{1,0:T(8,128)(2,1)S(1)} %get-tuple-element.338), channel_id=1, source_target_pairs={{0,16},{1,9},{2,18},{3,11},{4,20},{5,13},{6,22},{7,15},{8,24},{9,1... | collective-permute-start | bytes 589832 | tf_op jit(solution)/shard_map/ppermute | solution.py:741
  241.9 14.8 %collective-permute-start.74 = (bf16[4,400,128]{2,1,0:T(8,128)(2,1)S(1)}, bf16[4,400,128]{2,1,0:T(8,128)(2,1)S(1)}, u32[]{:S(2)}, u32[]{:S(2)}) collective-permute-start(bf16[4,400,128]{2,1,0:T(8,128)(2,1)S(1)} %get-tuple-element.342), channel_id=1, source_target_pairs={{0,4},{1,3},{2,6},{3,1},{4,0},{5,7},{6,2},{7,5},{8,12},{9,11},{10,... | collective-permute-start | bytes 1228808 | tf_op jit(solution)/shard_map/ppermute | solution.py:741
  242.5 14.1 %collective-permute-start.73 = (bf16[4,384,128]{2,1,0:T(8,128)(2,1)S(1)}, bf16[4,384,128]{2,1,0:T(8,128)(2,1)S(1)}, u32[]{:S(2)}, u32[]{:S(2)}) collective-permute-start(bf16[4,384,128]{2,1,0:T(8,128)(2,1)S(1)} %get-tuple-element.340), channel_id=1, source_target_pairs={{0,4},{1,3},{2,6},{3,1},{4,0},{5,7},{6,2},{7,5},{8,12},{9,11},{10,... | collective-permute-start | bytes 1179656 | tf_op jit(solution)/shard_map/ppermute | solution.py:741
  257.4 12.1 %collective-permute-start.78 = (bf16[2,784,128]{2,1,0:T(8,128)(2,1)S(1)}, bf16[2,784,128]{2,1,0:T(8,128)(2,1)S(1)}, u32[]{:S(2)}, u32[]{:S(2)}) collective-permute-start(bf16[2,784,128]{2,1,0:T(8,128)(2,1)S(1)} %get-tuple-element.355), channel_id=1, source_target_pairs={{0,8},{1,17},{2,10},{3,19},{4,12},{5,21},{6,14},{7,23},{8,0},{9,25... | collective-permute-start | bytes 1204232 | tf_op jit(solution)/shard_map/ppermute | solution.py:741
  (81 other events, 536.9 us)

commit v9 on v8

--- a/solution.py
+++ b/solution.py
@@ -365,12 +365,13 @@
 
 
 def put_columns(pos_ref, keep_ref, send_ref, start, value):
-    rows, width = value.shape[0] // NS, value.shape[1] // 2
-    x = pl.program_id(0)
-    for core in range(2):
+    count = NB // pl.num_programs(0)
+    rows, width = value.shape[0] // NS, value.shape[1] // count
+    for block in range(count):
+        x, core = pl.program_id(0) * (count // 2) + block // 2, block % 2
         parts = [
             value[:, left : left + LANE].astype(BF16).reshape(NS, rows, LANE)
-            for left in range(core * width, (core + 1) * width, LANE)
+            for left in range(block * width, (block + 1) * width, LANE)
         ]
 
         def put(ref):
@@ -381,7 +382,7 @@
 
 
 def put_rows(pos_ref, keep_ref, send_ref, value):
-    count = NS // STEPS
+    count = NS // pl.num_programs(0)
     for j in range(NB):
         part = value[:, j * LANE : (j + 1) * LANE].astype(BF16).reshape(count, -1, LANE)
 
@@ -692,10 +693,10 @@
 
 
 def up_weights(sz, pos, n2, gpre):
-    n, d, ff, f = sz.n, sz.d, sz.ff, sz.fb
+    n, d, ff = sz.n, sz.d, sz.ff
     dims = (NS, 2, d * ff // (32 * LANE), LANE)
     return call(
-        up_weight_kernel, STEPS, [whole(pos), whole(n2), (gpre, (n, f), lambda i: (0, i))],
+        up_weight_kernel, 1, [whole(pos), whole(n2), whole(gpre)],
         [whole_out(dims, BF16)] * 2, [], 5, "up_weights",
     )
 
@@ -704,7 +705,7 @@
     n, k, d = sz.n, left.shape[1], sz.d
     dims = (NS, 2, k // NS, LANE)
     return call(
-        row_weight_kernel, STEPS, [whole(pos), (left, (n, k // STEPS), lambda i: (0, i)), whole(right)],
+        row_weight_kernel, 1, [whole(pos), whole(left), whole(right)],
         [whole_out(dims, BF16)] * 2, [], 5, name,
     )
 
@@ -981,8 +982,8 @@
                 if step == 0:
                     return [line_g1] if l + 1 < LAYERS else []
                 if step == 1:
-                    diagonals.append(cross(after(near, other, beside), SECOND))
-                return []
+                    diagonals.append(cross(after(near, other, *([beside] if l == 0 else [])), SECOND))
+                return [beside] if step == 2 and l else []
 
             ent, _ = enter(fin, seqs, False, (), hold)
             diagonal = diagonals[l] = after(diagonals[l], ent)

time: 279 us -> 283 us (1.014); the launches traced: 279 us -> 280 us
    ppermute x28, waiting for transfers between devices: 53.2 us -> 49.4 us  [cross(): lax.ppermute(array, BOTH, [(i, i ^ bits[i % 2]) for i in range(count)])]
    ppermute x28, starting transfers between devices: 27.5 us -> 30.7 us  [cross(): lax.ppermute(array, BOTH, [(i, i ^ bits[i % 2]) for i in range(count)])]
where the time goes in v9:
time: 283 us; the launch traced here: 280 us
  Pallas kernels  108 us (38%)
  waiting for transfers between devices  94.6 us (33%)
  starting transfers between devices  68.7 us (24%)
  local copies, waits for them, and re-layouts  6.7 us (2%)
    pallas_call x46, Pallas kernels, call(): pl.pallas_call(kernel, grid=(grid,), in_specs=[spec(*one) for one in ins]...  108 us
    ppermute x28, waiting for transfers between devices, cross(): lax.ppermute(array, BOTH, [(i, i ^ bits[i % 2]) for i in range(count)])  49.4 us
    ppermute x28, starting transfers between devices, cross(): lax.ppermute(array, BOTH, [(i, i ^ bits[i % 2]) for i in range(count)])  30.7 us
    ppermute x41, starting transfers between devices, swap(): return lax.ppermute(array, axes, [(i, i ^ bits) for i in range(count)])  29.7 us
    ppermute x12, waiting for transfers between devices, enter(): other = lax.ppermute(message, 'seq', [(i, i ^ bit) for i in range(count)])  23.5 us
    ppermute x41, waiting for transfers between devices, swap(): return lax.ppermute(array, axes, [(i, i ^ bits) for i in range(count)])  21.7 us
    ppermute x12, starting transfers between devices, enter(): other = lax.ppermute(message, 'seq', [(i, i ^ bit) for i in range(count)])  8.36 us
  transfers between devices with their start and end apart: 81, of which 32 were waited for; matrix products, arithmetic and copies ran while one was open for 1% of the time, Pallas kernels for 28%

profile of v9, /device:TPU:0, one launch (start us, length us, event | category | flops | bytes accessed | tf_op | source)
XLA Modules:
  0.0 279.8 jit_solution(10234994501224146565)
XLA Ops:
  1.8 5.1 %collective-permute-start.2 = (bf16[400,128]{1,0:T(8,128)(2,1)S(1)}, bf16[400,128]{1,0:T(8,128)(2,1)S(1)}, u32[]{:S(2)}, u32[]{:S(2)}) collective-permute-start(bf16[400,128]{1,0:T(8,128)(2,1)S(1)} %get-tuple-element.195.refs_0_), channel_id=1, source_target_pairs={{0,24},{4,28},{8,16},{12,20},{16,8},{20,12},{24,0},{28,4},{1,25},{... | collective-permute-start | bytes 307208 | tf_op jit(solution)/shard_map/ppermute | solution.py:715
  10.7 4.8 %collective-permute-done.1.refs_2_ = bf16[400,128]{1,0:T(8,128)(2,1)S(1)} collective-permute-done((bf16[400,128]{1,0:T(8,128)(2,1)S(1)}, bf16[400,128]{1,0:T(8,128)(2,1)S(1)}, u32[]{:S(2)}, u32[]{:S(2)}) %collective-permute-start.1) | collective-permute-done | bytes 102432 | tf_op jit(solution)/shard_map/ppermute | solution.py:715
  29.9 4.6 %collective-permute-done.13.refs_2_ = bf16[640,128]{1,0:T(8,128)(2,1)S(1)} collective-permute-done((bf16[640,128]{1,0:T(8,128)(2,1)S(1)}, bf16[640,128]{1,0:T(8,128)(2,1)S(1)}, u32[]{:S(2)}, u32[]{:S(2)}) %collective-permute-start.13) | collective-permute-done | bytes 163872 | tf_op jit(solution)/shard_map/ppermute | solution.py:715
  43.6 6.4 %gates.2 = (bf16[512,512]{1,0:T(8,128)(2,1)}, f32[512,1024]{1,0:T(8,128)}, f32[512,1024]{1,0:T(8,128)S(1)}, f32[512,1024]{1,0:T(8,128)}, bf16[512,1024]{1,0:T(8,...) custom-call(bf16[512,512]{1,0:T(8,128)(2,1)S(1)} %bitcast.56, ...), custom_call_target="tpu_custom_call" | custom-call | flops 9900000256 | bytes 1024 | tf_op jit(solution)/shard_map/gates/pallas_call | solution.py:554
  56.8 3.7 %collective-permute-done.19 = f32[4,1024]{1,0:T(4,128)S(1)} collective-permute-done((f32[4,1024]{1,0:T(4,128)S(1)}, f32[4,1024]{1,0:T(4,128)S(1)}, u32[]{:S(2)}, u32[]{:S(2)}) %collective-permute-start.19) | collective-permute-done | bytes 16416 | tf_op jit(solution)/shard_map/ppermute | solution.py:872
  61.1 4.1 %collective-permute-done.20 = f32[4,1024]{1,0:T(4,128)S(1)} collective-permute-done((f32[4,1024]{1,0:T(4,128)S(1)}, f32[4,1024]{1,0:T(4,128)S(1)}, u32[]{:S(2)}, u32[]{:S(2)}) %collective-permute-start.20) | collective-permute-done | bytes 16416 | tf_op jit(solution)/shard_map/ppermute | solution.py:872
  75.6 8.9 %mix.2 = (f32[512,1024]{1,0:T(8,128)}, bf16[512,1024]{1,0:T(8,128)(2,1)}, f32[2,8,1024]{2,1,0:T(8,128)}, f32[512,512]{1,0:T(8,128)}, bf16[512,512]{1,0:T(8,128)(...) custom-call(bf16[512,512]{1,0:T(8,128)(2,1)S(1)} %bitcast.57, ...), custom_call_target="tpu_custom_call" | custom-call | flops 15400000512 | bytes 1024 | tf_op jit(solution)/shard_map/mix/pallas_call | solution.py:554
  86.2 6.7 %collective-permute-done.33.refs_3_ = bf16[4,384,128]{2,1,0:T(8,128)(2,1)S(1)} collective-permute-done((bf16[4,384,128]{2,1,0:T(8,128)(2,1)S(1)}, bf16[4,384,128]{2,1,0:T(8,128)(2,1)S(1)}, u32[]{:S(2)}, u32[]{:S(2)}) %collective-permute-start.33) | collective-permute-done | bytes 393248 | tf_op jit(solution)/shard_map/ppermute | solution.py:742
  95.5 6.5 %gates.3 = (bf16[512,512]{1,0:T(8,128)(2,1)}, f32[512,1024]{1,0:T(8,128)}, f32[512,1024]{1,0:T(8,128)S(1)}, f32[512,1024]{1,0:T(8,128)}, bf16[512,1024]{1,0:T(8,...) custom-call(f32[512,512]{1,0:T(8,128)S(1)} %get-tuple-element.212.x_, ...), custom_call_target="tpu_custom_call" | custom-call | flops 9900000256 | bytes 1024 | tf_op jit(solution)/shard_map/gates/pallas_call | solution.py:554
  107.9 3.7 %collective-permute-done.39 = f32[4,1024]{1,0:T(4,128)S(1)} collective-permute-done((f32[4,1024]{1,0:T(4,128)S(1)}, f32[4,1024]{1,0:T(4,128)S(1)}, u32[]{:S(2)}, u32[]{:S(2)}) %collective-permute-start.39) | collective-permute-done | bytes 16416 | tf_op jit(solution)/shard_map/ppermute | solution.py:872
  115.6 3.5 %collective-permute-done.41 = f32[4,1024]{1,0:T(4,128)S(1)} collective-permute-done((f32[4,1024]{1,0:T(4,128)S(1)}, f32[4,1024]{1,0:T(4,128)S(1)}, u32[]{:S(2)}, u32[]{:S(2)}) %collective-permute-start.41) | collective-permute-done | bytes 16416 | tf_op jit(solution)/shard_map/ppermute | solution.py:872
  124.1 3.4 %plane_gather.7 = bf16[4,2,2,2,640,128]{5,4,3,2,1,0:T(8,128)(2,1)S(1)} custom-call(s32[8]{0:T(128)S(1)} %stack.35.pos_ref, bf16[4,640,128]{2,1,0:T(8,128)(2,1)S(1)} %line_gather.7.refs_0_, bf16[4,640,128]{2,1,0:T(8,128)(2,1)S(1)} %collective-permute-done.42.refs_1_, bf16[4,640,128]{2,1,0:T(8,128)(2,1)S(1)} %collective-permute-done.40.refs_2_, ...), custom_call_target="tpu_custom_call" | custom-call | flops 5500000256 | bytes 1024 | tf_op jit(solution)/shard_map/plane_gather/pallas_call | solution.py:554
  127.5 7.3 %mix.3 = (f32[512,1024]{1,0:T(8,128)}, bf16[512,1024]{1,0:T(8,128)(2,1)S(1)}, f32[2,8,1024]{2,1,0:T(8,128)S(1)}, f32[512,512]{1,0:T(8,128)S(1)}, bf16[512,512]{1...) custom-call(f32[512,512]{1,0:T(8,128)S(1)} %copy-done.16, ...), custom_call_target="tpu_custom_call" | custom-call | flops 15400000512 | bytes 1024 | tf_op jit(solution)/shard_map/mix/pallas_call | solution.py:554
  134.8 7.0 %mlp_back.2 = (bf16[512,512]{1,0:T(8,128)(2,1)S(1)}, bf16[512,2048]{1,0:T(8,128)(2,1)S(1)}, f32[512,512]{1,0:T(8,128)S(1)}, bf16[512,512]{1,0:T(8,128)(2,1)S(1)}...) custom-call(bf16[512,512]{1,0:T(8,128)(2,1)S(1)} %bitcast.61, ...), custom_call_target="tpu_custom_call" | custom-call | flops 13200000000 | bytes 1024 | tf_op jit(solution)/shard_map/mlp_back/pallas_call | solution.py:554
  153.5 3.7 %collective-permute-done.49 = f32[4,1024]{1,0:T(4,128)S(1)} collective-permute-done((f32[4,1024]{1,0:T(4,128)S(1)}, f32[4,1024]{1,0:T(4,128)S(1)}, u32[]{:S(2)}, u32[]{:S(2)}) %collective-permute-start.49) | collective-permute-done | bytes 16416 | tf_op jit(solution)/shard_map/ppermute | solution.py:872
  158.7 3.5 %pair_sum.6 = (bf16[4,2,384,128]{3,2,1,0:T(8,128)(2,1)S(1)}, bf16[4,2,384,128]{3,2,1,0:T(8,128)(2,1)S(1)}) custom-call(s32[8]{0:T(128)S(1)} %stack.35.pos_ref, bf16[4,2,2,256,128]{4,3,2,1,0:T(8,128)(2,1)S(1)} %bitcast.103, bf16[4,2,2,128,128]{4,3,2,1,0:T(8,128)(2,1)S(1)} %bitcast.105, bf16[4,2,2,256,128]{4,3,2,1,0:T(8,128)(2,1)} %bitcast.26.refs_2_, ...), custom_call_target="tpu_custom_call" | custom-call | flops 3300000000 | bytes 1024 | tf_op jit(solution)/shard_map/pair_sum/pallas_call | solution.py:554
  162.3 8.3 %gate_back.2 = (bf16[8,2,384,128]{3,2,1,0:T(8,128)(2,1)S(1)}, bf16[8,2,384,128]{3,2,1,0:T(8,128)(2,1)S(1)}, f32[2,1024]{1,0:T(2,128)S(1)}, f32[512,512]{1,0:T(8,128)S(1)}, f32[1,512]{1,0:T(1,128)S(1)}) custom-call(s32[8]{0:T(128)S(1)} %stack.35.pos_ref, f32[512,512]{1,0:T(8,128)S(1)} %copy-done.17, f32[2,512]{1,0:T(2,128)S(1)} %get-tuple-element.213.gain_ref, ...), custom_call_target="tpu_custom_call" | custom-call | flops 17600000000 | bytes 1024 | tf_op jit(solution)/shard_map/gate_back/pallas_call | solution.py:554
  175.8 7.6 %mlp_back.3 = (bf16[512,512]{1,0:T(8,128)(2,1)S(1)}, bf16[512,2048]{1,0:T(8,128)(2,1)S(1)}, f32[512,512]{1,0:T(8,128)S(1)}, bf16[512,512]{1,0:T(8,128)(2,1)S(1)}...) custom-call(f32[512,512]{1,0:T(8,128)S(1)} %get-tuple-element.275.g_, ...), custom_call_target="tpu_custom_call" | custom-call | flops 13200000000 | bytes 1024 | tf_op jit(solution)/shard_map/mlp_back/pallas_call | solution.py:554
  205.5 9.0 %gate_back.3 = (bf16[8,2,400,128]{3,2,1,0:T(8,128)(2,1)S(1)}, bf16[8,2,400,128]{3,2,1,0:T(8,128)(2,1)S(1)}, f32[2,1024]{1,0:T(2,128)}, bf16[512,512]{1,0:T(8,128)(2,1)S(1)}, f32[1,512]{1,0:T(1,128)}) custom-call(s32[8]{0:T(128)S(1)} %stack.35.pos_ref, bf16[512,512]{1,0:T(8,128)(2,1)S(1)} %bitcast.58, f32[2,512]{1,0:T(2,128)S(1)} %get-tuple-element.196.gain_ref, ...), custom_call_target="tpu_custom_call" | custom-call | flops 17600000000 | bytes 1024 | tf_op jit(solution)/shard_map/gate_back/pallas_call | solution.py:554
  224.8 8.5 %collective-permute-done.67.got = bf16[2,768,128]{2,1,0:T(8,128)(2,1)S(1)} collective-permute-done((bf16[2,768,128]{2,1,0:T(8,128)(2,1)S(1)}, bf16[2,768,128]{2,1,0:T(8,128)(2,1)S(1)}, u32[]{:S(2)}, u32[]{:S(2)}) %collective-permute-start.67) | collective-permute-done | bytes 393248 | tf_op jit(solution)/shard_map/ppermute | solution.py:742
  236.6 4.1 %collective-permute-done.68.refs_1_ = bf16[4,2,384,128]{3,2,1,0:T(8,128)(2,1)S(1)} collective-permute-done((bf16[4,2,384,128]{3,2,1,0:T(8,128)(2,1)S(1)}, bf16[4,2,384,128]{3,2,1,0:T(8,128)(2,1)S(1)}, u32[]{:S(2)}, u32[]{:S(2)}) %collective-permute-start.68) | collective-permute-done | bytes 786464 | tf_op jit(solution)/shard_map/ppermute | solution.py:742
  252.2 4.4 %collective-permute-done.72.refs_1_ = bf16[1,2,256,128]{3,2,1,0:T(8,128)(2,1)S(1)} collective-permute-done((bf16[1,2,256,128]{3,2,1,0:T(8,128)(2,1)S(1)}, bf16[1,2,256,128]{3,2,1,0:T(8,128)(2,1)S(1)}, u32[]{:S(2)}, u32[]{:S(2)}) %collective-permute-start.72) | collective-permute-done | bytes 131104 | tf_op jit(solution)/shard_map/ppermute | solution.py:742
  266.0 4.1 %collective-permute-done.78.got = bf16[2,784,128]{2,1,0:T(8,128)(2,1)S(1)} collective-permute-done((bf16[2,784,128]{2,1,0:T(8,128)(2,1)S(1)}, bf16[2,784,128]{2,1,0:T(8,128)(2,1)S(1)}, u32[]{:S(2)}, u32[]{:S(2)}) %collective-permute-start.78) | collective-permute-done | bytes 401440 | tf_op jit(solution)/shard_map/ppermute | solution.py:742
  275.1 3.4 %collective-permute-done.79.refs_3_ = bf16[784,128]{1,0:T(8,128)(2,1)S(1)} collective-permute-done((bf16[784,128]{1,0:T(8,128)(2,1)S(1)}, bf16[784,128]{1,0:T(8,128)(2,1)S(1)}, u32[]{:S(2)}, u32[]{:S(2)}) %collective-permute-start.79) | collective-permute-done | bytes 200736 | tf_op jit(solution)/shard_map/ppermute | solution.py:742
  (260 shorter events, 145.8 us)
Async XLA Ops:
  21.7 12.8 %collective-permute-start.13 = (bf16[640,128]{1,0:T(8,128)(2,1)S(1)}, bf16[640,128]{1,0:T(8,128)(2,1)S(1)}, u32[]{:S(2)}, u32[]{:S(2)}) collective-permute-start(bf16[640,128]{1,0:T(8,128)(2,1)S(1)} %get-tuple-element.205.refs_0_), channel_id=1, source_target_pairs={{0,16},{4,20},{8,24},{12,28},{16,0},{20,4},{24,8},{28,12},{1,17},{... | collective-permute-start | bytes 491528 | tf_op jit(solution)/shard_map/ppermute | solution.py:715
  21.7 12.8 %collective-permute-start.12 = (bf16[640,128]{1,0:T(8,128)(2,1)S(1)}, bf16[640,128]{1,0:T(8,128)(2,1)S(1)}, u32[]{:S(2)}, u32[]{:S(2)}) collective-permute-start(bf16[640,128]{1,0:T(8,128)(2,1)S(1)} %get-tuple-element.205.refs_0_), channel_id=1, source_target_pairs={{0,8},{4,12},{8,0},{12,4},{16,24},{20,28},{24,16},{28,20},{1,9},{5... | collective-permute-start | bytes 491528 | tf_op jit(solution)/shard_map/ppermute | solution.py:715
  36.5 18.6 %collective-permute-start.22 = (bf16[4,640,128]{2,1,0:T(8,128)(2,1)S(1)}, bf16[4,640,128]{2,1,0:T(8,128)(2,1)S(1)}, u32[]{:S(2)}, u32[]{:S(2)}) collective-permute-start(bf16[4,640,128]{2,1,0:T(8,128)(2,1)S(1)} %line_gather.5.refs_0_), channel_id=1, source_target_pairs={{0,4},{1,3},{2,6},{3,1},{4,0},{5,7},{6,2},{7,5},{8,12},{9,11},{10,... | collective-permute-start | bytes 1966088 | tf_op jit(solution)/shard_map/ppermute | solution.py:742
  37.1 18.0 %collective-permute-start.21 = (bf16[4,640,128]{2,1,0:T(8,128)(2,1)S(1)}, bf16[4,640,128]{2,1,0:T(8,128)(2,1)S(1)}, u32[]{:S(2)}, u32[]{:S(2)}) collective-permute-start(bf16[4,640,128]{2,1,0:T(8,128)(2,1)S(1)} %line_gather.5.refs_0_), channel_id=1, source_target_pairs={{0,2},{1,5},{2,0},{3,7},{4,6},{5,1},{6,4},{7,3},{8,10},{9,13},{10,... | collective-permute-start | bytes 1966088 | tf_op jit(solution)/shard_map/ppermute | solution.py:742
  37.6 12.4 %collective-permute-start.17 = (bf16[384,128]{1,0:T(8,128)(2,1)S(1)}, bf16[384,128]{1,0:T(8,128)(2,1)S(1)}, u32[]{:S(2)}, u32[]{:S(2)}) collective-permute-start(bf16[384,128]{1,0:T(8,128)(2,1)S(1)} %get-tuple-element.207.refs_0_), channel_id=1, source_target_pairs={{0,24},{4,28},{8,16},{12,20},{16,8},{20,12},{24,0},{28,4},{1,25},{... | collective-permute-start | bytes 294920 | tf_op jit(solution)/shard_map/ppermute | solution.py:715
  65.9 18.5 %collective-permute-start.32 = (bf16[640,128]{1,0:T(8,128)(2,1)S(1)}, bf16[640,128]{1,0:T(8,128)(2,1)S(1)}, u32[]{:S(2)}, u32[]{:S(2)}) collective-permute-start(bf16[640,128]{1,0:T(8,128)(2,1)S(1)} %get-tuple-element.218.refs_0_), channel_id=1, source_target_pairs={{0,24},{4,28},{8,16},{12,20},{16,8},{20,12},{24,0},{28,4},{1,25},{... | collective-permute-start | bytes 491528 | tf_op jit(solution)/shard_map/ppermute | solution.py:715
  67.9 16.5 %collective-permute-start.31 = (bf16[640,128]{1,0:T(8,128)(2,1)S(1)}, bf16[640,128]{1,0:T(8,128)(2,1)S(1)}, u32[]{:S(2)}, u32[]{:S(2)}) collective-permute-start(bf16[640,128]{1,0:T(8,128)(2,1)S(1)} %get-tuple-element.218.refs_0_), channel_id=1, source_target_pairs={{0,16},{4,20},{8,24},{12,28},{16,0},{20,4},{24,8},{28,12},{1,17},{... | collective-permute-start | bytes 491528 | tf_op jit(solution)/shard_map/ppermute | solution.py:715
  67.9 16.5 %collective-permute-start.30 = (bf16[640,128]{1,0:T(8,128)(2,1)S(1)}, bf16[640,128]{1,0:T(8,128)(2,1)S(1)}, u32[]{:S(2)}, u32[]{:S(2)}) collective-permute-start(bf16[640,128]{1,0:T(8,128)(2,1)S(1)} %get-tuple-element.218.refs_0_), channel_id=1, source_target_pairs={{0,8},{4,12},{8,0},{12,4},{16,24},{20,28},{24,16},{28,20},{1,9},{5... | collective-permute-start | bytes 491528 | tf_op jit(solution)/shard_map/ppermute | solution.py:715
  70.3 15.4 %collective-permute-start.29 = (bf16[4,384,128]{2,1,0:T(8,128)(2,1)S(1)}, bf16[4,384,128]{2,1,0:T(8,128)(2,1)S(1)}, u32[]{:S(2)}, u32[]{:S(2)}) collective-permute-start(bf16[4,384,128]{2,1,0:T(8,128)(2,1)S(1)} %line_gather.6.refs_0_), channel_id=1, source_target_pairs={{0,4},{1,3},{2,6},{3,1},{4,0},{5,7},{6,2},{7,5},{8,12},{9,11},{10,... | collective-permute-start | bytes 1179656 | tf_op jit(solution)/shard_map/ppermute | solution.py:742
  71.8 13.2 %collective-permute-start.28 = (bf16[4,384,128]{2,1,0:T(8,128)(2,1)S(1)}, bf16[4,384,128]{2,1,0:T(8,128)(2,1)S(1)}, u32[]{:S(2)}, u32[]{:S(2)}) collective-permute-start(bf16[4,384,128]{2,1,0:T(8,128)(2,1)S(1)} %line_gather.6.refs_0_), channel_id=1, source_target_pairs={{0,2},{1,5},{2,0},{3,7},{4,6},{5,1},{6,4},{7,3},{8,10},{9,13},{10,... | collective-permute-start | bytes 1179656 | tf_op jit(solution)/shard_map/ppermute | solution.py:742
  92.9 12.5 %collective-permute-start.42 = (bf16[4,640,128]{2,1,0:T(8,128)(2,1)S(1)}, bf16[4,640,128]{2,1,0:T(8,128)(2,1)S(1)}, u32[]{:S(2)}, u32[]{:S(2)}) collective-permute-start(bf16[4,640,128]{2,1,0:T(8,128)(2,1)S(1)} %line_gather.7.refs_0_), channel_id=1, source_target_pairs={{0,2},{1,5},{2,0},{3,7},{4,6},{5,1},{6,4},{7,3},{8,10},{9,13},{10,... | collective-permute-start | bytes 1966088 | tf_op jit(solution)/shard_map/ppermute | solution.py:742
  107.1 14.5 %collective-permute-start.43 = (bf16[4,640,128]{2,1,0:T(8,128)(2,1)S(1)}, bf16[4,640,128]{2,1,0:T(8,128)(2,1)}, u32[]{:S(2)}, u32[]{:S(2)}) collective-permute-start(bf16[4,640,128]{2,1,0:T(8,128)(2,1)S(1)} %collective-permute-done.42.refs_1_), channel_id=1, source_target_pairs={{0,4},{1,3},{2,6},{3,1},{4,0},{5,7},{6,2},{7,5},{8,12},{9,11},{10,... | collective-permute-start | bytes 1966088 | tf_op jit(solution)/shard_map/ppermute | solution.py:742
  170.6 14.9 %collective-permute-start.56 = (bf16[2,1024,128]{2,1,0:T(8,128)(2,1)S(1)}, bf16[2,1024,128]{2,1,0:T(8,128)(2,1)S(1)}, u32[]{:S(2)}, u32[]{:S(2)}) collective-permute-start(bf16[2,1024,128]{2,1,0:T(8,128)(2,1)S(1)} %get-tuple-element.256), channel_id=1, source_target_pairs={{0,8},{1,17},{2,10},{3,19},{4,12},{5,21},{6,14},{7,23},{8,0},{9,25... | collective-permute-start | bytes 1572872 | tf_op jit(solution)/shard_map/ppermute | solution.py:742
  172.7 18.8 %collective-permute-start.57 = (bf16[4,2,384,128]{3,2,1,0:T(8,128)(2,1)S(1)}, bf16[4,2,384,128]{3,2,1,0:T(8,128)(2,1)S(1)}, u32[]{:S(2)}, u32[]{:S(2)}) collective-permute-start(bf16[4,2,384,128]{3,2,1,0:T(8,128)(2,1)S(1)} %get-tuple-element.258), channel_id=1, source_target_pairs={{0,2},{1,5},{2,0},{3,7},{4,6},{5,1},{6,4},{7,3},{8,10},{9,13},{10,... | collective-permute-start | bytes 2359304 | tf_op jit(solution)/shard_map/ppermute | solution.py:742
  175.1 18.0 %collective-permute-start.58 = (bf16[4,2,384,128]{3,2,1,0:T(8,128)(2,1)S(1)}, bf16[4,2,384,128]{3,2,1,0:T(8,128)(2,1)S(1)}, u32[]{:S(2)}, u32[]{:S(2)}) collective-permute-start(bf16[4,2,384,128]{3,2,1,0:T(8,128)(2,1)S(1)} %get-tuple-element.274), channel_id=1, source_target_pairs={{0,2},{1,5},{2,0},{3,7},{4,6},{5,1},{6,4},{7,3},{8,10},{9,13},{10,... | collective-permute-start | bytes 2359304 | tf_op jit(solution)/shard_map/ppermute | solution.py:742
  186.2 16.6 %collective-permute-start.60 = (bf16[1024,128]{1,0:T(8,128)(2,1)S(1)}, bf16[1024,128]{1,0:T(8,128)(2,1)S(1)}, u32[]{:S(2)}, u32[]{:S(2)}) collective-permute-start(bf16[1024,128]{1,0:T(8,128)(2,1)S(1)} %get-tuple-element.285), channel_id=1, source_target_pairs={{0,16},{1,9},{2,18},{3,11},{4,20},{5,13},{6,22},{7,15},{8,24},{9,1... | collective-permute-start | bytes 786440 | tf_op jit(solution)/shard_map/ppermute | solution.py:742
  200.2 14.3 %collective-permute-start.64 = (bf16[4,768,128]{2,1,0:T(8,128)(2,1)S(1)}, bf16[4,768,128]{2,1,0:T(8,128)(2,1)S(1)}, u32[]{:S(2)}, u32[]{:S(2)}) collective-permute-start(bf16[4,768,128]{2,1,0:T(8,128)(2,1)S(1)} %get-tuple-element.293), channel_id=1, source_target_pairs={{0,4},{1,3},{2,6},{3,1},{4,0},{5,7},{6,2},{7,5},{8,12},{9,11},{10,... | collective-permute-start | bytes 2359304 | tf_op jit(solution)/shard_map/ppermute | solution.py:742
  219.8 21.7 %collective-permute-start.69 = (bf16[4,2,400,128]{3,2,1,0:T(8,128)(2,1)S(1)}, bf16[4,2,400,128]{3,2,1,0:T(8,128)(2,1)S(1)}, u32[]{:S(2)}, u32[]{:S(2)}) collective-permute-start(bf16[4,2,400,128]{3,2,1,0:T(8,128)(2,1)S(1)} %get-tuple-element.333), channel_id=1, source_target_pairs={{0,2},{1,5},{2,0},{3,7},{4,6},{5,1},{6,4},{7,3},{8,10},{9,13},{10,... | collective-permute-start | bytes 2457608 | tf_op jit(solution)/shard_map/ppermute | solution.py:742
  220.5 20.2 %collective-permute-start.68 = (bf16[4,2,384,128]{3,2,1,0:T(8,128)(2,1)S(1)}, bf16[4,2,384,128]{3,2,1,0:T(8,128)(2,1)S(1)}, u32[]{:S(2)}, u32[]{:S(2)}) collective-permute-start(bf16[4,2,384,128]{3,2,1,0:T(8,128)(2,1)S(1)} %get-tuple-element.308), channel_id=1, source_target_pairs={{0,2},{1,5},{2,0},{3,7},{4,6},{5,1},{6,4},{7,3},{8,10},{9,13},{10,... | collective-permute-start | bytes 2359304 | tf_op jit(solution)/shard_map/ppermute | solution.py:742
  224.2 24.7 %collective-permute-start.71 = (bf16[2,1024,128]{2,1,0:T(8,128)(2,1)S(1)}, bf16[2,1024,128]{2,1,0:T(8,128)(2,1)S(1)}, u32[]{:S(2)}, u32[]{:S(2)}) collective-permute-start(bf16[2,1024,128]{2,1,0:T(8,128)(2,1)S(1)} %get-tuple-element.335), channel_id=1, source_target_pairs={{0,8},{1,17},{2,10},{3,19},{4,12},{5,21},{6,14},{7,23},{8,0},{9,25... | collective-permute-start | bytes 1572872 | tf_op jit(solution)/shard_map/ppermute | solution.py:742
  234.0 13.4 %collective-permute-start.70 = (bf16[768,128]{1,0:T(8,128)(2,1)S(1)}, bf16[768,128]{1,0:T(8,128)(2,1)S(1)}, u32[]{:S(2)}, u32[]{:S(2)}) collective-permute-start(bf16[768,128]{1,0:T(8,128)(2,1)S(1)} %get-tuple-element.340), channel_id=1, source_target_pairs={{0,16},{1,9},{2,18},{3,11},{4,20},{5,13},{6,22},{7,15},{8,24},{9,1... | collective-permute-start | bytes 589832 | tf_op jit(solution)/shard_map/ppermute | solution.py:742
  242.4 14.8 %collective-permute-start.74 = (bf16[4,400,128]{2,1,0:T(8,128)(2,1)S(1)}, bf16[4,400,128]{2,1,0:T(8,128)(2,1)S(1)}, u32[]{:S(2)}, u32[]{:S(2)}) collective-permute-start(bf16[4,400,128]{2,1,0:T(8,128)(2,1)S(1)} %get-tuple-element.344), channel_id=1, source_target_pairs={{0,4},{1,3},{2,6},{3,1},{4,0},{5,7},{6,2},{7,5},{8,12},{9,11},{10,... | collective-permute-start | bytes 1228808 | tf_op jit(solution)/shard_map/ppermute | solution.py:742
  243.9 13.3 %collective-permute-start.73 = (bf16[4,384,128]{2,1,0:T(8,128)(2,1)S(1)}, bf16[4,384,128]{2,1,0:T(8,128)(2,1)S(1)}, u32[]{:S(2)}, u32[]{:S(2)}) collective-permute-start(bf16[4,384,128]{2,1,0:T(8,128)(2,1)S(1)} %get-tuple-element.342), channel_id=1, source_target_pairs={{0,4},{1,3},{2,6},{3,1},{4,0},{5,7},{6,2},{7,5},{8,12},{9,11},{10,... | collective-permute-start | bytes 1179656 | tf_op jit(solution)/shard_map/ppermute | solution.py:742
  257.9 12.1 %collective-permute-start.78 = (bf16[2,784,128]{2,1,0:T(8,128)(2,1)S(1)}, bf16[2,784,128]{2,1,0:T(8,128)(2,1)S(1)}, u32[]{:S(2)}, u32[]{:S(2)}) collective-permute-start(bf16[2,784,128]{2,1,0:T(8,128)(2,1)S(1)} %get-tuple-element.357), channel_id=1, source_target_pairs={{0,8},{1,17},{2,10},{3,19},{4,12},{5,21},{6,14},{7,23},{8,0},{9,25... | collective-permute-start | bytes 1204232 | tf_op jit(solution)/shard_map/ppermute | solution.py:742
  (81 other events, 536.0 us)
